TPU v7x, 128 devices: a whole 4x4x4 slice. The times are simulated.
128 devices in a mesh: section: 2 (over core), ctx: 4 (over x), fsdp: 16 (over z, y).
Axes of the slice: x: 4, y: 4, z: 4, core: 2. Of those that a mesh axis runs over, the one named last changes fastest.
Arguments:
- inputs: bfloat16 [32, 1024, 768], P('fsdp', 'ctx'), may hold values from -6 to 6
- cotangent: bfloat16 [32, 1024, 768], P('fsdp', 'ctx'), may hold values from -6 to 6
- lengths: int32 [32], P('fsdp'), may hold values from 256 to 1024, as said below
- routes: int32 [2, 32, 1024, 2], P('section', 'fsdp', 'ctx'), may hold values from 0 to 2, all different within a row; in each aligned block of 256 rows (0 to 255, 256 to 511, ..., all dimensions but the last counted through in order) at most 208 rows name the same one
- step_count: int32 [1], replicated, may hold values from 1 to 20
- norm_gains: float32 [2, 2, 768], P('section', None, 'fsdp'), may hold values from 0.5 to 1.5
- gains_mean: float32 [2, 2, 768], P('section', None, 'fsdp'), may hold values from -0.0390625 to 0.0390625
- gains_square: float32 [2, 2, 768], P('section', None, 'fsdp'), may hold values from 3.4244793e-05 to 0.00013704428
- attn_weight: float32 [2, 768, 3072], P('section', 'fsdp')
- attn_mean: float32 [2, 768, 3072], P('section', 'fsdp'), may hold values from -0.0009765625 to 0.0009765625
- attn_square: float32 [2, 768, 3072], P('section', 'fsdp'), may hold values from 2.2294786e-08 to 8.922153e-08
- router_weight: float32 [2, 768, 3], P('section', 'fsdp'), may hold values from -0.4375 to 0.4375
- router_mean: float32 [2, 768, 3], P('section', 'fsdp'), may hold values from -0.03125 to 0.03125
- router_square: float32 [2, 768, 3], P('section', 'fsdp'), may hold values from 2.2829861e-05 to 9.136285e-05
- expert_in: float32 [2, 4, 768, 2, 2048], P('section', None, None, None, 'fsdp'), may hold values from -0.21875 to 0.21875
- in_mean: float32 [2, 4, 768, 2, 2048], P('section', None, None, None, 'fsdp'), may hold values from -0.00048828125 to 0.00048828125
- in_square: float32 [2, 4, 768, 2, 2048], P('section', None, None, None, 'fsdp'), may hold values from 4.1802726e-09 to 1.6729038e-08
- expert_out: float32 [2, 4, 2048, 768], P('section', None, 'fsdp'), may hold values from -0.125 to 0.125
- out_mean: float32 [2, 4, 2048, 768], P('section', None, 'fsdp'), may hold values from -0.00061035156 to 0.00061035156
- out_square: float32 [2, 4, 2048, 768], P('section', None, 'fsdp'), may hold values from 8.360545e-09 to 3.3458075e-08
Outputs:
- layer_outputs: bfloat16 [2, 32, 1024, 768], P('section', 'fsdp', 'ctx')
- input_grads: float32 [2, 32, 1024, 768], P('section', 'fsdp', 'ctx')
- gains_grad: float32 [2, 2, 768], P('section', None, 'fsdp')
- gains_mean_new: float32 [2, 2, 768], P('section', None, 'fsdp')
- gains_square_new: float32 [2, 2, 768], P('section', None, 'fsdp')
- gains_master: float32 [2, 2, 768], P('section', None, 'fsdp')
- gains_copy: bfloat16 [2, 2, 768], P('section', None, 'fsdp')
- attn_grad: float32 [2, 768, 3072], P('section', 'fsdp')
- attn_mean_new: float32 [2, 768, 3072], P('section', 'fsdp')
- attn_square_new: float32 [2, 768, 3072], P('section', 'fsdp')
- attn_master: float32 [2, 768, 3072], P('section', 'fsdp')
- attn_copy: bfloat16 [2, 768, 3072], P('section', 'fsdp')
- router_grad: float32 [2, 768, 3], P('section', 'fsdp')
- router_mean_new: float32 [2, 768, 3], P('section', 'fsdp')
- router_square_new: float32 [2, 768, 3], P('section', 'fsdp')
- router_master: float32 [2, 768, 3], P('section', 'fsdp')
- router_copy: bfloat16 [2, 768, 3], P('section', 'fsdp')
- in_grad: float32 [2, 4, 768, 2, 2048], P('section', None, None, None, 'fsdp')
- in_mean_new: float32 [2, 4, 768, 2, 2048], P('section', None, None, None, 'fsdp')
- in_square_new: float32 [2, 4, 768, 2, 2048], P('section', None, None, None, 'fsdp')
- in_master: float32 [2, 4, 768, 2, 2048], P('section', None, None, None, 'fsdp')
- in_copy: bfloat16 [2, 4, 768, 2, 2048], P('section', None, None, None, 'fsdp')
- out_grad: float32 [2, 4, 2048, 768], P('section', None, 'fsdp')
- out_mean_new: float32 [2, 4, 2048, 768], P('section', None, 'fsdp')
- out_square_new: float32 [2, 4, 2048, 768], P('section', None, 'fsdp')
- out_master: float32 [2, 4, 2048, 768], P('section', None, 'fsdp')
- out_copy: bfloat16 [2, 4, 2048, 768], P('section', None, 'fsdp')
- clip_norms: float32 [2, 5], P('section')
Inputs may be any that keep to these rules, and one draw needn't show every extreme that they name: One of the 32 lengths is 1024 in every draw. `routes`: each position names two different experts; among the 256 positions of one aligned block of a sequence row in one layer, no expert is named more than 208 times.
All inputs are finite; a program needn't handle non-finite values.
Results may differ from a plain program's by a relative error of at most 0.03.
Values may be sent and summed in bfloat16 or wider, within the bound.
A program may use at most 512 MiB of HBM per device.

v0:
```python
import jax
import jax.numpy as jnp
from jax import lax
from jax.sharding import PartitionSpec as P

D = 768
HEADS = 12
HEAD_DIM = 64
FFN = 2048
EXPERTS = 3
CAP = 208


EPS_NORM = 1e-06
BETA_ONE = 0.9
BETA_TWO = 0.95
RATE_FACTOR = 3.0
GAIN_RATE = 0.3
DECAY_RATE = 0.1
ADAM_EPS = 1e-08
CLIP_LIMIT = 1.0
MASK_VALUE = -1e30


def passed_along(block, axis, distance):
    devices = range(lax.axis_size(axis))
    route = [(i - distance, i) for i in devices if i - distance in devices]
    return lax.ppermute(block, axis, route)


def rotate(values, positions, direction):
    half_dim = HEAD_DIM // 2
    frequency = jnp.exp(
        -jnp.log(10000.0) * (2.0 * jnp.arange(half_dim, dtype=jnp.float32) / HEAD_DIM)
    )
    angles = positions.astype(jnp.float32)[:, None] * frequency[None, :]
    cosine = jnp.cos(angles)[:, None, :]
    sine_part = direction * jnp.sin(angles)[:, None, :]
    first_half = values[:, :, :half_dim]
    second_half = values[:, :, half_dim:]
    return jnp.concatenate(
        [
            first_half * cosine - second_half * sine_part,
            second_half * cosine + first_half * sine_part,
        ],
        axis=2,
    )


def slot_index(route_rows):
    flat_routes = route_rows.reshape(-1)
    onehot = (flat_routes[:, None] == jnp.arange(EXPERTS, dtype=jnp.int32)[None, :]).astype(
        jnp.int32
    )
    before = jnp.cumsum(onehot, axis=0) - onehot
    return flat_routes * CAP + jnp.sum(before * onehot, axis=1)


def score_block(queries, key_heads, positions, length):
    key_pos = jnp.arange(key_heads.shape[0], dtype=jnp.int32)
    scores = jnp.einsum(
        "qhd,khd->hqk", queries, key_heads, preferred_element_type=jnp.float32
    ) * HEAD_DIM ** (-0.5)
    allowed = (key_pos[None, :] <= positions[:, None]) & (key_pos[None, :] < length)
    return jnp.where(allowed[None], scores, MASK_VALUE)


def swiglu(hidden_pre):
    return (jax.nn.silu(hidden_pre[..., 0, :]) * hidden_pre[..., 1, :]).astype(jnp.bfloat16)


def swiglu_grad(hidden_pre, act_grad):
    gate_part = hidden_pre[..., 0, :]
    up_part = hidden_pre[..., 1, :]
    sigmoid_part = jax.nn.sigmoid(gate_part)
    gate_grad = act_grad * up_part * sigmoid_part * (1.0 + gate_part * (1.0 - sigmoid_part))
    up_grad = act_grad * gate_part * sigmoid_part
    return jnp.stack([gate_grad, up_grad], axis=-2).astype(jnp.bfloat16)


def expert_forward(weight_in, weight_out, buffer, second):
    hidden_pre = jnp.einsum(
        "pecd,edgf->pecgf", buffer, weight_in[:EXPERTS], preferred_element_type=jnp.float32
    )
    acted = swiglu(hidden_pre)
    slot_out = jnp.einsum(
        "pecf,efd->pecd", acted, weight_out[:EXPERTS], preferred_element_type=jnp.float32
    )
    shared_pre = jnp.einsum(
        "pnd,dgf->pngf", second, weight_in[EXPERTS], preferred_element_type=jnp.float32
    )
    shared_act = swiglu(shared_pre)
    shared_out = jnp.einsum(
        "pnf,fd->pnd", shared_act, weight_out[EXPERTS], preferred_element_type=jnp.float32
    )
    return (slot_out, shared_out, (hidden_pre, acted, shared_pre, shared_act))


def expert_backward(weight_in, weight_out, buffer, second, expert_kept, slot_grad, shared_grad):
    hidden_pre, acted, shared_pre, shared_act = expert_kept
    act_grad = jnp.einsum(
        "pecd,efd->pecf", slot_grad, weight_out[:EXPERTS], preferred_element_type=jnp.float32
    )
    out_experts = jnp.einsum("pecf,pecd->efd", acted, slot_grad, preferred_element_type=jnp.float32)
    pre_grad = swiglu_grad(hidden_pre, act_grad)
    in_experts = jnp.einsum(
        "pecd,pecgf->edgf", buffer, pre_grad, preferred_element_type=jnp.float32
    )
    buffer_grad = jnp.einsum(
        "pecgf,edgf->pecd", pre_grad, weight_in[:EXPERTS], preferred_element_type=jnp.float32
    )
    shared_act_grad = jnp.einsum(
        "pnd,fd->pnf", shared_grad, weight_out[EXPERTS], preferred_element_type=jnp.float32
    )
    out_shared = jnp.einsum(
        "pnf,pnd->fd", shared_act, shared_grad, preferred_element_type=jnp.float32
    )
    shared_pre_grad = swiglu_grad(shared_pre, shared_act_grad)
    in_shared = jnp.einsum(
        "pnd,pngf->dgf", second, shared_pre_grad, preferred_element_type=jnp.float32
    )
    second_grad = jnp.einsum(
        "pngf,dgf->pnd", shared_pre_grad, weight_in[EXPERTS], preferred_element_type=jnp.float32
    )
    in_grad = jnp.concatenate([in_experts, in_shared[None]], axis=0)
    out_grad = jnp.concatenate([out_experts, out_shared[None]], axis=0)
    return (buffer_grad, second_grad, in_grad, out_grad)


def layer_forward(weights, tokens_in, length, route_rows, offset):
    gain_pair, attn_w, router_w, weight_in, weight_out = weights
    seq_rows = tokens_in.shape[0]
    positions = offset + jnp.arange(seq_rows, dtype=jnp.int32)
    scale_one = lax.rsqrt(jnp.mean(tokens_in * tokens_in, axis=1, keepdims=True) + EPS_NORM)
    normed = (tokens_in * scale_one * gain_pair[0].astype(jnp.float32)).astype(jnp.bfloat16)
    mixed_rows = jnp.dot(normed, attn_w[:, : 3 * D], preferred_element_type=jnp.float32)
    queries = rotate(mixed_rows[:, :D].reshape(seq_rows, HEADS, HEAD_DIM), positions, 1.0).astype(
        jnp.bfloat16
    )
    keys_local = (
        rotate(mixed_rows[:, D : 2 * D].reshape(seq_rows, HEADS, HEAD_DIM), positions, 1.0)
        .astype(jnp.bfloat16)
        .reshape(seq_rows, D)
    )
    values_local = mixed_rows[:, 2 * D :].astype(jnp.bfloat16)
    key_all, value_all = (
        lax.all_gather(keys_local, "ctx", axis=0, tiled=True),
        lax.all_gather(values_local, "ctx", axis=0, tiled=True),
    )
    total_rows = key_all.shape[0]
    key_heads = key_all.reshape(total_rows, HEADS, HEAD_DIM)
    value_heads = value_all.reshape(total_rows, HEADS, HEAD_DIM)
    scores = score_block(queries, key_heads, positions, length)
    top_score = jnp.max(scores, axis=2, keepdims=True)
    weights_raw = jnp.exp(scores - top_score)
    total_mass = jnp.sum(weights_raw, axis=2, keepdims=True)
    probs_low = (weights_raw / total_mass).astype(jnp.bfloat16)
    log_mass = top_score + jnp.log(total_mass)
    attended = (
        jnp.einsum("hqk,khd->qhd", probs_low, value_heads, preferred_element_type=jnp.float32)
        .reshape(seq_rows, D)
        .astype(jnp.bfloat16)
    )
    residual = tokens_in + jnp.dot(attended, attn_w[:, 3 * D :], preferred_element_type=jnp.float32)
    scale_two = lax.rsqrt(jnp.mean(residual * residual, axis=1, keepdims=True) + EPS_NORM)
    second = (residual * scale_two * gain_pair[1].astype(jnp.float32)).astype(jnp.bfloat16)
    logits = jnp.dot(second, router_w, preferred_element_type=jnp.float32)
    chosen = jnp.take_along_axis(logits, route_rows, axis=1)
    chosen_top = jnp.max(chosen, axis=1, keepdims=True)
    chosen_raw = jnp.exp(chosen - chosen_top)
    gate_probs = chosen_raw / jnp.sum(chosen_raw, axis=1, keepdims=True)
    slot_ids = slot_index(route_rows)
    buffer = (
        jnp.zeros((EXPERTS * CAP, D), jnp.bfloat16).at[slot_ids].set(jnp.repeat(second, 2, axis=0))
    )
    expert_buffer = buffer.reshape(1, EXPERTS, CAP, D)
    expert_second = second[None]
    slot_out, shared_out, expert_kept = expert_forward(
        weight_in, weight_out, expert_buffer, expert_second
    )
    slot_rows = slot_out.reshape(EXPERTS * CAP, D)
    shared_rows = shared_out[0]
    picked = slot_rows[slot_ids].reshape(seq_rows, 2, D)
    output = residual + jnp.sum(picked * gate_probs[:, :, None], axis=1) + shared_rows
    saved_state = (
        tokens_in,
        scale_one,
        normed,
        queries,
        key_heads,
        value_heads,
        log_mass,
        attended,
        residual,
        scale_two,
        second,
        gate_probs,
        slot_ids,
        slot_rows,
        expert_buffer,
        expert_second,
        expert_kept,
        positions,
    )
    return (output, saved_state)


def layer_backward(weights, saved_state, grad_out, length, route_rows):
    gain_pair, attn_w, router_w, weight_in, weight_out = weights
    (
        tokens_in,
        scale_one,
        normed,
        queries,
        key_heads,
        value_heads,
        log_mass,
        attended,
        residual,
        scale_two,
        second,
        gate_probs,
        slot_ids,
        slot_rows,
        expert_buffer,
        expert_second,
        expert_kept,
        positions,
    ) = saved_state
    seq_rows = grad_out.shape[0]
    slot_grad = (
        jnp.zeros((EXPERTS * CAP, D), jnp.float32)
        .at[slot_ids]
        .set((gate_probs[:, :, None] * grad_out[:, None, :]).reshape(-1, D))
        .astype(jnp.bfloat16)
    )
    shared_grad = grad_out.astype(jnp.bfloat16)
    gate_grad = jnp.sum(slot_rows[slot_ids].reshape(seq_rows, 2, D) * grad_out[:, None, :], axis=2)
    buffer_grad, second_part, in_grad, out_grad = expert_backward(
        weight_in,
        weight_out,
        expert_buffer,
        expert_second,
        expert_kept,
        slot_grad.reshape(1, EXPERTS, CAP, D),
        shared_grad[None],
    )
    buffer_rows = buffer_grad.reshape(EXPERTS * CAP, D)
    second_grad = second_part[0]
    second_grad = second_grad + jnp.sum(buffer_rows[slot_ids].reshape(seq_rows, 2, D), axis=1)
    chosen_grad = gate_probs * (gate_grad - jnp.sum(gate_probs * gate_grad, axis=1, keepdims=True))
    expert_ids = jnp.arange(EXPERTS, dtype=jnp.int32)
    logit_grad = jnp.sum(
        chosen_grad[:, :, None]
        * (route_rows[:, :, None] == expert_ids[None, None, :]).astype(jnp.float32),
        axis=1,
    ).astype(jnp.bfloat16)
    router_grad = jnp.einsum("nd,ne->de", second, logit_grad, preferred_element_type=jnp.float32)
    second_grad = second_grad + jnp.einsum(
        "ne,de->nd", logit_grad, router_w, preferred_element_type=jnp.float32
    )
    normal_two = residual * scale_two
    gain_two_grad = jnp.sum(second_grad * normal_two, axis=0)
    scaled_two = second_grad * gain_pair[1].astype(jnp.float32)
    residual_grad = grad_out + scale_two * (
        scaled_two - normal_two * jnp.mean(scaled_two * normal_two, axis=1, keepdims=True)
    )
    branch_grad = residual_grad.astype(jnp.bfloat16)
    attn_out_grad = jnp.einsum(
        "nc,nd->cd", attended, branch_grad, preferred_element_type=jnp.float32
    )
    attended_grad = (
        jnp.einsum("nd,cd->nc", branch_grad, attn_w[:, 3 * D :], preferred_element_type=jnp.float32)
        .astype(jnp.bfloat16)
        .reshape(seq_rows, HEADS, HEAD_DIM)
    )
    scores = score_block(queries, key_heads, positions, length)
    prob_full = jnp.exp(scores - log_mass)
    prob_grad = jnp.einsum(
        "qhd,khd->hqk", attended_grad, value_heads, preferred_element_type=jnp.float32
    )
    value_part = jnp.einsum(
        "hqk,qhd->khd",
        prob_full.astype(jnp.bfloat16),
        attended_grad,
        preferred_element_type=jnp.float32,
    )
    delta_rows = jnp.sum(prob_full * prob_grad, axis=2, keepdims=True)
    score_grad = (prob_full * (prob_grad - delta_rows)).astype(jnp.bfloat16)
    score_scale = HEAD_DIM ** (-0.5)
    query_grad = (
        jnp.einsum("hqk,khd->qhd", score_grad, key_heads, preferred_element_type=jnp.float32)
        * score_scale
    )
    key_part = (
        jnp.einsum("hqk,qhd->khd", score_grad, queries, preferred_element_type=jnp.float32)
        * score_scale
    )
    total_rows = key_heads.shape[0]
    key_grad, value_grad = (
        lax.psum_scatter(
            key_part.reshape(total_rows, D).astype(jnp.bfloat16),
            "ctx",
            scatter_dimension=0,
            tiled=True,
        ).astype(jnp.float32),
        lax.psum_scatter(
            value_part.reshape(total_rows, D).astype(jnp.bfloat16),
            "ctx",
            scatter_dimension=0,
            tiled=True,
        ).astype(jnp.float32),
    )
    mixed_grad = jnp.concatenate(
        [
            rotate(query_grad, positions, -1.0).reshape(seq_rows, D),
            rotate(key_grad.reshape(seq_rows, HEADS, HEAD_DIM), positions, -1.0).reshape(
                seq_rows, D
            ),
            value_grad,
        ],
        axis=1,
    ).astype(jnp.bfloat16)
    attn_in_grad = jnp.einsum("nd,nc->dc", normed, mixed_grad, preferred_element_type=jnp.float32)
    normed_grad = jnp.einsum(
        "nc,dc->nd", mixed_grad, attn_w[:, : 3 * D], preferred_element_type=jnp.float32
    )
    normal_one = tokens_in * scale_one
    gain_one_grad = jnp.sum(normed_grad * normal_one, axis=0)
    scaled_one = normed_grad * gain_pair[0].astype(jnp.float32)
    input_grad = residual_grad + scale_one * (
        scaled_one - normal_one * jnp.mean(scaled_one * normal_one, axis=1, keepdims=True)
    )
    layer_grads = (
        jnp.stack([gain_one_grad, gain_two_grad]),
        jnp.concatenate([attn_in_grad, attn_out_grad], axis=1),
        router_grad,
        in_grad,
        out_grad,
    )
    return (input_grad, layer_grads)


def adam_update(gradient, clipped, master, mean_old, square_old, step_value, learn_rate):
    mean_new = BETA_ONE * mean_old + (1.0 - BETA_ONE) * clipped
    square_new = BETA_TWO * square_old + (1.0 - BETA_TWO) * clipped * clipped
    fix_one = 1.0 - BETA_ONE**step_value
    fix_two = 1.0 - BETA_TWO**step_value
    master_new = master - learn_rate * (
        mean_new / fix_one / (jnp.sqrt(square_new / fix_two) + ADAM_EPS) + DECAY_RATE * master
    )
    return (gradient, mean_new, square_new, master_new, master_new.astype(jnp.bfloat16))


def on_device(
    inputs,
    cotangent,
    lengths,
    routes,
    step_count,
    norm_gains,
    gains_mean,
    gains_square,
    attn_weight,
    attn_mean,
    attn_square,
    router_weight,
    router_mean,
    router_square,
    expert_in,
    in_mean,
    in_square,
    expert_out,
    out_mean,
    out_square,
):
    low_gains, low_attn, low_router, low_in, low_out = (
        lax.all_gather(norm_gains.astype(jnp.bfloat16), "fsdp", axis=2, tiled=True),
        lax.all_gather(attn_weight.astype(jnp.bfloat16), "fsdp", axis=1, tiled=True),
        lax.all_gather(router_weight.astype(jnp.bfloat16), "fsdp", axis=1, tiled=True),
        lax.all_gather(expert_in.astype(jnp.bfloat16), "fsdp", axis=4, tiled=True),
        lax.all_gather(expert_out.astype(jnp.bfloat16), "fsdp", axis=2, tiled=True),
    )
    weights = (low_gains[0], low_attn[0], low_router[0], low_in[0], low_out[0])
    section_index = lax.axis_index("section")
    ctx_index = lax.axis_index("ctx")
    micro_count = inputs.shape[0]
    seq_rows = inputs.shape[1]
    offset = ctx_index * seq_rows
    arriving = jnp.zeros((seq_rows, D), jnp.bfloat16)
    produced = []
    records = []
    for period in range(micro_count + 1):
        micro_index = jnp.clip(period - section_index, 0, micro_count - 1)
        own_rows = lax.dynamic_index_in_dim(inputs, micro_index, 0, keepdims=False)
        layer_in = jnp.where(section_index == 0, own_rows, arriving).astype(jnp.float32)
        length = lax.dynamic_index_in_dim(lengths, micro_index, 0, keepdims=False)
        route_rows = lax.dynamic_index_in_dim(routes[0], micro_index, 0, keepdims=False)
        output, saved_state = layer_forward(weights, layer_in, length, route_rows, offset)
        sending = output.astype(jnp.bfloat16)
        produced.append(sending)
        records.append((saved_state, length, route_rows, micro_index))
        if period < micro_count:
            arriving = passed_along(sending, "section", 1)
    layer_outputs = lax.dynamic_slice_in_dim(jnp.stack(produced), section_index, micro_count, 0)[
        None
    ]
    returning = jnp.zeros((seq_rows, D), jnp.bfloat16)
    local_pos = offset + jnp.arange(seq_rows, dtype=jnp.int32)
    grad_totals = None
    input_list = []
    for period in range(micro_count + 1):
        saved_state, length, route_rows, micro_index = records[micro_count - period]
        live_flag = jnp.where(section_index == 1, period < micro_count, period >= 1).astype(
            jnp.float32
        )
        cot_rows = (
            lax.dynamic_index_in_dim(cotangent, micro_index, 0, keepdims=False).astype(jnp.float32)
            * (local_pos < length).astype(jnp.float32)[:, None]
        )
        grad_out = (
            jnp.where(section_index == 1, cot_rows, returning.astype(jnp.float32)) * live_flag
        )
        input_grad, layer_grads = layer_backward(weights, saved_state, grad_out, length, route_rows)
        if grad_totals is None:
            grad_totals = layer_grads
        else:
            grad_totals = tuple(
                (left_sum + right_sum for left_sum, right_sum in zip(grad_totals, layer_grads))
            )
        input_list.append(input_grad)
        if period < micro_count:
            returning = passed_along(input_grad.astype(jnp.bfloat16), "section", -1)
    input_grads = lax.dynamic_slice_in_dim(
        jnp.stack(input_list[::-1]), section_index, micro_count, 0
    )[None]
    gain_total, attn_total, router_total, in_total, out_total = grad_totals
    gain_part, attn_part, router_part, in_part, out_part = (
        lax.psum_scatter(
            gain_total[None].astype(jnp.bfloat16), "fsdp", scatter_dimension=2, tiled=True
        ).astype(jnp.float32),
        lax.psum_scatter(
            attn_total[None].astype(jnp.bfloat16), "fsdp", scatter_dimension=1, tiled=True
        ).astype(jnp.float32),
        lax.psum_scatter(
            router_total[None].astype(jnp.bfloat16), "fsdp", scatter_dimension=1, tiled=True
        ).astype(jnp.float32),
        lax.psum_scatter(
            in_total[None].astype(jnp.bfloat16), "fsdp", scatter_dimension=4, tiled=True
        ).astype(jnp.float32),
        lax.psum_scatter(
            out_total[None].astype(jnp.bfloat16), "fsdp", scatter_dimension=2, tiled=True
        ).astype(jnp.float32),
    )
    gain_sum, attn_sum, router_sum, in_sum, out_sum = (
        lax.psum(gain_part.astype(jnp.bfloat16), "ctx").astype(jnp.float32),
        lax.psum(attn_part.astype(jnp.bfloat16), "ctx").astype(jnp.float32),
        lax.psum(router_part.astype(jnp.bfloat16), "ctx").astype(jnp.float32),
        lax.psum(in_part.astype(jnp.bfloat16), "ctx").astype(jnp.float32),
        lax.psum(out_part.astype(jnp.bfloat16), "ctx").astype(jnp.float32),
    )
    square_sums = lax.psum(
        (
            jnp.sum(gain_sum * gain_sum),
            jnp.sum(attn_sum * attn_sum),
            jnp.sum(router_sum * router_sum),
            jnp.sum(in_sum * in_sum),
            jnp.sum(out_sum * out_sum),
        ),
        "fsdp",
    )
    norm_list = [jnp.sqrt(square_value) for square_value in square_sums]
    factors = [jnp.minimum(1.0, CLIP_LIMIT / norm_value) for norm_value in norm_list]
    clip_norms = jnp.stack(norm_list)[None]
    step_value = step_count[0].astype(jnp.float32)
    wide_rate = RATE_FACTOR / D**0.5
    router_rate = RATE_FACTOR / (D // 4) ** 0.5
    down_rate = RATE_FACTOR / FFN**0.5
    gains_grad, gains_mean_new, gains_square_new, gains_master, gains_copy = adam_update(
        gain_sum, gain_sum * factors[0], norm_gains, gains_mean, gains_square, step_value, GAIN_RATE
    )
    attn_grad, attn_mean_new, attn_square_new, attn_master, attn_copy = adam_update(
        attn_sum, attn_sum * factors[1], attn_weight, attn_mean, attn_square, step_value, wide_rate
    )
    router_grad, router_mean_new, router_square_new, router_master, router_copy = adam_update(
        router_sum,
        router_sum * factors[2],
        router_weight,
        router_mean,
        router_square,
        step_value,
        router_rate,
    )
    in_grad, in_mean_new, in_square_new, in_master, in_copy = adam_update(
        in_sum, in_sum * factors[3], expert_in, in_mean, in_square, step_value, wide_rate
    )
    out_grad, out_mean_new, out_square_new, out_master, out_copy = adam_update(
        out_sum, out_sum * factors[4], expert_out, out_mean, out_square, step_value, down_rate
    )
    return (
        layer_outputs,
        input_grads,
        gains_grad,
        gains_mean_new,
        gains_square_new,
        gains_master,
        gains_copy,
        attn_grad,
        attn_mean_new,
        attn_square_new,
        attn_master,
        attn_copy,
        router_grad,
        router_mean_new,
        router_square_new,
        router_master,
        router_copy,
        in_grad,
        in_mean_new,
        in_square_new,
        in_master,
        in_copy,
        out_grad,
        out_mean_new,
        out_square_new,
        out_master,
        out_copy,
        clip_norms,
    )


def solution(mesh):
    placed = (
        P("fsdp", "ctx", None),
        P("fsdp", "ctx", None),
        P("fsdp"),
        P("section", "fsdp", "ctx", None),
        P(),
        P("section", None, "fsdp"),
        P("section", None, "fsdp"),
        P("section", None, "fsdp"),
        P("section", "fsdp", None),
        P("section", "fsdp", None),
        P("section", "fsdp", None),
        P("section", "fsdp", None),
        P("section", "fsdp", None),
        P("section", "fsdp", None),
        P("section", None, None, None, "fsdp"),
        P("section", None, None, None, "fsdp"),
        P("section", None, None, None, "fsdp"),
        P("section", None, "fsdp", None),
        P("section", None, "fsdp", None),
        P("section", None, "fsdp", None),
    )
    return jax.shard_map(
        on_device,
        mesh=mesh,
        in_specs=placed,
        out_specs=(
            P("section", "fsdp", "ctx", None),
            P("section", "fsdp", "ctx", None),
            P("section", None, "fsdp"),
            P("section", None, "fsdp"),
            P("section", None, "fsdp"),
            P("section", None, "fsdp"),
            P("section", None, "fsdp"),
            P("section", "fsdp", None),
            P("section", "fsdp", None),
            P("section", "fsdp", None),
            P("section", "fsdp", None),
            P("section", "fsdp", None),
            P("section", "fsdp", None),
            P("section", "fsdp", None),
            P("section", "fsdp", None),
            P("section", "fsdp", None),
            P("section", "fsdp", None),
            P("section", None, None, None, "fsdp"),
            P("section", None, None, None, "fsdp"),
            P("section", None, None, None, "fsdp"),
            P("section", None, None, None, "fsdp"),
            P("section", None, None, None, "fsdp"),
            P("section", None, "fsdp", None),
            P("section", None, "fsdp", None),
            P("section", None, "fsdp", None),
            P("section", None, "fsdp", None),
            P("section", None, "fsdp", None),
            P("section", None),
        ),
        check_vma=False,
    )
```

profile of v0, /device:TPU:0, one launch (start us, length us, event | category | flops | bytes accessed | tf_op | source)
XLA Modules:
  0.0 1749.7 jit_solution(8013138590458174219)
XLA Ops:
  9.9 25.9 %all_gather.33 = bf16[1,2,768]{1,0,2:T(2,128)(2,1)S(1)} all-gather(bf16[1,2,48]{1,0,2:T(2,128)(2,1)S(1)} %copy.409), channel_id=1, replica_groups=mesh['section'=2,'ctx'=4,'fsdp'=16] {'fsdp'}, dimensions={2}, use_global_device_ids=true | all-gather | bytes 3264 | tf_op jit(solution)/shard_map/all_gather | solution.py:378
  41.7 25.9 %all-gather.10.cloned.1.call-done = bf16[1,768,3072]{2,1,0:T(8,128)(2,1)} async-done(((bf16[1,48,3072]{2,1,0:T(8,128)(2,1)}), bf16[1,768,3072]{2,1,0:T(8,128)(2,1)}) %all-gather.10.cloned.1.call-update) | async-done | bytes 4718608 | tf_op jit(solution)/shard_map/all_gather | solution.py:379
  89.5 24.0 %all_gather.39 = bf16[1,768,3]{2,0,1:T(2,128)(2,1)S(1)} all-gather(bf16[1,48,3]{2,0,1:T(2,128)(2,1)S(1)} %copy.422), channel_id=1, replica_groups=mesh['section'=2,'ctx'=4,'fsdp'=16] {'fsdp'}, dimensions={1}, use_global_device_ids=true | all-gather | bytes 4896 | tf_op jit(solution)/shard_map/all_gather | solution.py:380
  119.6 10.9 all-gather.14.cloned.1.call-done
  156.1 141.9 %all-gather.16.cloned.1.call-done = bf16[1,4,768,2,2048]{4,2,3,1,0:T(8,128)(2,1)} async-done(((bf16[1,4,768,2,128]{4,2,3,1,0:T(8,128)(2,1)}), bf16[1,4,768,2,2048]{4,2,3,1,0:T(8,128)(2,1)}) %all-gather.16.cloned.1.call-update) | async-done | bytes 25165840 | tf_op jit(solution)/shard_map/all_gather | solution.py:381
  306.1 15.3 convolution_bitcast_fusion.12
  321.4 6.0 fusion.76
  327.4 62.5 %all-gather.18.cloned.1.call-done = bf16[1,4,2048,768]{3,2,1,0:T(8,128)(2,1)} async-done(((bf16[1,4,128,768]{3,2,1,0:T(8,128)(2,1)}), bf16[1,4,2048,768]{3,2,1,0:T(8,128)(2,1)}) %all-gather.18.cloned.1.call-update) | async-done | bytes 12582928 | tf_op jit(solution)/shard_map/all_gather | solution.py:382
  389.9 6.6 fusion.91
  424.0 22.2 %all-gather.22.cloned.1.call-done = bf16[1024,768]{0,1:T(8,128)(2,1)} async-done(((bf16[256,768]{0,1:T(8,128)(2,1)}), bf16[1024,768]{0,1:T(8,128)(2,1)}) %all-gather.22.cloned.1.call-update) | async-done | bytes 1572880 | tf_op jit(solution)/shard_map/all_gather | solution.py:147
  458.1 17.9 %all-gather.20.cloned.1.call-done = bf16[1024,768]{1,0:T(8,128)(2,1)} async-done(((bf16[256,768]{1,0:T(8,128)(2,1)}), bf16[1024,768]{1,0:T(8,128)(2,1)}) %all-gather.20.cloned.1.call-update) | async-done | bytes 1572880 | tf_op jit(solution)/shard_map/all_gather | solution.py:148
  477.7 7.1 fusion.179
  498.1 5.0 convolution_bitcast_fusion.17
  505.5 8.7 fusion.77
  518.0 6.8 fusion.90
  553.0 23.5 %all-gather.26.cloned.1.call-done = bf16[1024,768]{0,1:T(8,128)(2,1)} async-done(((bf16[256,768]{0,1:T(8,128)(2,1)}), bf16[1024,768]{0,1:T(8,128)(2,1)}) %all-gather.26.cloned.1.call-update) | async-done | bytes 1572880 | tf_op jit(solution)/shard_map/all_gather | solution.py:147
  585.0 21.3 %all-gather.24.cloned.1.call-done = bf16[1024,768]{1,0:T(8,128)(2,1)} async-done(((bf16[256,768]{1,0:T(8,128)(2,1)}), bf16[1024,768]{1,0:T(8,128)(2,1)}) %all-gather.24.cloned.1.call-update) | async-done | bytes 1572880 | tf_op jit(solution)/shard_map/all_gather | solution.py:148
  608.0 7.2 fusion.178
  640.0 8.7 fusion.80
  651.4 7.9 fusion.100
  659.3 11.0 fusion.11
  678.0 6.6 fusion.89
  698.9 5.4 fusion.176
  712.2 11.5 multiply_reduce_fusion.2
  724.9 6.9 multiply_convert_fusion.2
  735.0 9.1 fusion.130
  749.1 11.8 reduce-scatter.14.cloned.1.call-done
  763.0 26.2 %reduce-scatter.16.cloned.1.call-done = bf16[256,768]{0,1:T(8,128)(2,1)} async-done(((bf16[1024,768]{0,1:T(8,128)(2,1)}), bf16[256,768]{0,1:T(8,128)(2,1)}) %reduce-scatter.16.cloned.1.call-update) | async-done | bytes 393232 | tf_op jit(solution)/shard_map/reduce_scatter | solution.py:307
  807.6 10.4 fusion.101
  818.0 11.0 fusion.9
  840.3 5.4 fusion.175
  849.4 11.5 multiply_reduce_fusion.1
  860.9 6.7 multiply_convert_fusion.1
  870.9 7.9 fusion.133
  879.6 5.7 fusion.165
  885.3 11.1 reduce-scatter.18.cloned.1.call-done
  898.9 25.9 %reduce-scatter.20.cloned.1.call-done = bf16[256,768]{0,1:T(8,128)(2,1)} async-done(((bf16[1024,768]{0,1:T(8,128)(2,1)}), bf16[256,768]{0,1:T(8,128)(2,1)}) %reduce-scatter.20.cloned.1.call-update) | async-done | bytes 393232 | tf_op jit(solution)/shard_map/reduce_scatter | solution.py:307
  931.8 7.8 convolution_bitcast_fusion.11
  947.9 10.5 fusion.102
  958.3 11.0 fusion.7
  980.7 5.4 fusion.174
  990.3 11.5 multiply_reduce_fusion
  1001.8 6.8 multiply_convert_fusion
  1011.8 17.8 %convolution_bitcast_fusion.2 = f32[1,3,768,2,2048]{4,2,3,1,0:T(8,128)} fusion(bf16[3,208,768,1]{2,1,3,0:T(8,128)(2,1)S(1)} %bitcast.948, bf16[3,208,1,2048]{3,1,0,2:T(8,128)(2,1)} %get-tuple-element.266, bf16[3,208,1,2048]{3,1,0,2:T(8,128)(2,1)} %get-tuple-element.265), kind=kOutput, calls=%fused_computation.24 | convolution fusion | flops 3928424448 | bytes 43819008 | tf_op jit(solution)/shard_map/pecd,pecgf->edgf/dot_general | solution.py:106
  1029.6 7.8 convolution_bitcast_fusion.10
  1037.4 16.8 convolution_bitcast_fusion.1
  1054.2 7.8 convolution_bitcast_fusion.9
  1062.0 16.5 convolution_bitcast_fusion
  1078.5 8.0 fusion.136
  1086.6 55.8 %fusion.1 = bf16[1,4,768,2,2048]{4,2,3,1,0:T(8,128)(2,1)} fusion(f32[1,1,768,2,2048]{4,2,3,1,0:T(8,128)} %convolution_bitcast_fusion.11, f32[1,3,768,2,2048]{4,2,3,1,0:T(8,128)} %convolution_bitcast_fusion.2, f32[1,1,768,2,2048]{4,2,3,1,0:T(8,128)} %convolution_bitcast_fusion.10, f32[1,3,768,2,2048]{4,2,3,1,0:T(8,128)} %convolution_bitcast_fusion.1, ...), kind=kLoop, calls=%fused_computation.17 | loop fusion | flops 75497472 | bytes 176160768 | tf_op jit(solution)/shard_map/convert_element_type | solution.py:449
  1142.3 62.0 %copy.495 = bf16[1,4,768,2,2048]{2,3,1,0,4:T(2,128)(2,1)} copy(bf16[1,4,768,2,2048]{4,2,3,1,0:T(8,128)(2,1)} %fusion.1) | data formatting | bytes 50331648
  1204.4 51.5 %reshape.1986 = bf16[2048,6144]{1,0:T(8,128)(2,1)} reshape(bf16[2048,1,4,2,768]{4,3,2,1,0:T(2,128)(2,1)} %bitcast.916) | data formatting | bytes 50331648
  1281.0 8.1 fusion.21
  1289.8 5.8 convolution_bitcast_fusion.15
  1302.1 8.1 convolution_bitcast_fusion.4
  1313.9 8.8 convolution_bitcast_fusion.3
  1322.7 25.7 %fusion.3 = bf16[1,4,2048,768]{3,2,1,0:T(8,128)(2,1)} fusion(f32[1,1,2048,768]{3,2,1,0:T(8,128)} %convolution_bitcast_fusion.15, f32[1,3,2048,768]{3,2,1,0:T(8,128)S(1)} %convolution_bitcast_fusion.5, f32[1,1,2048,768]{3,2,1,0:T(8,128)} %convolution_bitcast_fusion.14, f32[1,3,2048,768]{3,2,1,0:T(8,128)} %convolution_bitcast_fusion.4, ...), kind=kLoop, calls=%fused_computation.20 | loop fusion | flops 37748736 | bytes 88080384 | tf_op jit(solution)/shard_map/convert_element_type | solution.py:452
  1348.4 61.6 %reduce-scatter.30.cloned.1.call-done = bf16[128,6144]{1,0:T(8,128)(2,1)} async-done(((bf16[2048,6144]{1,0:T(8,128)(2,1)}), bf16[128,6144]{1,0:T(8,128)(2,1)}) %reduce-scatter.30.cloned.1.call-update) | async-done | bytes 1572880
  1417.7 73.7 %reduce-scatter.26.cloned.1.call-done = bf16[1,48,3072]{2,1,0:T(8,128)(2,1)} async-done(((bf16[1,768,3072]{2,1,0:T(8,128)(2,1)}), bf16[1,48,3072]{2,1,0:T(8,128)(2,1)}) %reduce-scatter.26.cloned.1.call-update) | async-done | bytes 294928 | tf_op jit(solution)/shard_map/reduce_scatter | solution.py:442
  1491.4 97.4 %reduce-scatter.28.cloned.1.call-done = bf16[1,4,128,768]{3,2,1,0:T(8,128)(2,1)} async-done(((bf16[1,4,2048,768]{3,2,1,0:T(8,128)(2,1)}), bf16[1,4,128,768]{3,2,1,0:T(8,128)(2,1)}) %reduce-scatter.28.cloned.1.call-update) | async-done | bytes 786448 | tf_op jit(solution)/shard_map/reduce_scatter | solution.py:451
  1602.5 38.8 %all-reduce.3 = (bf16[1,2,768]{2,1,0:T(2,128)(2,1)S(1)}, bf16[1,768,3]{1,2,0:T(4,128)(2,1)S(1)}) all-reduce(bf16[1,2,768]{2,1,0:T(2,128)(2,1)S(1)} %fusion.328, bf16[1,768,3]{1,2,0:T(4,128)(2,1)S(1)} %fusion.194), channel_id=8, replica_groups=mesh['section'=2,'ctx'=4,'fsdp'=16] {'fsdp'}, use_global_device_ids=true, to_apply=%region_69.71.clone | all-reduce | flops 3840 | bytes 15360
  1641.5 10.5 all-reduce.4
  1669.3 41.2 %all-reduce.2 = (f32[]{:T(128)}, f32[]{:T(128)}, f32[]{:T(128)}, f32[]{:T(128)}, f32[]{:T(128)}) all-reduce(f32[]{:T(128)} %get-tuple-element.249, f32[]{:T(128)} %get-tuple-element.247, f32[]{:T(128)} %multiply_reduce_fusion.24, f32[]{:T(128)} %multiply_reduce_fusion.3, ...), channel_id=1, replica_groups=mesh['section'=2,'ctx'=4,'fsdp'=16] {'fsdp'}, use_global_device_ids=true, to_apply=%region_72.74 | all-reduce | flops 5 | bytes 40 | tf_op jit(solution)/shard_map/psum | solution.py:462
  1716.4 5.3 fusion.397
  (814 shorter events, 406.1 us)
Async XLA Ops:
  7.2 60.4 %all-gather.10.cloned.1.call-start = ((), (), s32[]{:S(2)}) async-start(), calls=%async_computation.9 | async-start | bytes 5013504 | tf_op jit(solution)/shard_map/all_gather | solution.py:379
  9.1 108.6 %all-gather.12.cloned.1.call-start = ((), (), s32[]{:S(2)}) async-start(), calls=%async_computation.10 | async-start | bytes 1966080 | tf_op jit(solution)/shard_map/all_gather | solution.py:148
  41.6 496.6 %copy-start.130 = (f32[768]{0:T(1024)}, f32[768]{0:T(1024)S(1)}, u32[]{:S(2)}) copy-start(f32[768]{0:T(1024)S(1)} %get-tuple-element.212) | copy-start | bytes 9220
  71.7 58.7 %all-gather.14.cloned.1.call-start = ((), (), s32[]{:S(2)}) async-start(), calls=%async_computation.11 | async-start | bytes 1966080 | tf_op jit(solution)/shard_map/all_gather | solution.py:147
  73.1 342.0 %copy-start.114 = (f32[256,32]{0,1:T(8,128)}, f32[256,32]{0,1:T(8,128)S(1)}, u32[]{:S(2)}) copy-start(f32[256,32]{0,1:T(8,128)S(1)} %get-tuple-element.327) | copy-start | bytes 98308
  73.1 342.0 %copy-start.149 = (f32[256,32]{0,1:T(8,128)}, f32[256,32]{0,1:T(8,128)S(1)}, u32[]{:S(2)}) copy-start(f32[256,32]{0,1:T(8,128)S(1)} %get-tuple-element.326) | copy-start | bytes 98308
  81.4 49.0 %copy-start.101 = (bf16[256,12,32]{0,2,1:T(8,128)(2,1)}, bf16[256,12,32]{0,2,1:T(8,128)(2,1)S(1)}, u32[]{:S(2)}) copy-start(bf16[256,12,32]{0,2,1:T(8,128)(2,1)S(1)} %get-tuple-element.303) | copy-start | bytes 589828
  82.3 215.7 %all-gather.16.cloned.1.call-start = ((), (), s32[]{:S(2)}) async-start(), calls=%async_computation.12 | async-start | bytes 26738688 | tf_op jit(solution)/shard_map/all_gather | solution.py:381
  83.8 306.1 %all-gather.18.cloned.1.call-start = ((), (), s32[]{:S(2)}) async-start(), calls=%async_computation.13 | async-start | bytes 13369344 | tf_op jit(solution)/shard_map/all_gather | solution.py:382
  86.3 360.0 %all-gather.22.cloned.1.call-start = ((), (), s32[]{:S(2)}) async-start(), calls=%async_computation.15 | async-start | bytes 1966080 | tf_op jit(solution)/shard_map/all_gather | solution.py:147
  86.9 330.6 %copy-start.177 = (s32[1,1,256,2]{2,3,1,0:T(2,128)}, s32[1,1,256,2]{2,3,1,0:T(2,128)S(1)}, u32[]{:S(2)}) copy-start(s32[1,1,256,2]{2,3,1,0:T(2,128)S(1)} %get-tuple-element.324) | copy-start | bytes 6148
  113.8 373.3 %copy-start.162 = (bf16[1,768,3]{1,2,0:T(4,128)(2,1)}, bf16[1,768,3]{1,2,0:T(4,128)(2,1)S(1)}, u32[]{:S(2)}) copy-start(bf16[1,768,3]{1,2,0:T(4,128)(2,1)S(1)} %copy.423) | copy-start | bytes 13828
  116.5 280.1 %copy-start.198 = (s32[1024]{0:T(1024)}, s32[1024]{0:T(1024)S(1)}, u32[]{:S(2)}) copy-start(s32[1024]{0:T(1024)S(1)} %pad_clamp_fusion.2) | copy-start | bytes 12292
  117.6 360.1 %copy-start.44 = (pred[256,1024]{1,0:T(8,128)(4,1)}, pred[256,1024]{1,0:T(8,128)(4,1)S(1)}, u32[]{:S(2)}) copy-start(pred[256,1024]{1,0:T(8,128)(4,1)S(1)} %get-tuple-element.329) | copy-start | bytes 786436
  144.9 258.4 %copy-start.38 = (f32[256,768]{1,0:T(8,128)}, f32[256,768]{1,0:T(8,128)S(1)}, u32[]{:S(2)}) copy-start(f32[256,768]{1,0:T(8,128)S(1)} %get-tuple-element.337) | copy-start | bytes 2359300
  145.1 152.9 %copy-start.21 = (bf16[256,768]{1,0:T(8,128)(2,1)}, bf16[256,768]{1,0:T(8,128)(2,1)S(1)}, u32[]{:S(2)}) copy-start(bf16[256,768]{1,0:T(8,128)(2,1)S(1)} %multiply_convert_fusion.11) | copy-start | bytes 1179652
  155.6 150.5 %copy-start.68 = (bf16[624,768]{1,0:T(8,128)(2,1)}, bf16[624,768]{1,0:T(8,128)(2,1)S(1)}, u32[]{:S(2)}) copy-start(bf16[624,768]{1,0:T(8,128)(2,1)S(1)} %scatter_custom_fusion) | copy-start | bytes 2875396
  156.1 245.3 %copy-start.86 = (f32[256,2]{1,0:T(8,128)}, f32[256,2]{1,0:T(8,128)S(1)}, u32[]{:S(2)}) copy-start(f32[256,2]{1,0:T(8,128)S(1)} %fusion.303) | copy-start | bytes 6148
  406.6 3.1 collective-permute-start
  409.9 75.0 %copy-start.80 = (bf16[256,768]{1,0:T(8,128)(2,1)}, bf16[256,768]{1,0:T(8,128)(2,1)S(1)}, u32[]{:S(2)}) copy-start(bf16[256,768]{1,0:T(8,128)(2,1)S(1)} %get-tuple-element.258) | copy-start | bytes 1179652
  416.3 59.7 %all-gather.20.cloned.1.call-start = ((), (), s32[]{:S(2)}) async-start(), calls=%async_computation.14 | async-start | bytes 1966080 | tf_op jit(solution)/shard_map/all_gather | solution.py:148
  422.0 154.5 %all-gather.26.cloned.1.call-start = ((), (), s32[]{:S(2)}) async-start(), calls=%async_computation.17 | async-start | bytes 1966080 | tf_op jit(solution)/shard_map/all_gather | solution.py:147
  424.0 70.4 %copy-start.209 = (s32[512,1]{0,1:T(1,128)}, s32[512,1]{0,1:T(1,128)S(1)}, u32[]{:S(2)}) copy-start(s32[512,1]{0,1:T(1,128)S(1)} %get-tuple-element.359) | copy-start | bytes 6148
  424.0 100.8 %copy-start.200 = (s32[1024]{0:T(1024)}, s32[1024]{0:T(1024)S(1)}, u32[]{:S(2)}) copy-start(s32[1024]{0:T(1024)S(1)} %pad_clamp_fusion.1) | copy-start | bytes 12292
  534.9 3.1 collective-permute-start.1
  538.2 77.0 %copy-start.83 = (bf16[256,768]{1,0:T(8,128)(2,1)}, bf16[256,768]{1,0:T(8,128)(2,1)S(1)}, u32[]{:S(2)}) copy-start(bf16[256,768]{1,0:T(8,128)(2,1)S(1)} %get-tuple-element.254) | copy-start | bytes 1179652
  546.6 59.7 %all-gather.24.cloned.1.call-start = ((), (), s32[]{:S(2)}) async-start(), calls=%async_computation.16 | async-start | bytes 1966080 | tf_op jit(solution)/shard_map/all_gather | solution.py:148
  548.7 212.2 %reduce-scatter.14.cloned.1.call-start = ((), (), s32[]{:S(2)}) async-start(), calls=%async_computation.18 | async-start | bytes 1966080 | tf_op jit(solution)/shard_map/reduce_scatter | solution.py:301
  709.2 84.2 %copy-start.36 = (f32[256,768]{1,0:T(8,128)}, f32[256,768]{1,0:T(8,128)S(1)}, u32[]{:S(2)}) copy-start(f32[256,768]{1,0:T(8,128)S(1)} %get-tuple-element.307) | copy-start | bytes 2359300
  735.0 54.3 %reduce-scatter.16.cloned.1.call-start = ((), (), s32[]{:S(2)}) async-start(), calls=%async_computation.19 | async-start | bytes 1966080 | tf_op jit(solution)/shard_map/reduce_scatter | solution.py:307
  744.2 152.2 %reduce-scatter.18.cloned.1.call-start = ((), (), s32[]{:S(2)}) async-start(), calls=%async_computation.20 | async-start | bytes 1966080 | tf_op jit(solution)/shard_map/reduce_scatter | solution.py:301
  794.6 3.9 collective-permute-start.2
  799.7 47.1 %copy-start.6 = (f32[256,768]{1,0:T(8,128)}, f32[256,768]{1,0:T(8,128)S(1)}, u32[]{:S(2)}) copy-start(f32[256,768]{1,0:T(8,128)S(1)} %fusion.248) | copy-start | bytes 2359300
  847.1 81.8 %copy-start.19 = (f32[256,768]{1,0:T(8,128)}, f32[256,768]{1,0:T(8,128)S(1)}, u32[]{:S(2)}) copy-start(f32[256,768]{1,0:T(8,128)S(1)} %multiply_add_fusion.2) | copy-start | bytes 2359300
  870.8 54.0 %reduce-scatter.20.cloned.1.call-start = ((), (), s32[]{:S(2)}) async-start(), calls=%async_computation.21 | async-start | bytes 1966080 | tf_op jit(solution)/shard_map/reduce_scatter | solution.py:307
  878.8 395.3 %reduce-scatter.22.cloned.1.call-start = ((), (), s32[]{:S(2)}) async-start(), calls=%async_computation.22 | async-start | bytes 1966080 | tf_op jit(solution)/shard_map/reduce_scatter | solution.py:301
  930.1 9.5 collective-permute-start.3
  939.8 47.3 %copy-start.8 = (f32[256,768]{1,0:T(8,128)}, f32[256,768]{1,0:T(8,128)S(1)}, u32[]{:S(2)}) copy-start(f32[256,768]{1,0:T(8,128)S(1)} %fusion.250) | copy-start | bytes 2359300
  1011.7 265.9 %reduce-scatter.24.cloned.1.call-start = ((), (), s32[]{:S(2)}) async-start(), calls=%async_computation.23 | async-start | bytes 1966080 | tf_op jit(solution)/shard_map/reduce_scatter | solution.py:307
  1086.5 323.5 %reduce-scatter.30.cloned.1.call-start = ((), (), s32[]{:S(2)}) async-start(), calls=%async_computation.26 | async-start | bytes 26738688
  1256.0 235.5 %reduce-scatter.26.cloned.1.call-start = ((), (), s32[]{:S(2)}) async-start(), calls=%async_computation.24 | async-start | bytes 5013504 | tf_op jit(solution)/shard_map/reduce_scatter | solution.py:442
  1289.2 299.6 %reduce-scatter.28.cloned.1.call-start = ((), (), s32[]{:S(2)}) async-start(), calls=%async_computation.25 | async-start | bytes 13369344 | tf_op jit(solution)/shard_map/reduce_scatter | solution.py:451
  1348.4 310.7 %all-reduce.8.cloned.1.call-start = ((), (), s32[]{:S(2)}) async-start(), calls=%async_computation.27 | async-start | bytes 5308416 | tf_op jit(solution)/shard_map/psum | solution.py:457
  1414.4 177.7 %copy-start.160 = (bf16[256,768]{1,0:T(8,128)(2,1)S(1)}, bf16[256,768]{1,0:T(8,128)(2,1)}, u32[]{:S(2)}) copy-start(bf16[256,768]{1,0:T(8,128)(2,1)} %copy-done.159) | copy-start | bytes 1179652
  1414.4 180.1 %copy-start.29 = (bf16[256,768]{1,0:T(8,128)(2,1)S(1)}, bf16[256,768]{1,0:T(8,128)(2,1)}, u32[]{:S(2)}) copy-start(bf16[256,768]{1,0:T(8,128)(2,1)} %copy-done.27) | copy-start | bytes 1179652
  1414.5 180.1 %copy-start.180 = (bf16[256,3]{0,1:T(4,128)(2,1)S(1)}, bf16[256,3]{0,1:T(4,128)(2,1)}, u32[]{:S(2)}) copy-start(bf16[256,3]{0,1:T(4,128)(2,1)} %copy-done.179) | copy-start | bytes 4612
  1417.7 178.4 %copy-start.26 = (bf16[256,768]{1,0:T(8,128)(2,1)S(1)}, bf16[256,768]{1,0:T(8,128)(2,1)}, u32[]{:S(2)}) copy-start(bf16[256,768]{1,0:T(8,128)(2,1)} %copy-done.24) | copy-start | bytes 1179652
  1417.7 178.4 %copy-start.182 = (bf16[256,3]{0,1:T(4,128)(2,1)S(1)}, bf16[256,3]{0,1:T(4,128)(2,1)}, u32[]{:S(2)}) copy-start(bf16[256,3]{0,1:T(4,128)(2,1)} %copy-done.181) | copy-start | bytes 4612
  1417.7 180.0 %copy-start.23 = (bf16[256,768]{1,0:T(8,128)(2,1)S(1)}, bf16[256,768]{1,0:T(8,128)(2,1)}, u32[]{:S(2)}) copy-start(bf16[256,768]{1,0:T(8,128)(2,1)} %copy-done.21) | copy-start | bytes 1179652
  1417.7 180.0 %copy-start.184 = (bf16[256,3]{0,1:T(4,128)(2,1)S(1)}, bf16[256,3]{0,1:T(4,128)(2,1)}, u32[]{:S(2)}) copy-start(bf16[256,3]{0,1:T(4,128)(2,1)} %copy-done.183) | copy-start | bytes 4612
  1417.7 180.1 %copy-start.64 = (bf16[2,256,768]{2,1,0:T(8,128)(2,1)S(1)}, bf16[2,256,768]{2,1,0:T(8,128)(2,1)}, u32[]{:S(2)}) copy-start(bf16[2,256,768]{2,1,0:T(8,128)(2,1)} %param.22) | copy-start | bytes 2359300
  1417.7 180.1 %copy-start.126 = (bf16[256,12,64]{0,2,1:T(8,128)(2,1)S(1)}, bf16[256,12,64]{0,2,1:T(8,128)(2,1)}, u32[]{:S(2)}) copy-start(bf16[256,12,64]{0,2,1:T(8,128)(2,1)} %copy-done.125) | copy-start | bytes 1179652
  1417.7 180.1 %copy-start.127 = (bf16[256,12,64]{0,2,1:T(8,128)(2,1)S(1)}, bf16[256,12,64]{0,2,1:T(8,128)(2,1)}, u32[]{:S(2)}) copy-start(bf16[256,12,64]{0,2,1:T(8,128)(2,1)} %pad_maximum_fusion.44) | copy-start | bytes 1179652
  1417.7 180.1 %copy-start.151 = (bf16[256,768]{0,1:T(8,128)(2,1)S(1)}, bf16[256,768]{0,1:T(8,128)(2,1)}, u32[]{:S(2)}) copy-start(bf16[256,768]{0,1:T(8,128)(2,1)} %reduce-scatter.24.cloned.1.call-done) | copy-start | bytes 1179652
  1597.9 55.3 %copy-start.18 = (f32[256,768]{1,0:T(8,128)S(1)}, f32[256,768]{1,0:T(8,128)}, u32[]{:S(2)}) copy-start(f32[256,768]{1,0:T(8,128)} %copy-done.16) | copy-start | bytes 2359300
  1597.9 55.3 %copy-start.187 = (f32[256]{0:T(256)S(1)}, f32[256]{0:T(256)}, u32[]{:S(2)}) copy-start(f32[256]{0:T(256)} %copy-done.185) | copy-start | bytes 3076
  1602.5 52.0 %copy-start.93 = (f32[1,256,768]{2,1,0:T(8,128)S(1)}, f32[1,256,768]{2,1,0:T(8,128)}, u32[]{:S(2)}) copy-start(f32[1,256,768]{2,1,0:T(8,128)} %get-tuple-element.279) | copy-start | bytes 2359300
  1602.5 52.0 %copy-start.94 = (f32[1,256,768]{2,1,0:T(8,128)S(1)}, f32[1,256,768]{2,1,0:T(8,128)}, u32[]{:S(2)}) copy-start(f32[1,256,768]{2,1,0:T(8,128)} %get-tuple-element.281) | copy-start | bytes 2359300
  1656.5 80.3 %copy-start.215 = (f32[1,2,48]{2,1,0:T(2,128)}, f32[1,2,48]{2,1,0:T(2,128)S(1)}, u32[]{:S(2)}) copy-start(f32[1,2,48]{2,1,0:T(2,128)S(1)} %get-tuple-element.250) | copy-start | bytes 1156
  1661.9 52.2 %copy-start.212 = (f32[1,48,3]{1,0,2:T(1,128)S(1)}, f32[1,48,3]{1,0,2:T(1,128)}, u32[]{:S(2)}) copy-start(f32[1,48,3]{1,0,2:T(1,128)} %param.33) | copy-start | bytes 1732
  1661.9 52.2 %copy-start.216 = (f32[1,48,3]{1,0,2:T(1,128)S(1)}, f32[1,48,3]{1,0,2:T(1,128)}, u32[]{:S(2)}) copy-start(f32[1,48,3]{1,0,2:T(1,128)} %param.35) | copy-start | bytes 1732
  1661.9 52.2 %copy-start.217 = (f32[1,48,3]{1,0,2:T(1,128)S(1)}, f32[1,48,3]{1,0,2:T(1,128)}, u32[]{:S(2)}) copy-start(f32[1,48,3]{1,0,2:T(1,128)} %param.34) | copy-start | bytes 1732
  1661.9 54.5 %copy-start.14 = (bf16[1,4,768,2,128]{4,2,3,1,0:T(8,128)(2,1)S(1)}, bf16[1,4,768,2,128]{4,2,3,1,0:T(8,128)(2,1)}, u32[]{:S(2)}) copy-start(bf16[1,4,768,2,128]{4,2,3,1,0:T(8,128)(2,1)} %get-tuple-element.223) | copy-start | bytes 4718596
  1669.3 69.8 %copy-start.50 = (f32[1,4,128,768]{3,2,1,0:T(8,128)}, f32[1,4,128,768]{3,2,1,0:T(8,128)S(1)}, u32[]{:S(2)}) copy-start(f32[1,4,128,768]{3,2,1,0:T(8,128)S(1)} %get-tuple-element.246) | copy-start | bytes 4718596
  (193 other events, 1795.4 us)
Sparse Core Ops, SparseCore 0:
  10.7 56.8 all-gather.9
  71.8 26.0 all-gather.11
  100.2 30.2 all-gather.13
  133.0 164.9 all-gather.15
  300.5 89.3 all-gather.17
  416.4 29.7 all-gather.21
  448.5 27.4 all-gather.19
  546.7 29.7 all-gather.25
  578.8 27.4 all-gather.23
  735.1 25.7 reduce-scatter.13
  763.8 25.3 reduce-scatter.15
  871.0 25.3 reduce-scatter.17
  899.4 25.3 reduce-scatter.19
  1011.8 26.2 reduce-scatter.21
  1086.6 26.2 reduce-scatter.23
  1256.0 153.9 reduce-scatter.29
  1413.2 78.2 reduce-scatter.25
  1494.7 94.0 reduce-scatter.27
  1591.9 67.1 all-reduce.7
where the time goes:
time: 1760 us; the launch traced here: 1750 us
  waiting for transfers between devices  641 us (36%)
  matrix products  442 us (25%)
  local copies, waits for them, and re-layouts  262 us (15%)
  other arithmetic  233 us (13%)
  blocking collectives  140 us (8%)
  between operations  22.8 us (1%)
    unnamed x486, local copies, waits for them, and re-layouts  167 us
    all_gather x1, waiting for transfers between devices, on_device(): lax.all_gather(expert_in.astype(jnp.bfloat16), 'fsdp', axis=4, tiled=True)  142 us
    reduce_scatter x1, waiting for transfers between devices, on_device(): lax.psum_scatter(out_total[None].astype(jnp.bfloat16), 'fsdp', scatter_di...  97.4 us
    reduce_scatter x1, waiting for transfers between devices, on_device(): lax.psum_scatter(attn_total[None].astype(jnp.bfloat16), 'fsdp', scatter_d...  73.7 us
    all_gather x1, waiting for transfers between devices, on_device(): lax.all_gather(expert_out.astype(jnp.bfloat16), 'fsdp', axis=2, tiled=True)  62.5 us
    unnamed x20, waiting for transfers between devices  61.9 us
    all_gather x3, waiting for transfers between devices, layer_forward(): lax.all_gather(keys_local, 'ctx', axis=0, tiled=True)  56.5 us
    convert_element_type x1, other arithmetic, on_device(): in_total[None].astype(jnp.bfloat16)  55.8 us
  transfers between devices with their start and end apart: 23, of which 19 were waited for; matrix products, arithmetic and copies ran while one was open for 29% of the time, Pallas kernels for 0%

commit v1 on v0

v1 whole, which is shorter than its diff:
```python
import functools

import jax
import jax.numpy as jnp
from jax import lax
from jax.experimental import pallas as pl
from jax.experimental.pallas import tpu as pltpu
from jax.sharding import PartitionSpec as P

D = 768
HEADS = 12
HEAD_DIM = 64
FFN = 2048
EXPERTS = 3
ROWS = 256
CTX = 4
SEQ = ROWS * CTX
HEADS_DEV = HEADS // CTX
WIDE = 128
EXT = 3 * HEADS_DEV * WIDE
COLS = HEADS_DEV * HEAD_DIM

EPS_NORM = 1e-06
BETA_ONE = 0.9
BETA_TWO = 0.95
RATE_FACTOR = 3.0
GAIN_RATE = 0.3
DECAY_RATE = 0.1
ADAM_EPS = 1e-08
CLIP_LIMIT = 1.0
MASK_VALUE = -1e30
SCORE_SCALE = HEAD_DIM ** (-0.5) / 2.0
BF16 = jnp.bfloat16
F32 = jnp.float32
VMEM_LIMIT = 56 * 1024 * 1024
NT = (((1,), (1,)), ((), ()))
TN = (((0,), (0,)), ((), ()))
HALF = ROWS // 2
LANES = 128
MESH = pl.DeviceIdType.MESH
EXACT = lax.Precision.HIGHEST


def dot(left, right):
    return jnp.dot(left, right, preferred_element_type=F32)


def dot_nt(left, right):
    return lax.dot_general(left, right, NT, preferred_element_type=F32)


def dot_tn(left, right):
    return lax.dot_general(left, right, TN, preferred_element_type=F32)


def params(collective_id):
    return pltpu.CompilerParams(
        vmem_limit_bytes=VMEM_LIMIT, collective_id=collective_id, has_side_effects=True
    )


def whole(shape):
    return pl.BlockSpec(shape, lambda *_: (0,) * len(shape))


def allowed_keys(block, keys, length):
    key_pos = lax.broadcasted_iota(jnp.int32, (ROWS, keys), 1)
    query_pos = lax.broadcasted_iota(jnp.int32, (ROWS, keys), 0) + block * ROWS
    return (key_pos <= query_pos) & (key_pos < length)


VMEM = pl.BlockSpec(memory_space=pltpu.VMEM)
SMEM = pl.BlockSpec(memory_space=pltpu.SMEM)


def ring():
    me = lax.axis_index("ctx")
    return me, lax.rem(me + 1, CTX), lax.rem(me + 3, CTX), lax.rem(me + 2, CTX)


def greet(peers):
    barrier = pltpu.get_barrier_semaphore()
    for peer in peers:
        pl.semaphore_signal(barrier, inc=1, device_id={"ctx": peer}, device_id_type=MESH)


def met(count):
    pl.semaphore_wait(pltpu.get_barrier_semaphore(), count)


def remote(source, target, send, recv, peer):
    return pltpu.make_async_remote_copy(
        src_ref=source,
        dst_ref=target,
        send_sem=send,
        recv_sem=recv,
        device_id={"ctx": peer},
        device_id_type=MESH,
    )


def rows_of(block, half=None):
    if half is None:
        return pl.ds(pl.multiple_of(block * ROWS, ROWS), ROWS)
    return pl.ds(pl.multiple_of(block * ROWS + half * HALF, HALF), HALF)


def gather_rows(all_ref, send, recv):
    me, right, left, _ = ring()

    def piece(index, block, half, peer):
        spot = all_ref.at[rows_of(block, half)]
        return remote(spot, spot, send.at[index], recv.at[index], peer)

    copies = [
        piece(0, me, 0, right),
        piece(1, me, 1, left),
        piece(2, me, 1, right),
        piece(3, me, 0, left),
    ]
    for copy in copies:
        copy.start()
    copies[0].wait_recv()
    copies.append(piece(4, left, 0, right))
    copies[4].start()
    copies[1].wait_recv()
    copies.append(piece(5, right, 1, left))
    copies[5].start()
    for index in range(2, 6):
        copies[index].wait_recv()
    for copy in copies:
        copy.wait_send()


def reduce_rows(make, part, across_in, from_left, from_right, send, recv, beside=None):
    me, right, left, across = ring()
    top, bottom = pl.ds(0, HALF), pl.ds(HALF, HALF)

    def piece(index, block, half, target, peer):
        return remote(part.at[rows_of(block, half)], target, send.at[index], recv.at[index], peer)

    make(across)
    copies = [
        piece(0, across, 0, across_in.at[0], right),
        piece(1, across, 1, across_in.at[1], left),
    ]
    copies[0].start()
    copies[1].start()
    make(right)
    copies.append(piece(2, right, 1, from_left.at[bottom], right))
    copies[2].start()
    make(left)
    copies.append(piece(3, left, 0, from_right.at[top], left))
    copies[3].start()
    copies[0].wait_recv()
    spot = rows_of(right, 0)
    part[spot, :] = (part[spot, :].astype(F32) + across_in[0].astype(F32)).astype(BF16)
    copies.append(piece(4, right, 0, from_left.at[top], right))
    copies[4].start()
    copies[1].wait_recv()
    spot = rows_of(left, 1)
    part[spot, :] = (part[spot, :].astype(F32) + across_in[1].astype(F32)).astype(BF16)
    copies.append(piece(5, left, 1, from_right.at[bottom], left))
    copies[5].start()
    make(me)
    if beside is not None:
        beside()
    for index in range(2, 6):
        copies[index].wait_recv()
    for copy in copies:
        copy.wait_send()
    return (
        part[rows_of(me), :].astype(F32) + from_left[...].astype(F32) + from_right[...].astype(F32)
    )


REDUCE_SCRATCH = [
    pltpu.VMEM((SEQ, D), BF16),
    pltpu.VMEM((2, HALF, D), BF16),
    pltpu.VMEM((ROWS, D), BF16),
    pltpu.VMEM((ROWS, D), BF16),
    pltpu.SemaphoreType.DMA((6,)),
    pltpu.SemaphoreType.DMA((6,)),
]


def inverse_size(values):
    return lax.rsqrt(jnp.mean(values * values, axis=1, keepdims=True) + EPS_NORM)


def attn_forward_kernel(
    length_ref, u_ref, gains_ref, router_ref, routes_ref, w_ref, back_ref, table_ref,
    a_ref, qkv_ref, mass_ref, attended_ref, residual_ref, b_ref, gates_ref, gate_ref,
    heads_out, send_a, recv_a, send_o, recv_o, send_b, recv_b,
):
    me, right, left, across = ring()
    greet((right, left, across))
    length = length_ref[0]
    tokens = u_ref[...].astype(F32)
    a_ref[rows_of(me), :] = (tokens * inverse_size(tokens) * gains_ref[0:1, :]).astype(BF16)
    met(3)
    gather_rows(a_ref, send_a, recv_a)
    for block in range(CTX):
        rows = pl.ds(block * ROWS, ROWS)
        table = table_ref[rows, :]
        mixed = dot(a_ref[rows, :], w_ref[...])
        for part in range(3 * HEADS_DEV):
            lanes = slice(part * WIDE, (part + 1) * WIDE)
            piece = mixed[:, lanes]
            if part < 2 * HEADS_DEV:
                turned = piece * table
                piece = turned + pltpu.roll(turned, WIDE // 2, 1)
            qkv_ref[rows, lanes] = piece.astype(BF16)

    def handed(block):
        step = lax.rem(block - me + CTX, CTX)
        return remote(
            heads_out.at[block], attended_ref.at[me], send_o.at[step], recv_o.at[step], block
        )

    for block in reversed(range(CTX)):
        rows = pl.ds(block * ROWS, ROWS)
        keys = (block + 1) * ROWS
        allowed = allowed_keys(block, keys, length)
        outs = []
        for head in range(HEADS_DEV):
            queries = qkv_ref[rows, head * WIDE : (head + 1) * WIDE]
            key_lanes = slice((HEADS_DEV + head) * WIDE, (HEADS_DEV + head + 1) * WIDE)
            value_lanes = slice((2 * HEADS_DEV + head) * WIDE, (2 * HEADS_DEV + head + 1) * WIDE)
            scores = dot_nt(queries, qkv_ref[:keys, key_lanes]) * SCORE_SCALE
            scores = jnp.where(allowed, scores, MASK_VALUE)
            top = jnp.max(scores, axis=1, keepdims=True)
            raw = jnp.exp(scores - top)
            total = jnp.sum(raw, axis=1, keepdims=True)
            probs = (raw * (1.0 / total)).astype(BF16)
            outs.append(dot(probs, qkv_ref[:keys, value_lanes]))
            mass_ref[head, rows, :] = top + jnp.log(total)
        first = (outs[0] + pltpu.roll(outs[1], WIDE // 2, 1)).astype(BF16)
        second = outs[2][:, : WIDE // 2].astype(BF16)
        heads_out[block, :, :WIDE] = first
        heads_out[block, :, WIDE:] = second

        @pl.when(block != me)
        def _():
            handed(block).start()

    attended_ref[me] = heads_out[me]
    for step in range(1, CTX):
        pltpu.make_async_copy(heads_out.at[0], attended_ref.at[0], recv_o.at[step]).wait()
    residual = tokens
    for block in range(CTX):
        residual = residual + dot(attended_ref[block], back_ref[block * COLS : (block + 1) * COLS, :])
    residual_ref[...] = residual
    b_ref[rows_of(me), :] = (residual * inverse_size(residual) * gains_ref[1:2, :]).astype(BF16)
    for step in range(1, CTX):
        pltpu.make_async_copy(heads_out.at[0], attended_ref.at[0], send_o.at[step]).wait()
    gather_rows(b_ref, send_b, recv_b)
    lanes = lax.broadcasted_iota(jnp.int32, (ROWS, LANES), 1)
    for block in range(CTX):
        rows = pl.ds(block * ROWS, ROWS)
        logits = dot(b_ref[rows, :], router_ref[...])
        named = (lanes == routes_ref[rows, 0:1]) | (lanes == routes_ref[rows, 1:2])
        chosen = jnp.where(named, logits, MASK_VALUE)
        raw = jnp.where(named, jnp.exp(chosen - jnp.max(chosen, axis=1, keepdims=True)), 0.0)
        gates = raw / jnp.sum(raw, axis=1, keepdims=True)
        gates_ref[rows, :] = gates
        gates = jnp.where(lanes == EXPERTS, 1.0, gates)
        gate_ref[rows, :] = jnp.sum(jnp.where(lanes == me, gates, 0.0), axis=1, keepdims=True)


def attn_forward(length, u, gains, router, routes, w_ext, w_back, table):
    sems = pltpu.SemaphoreType.DMA
    return pl.pallas_call(
        attn_forward_kernel,
        out_shape=(
            jax.ShapeDtypeStruct((SEQ, D), BF16),
            jax.ShapeDtypeStruct((SEQ, EXT), BF16),
            jax.ShapeDtypeStruct((HEADS_DEV, SEQ, 1), F32),
            jax.ShapeDtypeStruct((CTX, ROWS, COLS), BF16),
            jax.ShapeDtypeStruct((ROWS, D), F32),
            jax.ShapeDtypeStruct((SEQ, D), BF16),
            jax.ShapeDtypeStruct((SEQ, LANES), F32),
            jax.ShapeDtypeStruct((SEQ, 1), F32),
        ),
        in_specs=[SMEM] + [VMEM] * 7,
        out_specs=[VMEM] * 8,
        scratch_shapes=[pltpu.VMEM((CTX, ROWS, COLS), BF16)]
        + [sems((6,)), sems((6,)), sems((CTX,)), sems((CTX,)), sems((6,)), sems((6,))],
        compiler_params=params(1),
        name="attn_forward",
    )(length, u, gains, router, routes, w_ext, w_back, table)


def attn_backward_kernel(
    last, length_ref, u_ref, gains_ref, router_ref, w_ref, back_ref, table_ref,
    a_ref, qkv_ref, mass_ref, attended_ref, residual_ref, second_ref, gates_ref,
    delta_ref, db_ref, gate_grad_ref, *rest,
):
    if last:
        input_ref, dheads_ref, dback_ref, small_ref = rest[:4]
        rest = rest[4:]
    else:
        input_ref, lower_ref, dheads_ref, dback_ref, small_ref = rest[:5]
        rest = rest[5:]
    key_acc, value_acc, dz, grads_out, grads_in, send_o, recv_o = rest[:7]
    part, across_in, from_left, from_right, send_r, recv_r = rest[7:13]
    me, right, left, across = ring()
    greet((right, left, across))
    length = length_ref[0]
    lanes = lax.broadcasted_iota(jnp.int32, (ROWS, LANES), 1)
    gates = gates_ref[...]
    gate_grads = jnp.where(lanes < EXPERTS, gate_grad_ref[...], 0.0)
    logit_grad = gates * (gate_grads - jnp.sum(gates * gate_grads, axis=1, keepdims=True))
    logit_grad = logit_grad.astype(BF16)
    second_grad = db_ref[...] + dot_nt(logit_grad, router_ref[...])
    residual = residual_ref[...]
    scale_two = inverse_size(residual)
    normal_two = residual * scale_two
    gain_two_terms = second_grad * normal_two
    scaled_two = second_grad * gains_ref[1:2, :]
    residual_grad = delta_ref[...].astype(F32) + scale_two * (
        scaled_two - normal_two * jnp.mean(scaled_two * normal_two, axis=1, keepdims=True)
    )
    input_ref[...] = residual_grad
    branch_grad = residual_grad.astype(BF16)
    met(3)

    for block in range(CTX):
        grads_out[block] = dot_nt(branch_grad, back_ref[block * COLS : (block + 1) * COLS, :]).astype(
            BF16
        )

        @pl.when(block != me)
        def _():
            step = lax.rem(block - me + CTX, CTX)
            remote(
                grads_out.at[block], grads_in.at[me], send_o.at[step], recv_o.at[step], block
            ).start()

    grads_in[me] = grads_out[me]
    for block in range(CTX):
        dback_ref[block * COLS : (block + 1) * COLS, :] = dot_tn(
            attended_ref[block], branch_grad
        ).astype(BF16)
    router_terms = dot_tn(second_ref[...], logit_grad)
    ones = jnp.ones((ROWS, LANES), F32)
    gain_two_column = lax.dot_general(
        gain_two_terms, ones, TN, precision=EXACT, preferred_element_type=F32
    )
    key_acc[...] = jnp.zeros_like(key_acc)
    value_acc[...] = jnp.zeros_like(value_acc)
    for step in range(1, CTX):
        pltpu.make_async_copy(grads_out.at[0], grads_in.at[0], recv_o.at[step]).wait()
    for step in range(1, CTX):
        pltpu.make_async_copy(grads_out.at[0], grads_in.at[0], send_o.at[step]).wait()
    for block in range(CTX):
        rows = pl.ds(block * ROWS, ROWS)
        keys = (block + 1) * ROWS
        allowed = allowed_keys(block, keys, length)
        pair = grads_in[block, :, :WIDE]
        tail = grads_in[block, :, WIDE:]
        head_grads = (
            pair,
            pltpu.roll(pair.astype(F32), WIDE // 2, 1).astype(BF16),
            jnp.concatenate([tail, jnp.zeros_like(tail)], axis=1),
        )
        for head in range(HEADS_DEV):
            queries = qkv_ref[rows, head * WIDE : (head + 1) * WIDE]
            keys_all = qkv_ref[:keys, (HEADS_DEV + head) * WIDE : (HEADS_DEV + head + 1) * WIDE]
            values_all = qkv_ref[
                :keys, (2 * HEADS_DEV + head) * WIDE : (2 * HEADS_DEV + head + 1) * WIDE
            ]
            grads = head_grads[head]
            scores = dot_nt(queries, keys_all) * SCORE_SCALE
            probs = jnp.where(allowed, jnp.exp(scores - mass_ref[head, rows, :]), 0.0)
            prob_grad = dot_nt(grads, values_all)
            row_sum = jnp.sum(probs * prob_grad, axis=1, keepdims=True)
            score_grad = (probs * (prob_grad - row_sum)).astype(BF16)
            query_grad = dot(score_grad, keys_all) * (HEAD_DIM**-0.5)
            dz[rows, head * WIDE : (head + 1) * WIDE] = (query_grad * table_ref[rows, :]).astype(BF16)
            spot = slice(head * WIDE, (head + 1) * WIDE)
            key_acc[:keys, spot] += dot_tn(score_grad, queries)
            value_acc[:keys, spot] += dot_tn(probs.astype(BF16), grads)
    for block in range(CTX):
        rows = pl.ds(block * ROWS, ROWS)
        table = table_ref[rows, :] * (HEAD_DIM**-0.5)
        for head in range(HEADS_DEV):
            spot = slice(head * WIDE, (head + 1) * WIDE)
            at = (HEADS_DEV + head) * WIDE
            dz[rows, at : at + WIDE] = (key_acc[rows, spot] * table).astype(BF16)
            at = (2 * HEADS_DEV + head) * WIDE
            dz[rows, at : at + WIDE] = value_acc[rows, spot].astype(BF16)

    def make(block):
        part[rows_of(block), :] = dot_nt(dz[rows_of(block), :], w_ref[...]).astype(BF16)

    def beside():
        wide_lanes = lax.broadcasted_iota(jnp.int32, (D, WIDE), 1)
        pieces = []
        for piece in range(3):
            spot = slice(piece * HEADS_DEV * WIDE, (piece + 1) * HEADS_DEV * WIDE)
            terms = dot_tn(a_ref[...], dz[:, spot])
            for head in range(HEADS_DEV):
                term = terms[:, head * WIDE : (head + 1) * WIDE]
                if piece < 2:
                    term = term + jnp.where(
                        wide_lanes < HEAD_DIM // 2,
                        pltpu.roll(term, HEAD_DIM // 2, 1),
                        -pltpu.roll(term, WIDE - HEAD_DIM // 2, 1),
                    )
                pieces.append(term)
        for pair in range(4):
            joined = jnp.where(
                wide_lanes < HEAD_DIM,
                pieces[2 * pair],
                pltpu.roll(pieces[2 * pair + 1], HEAD_DIM, 1),
            )
            dheads_ref[:, pair * WIDE : (pair + 1) * WIDE] = joined.astype(BF16)
        dheads_ref[:, 4 * WIDE :] = pieces[8][:, :HEAD_DIM].astype(BF16)

    normed_grad = reduce_rows(make, part, across_in, from_left, from_right, send_r, recv_r, beside)
    tokens = u_ref[...].astype(F32)
    scale_one = inverse_size(tokens)
    normal_one = tokens * scale_one
    gain_one_column = lax.dot_general(
        normed_grad * normal_one, ones, TN, precision=EXACT, preferred_element_type=F32
    )
    scaled_one = normed_grad * gains_ref[0:1, :]
    input_grad = input_ref[...] + scale_one * (
        scaled_one - normal_one * jnp.mean(scaled_one * normal_one, axis=1, keepdims=True)
    )
    input_ref[...] = input_grad
    small_lanes = lax.broadcasted_iota(jnp.int32, (D, LANES), 1)
    small_ref[...] = jnp.where(
        small_lanes == EXPERTS,
        gain_one_column,
        jnp.where(small_lanes == EXPERTS + 1, gain_two_column, router_terms),
    ).astype(BF16)
    if not last:
        lower_ref[rows_of(me), :] = input_grad.astype(BF16)
        gather_rows(lower_ref, *rest[13:])


def attn_backward(last, length, *arrays):
    sems = pltpu.SemaphoreType.DMA
    out_shape = [jax.ShapeDtypeStruct((ROWS, D), F32)]
    if not last:
        out_shape.append(jax.ShapeDtypeStruct((SEQ, D), BF16))
    out_shape += [
        jax.ShapeDtypeStruct((D, 3 * COLS), BF16),
        jax.ShapeDtypeStruct((D, D), BF16),
        jax.ShapeDtypeStruct((D, LANES), BF16),
    ]
    scratch = [
        pltpu.VMEM((SEQ, HEADS_DEV * WIDE), F32),
        pltpu.VMEM((SEQ, HEADS_DEV * WIDE), F32),
        pltpu.VMEM((SEQ, EXT), BF16),
        pltpu.VMEM((CTX, ROWS, COLS), BF16),
        pltpu.VMEM((CTX, ROWS, COLS), BF16),
        sems((CTX,)),
        sems((CTX,)),
    ] + REDUCE_SCRATCH
    if not last:
        scratch += [sems((6,)), sems((6,))]
    return pl.pallas_call(
        functools.partial(attn_backward_kernel, last),
        out_shape=tuple(out_shape),
        in_specs=[SMEM] + [VMEM] * len(arrays),
        out_specs=[VMEM] * len(out_shape),
        scratch_shapes=scratch,
        compiler_params=params(3 if last else 4),
        name="attn_backward",
    )(length, *arrays)


SHARDS_STEP = 4
IN_ROWS = D
HALF_ROWS = (D + D * 128 // 256) // 2


def assemble(w_ref, win, wout):
    shards, units = win.shape[0], LANES
    width = 2 * units
    split = HALF_ROWS
    for shard in range(shards):
        win[shard, :split, :] = w_ref[0, shard]
        win[shard, split:, :] = w_ref[1, shard, : D - split, :]
        for piece in range(D // width):
            at = D - split + piece * units
            wout[shard * units : (shard + 1) * units, piece * width : (piece + 1) * width] = w_ref[
                1, shard, at : at + units, :
            ]


def ffn_forward_kernel(
    b_ref, gate_ref, residual_ref, w_ref, y_ref, kept_ref, acc, win, wout,
    part, across_in, from_left, from_right, send, recv,
):
    step = pl.program_id(0)
    final = pl.num_programs(0) - 1
    shards, units = win.shape[0], LANES

    @pl.when(step == 0)
    def _():
        _, right, left, _ = ring()
        greet((right, left))
        acc[...] = jnp.zeros_like(acc)

    assemble(w_ref, win, wout)

    def terms(block):
        rows = rows_of(block)
        b_rows = b_ref[rows, :]
        acted = []
        for shard in range(shards):
            hidden = dot(b_rows, win[shard])
            kept_ref[shard, rows, :] = hidden.astype(BF16)
            gate_part = hidden[:, :units]
            acted.append(
                (gate_part / (1.0 + jnp.exp(-gate_part)) * hidden[:, units:]).astype(BF16)
            )
        return acc[rows, :] + dot(jnp.concatenate(acted, axis=1), wout[...])

    @pl.when(step < final)
    def _():
        for block in range(CTX):
            acc[pl.ds(block * ROWS, ROWS), :] = terms(block)

    @pl.when(step == final)
    def _():
        met(2)

        def make(block):
            rows = rows_of(block)
            part[rows, :] = (terms(block) * gate_ref[rows, :]).astype(BF16)

        total = reduce_rows(make, part, across_in, from_left, from_right, send, recv)
        y_ref[...] = (residual_ref[...] + total).astype(BF16)


def ffn_forward(b_all, gate_col, residual, weights):
    _, count, half_rows, double = weights.shape
    shards = SHARDS_STEP
    return pl.pallas_call(
        ffn_forward_kernel,
        grid=(count // shards,),
        out_shape=(
            jax.ShapeDtypeStruct((ROWS, D), BF16),
            jax.ShapeDtypeStruct((count, SEQ, double), BF16),
        ),
        in_specs=[
            whole((SEQ, D)),
            whole((SEQ, 1)),
            whole((ROWS, D)),
            pl.BlockSpec((2, shards, half_rows, double), lambda i: (0, i, 0, 0)),
        ],
        out_specs=[whole((ROWS, D)), pl.BlockSpec((shards, SEQ, double), lambda i: (i, 0, 0))],
        scratch_shapes=[
            pltpu.VMEM((SEQ, D), F32),
            pltpu.VMEM((shards, D, double), BF16),
            pltpu.VMEM((shards * double // 2, D), BF16),
        ]
        + REDUCE_SCRATCH,
        compiler_params=params(5),
        name="ffn_forward",
    )(b_all, gate_col, residual, weights)


def ffn_backward_kernel(
    b_ref, gate_ref, delta_ref, kept_ref, w_ref, db_ref, gate_grad_ref, dw_ref,
    acc, gate_acc, b_turned, slot_grad, hidden_grad, acted, win, wout, rows_out, rows_in, send_g, recv_g,
    part, across_in, from_left, from_right, send, recv,
):
    step = pl.program_id(0)
    final = pl.num_programs(0) - 1
    shards, units = win.shape[0], LANES
    width = 2 * units

    @pl.when(step == 0)
    def _():
        _, right, left, across = ring()
        greet((right, left, across))
        acc[...] = jnp.zeros_like(acc)
        gate_acc[...] = jnp.zeros_like(gate_acc)
        b_turned[...] = b_ref[...].T
        slot_grad[...] = (delta_ref[...].astype(F32) * gate_ref[...]).astype(BF16)

    assemble(w_ref, win, wout)

    def terms(block):
        rows = rows_of(block)
        gate = gate_ref[rows, :]
        act_grad_all = dot_nt(delta_ref[rows, :], wout[...])
        gate_sum = gate_acc[rows, :]
        second_grad = acc[rows, :]
        for shard in range(shards):
            hidden = kept_ref[shard, rows, :].astype(F32)
            gate_part = hidden[:, :units]
            up_part = hidden[:, units:]
            act_grad = act_grad_all[:, shard * units : (shard + 1) * units]
            sigmoid = 1.0 / (1.0 + jnp.exp(-gate_part))
            silu = gate_part * sigmoid
            act = (silu * up_part).astype(BF16)
            acted[rows, shard * units : (shard + 1) * units] = act
            gate_sum += act.astype(F32) * act_grad
            act_grad = act_grad * gate
            gate_grad = act_grad * up_part * (sigmoid * (1.0 + gate_part * (1.0 - sigmoid)))
            pair = jnp.concatenate([gate_grad, act_grad * silu], axis=1).astype(BF16)
            hidden_grad[shard, rows, :] = pair
            second_grad += dot_nt(pair, win[shard])
        gate_acc[rows, :] = gate_sum
        return second_grad

    def weight_terms():
        split = HALF_ROWS
        for shard in range(shards):
            whole_in = dot(b_turned[...], hidden_grad[shard]).astype(BF16)
            dw_ref[0, shard] = whole_in[:split]
            dw_ref[1, shard, : D - split, :] = whole_in[split:]
        whole_out = dot_tn(acted[...], slot_grad[...]).astype(BF16)
        for shard in range(shards):
            for piece in range(D // width):
                at = D - split + piece * units
                dw_ref[1, shard, at : at + units, :] = whole_out[
                    shard * units : (shard + 1) * units, piece * width : (piece + 1) * width
                ]

    @pl.when(step < final)
    def _():
        for block in range(CTX):
            acc[pl.ds(block * ROWS, ROWS), :] = terms(block)
        weight_terms()

    @pl.when(step == final)
    def _():
        met(3)
        me, right, left, across = ring()

        def make(block):
            part[rows_of(block), :] = terms(block).astype(BF16)

        def handed(step_to, peer):
            return remote(
                rows_out.at[peer], rows_in.at[step_to], send_g.at[step_to], recv_g.at[step_to], peer
            )

        def beside():
            own_row = lax.broadcasted_iota(jnp.int32, (8, LANES), 0) == me
            picker = jnp.where(own_row, 1.0, 0.0)
            for block in range(CTX):
                rows_out[block] = lax.dot_general(
                    picker,
                    gate_acc[pl.ds(block * ROWS, ROWS), :],
                    NT,
                    precision=EXACT,
                    preferred_element_type=F32,
                )
            for step_to, peer in ((0, right), (1, left), (2, across)):
                handed(step_to, peer).start()
            weight_terms()

        db_ref[...] = reduce_rows(
            make, part, across_in, from_left, from_right, send, recv, beside
        )
        for step_to, peer in ((0, right), (1, left), (2, across)):
            handed(step_to, peer).wait()
        rows_all = rows_out[me] + rows_in[0] + rows_in[1] + rows_in[2]
        picker = jnp.where(
            lax.broadcasted_iota(jnp.int32, (8, LANES), 0)
            == lax.broadcasted_iota(jnp.int32, (8, LANES), 1),
            1.0,
            0.0,
        )
        gate_grad_ref[...] = lax.dot_general(
            rows_all, picker, TN, precision=EXACT, preferred_element_type=F32
        )


def ffn_backward(b_all, gate_col, delta_all, kept, weights):
    _, count, half_rows, double = weights.shape
    shards = SHARDS_STEP
    units = double // 2
    sems = pltpu.SemaphoreType.DMA
    return pl.pallas_call(
        ffn_backward_kernel,
        grid=(count // shards,),
        out_shape=(
            jax.ShapeDtypeStruct((ROWS, D), F32),
            jax.ShapeDtypeStruct((ROWS, LANES), F32),
            jax.ShapeDtypeStruct(weights.shape, BF16),
        ),
        in_specs=[
            whole((SEQ, D)),
            whole((SEQ, 1)),
            whole((SEQ, D)),
            pl.BlockSpec((shards, SEQ, double), lambda i: (i, 0, 0)),
            pl.BlockSpec((2, shards, half_rows, double), lambda i: (0, i, 0, 0)),
        ],
        out_specs=[
            whole((ROWS, D)),
            whole((ROWS, LANES)),
            pl.BlockSpec((2, shards, half_rows, double), lambda i: (0, i, 0, 0)),
        ],
        scratch_shapes=[
            pltpu.VMEM((SEQ, D), F32),
            pltpu.VMEM((SEQ, units), F32),
            pltpu.VMEM((D, SEQ), BF16),
            pltpu.VMEM((SEQ, D), BF16),
            pltpu.VMEM((shards, SEQ, double), BF16),
            pltpu.VMEM((SEQ, shards * units), BF16),
            pltpu.VMEM((shards, D, double), BF16),
            pltpu.VMEM((shards * units, D), BF16),
            pltpu.VMEM((CTX, 8, ROWS), F32),
            pltpu.VMEM((3, 8, ROWS), F32),
            sems((3,)),
            sems((3,)),
        ]
        + REDUCE_SCRATCH,
        compiler_params=params(6),
        name="ffn_backward",
    )(b_all, gate_col, delta_all, kept, weights)

def rotary_table():
    half_dim = HEAD_DIM // 2
    frequency = jnp.exp(
        -jnp.log(10000.0) * (2.0 * jnp.arange(half_dim, dtype=F32) / HEAD_DIM)
    )
    angles = jnp.arange(SEQ, dtype=jnp.int32).astype(F32)[:, None] * frequency[None, :]
    cosine, sine = jnp.cos(angles), jnp.sin(angles)
    return jnp.concatenate([cosine, cosine, sine, sine], axis=1)


def extended(w_heads):
    half_dim = HEAD_DIM // 2
    turning = w_heads[:, : 2 * COLS].reshape(D, 2 * HEADS_DEV, 2, half_dim)
    first, second = turning[:, :, 0], turning[:, :, 1]
    turning = jnp.concatenate([first, second, -second, first], axis=2)
    values = w_heads[:, 2 * COLS :].reshape(D, HEADS_DEV, HEAD_DIM)
    values = jnp.concatenate([values, jnp.zeros_like(values)], axis=2)
    return jnp.concatenate(
        [turning.reshape(D, 2 * HEADS_DEV * WIDE), values.reshape(D, HEADS_DEV * WIDE)], axis=1
    )


def layer_forward(weights, tokens_in, length, routes_all, table):
    gains, router, w_ext, w_back, experts = weights
    a_all, qkv, mass, attended, residual, b_all, gates, gate_col = attn_forward(
        length, tokens_in, gains, router, routes_all, w_ext, w_back, table
    )
    output, kept = ffn_forward(b_all, gate_col, residual, experts)
    return output, (tokens_in, a_all, qkv, mass, attended, residual, b_all, gates, gate_col, kept)


def layer_backward(weights, saved, delta_all, delta_own, length, table, ctx_index, last):
    gains, router, w_ext, w_back, experts = weights
    tokens_in, a_all, qkv, mass, attended, residual, b_all, gates, gate_col, kept = saved
    db, gate_grads, dexperts = ffn_backward(b_all, gate_col, delta_all, kept, experts)
    second = lax.dynamic_slice_in_dim(b_all, ctx_index * ROWS, ROWS, 0)
    own_gates = lax.dynamic_slice_in_dim(gates, ctx_index * ROWS, ROWS, 0)
    results = attn_backward(
        last, length, tokens_in, gains, router, w_ext, w_back, table, a_all, qkv, mass,
        attended, residual, second, own_gates, delta_own, db, gate_grads,
    )
    return dexperts, results

def adam_update(gradient, clipped, master, mean_old, square_old, step_value, learn_rate):
    mean_new = BETA_ONE * mean_old + (1.0 - BETA_ONE) * clipped
    square_new = BETA_TWO * square_old + (1.0 - BETA_TWO) * clipped * clipped
    fix_one = 1.0 - BETA_ONE**step_value
    fix_two = 1.0 - BETA_TWO**step_value
    master_new = master - learn_rate * (
        mean_new / fix_one / (jnp.sqrt(square_new / fix_two) + ADAM_EPS) + DECAY_RATE * master
    )
    return (gradient, mean_new, square_new, master_new, master_new.astype(BF16))


def on_device(
    inputs, cotangent, lengths, routes, step_count,
    norm_gains, gains_mean, gains_square,
    attn_weight, attn_mean, attn_square,
    router_weight, router_mean, router_square,
    expert_in, in_mean, in_square,
    expert_out, out_mean, out_square,
):
    section = lax.axis_index("section")
    ctx_index = lax.axis_index("ctx")
    fsdp = lax.axis_size("fsdp")
    everyone = ("section", "fsdp")
    shard_rows = attn_weight.shape[1]
    units = expert_in.shape[4]
    first_core = section == 0

    def own_columns(matrix, part):
        return lax.dynamic_slice_in_dim(matrix, part * D + ctx_index * COLS, COLS, 1)

    def swap(block):
        return lax.ppermute(block, "section", [(0, 1), (1, 0)])

    attn_shard = jnp.concatenate(
        [own_columns(attn_weight[0], part) for part in range(3)]
        + [attn_weight[0][:, 3 * D :], norm_gains[0].T, router_weight[0]],
        axis=1,
    ).astype(BF16)
    in_shard = (
        lax.dynamic_index_in_dim(expert_in[0], ctx_index, 0, keepdims=False)
        .astype(BF16)
        .reshape(D, 2 * units)
    )
    out_shard = lax.dynamic_index_in_dim(expert_out[0], ctx_index, 0, keepdims=False).astype(BF16)
    halves = jnp.concatenate(
        [in_shard] + [out_shard[:, at : at + 2 * units] for at in range(0, D, 2 * units)], axis=0
    ).reshape(2, HALF_ROWS, 2 * units)
    other = swap(jnp.where(first_core, halves[1], halves[0]))
    attn_full = lax.all_gather(attn_shard, everyone, tiled=True).reshape(2, D, -1)
    pieces = (jnp.where(first_core, halves[0], other), jnp.where(first_core, other, halves[1]))
    experts = [
        lax.all_gather(piece, everyone).reshape(2, fsdp, HALF_ROWS, 2 * units) for piece in pieces
    ]
    routes_all = lax.all_gather(routes[0], ("section", "ctx")).reshape((2, CTX) + routes.shape[1:])
    routes_all = lax.dynamic_index_in_dim(routes_all, section, 2, keepdims=False).reshape(2, SEQ, 2)
    length = lax.dynamic_slice_in_dim(lengths, section, 1, 0)
    tokens = lax.dynamic_index_in_dim(inputs, section, 0, keepdims=False)
    positions = ctx_index * ROWS + jnp.arange(ROWS, dtype=jnp.int32)
    seed = lax.dynamic_index_in_dim(cotangent, section, 0, keepdims=False)
    seed = jnp.where((positions < length[0])[:, None], seed, jnp.zeros_like(seed))
    seed_all = lax.all_gather(seed, "ctx", tiled=True)
    table = rotary_table()

    layers = []
    for layer in range(2):
        full = attn_full[layer]
        small_at = 3 * COLS + D
        gains = full[:, small_at : small_at + 2].astype(F32).T
        router = jnp.pad(full[:, small_at + 2 :], ((0, 0), (0, LANES - EXPERTS)))
        layers.append(
            (
                jnp.pad(gains, ((0, 6), (0, 0))),
                router,
                extended(full[:, : 3 * COLS]),
                full[:, 3 * COLS : small_at],
                experts[layer],
            )
        )
    lower_out, lower_saved = layer_forward(layers[0], tokens, length, routes_all[0], table)
    upper_out, upper_saved = layer_forward(layers[1], lower_out, length, routes_all[1], table)

    def scattered(terms):
        return lax.psum_scatter(
            terms.reshape((2 * fsdp,) + terms.shape[2:]), everyone, scatter_dimension=0, tiled=True
        )[0]

    upper_experts, (upper_grad, lower_seed, *upper_rest) = layer_backward(
        layers[1], upper_saved, seed_all, seed, length, table, ctx_index, False
    )
    upper_half = scattered(upper_experts)
    own_seed = upper_grad.astype(BF16)
    lower_experts, (lower_grad, *lower_rest) = layer_backward(
        layers[0], lower_saved, lower_seed, own_seed, length, table, ctx_index, True
    )
    lower_half = scattered(lower_experts)

    def paired(first, second):
        kept = jnp.where(first_core, first, second)
        other = swap(jnp.where(first_core, second, first))
        return jnp.stack(
            [jnp.where(first_core, kept, other), jnp.where(first_core, other, kept)]
        )

    layer_outputs = paired(lower_out, upper_out)[None]
    input_grads = paired(lower_grad, upper_grad)[None]
    expert_part = paired(lower_half, upper_half).reshape(2 * HALF_ROWS, 2 * units)
    attn_terms = jnp.stack([jnp.concatenate(lower_rest, axis=1), jnp.concatenate(upper_rest, axis=1)])
    attn_part = scattered(attn_terms.reshape(2, fsdp, shard_rows, -1))
    expert_all = lax.all_gather(expert_part, "ctx")
    attn_all = lax.all_gather(attn_part, "ctx")
    in_sum = expert_all[:, :D].astype(F32).reshape(1, CTX, D, 2, units)
    out_sum = jnp.concatenate(
        [expert_all[:, at : at + units] for at in range(D, 2 * HALF_ROWS, units)], axis=2
    ).astype(F32)[None]
    heads_sum = attn_all[:, :, : 3 * COLS].astype(F32)
    heads_sum = (
        heads_sum.reshape(CTX, shard_rows, 3, COLS).transpose(1, 2, 0, 3).reshape(shard_rows, 3 * D)
    )
    rest_sum = jnp.sum(attn_all[:, :, 3 * COLS :].astype(F32), axis=0)
    attn_sum = jnp.concatenate([heads_sum, rest_sum[:, :D]], axis=1)[None]
    router_sum = rest_sum[:, D : D + EXPERTS][None]
    gain_sum = rest_sum[:, D + EXPERTS : D + EXPERTS + 2].T[None]
    sums = (gain_sum, attn_sum, router_sum, in_sum, out_sum)
    squares = lax.psum(jnp.stack([jnp.sum(total * total) for total in sums]), "fsdp")
    norms = jnp.sqrt(squares)
    factors = jnp.minimum(1.0, CLIP_LIMIT / norms)
    step_value = step_count[0].astype(F32)
    wide_rate = RATE_FACTOR / D**0.5
    router_rate = RATE_FACTOR / (D // 4) ** 0.5
    down_rate = RATE_FACTOR / FFN**0.5
    olds = (
        (norm_gains, gains_mean, gains_square, GAIN_RATE),
        (attn_weight, attn_mean, attn_square, wide_rate),
        (router_weight, router_mean, router_square, router_rate),
        (expert_in, in_mean, in_square, wide_rate),
        (expert_out, out_mean, out_square, down_rate),
    )
    results = [layer_outputs, input_grads]
    for index, (total, (master, mean_old, square_old, rate)) in enumerate(zip(sums, olds)):
        results.extend(
            adam_update(total, total * factors[index], master, mean_old, square_old, step_value, rate)
        )
    return tuple(results) + (norms[None],)


def solution(mesh):
    gains = P("section", None, "fsdp")
    rows = P("section", "fsdp", None)
    wide = P("section", None, None, None, "fsdp")
    down = P("section", None, "fsdp", None)
    tokens = P("section", "fsdp", "ctx", None)
    return jax.shard_map(
        on_device,
        mesh=mesh,
        in_specs=(
            P("fsdp", "ctx", None),
            P("fsdp", "ctx", None),
            P("fsdp"),
            tokens,
            P(),
        )
        + (gains,) * 3
        + (rows,) * 6
        + (wide,) * 3
        + (down,) * 3,
        out_specs=(tokens, tokens)
        + (gains,) * 5
        + (rows,) * 10
        + (wide,) * 5
        + (down,) * 5
        + (P("section", None),),
        check_vma=False,
    )
```

time: 1760 us -> 807 us (0.46)
  matrix products: 442 us -> 0 us
  waiting for transfers between devices: 641 us -> 257 us
  Pallas kernels: 0 us -> 329 us
  local copies, waits for them, and re-layouts: 262 us -> 56.9 us
  other arithmetic: 233 us -> 58.9 us
  blocking collectives: 140 us -> 76.6 us
    dot_general x81 -> x0, matrix products: 442 us -> none  [the longest x3 51.1 us: expert_backward(): jnp.einsum('pecd,pecgf->edgf', buffer, pre_grad, preferred_element_type=j...]
    pallas_call x0 -> x8, Pallas kernels: none -> 329 us  [the longest x2 107 us: attn_forward(): pl.pallas_call(attn_forward_kernel, out_shape=(jax.ShapeDtypeStruct((SEQ,...]
    all_gather x9 -> x5, waiting for transfers between devices: 326 us -> 28.5 us  [the longest x1 15.7 us: on_device(): expert_all = lax.all_gather(expert_part, 'ctx')]
    unnamed x486 -> x58, local copies, waits for them, and re-layouts: 167 us -> 5.01 us
    convert_element_type x34 -> x8, other arithmetic: 150 us -> 29.4 us  [the longest x5 26.9 us: adam_update(): return (gradient, mean_new, square_new, master_new, master_new.astype(BF16))]
    unnamed x20 -> x8, waiting for transfers between devices: 61.9 us -> 1.29 us
    unnamed x1 -> x0, blocking collectives: 38.8 us -> none
    gather x15 -> x0, local copies, waits for them, and re-layouts: 31.1 us -> none  [the longest x9 15.6 us: layer_forward(): chosen = jnp.take_along_axis(logits, route_rows, axis=1)]
  transfers between devices with their start and end apart: 23 -> 12, of which waited for: 19 -> 9; matrix products, arithmetic and copies ran while one was open for 29% -> 9% of each run, Pallas kernels for 0% -> 26%
where the time goes in v1:
time: 807 us; the launch traced here: 795 us
  Pallas kernels  329 us (41%)
  waiting for transfers between devices  257 us (32%)
  blocking collectives  76.6 us (9%)
  other arithmetic  58.9 us (7%)
  local copies, waits for them, and re-layouts  56.9 us (7%)
  between operations  15.8 us (2%)
    reduce_scatter x3, waiting for transfers between devices, scattered(): lax.psum_scatter(terms.reshape((2 * fsdp,) + terms.shape[2:]), everyone,...  223 us
    pallas_call x2, Pallas kernels, attn_forward(): pl.pallas_call(attn_forward_kernel, out_shape=(jax.ShapeDtypeStruct((SEQ,...  107 us
    pallas_call x2, Pallas kernels, attn_backward(): pl.pallas_call(functools.partial(attn_backward_kernel, last), out_shape=t...  88.9 us
    pallas_call x2, Pallas kernels, ffn_backward(): pl.pallas_call(ffn_backward_kernel, grid=(count // shards,), out_shape=(j...  74.2 us
    pallas_call x2, Pallas kernels, ffn_forward(): pl.pallas_call(ffn_forward_kernel, grid=(count // shards,), out_shape=(ja...  58.9 us
    psum x1, blocking collectives, on_device(): lax.psum(jnp.stack([jnp.sum(total * total) for total in sums]), 'fsdp')  40.7 us
    convert_element_type x5, other arithmetic, adam_update(): return (gradient, mean_new, square_new, master_new, master_new.astype(BF16))  26.9 us
    all_gather x1, blocking collectives, on_device(): lax.all_gather(routes[0], ('section', 'ctx'))  21.7 us
  transfers between devices with their start and end apart: 12, of which 9 were waited for; matrix products, arithmetic and copies ran while one was open for 9% of the time, Pallas kernels for 26%

profile of v1, /device:TPU:0, one launch (start us, length us, event | category | flops | bytes accessed | tf_op | source)
XLA Modules:
  0.0 794.8 jit_solution(1216407499118250459)
XLA Ops:
  7.3 1.2 convert_bitcast_fusion
  10.0 1.0 fusion.8
  11.9 1.4 dynamic-slice_convert_fusion
  13.6 1.0 fusion.5
  14.9 1.6 collective-permute-done
  16.5 0.9 broadcast_select_fusion.5
  19.5 0.9 bitcast_select_fusion.delta_ref
  20.4 21.7 %all_gather.28 = s32[8,2,256,2]{2,3,1,0:T(2,128)S(1)} all-gather(s32[1,2,256,2]{2,3,1,0:T(2,128)S(1)} %copy-done.17), channel_id=1, replica_groups=mesh['section'=2,'ctx'=4,'fsdp'=16] {'section','ctx'}, dimensions={0}, use_global_device_ids=true | all-gather | bytes 36864 | tf_op jit(solution)/shard_map/all_gather | solution.py:819
  42.2 1.0 copy.209
  44.0 1.0 copy.210
  45.0 1.9 multiply_cosine_fusion
  46.9 1.3 pad_maximum_fusion.7.table_ref
  48.1 12.9 %all-gather.8.cloned.1.call-done = bf16[1536,1349]{1,0:T(8,128)(2,1)} async-done(((bf16[48,1349]{1,0:T(8,128)(2,1)}), bf16[1536,1349]{1,0:T(8,128)(2,1)}) %all-gather.8.cloned.1.call-update) | async-done | bytes 4144144 | tf_op jit(solution)/shard_map/all_gather | solution.py:814
  61.0 1.4 fusion.24
  62.7 1.9 fusion.25
  64.6 1.9 slice_bitcast_fusion.7
  67.4 1.1 copy.191
  69.3 1.9 fusion.26
  72.3 0.9 copy.196
  73.2 1.2 copy.195
  74.3 0.9 concatenate.96
  75.2 1.4 copy.197
  76.6 1.7 pad_convert_fusion
  78.3 1.7 copy.198.gains_ref
  80.0 1.6 pad.25.router_ref
  81.7 1.3 pad_maximum_fusion.1.w_ref
  83.0 4.3 fusion.23
  87.3 53.6 %attn_forward.2 = (bf16[1024,768]{1,0:T(8,128)(2,1)}, bf16[1024,1152]{1,0:T(8,128)(2,1)}, f32[3,1024,1]{2,1,0:T(8,128)}, bf16[4,256,192]{2,1,0:T(8,128)(2,1)}, f...) custom-call(s32[1]{0:T(128)} %dynamic_slice.49.length_ref, ...), custom_call_target="tpu_custom_call" | custom-call | tf_op jit(solution)/shard_map/attn_forward/pallas_call | solution.py:273
  140.9 1.3 pad_maximum_fusion.2.w_ref
  142.2 32.0 %ffn_forward.2 = (bf16[256,768]{1,0:T(8,128)(2,1)}, bf16[16,1024,256]{2,1,0:T(8,128)(2,1)}) custom-call(bf16[1024,768]{1,0:T(8,128)(2,1)} %get-tuple-element.63.b_ref, f32[1024,1]{1,0:T(8,128)} %get-tuple-element.64.gate_ref, f32[256,768]{1,0:T(8,128)} %get-tuple-element.65.residual_ref, bf16[2,16,576,256]{3,2,1,0:T(8,128)(2,1)} %bitcast.141), custom_call_target="tpu_custom_call" | custom-call | tf_op jit(solution)/shard_map/ffn_forward/pallas_call | solution.py:544
  174.2 53.4 %attn_forward.3 = (bf16[1024,768]{1,0:T(8,128)(2,1)}, bf16[1024,1152]{1,0:T(8,128)(2,1)}, f32[3,1024,1]{2,1,0:T(8,128)}, bf16[4,256,192]{2,1,0:T(8,128)(2,1)}, f...) custom-call(s32[1]{0:T(128)} %dynamic_slice.49.length_ref, ...), custom_call_target="tpu_custom_call" | custom-call | tf_op jit(solution)/shard_map/attn_forward/pallas_call | solution.py:273
  227.7 26.9 %ffn_forward.3 = (bf16[256,768]{1,0:T(8,128)(2,1)}, bf16[16,1024,256]{2,1,0:T(8,128)(2,1)}) custom-call(bf16[1024,768]{1,0:T(8,128)(2,1)} %get-tuple-element.67.b_ref, f32[1024,1]{1,0:T(8,128)} %get-tuple-element.68.gate_ref, f32[256,768]{1,0:T(8,128)} %get-tuple-element.69.residual_ref, bf16[2,16,576,256]{3,2,1,0:T(8,128)(2,1)} %bitcast.143), custom_call_target="tpu_custom_call" | custom-call | tf_op jit(solution)/shard_map/ffn_forward/pallas_call | solution.py:544
  254.6 1.7 constant_dynamic-slice_fusion.1
  256.3 2.0 constant_dynamic-slice_fusion.2
  258.3 38.1 %ffn_backward.2 = (f32[256,768]{1,0:T(8,128)}, f32[256,128]{1,0:T(8,128)}, bf16[2,16,576,256]{3,2,1,0:T(8,128)(2,1)}) custom-call(bf16[1024,768]{1,0:T(8,128)(2,1)} %get-tuple-element.67.b_ref, f32[1024,1]{1,0:T(8,128)} %get-tuple-element.68.gate_ref, bf16[1024,768]{1,0:T(8,128)(2,1)} %all-gather.10.cloned.1.call-done.delta_ref, ...), custom_call_target="tpu_custom_call" | custom-call | tf_op jit(solution)/shard_map/ffn_backward/pallas_call | solution.py:684
  296.5 51.0 %attn_backward.2 = (f32[256,768]{1,0:T(8,128)}, bf16[1024,768]{1,0:T(8,128)(2,1)}, bf16[768,576]{1,0:T(8,128)(2,1)}, bf16[768,768]{1,0:T(8,128)(2,1)}, bf16[768,128]{1,0:T(8,128)(2,1)}) custom-call(s32[1]{0:T(128)} %dynamic_slice.49.length_ref, bf16[256,768]{1,0:T(8,128)(2,1)} %get-tuple-element.66.u_ref, f32[8,768]{1,0:T(8,128)} %copy.198.gains_ref, ...), custom_call_target="tpu_custom_call" | custom-call | tf_op jit(solution)/shard_map/attn_backward/pallas_call | solution.py:465
  347.5 36.1 %ffn_backward.3 = (f32[256,768]{1,0:T(8,128)}, f32[256,128]{1,0:T(8,128)}, bf16[2,16,576,256]{3,2,1,0:T(8,128)(2,1)}) custom-call(bf16[1024,768]{1,0:T(8,128)(2,1)} %get-tuple-element.63.b_ref, f32[1024,1]{1,0:T(8,128)} %get-tuple-element.64.gate_ref, bf16[1024,768]{1,0:T(8,128)(2,1)} %get-tuple-element.85.delta_ref, ...), custom_call_target="tpu_custom_call" | custom-call | tf_op jit(solution)/shard_map/ffn_backward/pallas_call | solution.py:684
  385.6 37.9 %attn_backward.3 = (f32[256,768]{1,0:T(8,128)}, bf16[768,576]{1,0:T(8,128)(2,1)}, bf16[768,768]{1,0:T(8,128)(2,1)}, bf16[768,128]{1,0:T(8,128)(2,1)}) custom-call(s32[1]{0:T(128)} %dynamic_slice.49.length_ref, bf16[256,768]{1,0:T(8,128)(2,1)} %dynamic-slice_bitcast_fusion.u_ref, f32[8,768]{1,0:T(8,128)} %copy.193.gains_ref, ...), custom_call_target="tpu_custom_call" | custom-call | tf_op jit(solution)/shard_map/attn_backward/pallas_call | solution.py:465
  423.5 4.3 concatenate.98
  427.7 5.2 concatenate.99
  432.9 4.3 pad_maximum_fusion
  437.3 46.5 %reduce-scatter.6.cloned.1.call-done = bf16[1,576,256]{2,1,0:T(8,128)(2,1)} async-done(((bf16[32,576,256]{2,1,0:T(8,128)(2,1)}), bf16[1,576,256]{2,1,0:T(8,128)(2,1)}) %reduce-scatter.6.cloned.1.call-update) | async-done | bytes 294928 | tf_op jit(solution)/shard_map/reduce_scatter | solution.py:848
  483.8 99.0 %reduce-scatter.8.cloned.1.call-done = bf16[1,576,256]{2,1,0:T(8,128)(2,1)} async-done(((bf16[32,576,256]{2,1,0:T(8,128)(2,1)}), bf16[1,576,256]{2,1,0:T(8,128)(2,1)}) %reduce-scatter.8.cloned.1.call-update) | async-done | bytes 294928 | tf_op jit(solution)/shard_map/reduce_scatter | solution.py:848
  582.8 1.0 select_bitcast_fusion.4
  583.9 1.6 collective-permute-done.3
  585.5 1.0 fusion.3
  586.5 0.9 pad_maximum_fusion.6
  589.3 0.9 maximum_bitcast_fusion.1
  590.5 1.2 maximum_bitcast_fusion
  591.8 77.8 %reduce-scatter.4.cloned.1.call-done = bf16[1,48,1472]{2,1,0:T(8,128)(2,1)} async-done(((bf16[32,48,1472]{2,1,0:T(8,128)(2,1)}), bf16[1,48,1472]{2,1,0:T(8,128)(2,1)}) %reduce-scatter.4.cloned.1.call-update) | async-done | bytes 141328 | tf_op jit(solution)/shard_map/reduce_scatter | solution.py:848
  669.6 14.2 %all_gather.34 = bf16[4,48,1472]{2,1,0:T(8,128)(2,1)S(1)} all-gather(bf16[1,48,1472]{2,1,0:T(8,128)(2,1)} %reduce-scatter.4.cloned.1.call-done), channel_id=1, replica_groups=mesh['section'=2,'ctx'=4,'fsdp'=16] {'ctx'}, dimensions={0}, use_global_device_ids=true | all-gather | bytes 706560 | tf_op jit(solution)/shard_map/all_gather | solution.py:875
  687.7 0.9 maximum_bitcast_fusion.2
  688.5 15.7 %all-gather.12.cloned.1.call-done = bf16[4,1152,256]{2,1,0:T(8,128)(2,1)} async-done(((bf16[1,1152,256]{2,1,0:T(8,128)(2,1)}), bf16[4,1152,256]{2,1,0:T(8,128)(2,1)}) %all-gather.12.cloned.1.call-update) | async-done | bytes 2359312 | tf_op jit(solution)/shard_map/all_gather | solution.py:874
  704.2 1.3 slice_bitcast_fusion.6
  705.5 2.1 multiply_reduce_fusion.1
  707.6 1.4 multiply_reduce_fusion
  709.0 3.3 stack.71
  712.9 40.7 %psum.7 = f32[5]{0:T(128)S(1)} all-reduce(f32[5]{0:T(128)S(1)} %stack.71), channel_id=1, replica_groups=mesh['section'=2,'ctx'=4,'fsdp'=16] {'fsdp'}, use_global_device_ids=true, to_apply=%region_9.10 | all-reduce | flops 5 | bytes 40 | tf_op jit(solution)/shard_map/psum | solution.py:889
  754.7 1.7 slice_convert_fusion
  756.5 3.0 reshape.405
  761.4 4.3 fusion.19
  765.8 1.2 fusion.21
  767.0 6.8 fusion.14
  773.9 13.9 %fusion.16 = (bf16[1,4,768,2,128]{4,3,2,1,0:T(2,128)(2,1)}, f32[1,4,768,2,128]{4,3,2,1,0:T(2,128)}, f32[1,4,768,2,128]{4,3,2,1,0:T(2,128)}, f32[1,4,768,2,128]{4,3,2,1,0:T(2,128)}) fusion(f32[1,4,768,2,128]{4,3,2,1,0:T(2,128)S(1)} %copy-done.8, f32[]{:T(128)} %bitcast.62, f32[]{:T(128)} %bitcast.61, f32[1,4,768,2,128]{4,3,2,1,0:T(2,128)S(1)} %copy-done.2, ...), kind=kLoop, calls=%fused_computation.107 | loop fusion | flops 13369344 | bytes 23592972 | tf_op jit(solution)/shard_map/convert_element_type | solution.py:774
  (129 shorter events, 20.0 us)
Async XLA Ops:
  7.2 36.0 %copy-start = (bf16[2,256,768]{2,1,0:T(8,128)(2,1)S(1)}, bf16[2,256,768]{2,1,0:T(8,128)(2,1)}, u32[]{:S(2)}) copy-start(bf16[2,256,768]{2,1,0:T(8,128)(2,1)} %param.20) | copy-start | bytes 2359300
  7.2 53.8 %all-gather.8.cloned.1.call-start = ((), (), s32[]{:S(2)}) async-start(), calls=%async_computation.3 | async-start | bytes 4460544 | tf_op jit(solution)/shard_map/all_gather | solution.py:814
  11.9 130.3 %all-gather.14.cloned.1.call-start = ((), (), s32[]{:S(2)}) async-start(), calls=%async_computation.9 | async-start | bytes 9732096 | tf_op jit(solution)/shard_map/all_gather | solution.py:817
  14.7 3.5 copy-start.24
  14.7 4.8 copy-start.15
  14.8 5.6 copy-start.17
  14.8 1.7 collective-permute-start
  17.4 210.2 %all-gather.16.cloned.1.call-start = ((), (), s32[]{:S(2)}) async-start(), calls=%async_computation.10 | async-start | bytes 9732096 | tf_op jit(solution)/shard_map/all_gather | solution.py:817
  18.2 240.2 %all-gather.10.cloned.1.call-start = ((), (), s32[]{:S(2)}) async-start(), calls=%async_computation.4 | async-start | bytes 1966080 | tf_op jit(solution)/shard_map/all_gather | solution.py:826
  20.4 463.5 %reduce-scatter.6.cloned.1.call-start = ((), (), s32[]{:S(2)}) async-start(), calls=%async_computation.6 | async-start | bytes 9732096 | tf_op jit(solution)/shard_map/reduce_scatter | solution.py:848
  74.3 7.3 copy-start.12
  383.6 199.2 %reduce-scatter.8.cloned.1.call-start = ((), (), s32[]{:S(2)}) async-start(), calls=%async_computation.7 | async-start | bytes 9732096 | tf_op jit(solution)/shard_map/reduce_scatter | solution.py:848
  383.7 1.1 copy-start.3
  384.2 285.4 %reduce-scatter.4.cloned.1.call-start = ((), (), s32[]{:S(2)}) async-start(), calls=%async_computation.5 | async-start | bytes 4866048 | tf_op jit(solution)/shard_map/reduce_scatter | solution.py:848
  423.4 4.3 copy-start.14
  437.2 266.9 %all-gather.12.cloned.1.call-start = ((), (), s32[]{:S(2)}) async-start(), calls=%async_computation.8 | async-start | bytes 2949120 | tf_op jit(solution)/shard_map/all_gather | solution.py:874
  583.8 3.6 copy-start.5
  583.8 3.6 copy-start.13
  583.8 1.7 collective-permute-start.3
  586.5 1.3 copy-start.9
  587.5 1.8 collective-permute-start.1
  587.9 2.5 collective-permute-start.2
  685.1 68.9 %copy-start.7 = (f32[1,48,2304]{2,1,0:T(8,128)}, f32[1,48,2304]{2,1,0:T(8,128)S(1)}, u32[]{:S(2)}) copy-start(f32[1,48,2304]{2,1,0:T(8,128)S(1)} %concatenate.100) | copy-start | bytes 1327108
  685.7 80.1 %copy-start.18 = (f32[48,2]{0,1:T(2,128)}, f32[48,2]{0,1:T(2,128)S(1)}, u32[]{:S(2)}) copy-start(f32[48,2]{0,1:T(2,128)S(1)} %copy.211) | copy-start | bytes 1156
  704.2 3.4 copy-start.4
  756.4 3.8 copy-start.16
  756.4 3.8 copy-start.19
  756.5 3.8 copy-start.20
  756.5 9.3 %copy-start.21 = (f32[1,2,48]{2,1,0:T(2,128)S(1)}, f32[1,2,48]{2,1,0:T(2,128)}, u32[]{:S(2)}) copy-start(f32[1,2,48]{2,1,0:T(2,128)} %param.25) | copy-start | bytes 1156
  756.5 9.3 %copy-start.22 = (f32[1,2,48]{2,1,0:T(2,128)S(1)}, f32[1,2,48]{2,1,0:T(2,128)}, u32[]{:S(2)}) copy-start(f32[1,2,48]{2,1,0:T(2,128)} %param.27) | copy-start | bytes 1156
  756.5 9.3 %copy-start.23 = (f32[1,2,48]{2,1,0:T(2,128)S(1)}, f32[1,2,48]{2,1,0:T(2,128)}, u32[]{:S(2)}) copy-start(f32[1,2,48]{2,1,0:T(2,128)} %param.26) | copy-start | bytes 1156
  761.4 5.6 copy-start.6
  761.4 12.4 %copy-start.11 = (f32[1,4,768,2,128]{4,3,2,1,0:T(2,128)S(1)}, f32[1,4,768,2,128]{4,3,2,1,0:T(2,128)}, u32[]{:S(2)}) copy-start(f32[1,4,768,2,128]{4,3,2,1,0:T(2,128)} %param.35) | copy-start | bytes 9437188
  767.0 6.8 copy-start.2
  767.0 6.8 copy-start.8
  767.0 6.8 copy-start.10
  773.8 14.0 %copy-start.1 = (bf16[2,256,768]{2,1,0:T(8,128)(2,1)S(1)}, bf16[2,256,768]{2,1,0:T(8,128)(2,1)}, u32[]{:S(2)}) copy-start(bf16[2,256,768]{2,1,0:T(8,128)(2,1)} %param.20) | copy-start | bytes 2359300
Sparse Core Ops, SparseCore 0:
  12.0 48.9 all-gather.7
  63.8 54.7 all-gather.13
  121.5 54.9 all-gather.15
  178.6 31.5 all-gather.9
  383.7 100.0 reduce-scatter.5
  487.9 94.8 reduce-scatter.7
  586.5 83.0 reduce-scatter.3
  671.9 32.1 all-gather.11

commit v2 on v1

--- a/solution.py
+++ b/solution.py
@@ -105,7 +105,7 @@
     return pl.ds(pl.multiple_of(block * ROWS + half * HALF, HALF), HALF)
 
 
-def gather_rows(all_ref, send, recv):
+def gather_rows(all_ref, send, recv, beside=None):
     me, right, left, _ = ring()
 
     def piece(index, block, half, peer):
@@ -120,6 +120,8 @@
     ]
     for copy in copies:
         copy.start()
+    if beside is not None:
+        beside()
     copies[0].wait_recv()
     copies.append(piece(4, left, 0, right))
     copies[4].start()
@@ -184,22 +186,496 @@
 ]
 
 
+def greet_ids(peers):
+    barrier = pltpu.get_barrier_semaphore()
+    for peer in peers:
+        pl.semaphore_signal(barrier, inc=1, device_id=peer, device_id_type=MESH)
+
+
+class Ring:
+    def __init__(self, axis):
+        if axis == "x":
+            self.me = lax.axis_index("ctx")
+            self.place = lambda index: {"ctx": index}
+        else:
+            shard = lax.axis_index("fsdp")
+            inner, outer = lax.rem(shard, CTX), lax.div(shard, CTX)
+            if axis == "y":
+                self.me = inner
+                self.place = lambda index: {"fsdp": outer * CTX + index}
+            else:
+                self.me = outer
+                self.place = lambda index: {"fsdp": index * CTX + inner}
+        self.right = lax.rem(self.me + 1, CTX)
+        self.left = lax.rem(self.me + 3, CTX)
+        self.across = lax.rem(self.me + 2, CTX)
+
+    def order(self):
+        return (self.across, self.right, self.left, self.me)
+
+    def near(self):
+        return [self.place(self.right), self.place(self.left)]
+
+    def copy(self, source, target, send, recv, index):
+        return pltpu.make_async_remote_copy(
+            src_ref=source,
+            dst_ref=target,
+            send_sem=send,
+            recv_sem=recv,
+            device_id=self.place(index),
+            device_id_type=MESH,
+        )
+
+
+class RingGather:
+    def __init__(self, ring, at, send, recv):
+        self.ring, self.at, self.send, self.recv = ring, at, send, recv
+        self.copies = []
+
+    def go(self, block, half, to):
+        spot = self.at(block, half)
+        index = len(self.copies)
+        self.copies.append(
+            self.ring.copy(spot, spot, self.send.at[index], self.recv.at[index], to)
+        )
+        self.copies[-1].start()
+
+    def start(self):
+        ring = self.ring
+        self.go(ring.me, 0, ring.right)
+        self.go(ring.me, 1, ring.left)
+        self.go(ring.me, 1, ring.right)
+        self.go(ring.me, 0, ring.left)
+
+    def forward(self):
+        ring = self.ring
+        spot = self.at(ring.left, 0)
+        ring.copy(spot, spot, self.send.at[0], self.recv.at[0], ring.right).wait_recv()
+        self.go(ring.left, 0, ring.right)
+        spot = self.at(ring.right, 1)
+        ring.copy(spot, spot, self.send.at[1], self.recv.at[1], ring.left).wait_recv()
+        self.go(ring.right, 1, ring.left)
+
+    def finish(self):
+        ring = self.ring
+        for index, block, half in (
+            (2, ring.left, 1), (3, ring.right, 0), (4, ring.across, 0), (5, ring.across, 1),
+        ):
+            spot = self.at(block, half)
+            ring.copy(spot, spot, self.send.at[index], self.recv.at[index], ring.right).wait_recv()
+        for copy in self.copies:
+            copy.wait_send()
+
+
+class RingSum:
+    def __init__(self, ring, part, across_in, from_left, from_right, send, recv, cut, make):
+        self.ring, self.part, self.across_in = ring, part, across_in
+        self.from_left, self.from_right, self.send, self.recv = from_left, from_right, send, recv
+        size = part.shape[1]
+        self.halves = (pl.ds(0, cut), pl.ds(cut, size - cut))
+        self.make = make
+        self.copies = []
+
+    def go(self, block, half, target, to):
+        index = len(self.copies)
+        self.copies.append(
+            self.ring.copy(
+                self.part.at[block, self.halves[half]], target, self.send.at[index], self.recv.at[index], to
+            )
+        )
+        self.copies[-1].start()
+
+    def arrived(self, half, block):
+        self.copies[half].wait_recv()
+        incoming = self.across_in[half]
+        if len(self.part.shape) == 3:
+            spot = (block, self.halves[half])
+            self.part[spot] = (self.part[spot].astype(F32) + incoming[...].astype(F32)).astype(BF16)
+            return
+        start = (0, self.part.shape[1] - incoming.shape[0])[half]
+        for index in range(incoming.shape[0]):
+            self.part[block, start + index] = (
+                self.part[block, start + index].astype(F32) + incoming[index].astype(F32)
+            ).astype(BF16)
+
+    def stage(self, number):
+        ring = self.ring
+        if number == 0:
+            self.make(0, ring.across)
+            self.go(ring.across, 0, self.across_in[0], ring.right)
+            self.go(ring.across, 1, self.across_in[1], ring.left)
+        elif number == 1:
+            self.make(1, ring.right)
+            self.go(ring.right, 1, self.from_left.at[self.halves[1]], ring.right)
+        elif number == 2:
+            self.make(2, ring.left)
+            self.go(ring.left, 0, self.from_right.at[self.halves[0]], ring.left)
+        elif number == 3:
+            self.arrived(0, ring.right)
+            self.go(ring.right, 0, self.from_left.at[self.halves[0]], ring.right)
+            self.arrived(1, ring.left)
+            self.go(ring.left, 1, self.from_right.at[self.halves[1]], ring.left)
+        elif number == 4:
+            self.make(3, ring.me)
+        else:
+            for copy in self.copies[2:]:
+                copy.wait_recv()
+            for copy in self.copies:
+                copy.wait_send()
+
+    def total(self, index=None):
+        spot = (self.ring.me,) if index is None else (self.ring.me, index)
+        tail = () if index is None else (index,)
+        return (
+            self.part[spot].astype(F32)
+            + self.from_left[tail or ...].astype(F32)
+            + self.from_right[tail or ...].astype(F32)
+        )
+
+
+UNIT = 256
+EXPERT_ROWS = D + D // 2
+ATTN_ROWS = 288
+SHARD_ROWS = EXPERT_ROWS + ATTN_ROWS
+FIRST = SHARD_ROWS // 2
+KEPT = EXPERT_ROWS - FIRST
+CUT = 352
+SEMS = pltpu.SemaphoreType.DMA
+
+
+def gather_shards_kernel(shard_ref, out_ref, *sems):
+    section = lax.axis_index("section")
+    sibling = {"section": 1 - section}
+    ring_y, ring_z = Ring("y"), Ring("z")
+    y, z = ring_y.me, ring_z.me
+    greet_ids([sibling] + ring_y.near() + ring_z.near())
+    out_ref[section, z, y] = shard_ref[...]
+    met(5)
+    half = ATTN_ROWS // 2
+    low = (pl.ds(0, 64), pl.ds(64, half - 64))
+    high = (pl.ds(half, 64), pl.ds(half + 64, half - 64))
+    pair = (pl.ds(0, 2), pl.ds(2, 2))
+    near_y = RingGather(ring_y, lambda b, h: out_ref.at[section, z, b, low[h]], sems[0], sems[1])
+    near_z = RingGather(ring_z, lambda b, h: out_ref.at[section, b, y, high[h]], sems[2], sems[3])
+    far_z = RingGather(
+        ring_z, lambda b, h: out_ref.at[section, b, pair[h], pl.ds(0, half)], sems[4], sems[5]
+    )
+    far_y = RingGather(
+        ring_y, lambda b, h: out_ref.at[section, pair[h], b, pl.ds(half, half)], sems[6], sems[7]
+    )
+    for rings in ((near_y, near_z), (far_z, far_y)):
+        for one in rings:
+            one.start()
+        for one in rings:
+            one.forward()
+        for one in rings:
+            one.finish()
+    across = pltpu.make_async_remote_copy(
+        src_ref=out_ref.at[section],
+        dst_ref=out_ref.at[section],
+        send_sem=sems[8],
+        recv_sem=sems[9],
+        device_id=sibling,
+        device_id_type=MESH,
+    )
+    across.start()
+    across.wait()
+
+
+def gather_shards(shard):
+    return pl.pallas_call(
+        gather_shards_kernel,
+        out_shape=jax.ShapeDtypeStruct((2, CTX, CTX, ATTN_ROWS, UNIT), BF16),
+        in_specs=[VMEM],
+        out_specs=VMEM,
+        scratch_shapes=[SEMS((6,))] * 8 + [SEMS, SEMS],
+        compiler_params=params(7),
+        name="gather_shards",
+    )(shard)
+
+
+def sum_shards_kernel(
+    lower_e, lower_a, upper_e, upper_a, out_ref,
+    part_y, in_y, part_z, in_z, top_y, bottom_y, left_y, right_y, top_z, bottom_z, left_z, right_z,
+    more_z, more_y, top_zz, bottom_zz, left_zz, right_zz, top_yy, bottom_yy, left_yy, right_yy, *sems,
+):
+    section = lax.axis_index("section")
+    sibling = {"section": 1 - section}
+    ring_y, ring_z = Ring("y"), Ring("z")
+    greet_ids([sibling] + ring_y.near() + ring_z.near())
+    local, send_s, recv_s = sems[:3]
+
+    def pieces(index, experts, attn, target_y, target_z):
+        b_y, b_z = ring_y.order()[index], ring_z.order()[index]
+        return (
+            (experts.at[:, b_y, pl.ds(0, FIRST), :], target_y.at[b_y]),
+            (experts.at[b_z, :, pl.ds(FIRST, KEPT), :], target_z.at[b_z, :, pl.ds(0, KEPT), :]),
+            (attn.at[b_z], target_z.at[b_z, :, pl.ds(KEPT, ATTN_ROWS), :]),
+        )
+
+    def fetch(index, number, source, target):
+        return pltpu.make_async_copy(source, target, local.at[index * 3 + number])
+
+    def pass_on(index, number, source, target):
+        at = index * 3 + number
+        return pltpu.make_async_remote_copy(
+            src_ref=source,
+            dst_ref=target,
+            send_sem=send_s.at[at],
+            recv_sem=recv_s.at[at],
+            device_id=sibling,
+            device_id_type=MESH,
+        )
+
+    def begin(own_e, own_a, other_e, other_a):
+        for index in range(CTX):
+            for number, (source, target) in enumerate(pieces(index, own_e, own_a, part_y, part_z)):
+                fetch(index, number, source, target).start()
+
+    def lend(other_e, other_a):
+        for index in range(CTX):
+            for number, (source, target) in enumerate(pieces(index, other_e, other_a, in_y, in_z)):
+                pass_on(index, number, source, target).start()
+
+    @pl.when(section == 0)
+    def _():
+        begin(lower_e, lower_a, upper_e, upper_a)
+
+    @pl.when(section == 1)
+    def _():
+        begin(upper_e, upper_a, lower_e, lower_a)
+
+    met(5)
+
+    @pl.when(section == 0)
+    def _():
+        lend(upper_e, upper_a)
+
+    @pl.when(section == 1)
+    def _():
+        lend(lower_e, lower_a)
+
+    def ready(index, number):
+        source, target = pieces(index, lower_e, lower_a, part_y, part_z)[number]
+        fetch(index, number, source, target).wait()
+        source, target = pieces(index, lower_e, lower_a, in_y, in_z)[number]
+        pass_on(index, number, source, target).wait_recv()
+
+    def make_y(index, block):
+        ready(index, 0)
+        for other in range(CTX):
+            part_y[block, other] = (
+                part_y[block, other].astype(F32) + in_y[block, other].astype(F32)
+            ).astype(BF16)
+
+    def make_z(index, block):
+        ready(index, 1)
+        ready(index, 2)
+        for other in range(CTX):
+            part_z[block, other] = (
+                part_z[block, other].astype(F32) + in_z[block, other].astype(F32)
+            ).astype(BF16)
+
+    first_y = RingSum(ring_y, part_y, (top_y, bottom_y), left_y, right_y, sems[3], sems[4], 2, make_y)
+    first_z = RingSum(ring_z, part_z, (top_z, bottom_z), left_z, right_z, sems[5], sems[6], 2, make_z)
+
+    def make_zz(index, block):
+        more_z[block] = first_y.total(block).astype(BF16)
+
+    def make_yy(index, block):
+        more_y[block] = first_z.total(block).astype(BF16)
+
+    then_z = RingSum(
+        ring_z, more_z, (top_zz, bottom_zz), left_zz, right_zz, sems[7], sems[8], CUT, make_zz
+    )
+    then_y = RingSum(
+        ring_y, more_y, (top_yy, bottom_yy), left_yy, right_yy, sems[9], sems[10], CUT, make_yy
+    )
+    for number in range(6):
+        first_y.stage(number)
+        first_z.stage(number)
+    for number in range(6):
+        then_z.stage(number)
+        then_y.stage(number)
+    out_ref[:FIRST, :] = then_z.total().astype(BF16)
+    out_ref[FIRST:, :] = then_y.total().astype(BF16)
+    for index in range(CTX):
+        for number, (source, target) in enumerate(pieces(index, lower_e, lower_a, in_y, in_z)):
+            pass_on(index, number, source, target).wait_send()
+
+
+def sum_shards(lower_e, lower_a, upper_e, upper_a):
+    block = pltpu.VMEM((CTX, FIRST, UNIT), BF16)
+    pair = pltpu.VMEM((2, FIRST, UNIT), BF16)
+    one = pltpu.VMEM((FIRST, UNIT), BF16)
+    top, bottom = pltpu.VMEM((CUT, UNIT), BF16), pltpu.VMEM((FIRST - CUT, UNIT), BF16)
+    full = pltpu.VMEM((CTX, CTX, FIRST, UNIT), BF16)
+    anywhere = pl.BlockSpec(memory_space=pl.ANY)
+    return pl.pallas_call(
+        sum_shards_kernel,
+        out_shape=jax.ShapeDtypeStruct((SHARD_ROWS, UNIT), BF16),
+        in_specs=[anywhere] * 4,
+        out_specs=VMEM,
+        scratch_shapes=[full] * 4
+        + [pair, pair, block, block] * 2
+        + [block, block]
+        + [top, bottom, one, one] * 2
+        + [SEMS((12,))] * 3
+        + [SEMS((6,))] * 8,
+        compiler_params=params(8),
+        name="sum_shards",
+    )(*(
+        array.reshape((CTX, CTX) + array.shape[1:])
+        for array in (lower_e, lower_a, upper_e, upper_a)
+    ))
+
+
+def spread_sums_kernel(shard_ref, all_ref, squares_ref, from_y, from_z, *sems):
+    ring_x, ring_y, ring_z = Ring("x"), Ring("y"), Ring("z")
+    far = [
+        one.place(index)
+        for one in (ring_y, ring_z)
+        for index in (one.right, one.left, one.across)
+    ]
+    greet_ids(ring_x.near() + far)
+    all_ref[ring_x.me] = shard_ref[...]
+    met(8)
+    halves = (pl.ds(0, FIRST), pl.ds(FIRST, FIRST))
+    rows = RingGather(ring_x, lambda b, h: all_ref.at[b, halves[h]], sems[0], sems[1])
+    rows.start()
+    rows.forward()
+    rows.finish()
+
+    def folded(values):
+        squared = values * values
+        return jnp.sum(squared, axis=0, keepdims=True)
+
+    in_row = jnp.zeros((1, UNIT), F32)
+    out_row = jnp.zeros((1, UNIT), F32)
+    attn_row = jnp.zeros((1, UNIT), F32)
+    back = jnp.zeros((ATTN_ROWS // 2, UNIT), F32)
+    small = jnp.zeros((48, UNIT), F32)
+    lanes = lax.broadcasted_iota(jnp.int32, (1, UNIT), 1)
+    for block in range(CTX):
+        in_row += folded(all_ref[block, :D, :].astype(F32))
+        out_row += folded(all_ref[block, D:EXPERT_ROWS, :].astype(F32))
+        middle = EXPERT_ROWS + ATTN_ROWS // 2
+        back += all_ref[block, EXPERT_ROWS:middle, :].astype(F32)
+        attn_row += folded(all_ref[block, middle : middle + 96, :].astype(F32))
+        final = all_ref[block, middle + 96 :, :].astype(F32)
+        attn_row += jnp.where(lanes < HEAD_DIM, folded(final), 0.0)
+        small += final
+    attn_row += folded(back)
+    small_row = folded(small)
+    is_router = (lanes >= LANES) & (lanes < LANES + EXPERTS)
+    is_gain = (lanes >= LANES + EXPERTS) & (lanes < LANES + EXPERTS + 2)
+    sums = [
+        jnp.where(is_gain, small_row, 0.0),
+        attn_row,
+        jnp.where(is_router, small_row, 0.0),
+        in_row,
+        out_row,
+    ]
+    places = lax.broadcasted_iota(jnp.int32, (8, LANES), 1)
+    tile = jnp.zeros((8, LANES), F32)
+    for index, row in enumerate(sums):
+        tile = jnp.where(places == index, jnp.sum(row, axis=1, keepdims=True), tile)
+
+    def shared(one, slots, send, recv, tile):
+        slots[one.me] = tile
+        copies = []
+        for index, peer in enumerate((one.right, one.left, one.across)):
+            spot = slots.at[one.me]
+            copies.append(one.copy(spot, spot, send.at[index], recv.at[index], peer))
+            copies[-1].start()
+        for copy in copies:
+            copy.wait()
+        return (slots[0] + slots[1]) + (slots[2] + slots[3])
+
+    tile = shared(ring_y, from_y, sems[2], sems[3], tile)
+    squares_ref[...] = shared(ring_z, from_z, sems[4], sems[5], tile)
+
+
+def spread_sums(shard):
+    slots = pltpu.VMEM((CTX, 8, LANES), F32)
+    return pl.pallas_call(
+        spread_sums_kernel,
+        out_shape=(
+            jax.ShapeDtypeStruct((CTX, SHARD_ROWS, UNIT), BF16),
+            jax.ShapeDtypeStruct((8, LANES), F32),
+        ),
+        in_specs=[VMEM],
+        out_specs=[VMEM, VMEM],
+        scratch_shapes=[slots, slots, SEMS((6,)), SEMS((6,))] + [SEMS((3,))] * 4,
+        compiler_params=params(9),
+        name="spread_sums",
+    )(shard)
+
+
 def inverse_size(values):
     return lax.rsqrt(jnp.mean(values * values, axis=1, keepdims=True) + EPS_NORM)
 
 
+def unpack(pack_ref, back_ref, heads_ref):
+    def body(index, _):
+        rows = pl.ds(pl.multiple_of(index * 48, 16), 48)
+        for piece in range(6):
+            target = back_ref if piece < 3 else heads_ref
+            at = (piece % 3) * UNIT
+            target[rows, at : at + UNIT] = pack_ref[index, piece * 48 : (piece + 1) * 48, :]
+        return 0
+
+    lax.fori_loop(0, 16, body, 0)
+
+
+def repack(back_ref, heads_ref, pack_ref):
+    def body(index, _):
+        rows = pl.ds(pl.multiple_of(index * 48, 16), 48)
+        for piece in range(6):
+            source = back_ref if piece < 3 else heads_ref
+            at = (piece % 3) * UNIT
+            pack_ref[index, piece * 48 : (piece + 1) * 48, :] = source[rows, at : at + UNIT]
+        return 0
+
+    lax.fori_loop(0, 16, body, 0)
+
+
+def extend(heads_ref, w_ref):
+    lanes = lax.broadcasted_iota(jnp.int32, (D, WIDE), 1)
+    for head in range(3 * HEADS_DEV):
+        at = head // 2 * WIDE
+        values = heads_ref[:, at : at + WIDE].astype(F32)
+        if head % 2:
+            values = pltpu.roll(values, HEAD_DIM, 1)
+        if head < 2 * HEADS_DEV:
+            upper = jnp.where(
+                lanes < 96, -pltpu.roll(values, 32, 1), pltpu.roll(values, 96, 1)
+            )
+        else:
+            upper = jnp.zeros_like(values)
+        w_ref[:, head * WIDE : (head + 1) * WIDE] = jnp.where(
+            lanes < HEAD_DIM, values, upper
+        ).astype(BF16)
+
+
 def attn_forward_kernel(
-    length_ref, u_ref, gains_ref, router_ref, routes_ref, w_ref, back_ref, table_ref,
+    length_ref, u_ref, routes_ref, pack_ref, table_ref,
     a_ref, qkv_ref, mass_ref, attended_ref, residual_ref, b_ref, gates_ref, gate_ref,
-    heads_out, send_a, recv_a, send_o, recv_o, send_b, recv_b,
+    gains_ref, router_ref, w_ref, back_ref,
+    heads_out, heads_w, send_a, recv_a, send_o, recv_o, send_b, recv_b,
 ):
     me, right, left, across = ring()
     greet((right, left, across))
     length = length_ref[0]
     tokens = u_ref[...].astype(F32)
+    unpack(pack_ref, back_ref, heads_w)
+    router_ref[...] = heads_w[:, D - LANES :]
+    places = lax.broadcasted_iota(jnp.int32, (8, LANES), 0) + EXPERTS
+    picker = jnp.where(places == lax.broadcasted_iota(jnp.int32, (8, LANES), 1), 1.0, 0.0)
+    gains_ref[...] = dot_nt(picker.astype(BF16), router_ref[...])
     a_ref[rows_of(me), :] = (tokens * inverse_size(tokens) * gains_ref[0:1, :]).astype(BF16)
     met(3)
-    gather_rows(a_ref, send_a, recv_a)
+    gather_rows(a_ref, send_a, recv_a, lambda: extend(heads_w, w_ref))
     for block in range(CTX):
         rows = pl.ds(block * ROWS, ROWS)
         table = table_ref[rows, :]
@@ -268,7 +744,7 @@
         gate_ref[rows, :] = jnp.sum(jnp.where(lanes == me, gates, 0.0), axis=1, keepdims=True)
 
 
-def attn_forward(length, u, gains, router, routes, w_ext, w_back, table):
+def attn_forward(length, u, routes, pack, table):
     sems = pltpu.SemaphoreType.DMA
     return pl.pallas_call(
         attn_forward_kernel,
@@ -281,14 +757,18 @@
             jax.ShapeDtypeStruct((SEQ, D), BF16),
             jax.ShapeDtypeStruct((SEQ, LANES), F32),
             jax.ShapeDtypeStruct((SEQ, 1), F32),
+            jax.ShapeDtypeStruct((8, D), F32),
+            jax.ShapeDtypeStruct((D, LANES), BF16),
+            jax.ShapeDtypeStruct((D, EXT), BF16),
+            jax.ShapeDtypeStruct((D, D), BF16),
         ),
-        in_specs=[SMEM] + [VMEM] * 7,
-        out_specs=[VMEM] * 8,
-        scratch_shapes=[pltpu.VMEM((CTX, ROWS, COLS), BF16)]
+        in_specs=[SMEM] + [VMEM] * 4,
+        out_specs=[VMEM] * 12,
+        scratch_shapes=[pltpu.VMEM((CTX, ROWS, COLS), BF16), pltpu.VMEM((D, D), BF16)]
         + [sems((6,)), sems((6,)), sems((CTX,)), sems((CTX,)), sems((6,)), sems((6,))],
         compiler_params=params(1),
         name="attn_forward",
-    )(length, u, gains, router, routes, w_ext, w_back, table)
+    )(length, u, routes, pack, table)
 
 
 def attn_backward_kernel(
@@ -297,11 +777,13 @@
     delta_ref, db_ref, gate_grad_ref, *rest,
 ):
     if last:
-        input_ref, dheads_ref, dback_ref, small_ref = rest[:4]
-        rest = rest[4:]
+        input_ref, pack_ref = rest[:2]
+        rest = rest[2:]
     else:
-        input_ref, lower_ref, dheads_ref, dback_ref, small_ref = rest[:5]
-        rest = rest[5:]
+        input_ref, pack_ref, lower_ref = rest[:3]
+        rest = rest[3:]
+    dheads_ref, dback_ref = rest[:2]
+    rest = rest[2:]
     key_acc, value_acc, dz, grads_out, grads_in, send_o, recv_o = rest[:7]
     part, across_in, from_left, from_right, send_r, recv_r = rest[7:13]
     me, right, left, across = ring()
@@ -416,7 +898,9 @@
                 pltpu.roll(pieces[2 * pair + 1], HEAD_DIM, 1),
             )
             dheads_ref[:, pair * WIDE : (pair + 1) * WIDE] = joined.astype(BF16)
-        dheads_ref[:, 4 * WIDE :] = pieces[8][:, :HEAD_DIM].astype(BF16)
+        dheads_ref[:, 4 * WIDE : 5 * WIDE] = jnp.where(
+            wide_lanes < HEAD_DIM, pieces[8], 0.0
+        ).astype(BF16)
 
     normed_grad = reduce_rows(make, part, across_in, from_left, from_right, send_r, recv_r, beside)
     tokens = u_ref[...].astype(F32)
@@ -431,11 +915,12 @@
     )
     input_ref[...] = input_grad
     small_lanes = lax.broadcasted_iota(jnp.int32, (D, LANES), 1)
-    small_ref[...] = jnp.where(
+    dheads_ref[:, D - LANES :] = jnp.where(
         small_lanes == EXPERTS,
         gain_one_column,
         jnp.where(small_lanes == EXPERTS + 1, gain_two_column, router_terms),
     ).astype(BF16)
+    repack(dback_ref, dheads_ref, pack_ref)
     if not last:
         lower_ref[rows_of(me), :] = input_grad.astype(BF16)
         gather_rows(lower_ref, *rest[13:])
@@ -443,15 +928,15 @@
 
 def attn_backward(last, length, *arrays):
     sems = pltpu.SemaphoreType.DMA
-    out_shape = [jax.ShapeDtypeStruct((ROWS, D), F32)]
+    out_shape = [
+        jax.ShapeDtypeStruct((ROWS, D), F32),
+        jax.ShapeDtypeStruct((16, ATTN_ROWS, UNIT), BF16),
+    ]
     if not last:
         out_shape.append(jax.ShapeDtypeStruct((SEQ, D), BF16))
-    out_shape += [
-        jax.ShapeDtypeStruct((D, 3 * COLS), BF16),
-        jax.ShapeDtypeStruct((D, D), BF16),
-        jax.ShapeDtypeStruct((D, LANES), BF16),
-    ]
     scratch = [
+        pltpu.VMEM((D, D), BF16),
+        pltpu.VMEM((D, D), BF16),
         pltpu.VMEM((SEQ, HEADS_DEV * WIDE), F32),
         pltpu.VMEM((SEQ, HEADS_DEV * WIDE), F32),
         pltpu.VMEM((SEQ, EXT), BF16),
@@ -612,16 +1097,13 @@
         return second_grad
 
     def weight_terms():
-        split = HALF_ROWS
         for shard in range(shards):
-            whole_in = dot(b_turned[...], hidden_grad[shard]).astype(BF16)
-            dw_ref[0, shard] = whole_in[:split]
-            dw_ref[1, shard, : D - split, :] = whole_in[split:]
+            dw_ref[shard, :D, :] = dot(b_turned[...], hidden_grad[shard]).astype(BF16)
         whole_out = dot_tn(acted[...], slot_grad[...]).astype(BF16)
         for shard in range(shards):
             for piece in range(D // width):
-                at = D - split + piece * units
-                dw_ref[1, shard, at : at + units, :] = whole_out[
+                at = D + piece * units
+                dw_ref[shard, at : at + units, :] = whole_out[
                     shard * units : (shard + 1) * units, piece * width : (piece + 1) * width
                 ]
 
@@ -687,7 +1169,7 @@
         out_shape=(
             jax.ShapeDtypeStruct((ROWS, D), F32),
             jax.ShapeDtypeStruct((ROWS, LANES), F32),
-            jax.ShapeDtypeStruct(weights.shape, BF16),
+            jax.ShapeDtypeStruct((count, 2 * half_rows, double), BF16),
         ),
         in_specs=[
             whole((SEQ, D)),
@@ -699,7 +1181,7 @@
         out_specs=[
             whole((ROWS, D)),
             whole((ROWS, LANES)),
-            pl.BlockSpec((2, shards, half_rows, double), lambda i: (0, i, 0, 0)),
+            pl.BlockSpec((shards, 2 * half_rows, double), lambda i: (i, 0, 0)),
         ],
         scratch_shapes=[
             pltpu.VMEM((SEQ, D), F32),
@@ -730,35 +1212,25 @@
     return jnp.concatenate([cosine, cosine, sine, sine], axis=1)
 
 
-def extended(w_heads):
-    half_dim = HEAD_DIM // 2
-    turning = w_heads[:, : 2 * COLS].reshape(D, 2 * HEADS_DEV, 2, half_dim)
-    first, second = turning[:, :, 0], turning[:, :, 1]
-    turning = jnp.concatenate([first, second, -second, first], axis=2)
-    values = w_heads[:, 2 * COLS :].reshape(D, HEADS_DEV, HEAD_DIM)
-    values = jnp.concatenate([values, jnp.zeros_like(values)], axis=2)
-    return jnp.concatenate(
-        [turning.reshape(D, 2 * HEADS_DEV * WIDE), values.reshape(D, HEADS_DEV * WIDE)], axis=1
-    )
-
-
 def layer_forward(weights, tokens_in, length, routes_all, table):
-    gains, router, w_ext, w_back, experts = weights
-    a_all, qkv, mass, attended, residual, b_all, gates, gate_col = attn_forward(
-        length, tokens_in, gains, router, routes_all, w_ext, w_back, table
+    pack, experts = weights
+    a_all, qkv, mass, attended, residual, b_all, gates, gate_col, *unpacked = attn_forward(
+        length, tokens_in, routes_all, pack, table
     )
     output, kept = ffn_forward(b_all, gate_col, residual, experts)
-    return output, (tokens_in, a_all, qkv, mass, attended, residual, b_all, gates, gate_col, kept)
+    return output, (
+        tokens_in, a_all, qkv, mass, attended, residual, b_all, gates, gate_col, kept, unpacked,
+    )
 
 
 def layer_backward(weights, saved, delta_all, delta_own, length, table, ctx_index, last):
-    gains, router, w_ext, w_back, experts = weights
-    tokens_in, a_all, qkv, mass, attended, residual, b_all, gates, gate_col, kept = saved
+    _, experts = weights
+    tokens_in, a_all, qkv, mass, attended, residual, b_all, gates, gate_col, kept, unpacked = saved
     db, gate_grads, dexperts = ffn_backward(b_all, gate_col, delta_all, kept, experts)
     second = lax.dynamic_slice_in_dim(b_all, ctx_index * ROWS, ROWS, 0)
     own_gates = lax.dynamic_slice_in_dim(gates, ctx_index * ROWS, ROWS, 0)
     results = attn_backward(
-        last, length, tokens_in, gains, router, w_ext, w_back, table, a_all, qkv, mass,
+        last, length, tokens_in, *unpacked, table, a_all, qkv, mass,
         attended, residual, second, own_gates, delta_own, db, gate_grads,
     )
     return dexperts, results
@@ -797,10 +1269,14 @@
         return lax.ppermute(block, "section", [(0, 1), (1, 0)])
 
     attn_shard = jnp.concatenate(
-        [own_columns(attn_weight[0], part) for part in range(3)]
-        + [attn_weight[0][:, 3 * D :], norm_gains[0].T, router_weight[0]],
+        [attn_weight[0][:, 3 * D :]]
+        + [own_columns(attn_weight[0], part) for part in range(3)]
+        + [jnp.zeros((shard_rows, HEAD_DIM), F32), router_weight[0], norm_gains[0].T]
+        + [jnp.zeros((shard_rows, LANES - EXPERTS - 2), F32)],
         axis=1,
     ).astype(BF16)
+    attn_shard = attn_shard.reshape(shard_rows, 6, UNIT).transpose(1, 0, 2).reshape(-1, UNIT)
+    packs = gather_shards(attn_shard).reshape(2, fsdp, ATTN_ROWS, UNIT)
     in_shard = (
         lax.dynamic_index_in_dim(expert_in[0], ctx_index, 0, keepdims=False)
         .astype(BF16)
@@ -811,7 +1287,6 @@
         [in_shard] + [out_shard[:, at : at + 2 * units] for at in range(0, D, 2 * units)], axis=0
     ).reshape(2, HALF_ROWS, 2 * units)
     other = swap(jnp.where(first_core, halves[1], halves[0]))
-    attn_full = lax.all_gather(attn_shard, everyone, tiled=True).reshape(2, D, -1)
     pieces = (jnp.where(first_core, halves[0], other), jnp.where(first_core, other, halves[1]))
     experts = [
         lax.all_gather(piece, everyone).reshape(2, fsdp, HALF_ROWS, 2 * units) for piece in pieces
@@ -826,38 +1301,17 @@
     seed_all = lax.all_gather(seed, "ctx", tiled=True)
     table = rotary_table()
 
-    layers = []
-    for layer in range(2):
-        full = attn_full[layer]
-        small_at = 3 * COLS + D
-        gains = full[:, small_at : small_at + 2].astype(F32).T
-        router = jnp.pad(full[:, small_at + 2 :], ((0, 0), (0, LANES - EXPERTS)))
-        layers.append(
-            (
-                jnp.pad(gains, ((0, 6), (0, 0))),
-                router,
-                extended(full[:, : 3 * COLS]),
-                full[:, 3 * COLS : small_at],
-                experts[layer],
-            )
-        )
+    layers = [(packs[layer], experts[layer]) for layer in range(2)]
     lower_out, lower_saved = layer_forward(layers[0], tokens, length, routes_all[0], table)
     upper_out, upper_saved = layer_forward(layers[1], lower_out, length, routes_all[1], table)
 
-    def scattered(terms):
-        return lax.psum_scatter(
-            terms.reshape((2 * fsdp,) + terms.shape[2:]), everyone, scatter_dimension=0, tiled=True
-        )[0]
-
-    upper_experts, (upper_grad, lower_seed, *upper_rest) = layer_backward(
+    upper_experts, (upper_grad, upper_attn, lower_seed) = layer_backward(
         layers[1], upper_saved, seed_all, seed, length, table, ctx_index, False
     )
-    upper_half = scattered(upper_experts)
     own_seed = upper_grad.astype(BF16)
-    lower_experts, (lower_grad, *lower_rest) = layer_backward(
+    lower_experts, (lower_grad, lower_attn) = layer_backward(
         layers[0], lower_saved, lower_seed, own_seed, length, table, ctx_index, True
     )
-    lower_half = scattered(lower_experts)
 
     def paired(first, second):
         kept = jnp.where(first_core, first, second)
@@ -868,26 +1322,23 @@
 
     layer_outputs = paired(lower_out, upper_out)[None]
     input_grads = paired(lower_grad, upper_grad)[None]
-    expert_part = paired(lower_half, upper_half).reshape(2 * HALF_ROWS, 2 * units)
-    attn_terms = jnp.stack([jnp.concatenate(lower_rest, axis=1), jnp.concatenate(upper_rest, axis=1)])
-    attn_part = scattered(attn_terms.reshape(2, fsdp, shard_rows, -1))
-    expert_all = lax.all_gather(expert_part, "ctx")
-    attn_all = lax.all_gather(attn_part, "ctx")
-    in_sum = expert_all[:, :D].astype(F32).reshape(1, CTX, D, 2, units)
+    shard_sum = sum_shards(lower_experts, lower_attn, upper_experts, upper_attn)
+    sums_all, squares = spread_sums(shard_sum)
+    in_sum = sums_all[:, :D].astype(F32).reshape(1, CTX, D, 2, units)
     out_sum = jnp.concatenate(
-        [expert_all[:, at : at + units] for at in range(D, 2 * HALF_ROWS, units)], axis=2
+        [sums_all[:, at : at + units] for at in range(D, EXPERT_ROWS, units)], axis=2
     ).astype(F32)[None]
-    heads_sum = attn_all[:, :, : 3 * COLS].astype(F32)
-    heads_sum = (
-        heads_sum.reshape(CTX, shard_rows, 3, COLS).transpose(1, 2, 0, 3).reshape(shard_rows, 3 * D)
-    )
-    rest_sum = jnp.sum(attn_all[:, :, 3 * COLS :].astype(F32), axis=0)
-    attn_sum = jnp.concatenate([heads_sum, rest_sum[:, :D]], axis=1)[None]
-    router_sum = rest_sum[:, D : D + EXPERTS][None]
-    gain_sum = rest_sum[:, D + EXPERTS : D + EXPERTS + 2].T[None]
+    attn_all = sums_all[:, EXPERT_ROWS:].astype(F32).reshape(CTX, 6, shard_rows, UNIT)
+    back_sum = jnp.sum(attn_all[:, :3], axis=0).transpose(1, 0, 2).reshape(shard_rows, D)
+    heads_sum = attn_all[:, 3:].transpose(0, 2, 1, 3).reshape(CTX, shard_rows, D)
+    small_sum = jnp.sum(heads_sum[:, :, D - LANES :], axis=0)
+    heads_sum = heads_sum[:, :, : 3 * COLS].reshape(CTX, shard_rows, 3, COLS)
+    heads_sum = heads_sum.transpose(1, 2, 0, 3).reshape(shard_rows, 3 * D)
+    attn_sum = jnp.concatenate([heads_sum, back_sum], axis=1)[None]
+    router_sum = small_sum[:, :EXPERTS][None]
+    gain_sum = small_sum[:, EXPERTS : EXPERTS + 2].T[None]
     sums = (gain_sum, attn_sum, router_sum, in_sum, out_sum)
-    squares = lax.psum(jnp.stack([jnp.sum(total * total) for total in sums]), "fsdp")
-    norms = jnp.sqrt(squares)
+    norms = jnp.sqrt(squares[0, : len(sums)])
     factors = jnp.minimum(1.0, CLIP_LIMIT / norms)
     step_value = step_count[0].astype(F32)
     wide_rate = RATE_FACTOR / D**0.5

time: 807 us -> 631 us (0.78)
  waiting for transfers between devices: 257 us -> 2.35 us
  Pallas kernels: 329 us -> 499 us
  blocking collectives: 76.6 us -> 22.8 us
  local copies, waits for them, and re-layouts: 56.9 us -> 38.1 us
  other arithmetic: 58.9 us -> 46 us
    reduce_scatter x3 -> x0, waiting for transfers between devices: 223 us -> none  [scattered(): lax.psum_scatter(terms.reshape((2 * fsdp,) + terms.shape[2:]), everyone,...]
    pallas_call x0 -> x3, Pallas kernels: none -> 149 us  [the longest x1 75.6 us: sum_shards(): pl.pallas_call(sum_shards_kernel, out_shape=jax.ShapeDtypeStruct((SHARD_R...]
    psum x1 -> x0, blocking collectives: 40.7 us -> none  [on_device(): lax.psum(jnp.stack([jnp.sum(total * total) for total in sums]), 'fsdp')]
    all_gather x2 -> x0, waiting for transfers between devices: 28.5 us -> none  [the longest x1 15.7 us: on_device(): expert_all = lax.all_gather(expert_part, 'ctx')]
    pallas_call x2, Pallas kernels: 58.9 us -> 77 us  [ffn_forward(): pl.pallas_call(ffn_forward_kernel, grid=(count // shards,), out_shape=(ja...]
    all_gather x1 -> x0, blocking collectives: 14.2 us -> none  [on_device(): attn_all = lax.all_gather(attn_part, 'ctx')]
    concatenate x7 -> x4, local copies, waits for them, and re-layouts: 12.8 us -> 4.16 us  [the longest x2 2.05 us: on_device(): attn_sum = jnp.concatenate([heads_sum, back_sum], axis=1)[None]]
  transfers between devices with their start and end apart: 12 -> 6, of which waited for: 9 -> 1; matrix products, arithmetic and copies ran while one was open for 9% -> 8% of each run, Pallas kernels for 26% -> 35%
where the time goes in v2:
time: 631 us; the launch traced here: 625 us
  Pallas kernels  499 us (79%)
  other arithmetic  46 us (7%)
  local copies, waits for them, and re-layouts  38.1 us (6%)
  blocking collectives  22.8 us (4%)
  between operations  15.4 us (2%)
    pallas_call x2, Pallas kernels, attn_forward(): pl.pallas_call(attn_forward_kernel, out_shape=(jax.ShapeDtypeStruct((SEQ,...  106 us
    pallas_call x2, Pallas kernels, attn_backward(): pl.pallas_call(functools.partial(attn_backward_kernel, last), out_shape=t...  91.6 us
    pallas_call x2, Pallas kernels, ffn_forward(): pl.pallas_call(ffn_forward_kernel, grid=(count // shards,), out_shape=(ja...  77 us
    pallas_call x2, Pallas kernels, ffn_backward(): pl.pallas_call(ffn_backward_kernel, grid=(count // shards,), out_shape=(j...  76.2 us
    pallas_call x1, Pallas kernels, sum_shards(): pl.pallas_call(sum_shards_kernel, out_shape=jax.ShapeDtypeStruct((SHARD_R...  75.6 us
    pallas_call x1, Pallas kernels, spread_sums(): pl.pallas_call(spread_sums_kernel, out_shape=(jax.ShapeDtypeStruct((CTX,...  38.5 us
    pallas_call x1, Pallas kernels, gather_shards(): pl.pallas_call(gather_shards_kernel, out_shape=jax.ShapeDtypeStruct((2, C...  34.7 us
    convert_element_type x5, other arithmetic, adam_update(): return (gradient, mean_new, square_new, master_new, master_new.astype(BF16))  23.4 us
  transfers between devices with their start and end apart: 6, of which 1 were waited for; matrix products, arithmetic and copies ran while one was open for 8% of the time, Pallas kernels for 35%

profile of v2, /device:TPU:0, one launch (start us, length us, event | category | flops | bytes accessed | tf_op | source)
XLA Modules:
  0.0 624.8 jit_solution(4095473212182006337)
XLA Ops:
  7.3 1.1 fusion.3
  8.4 1.4 dynamic-slice_convert_fusion
  10.3 1.6 collective-permute-done
  11.9 0.9 broadcast_select_fusion.4
  12.9 0.7 all-gather.10.cloned.1.call-update
  13.6 0.6 dynamic_slice.49.length_ref
  14.2 0.7 add_compare_fusion
  14.9 0.9 bitcast_select_fusion.delta_ref
  16.5 0.7 copy.105
  17.2 34.7 %gather_shards.1 = bf16[2,4,4,288,256]{4,3,2,1,0:T(8,128)(2,1)} custom-call(bf16[288,256]{1,0:T(8,128)(2,1)} %bitcast.125), custom_call_target="tpu_custom_call" | custom-call | tf_op jit(solution)/shard_map/gather_shards/pallas_call | solution.py:386
  51.9 22.8 %all_gather.18 = s32[8,2,256,2]{2,3,1,0:T(2,128)S(1)} all-gather(s32[1,2,256,2]{2,3,1,0:T(2,128)S(1)} %copy-done.20), channel_id=1, replica_groups=mesh['section'=2,'ctx'=4,'fsdp'=16] {'section','ctx'}, dimensions={0}, use_global_device_ids=true | all-gather | bytes 36864 | tf_op jit(solution)/shard_map/all_gather | solution.py:1294
  74.7 1.0 copy.119
  75.7 1.0 copy.120
  77.5 0.8 dynamic-slice_bitcast_fusion.u_ref
  78.3 1.9 multiply_cosine_fusion
  80.2 1.3 pad_maximum_fusion.table_ref
  81.5 4.9 fusion.18
  86.3 54.4 %attn_forward.2 = (bf16[1024,768]{1,0:T(8,128)(2,1)}, bf16[1024,1152]{1,0:T(8,128)(2,1)}, f32[3,1024,1]{2,1,0:T(8,128)}, bf16[4,256,192]{2,1,0:T(8,128)(2,1)}, f...) custom-call(s32[1]{0:T(128)} %dynamic_slice.49.length_ref, ...), custom_call_target="tpu_custom_call" | custom-call | tf_op jit(solution)/shard_map/attn_forward/pallas_call | solution.py:749
  140.7 32.8 %ffn_forward.2 = (bf16[256,768]{1,0:T(8,128)(2,1)}, bf16[16,1024,256]{2,1,0:T(8,128)(2,1)}) custom-call(bf16[1024,768]{1,0:T(8,128)(2,1)} %get-tuple-element.69.b_ref, f32[1024,1]{1,0:T(8,128)} %get-tuple-element.70.gate_ref, f32[256,768]{1,0:T(8,128)} %get-tuple-element.71.residual_ref, bf16[2,16,576,256]{3,2,1,0:T(8,128)(2,1)} %bitcast.102), custom_call_target="tpu_custom_call" | custom-call | tf_op jit(solution)/shard_map/ffn_forward/pallas_call | solution.py:1029
  173.5 51.4 %attn_forward.3 = (bf16[1024,768]{1,0:T(8,128)(2,1)}, bf16[1024,1152]{1,0:T(8,128)(2,1)}, f32[3,1024,1]{2,1,0:T(8,128)}, bf16[4,256,192]{2,1,0:T(8,128)(2,1)}, f...) custom-call(s32[1]{0:T(128)} %dynamic_slice.49.length_ref, ...), custom_call_target="tpu_custom_call" | custom-call | tf_op jit(solution)/shard_map/attn_forward/pallas_call | solution.py:749
  224.9 44.2 %ffn_forward.3 = (bf16[256,768]{1,0:T(8,128)(2,1)}, bf16[16,1024,256]{2,1,0:T(8,128)(2,1)}) custom-call(bf16[1024,768]{1,0:T(8,128)(2,1)} %get-tuple-element.73.b_ref, f32[1024,1]{1,0:T(8,128)} %get-tuple-element.74.gate_ref, f32[256,768]{1,0:T(8,128)} %get-tuple-element.75.residual_ref, bf16[2,16,576,256]{3,2,1,0:T(8,128)(2,1)} %bitcast.104), custom_call_target="tpu_custom_call" | custom-call | tf_op jit(solution)/shard_map/ffn_forward/pallas_call | solution.py:1029
  269.1 1.7 constant_dynamic-slice_fusion.1
  270.8 2.0 constant_dynamic-slice_fusion.2
  272.8 38.5 %ffn_backward.2 = (f32[256,768]{1,0:T(8,128)}, f32[256,128]{1,0:T(8,128)}, bf16[16,1152,256]{2,1,0:T(8,128)(2,1)}) custom-call(bf16[1024,768]{1,0:T(8,128)(2,1)} %get-tuple-element.73.b_ref, f32[1024,1]{1,0:T(8,128)} %get-tuple-element.74.gate_ref, bf16[1024,768]{1,0:T(8,128)(2,1)} %all-gather.6.cloned.1.call-done.delta_ref, ...), custom_call_target="tpu_custom_call" | custom-call | tf_op jit(solution)/shard_map/ffn_backward/pallas_call | solution.py:1166
  311.4 53.3 %attn_backward.2 = (f32[256,768]{1,0:T(8,128)}, bf16[16,288,256]{2,1,0:T(8,128)(2,1)}, bf16[1024,768]{1,0:T(8,128)(2,1)}) custom-call(s32[1]{0:T(128)} %dynamic_slice.49.length_ref, bf16[256,768]{1,0:T(8,128)(2,1)} %get-tuple-element.72.u_ref, f32[8,768]{1,0:T(8,128)} %get-tuple-element.86.gains_ref, bf16[768,128]{1,0:T(8,128)(2,1)} %get-tuple-element.87.router_ref, ...), custom_call_target="tpu_custom_call" | custom-call | tf_op jit(solution)/shard_map/attn_backward/pallas_call | solution.py:950
  364.7 1.9 convert_element_type.79.delta_ref
  366.6 37.6 %ffn_backward.3 = (f32[256,768]{1,0:T(8,128)}, f32[256,128]{1,0:T(8,128)}, bf16[16,1152,256]{2,1,0:T(8,128)(2,1)}) custom-call(bf16[1024,768]{1,0:T(8,128)(2,1)} %get-tuple-element.69.b_ref, f32[1024,1]{1,0:T(8,128)} %get-tuple-element.70.gate_ref, bf16[1024,768]{1,0:T(8,128)(2,1)} %get-tuple-element.99.delta_ref, ...), custom_call_target="tpu_custom_call" | custom-call | tf_op jit(solution)/shard_map/ffn_backward/pallas_call | solution.py:1166
  404.2 38.3 %attn_backward.3 = (f32[256,768]{1,0:T(8,128)}, bf16[16,288,256]{2,1,0:T(8,128)(2,1)}) custom-call(s32[1]{0:T(128)} %dynamic_slice.49.length_ref, bf16[256,768]{1,0:T(8,128)(2,1)} %dynamic-slice_bitcast_fusion.u_ref, f32[8,768]{1,0:T(8,128)} %get-tuple-element.77.gains_ref, bf16[768,128]{1,0:T(8,128)(2,1)} %get-tuple-element.78.router_ref, ...), custom_call_target="tpu_custom_call" | custom-call | tf_op jit(solution)/shard_map/attn_backward/pallas_call | solution.py:950
  442.5 75.6 %sum_shards.1.shard_ref = bf16[1440,256]{1,0:T(8,128)(2,1)} custom-call(bf16[4,4,1152,256]{3,2,1,0:T(8,128)(2,1)} %bitcast.109, bf16[4,4,288,256]{3,2,1,0:T(8,128)(2,1)} %bitcast.118, bf16[4,4,1152,256]{3,2,1,0:T(8,128)(2,1)} %bitcast.108, bf16[4,4,288,256]{3,2,1,0:T(8,128)(2,1)} %bitcast.117), custom_call_target="tpu_custom_call" | custom-call | tf_op jit(solution)/shard_map/sum_shards/pallas_call | solution.py:514
  518.1 38.5 %spread_sums.1 = (bf16[4,1440,256]{2,1,0:T(8,128)(2,1)}, f32[8,128]{1,0:T(8,128)}) custom-call(bf16[1440,256]{1,0:T(8,128)(2,1)} %sum_shards.1.shard_ref), custom_call_target="tpu_custom_call" | custom-call | tf_op jit(solution)/shard_map/spread_sums/pallas_call | solution.py:601
  556.7 2.0 slice_bitcast_fusion.2
  558.7 1.7 slice_convert_fusion
  560.4 1.9 slice.110
  562.3 1.0 slice.132
  563.3 1.3 copy.133
  564.6 2.4 reshape.362
  566.9 0.9 slice_reduce_fusion.1
  567.8 1.8 slice.135
  569.7 2.2 convert.38
  571.9 1.2 slice_sqrt_fusion
  573.1 0.7 fusion.20
  573.8 3.0 reshape.371
  576.8 0.7 slice.134
  577.5 1.4 reshape.363
  579.7 1.2 slice_reduce_fusion
  580.9 0.8 copy.110
  581.7 1.7 concatenate.59
  583.4 0.8 copy.122
  584.2 1.0 broadcast_select_fusion
  585.2 0.8 broadcast_select_fusion.2
  586.0 0.7 collective-permute-start.1
  586.7 0.6 multiply_bitcast_fusion
  587.4 15.1 %fusion.11 = (bf16[1,4,768,2,128]{4,3,2,1,0:T(2,128)(2,1)}, f32[1,4,768,2,128]{4,3,2,1,0:T(2,128)}, f32[1,4,768,2,128]{4,3,2,1,0:T(2,128)}, f32[1,4,768,2,128]{4,3,2,1,0:T(2,128)}) fusion(f32[1,4,768,2,128]{4,3,2,1,0:T(2,128)} %param.34, f32[]{:T(128)} %bitcast.38, f32[]{:T(128)} %bitcast.37, f32[1,4,768,2,128]{4,3,2,1,0:T(2,128)S(1)} %copy-done.2, ...), kind=kLoop, calls=%fused_computation.78 | loop fusion | flops 13369344 | bytes 23592972 | tf_op jit(solution)/shard_map/convert_element_type | solution.py:1246
  602.5 0.6 fusion.13
  603.2 2.4 fusion.14
  605.6 4.1 fusion.9
  609.7 1.3 fusion.16
  611.4 0.6 copy.116
  612.0 0.6 copy.115
  612.5 0.9 maximum_bitcast_fusion.2
  613.4 1.1 select_bitcast_fusion.3
  614.4 0.9 maximum_bitcast_fusion.1
  615.4 1.3 select_bitcast_fusion.1
  616.7 1.2 maximum_bitcast_fusion
  (93 shorter events, 2.8 us)
Async XLA Ops:
  7.2 70.3 %copy-start = (bf16[2,256,768]{2,1,0:T(8,128)(2,1)S(1)}, bf16[2,256,768]{2,1,0:T(8,128)(2,1)}, u32[]{:S(2)}) copy-start(bf16[2,256,768]{2,1,0:T(8,128)(2,1)} %param.20) | copy-start | bytes 2359300
  7.2 133.5 %all-gather.8.cloned.1.call-start = ((), (), s32[]{:S(2)}) async-start(), calls=%async_computation.1 | async-start | bytes 9732096 | tf_op jit(solution)/shard_map/all_gather | solution.py:1292
  10.1 3.5 copy-start.28
  10.1 4.8 copy-start.18
  10.2 5.6 copy-start.6
  10.2 1.7 collective-permute-start
  12.8 3.1 copy-start.19
  12.8 3.2 copy-start.24
  12.8 212.1 %all-gather.10.cloned.1.call-start = ((), (), s32[]{:S(2)}) async-start(), calls=%async_computation.2 | async-start | bytes 9732096 | tf_op jit(solution)/shard_map/all_gather | solution.py:1292
  13.6 259.3 %all-gather.6.cloned.1.call-start = ((), (), s32[]{:S(2)}) async-start(), calls=%async_computation | async-start | bytes 1966080 | tf_op jit(solution)/shard_map/all_gather | solution.py:1301
  17.2 34.7 %copy-start.20 = (s32[1,2,256,2]{2,3,1,0:T(2,128)S(1)}, s32[1,2,256,2]{2,3,1,0:T(2,128)}, u32[]{:S(2)}) copy-start(s32[1,2,256,2]{2,3,1,0:T(2,128)} %param.23) | copy-start | bytes 12292
  579.3 4.9 copy-start.3
  579.3 4.9 copy-start.5
  580.9 4.3 copy-start.4
  580.9 4.3 copy-start.11
  584.2 25.5 %copy-start.21 = (f32[48,2]{0,1:T(2,128)}, f32[48,2]{0,1:T(2,128)S(1)}, u32[]{:S(2)}) copy-start(f32[48,2]{0,1:T(2,128)S(1)} %copy.122) | copy-start | bytes 1156
  584.2 3.1 copy-start.2
  585.2 30.2 %collective-permute-start.2 = (f32[256,768]{1,0:T(8,128)}, f32[256,768]{1,0:T(8,128)}, u32[]{:S(2)}, u32[]{:S(2)}) collective-permute-start(f32[256,768]{1,0:T(8,128)} %broadcast_select_fusion), channel_id=1, source_target_pairs={{0,64},{64,0},{1,65},{65,1},{2,66},{66,2},{3,67},{67,3},{4,68},{68... | collective-permute-start | bytes 2359304 | tf_op jit(solution)/shard_map/ppermute | solution.py:1269
  586.0 27.4 %collective-permute-start.1 = (bf16[256,768]{1,0:T(8,128)(2,1)}, bf16[256,768]{1,0:T(8,128)(2,1)}, u32[]{:S(2)}, u32[]{:S(2)}) collective-permute-start(bf16[256,768]{1,0:T(8,128)(2,1)} %broadcast_select_fusion.2), channel_id=1, source_target_pairs={{0,64},{64,0},{1,65},{65,1},{2,66},{66,2},{3,67},{67,3},{4,68},{68... | collective-permute-start | bytes 1179656 | tf_op jit(solution)/shard_map/ppermute | solution.py:1269
  587.3 15.1 %copy-start.22 = (f32[1,48,3]{1,0,2:T(1,128)S(1)}, f32[1,48,3]{1,0,2:T(1,128)}, u32[]{:S(2)}) copy-start(f32[1,48,3]{1,0,2:T(1,128)} %param.33) | copy-start | bytes 1732
  587.3 15.1 %copy-start.23 = (f32[1,48,3]{1,0,2:T(1,128)S(1)}, f32[1,48,3]{1,0,2:T(1,128)}, u32[]{:S(2)}) copy-start(f32[1,48,3]{1,0,2:T(1,128)} %param.32) | copy-start | bytes 1732
  587.4 15.7 %copy-start.7 = (f32[1,48,3072]{2,1,0:T(8,128)S(1)}, f32[1,48,3072]{2,1,0:T(8,128)}, u32[]{:S(2)}) copy-start(f32[1,48,3072]{2,1,0:T(8,128)} %param.28) | copy-start | bytes 1769476
  587.4 15.7 %copy-start.15 = (f32[1,48,3072]{2,1,0:T(8,128)S(1)}, f32[1,48,3072]{2,1,0:T(8,128)}, u32[]{:S(2)}) copy-start(f32[1,48,3072]{2,1,0:T(8,128)} %param.30) | copy-start | bytes 1769476
  587.4 15.7 %copy-start.16 = (f32[1,48,3072]{2,1,0:T(8,128)S(1)}, f32[1,48,3072]{2,1,0:T(8,128)}, u32[]{:S(2)}) copy-start(f32[1,48,3072]{2,1,0:T(8,128)} %param.29) | copy-start | bytes 1769476
  587.4 15.7 %copy-start.17 = (f32[1,48,768]{2,1,0:T(8,128)S(1)}, f32[1,48,768]{2,1,0:T(8,128)}, u32[]{:S(2)}) copy-start(f32[1,48,768]{2,1,0:T(8,128)} %concatenate.59) | copy-start | bytes 442372
  587.4 18.2 %copy-start.10 = (f32[1,4,128,768]{3,2,1,0:T(8,128)S(1)}, f32[1,4,128,768]{3,2,1,0:T(8,128)}, u32[]{:S(2)}) copy-start(f32[1,4,128,768]{3,2,1,0:T(8,128)} %param.38) | copy-start | bytes 4718596
  603.1 2.5 copy-start.8
  603.1 2.5 copy-start.9
  603.1 2.4 copy-start.12
  603.1 2.4 copy-start.13
  603.1 2.4 copy-start.14
  605.6 4.1 copy-start.25
  605.6 4.1 copy-start.26
  605.6 4.1 copy-start.27
  616.7 1.4 copy-start.1
Sparse Core Ops, SparseCore 0:
  12.9 60.4 all-gather.7
  76.2 54.9 all-gather.9
  133.5 26.6 all-gather.5

commit v3 on v2

--- a/solution.py
+++ b/solution.py
@@ -256,15 +256,28 @@
         ring.copy(spot, spot, self.send.at[1], self.recv.at[1], ring.left).wait_recv()
         self.go(ring.right, 1, ring.left)
 
-    def finish(self):
-        ring = self.ring
-        for index, block, half in (
-            (2, ring.left, 1), (3, ring.right, 0), (4, ring.across, 0), (5, ring.across, 1),
-        ):
-            spot = self.at(block, half)
-            ring.copy(spot, spot, self.send.at[index], self.recv.at[index], ring.right).wait_recv()
+    def landed(self, index, block, half):
+        spot = self.at(block, half)
+        self.ring.copy(
+            spot, spot, self.send.at[index], self.recv.at[index], self.ring.right
+        ).wait_recv()
+
+    def near(self):
+        self.landed(2, self.ring.left, 1)
+        self.landed(3, self.ring.right, 0)
+
+    def far(self):
+        self.landed(4, self.ring.across, 0)
+        self.landed(5, self.ring.across, 1)
+
+    def sent(self):
         for copy in self.copies:
             copy.wait_send()
+
+    def finish(self):
+        self.near()
+        self.far()
+        self.sent()
 
 
 class RingSum:
@@ -274,16 +287,13 @@
         size = part.shape[1]
         self.halves = (pl.ds(0, cut), pl.ds(cut, size - cut))
         self.make = make
-        self.copies = []
-
-    def go(self, block, half, target, to):
-        index = len(self.copies)
-        self.copies.append(
-            self.ring.copy(
-                self.part.at[block, self.halves[half]], target, self.send.at[index], self.recv.at[index], to
-            )
+        self.copies = {}
+
+    def go(self, index, block, half, target, to):
+        self.copies[index] = self.ring.copy(
+            self.part.at[block, self.halves[half]], target, self.send.at[index], self.recv.at[index], to
         )
-        self.copies[-1].start()
+        self.copies[index].start()
 
     def arrived(self, half, block):
         self.copies[half].wait_recv()
@@ -302,26 +312,26 @@
         ring = self.ring
         if number == 0:
             self.make(0, ring.across)
-            self.go(ring.across, 0, self.across_in[0], ring.right)
-            self.go(ring.across, 1, self.across_in[1], ring.left)
+            self.go(0, ring.across, 0, self.across_in[0], ring.right)
+            self.go(1, ring.across, 1, self.across_in[1], ring.left)
         elif number == 1:
             self.make(1, ring.right)
-            self.go(ring.right, 1, self.from_left.at[self.halves[1]], ring.right)
+            self.go(2, ring.right, 1, self.from_left.at[self.halves[1]], ring.right)
         elif number == 2:
             self.make(2, ring.left)
-            self.go(ring.left, 0, self.from_right.at[self.halves[0]], ring.left)
+            self.go(3, ring.left, 0, self.from_right.at[self.halves[0]], ring.left)
         elif number == 3:
             self.arrived(0, ring.right)
-            self.go(ring.right, 0, self.from_left.at[self.halves[0]], ring.right)
+            self.go(4, ring.right, 0, self.from_left.at[self.halves[0]], ring.right)
             self.arrived(1, ring.left)
-            self.go(ring.left, 1, self.from_right.at[self.halves[1]], ring.left)
+            self.go(5, ring.left, 1, self.from_right.at[self.halves[1]], ring.left)
         elif number == 4:
             self.make(3, ring.me)
         else:
-            for copy in self.copies[2:]:
-                copy.wait_recv()
-            for copy in self.copies:
-                copy.wait_send()
+            for index in range(2, 6):
+                self.copies[index].wait_recv()
+            for index in range(6):
+                self.copies[index].wait_send()
 
     def total(self, index=None):
         spot = (self.ring.me,) if index is None else (self.ring.me, index)
@@ -343,14 +353,26 @@
 SEMS = pltpu.SemaphoreType.DMA
 
 
-def gather_shards_kernel(shard_ref, out_ref, *sems):
+def gather_shards_kernel(shard_ref, code_ref, out_ref, codes_ref, *sems):
     section = lax.axis_index("section")
     sibling = {"section": 1 - section}
     ring_y, ring_z = Ring("y"), Ring("z")
     y, z = ring_y.me, ring_z.me
-    greet_ids([sibling] + ring_y.near() + ring_z.near())
+    ring_x = Ring("x")
+    x_peers = (ring_x.right, ring_x.left, ring_x.across)
+    greet_ids(
+        [sibling] + ring_y.near() + ring_z.near() + [ring_x.place(peer) for peer in x_peers]
+    )
     out_ref[section, z, y] = shard_ref[...]
-    met(5)
+    codes_ref[section, ring_x.me] = code_ref[...]
+    met(8)
+    spot = codes_ref.at[section, ring_x.me]
+    code_copies = [
+        ring_x.copy(spot, spot, sems[10].at[index], sems[11].at[index], peer)
+        for index, peer in enumerate(x_peers)
+    ]
+    for copy in code_copies:
+        copy.start()
     half = ATTN_ROWS // 2
     low = (pl.ds(0, 64), pl.ds(64, half - 64))
     high = (pl.ds(half, 64), pl.ds(half + 64, half - 64))
@@ -379,19 +401,34 @@
         device_id_type=MESH,
     )
     across.start()
+    for copy in code_copies:
+        copy.wait()
+    codes_across = pltpu.make_async_remote_copy(
+        src_ref=codes_ref.at[section],
+        dst_ref=codes_ref.at[section],
+        send_sem=sems[12],
+        recv_sem=sems[13],
+        device_id=sibling,
+        device_id_type=MESH,
+    )
+    codes_across.start()
+    codes_across.wait()
     across.wait()
 
 
-def gather_shards(shard):
+def gather_shards(shard, codes):
     return pl.pallas_call(
         gather_shards_kernel,
-        out_shape=jax.ShapeDtypeStruct((2, CTX, CTX, ATTN_ROWS, UNIT), BF16),
-        in_specs=[VMEM],
-        out_specs=VMEM,
-        scratch_shapes=[SEMS((6,))] * 8 + [SEMS, SEMS],
+        out_shape=(
+            jax.ShapeDtypeStruct((2, CTX, CTX, ATTN_ROWS, UNIT), BF16),
+            jax.ShapeDtypeStruct((2, CTX, 8, ROWS), F32),
+        ),
+        in_specs=[VMEM, VMEM],
+        out_specs=[VMEM, VMEM],
+        scratch_shapes=[SEMS((6,))] * 8 + [SEMS, SEMS, SEMS((3,)), SEMS((3,)), SEMS, SEMS],
         compiler_params=params(7),
         name="gather_shards",
-    )(shard)
+    )(shard, codes)
 
 
 def sum_shards_kernel(
@@ -659,10 +696,10 @@
 
 
 def attn_forward_kernel(
-    length_ref, u_ref, routes_ref, pack_ref, table_ref,
-    a_ref, qkv_ref, mass_ref, attended_ref, residual_ref, b_ref, gates_ref, gate_ref,
+    length_ref, u_ref, pack_ref, table_ref,
+    a_ref, qkv_ref, mass_ref, attended_ref, residual_ref, b_ref,
     gains_ref, router_ref, w_ref, back_ref,
-    heads_out, heads_w, send_a, recv_a, send_o, recv_o, send_b, recv_b,
+    heads_out, heads_w, send_a, recv_a, send_o, recv_o,
 ):
     me, right, left, across = ring()
     greet((right, left, across))
@@ -727,24 +764,12 @@
     for block in range(CTX):
         residual = residual + dot(attended_ref[block], back_ref[block * COLS : (block + 1) * COLS, :])
     residual_ref[...] = residual
-    b_ref[rows_of(me), :] = (residual * inverse_size(residual) * gains_ref[1:2, :]).astype(BF16)
+    b_ref[...] = (residual * inverse_size(residual) * gains_ref[1:2, :]).astype(BF16)
     for step in range(1, CTX):
         pltpu.make_async_copy(heads_out.at[0], attended_ref.at[0], send_o.at[step]).wait()
-    gather_rows(b_ref, send_b, recv_b)
-    lanes = lax.broadcasted_iota(jnp.int32, (ROWS, LANES), 1)
-    for block in range(CTX):
-        rows = pl.ds(block * ROWS, ROWS)
-        logits = dot(b_ref[rows, :], router_ref[...])
-        named = (lanes == routes_ref[rows, 0:1]) | (lanes == routes_ref[rows, 1:2])
-        chosen = jnp.where(named, logits, MASK_VALUE)
-        raw = jnp.where(named, jnp.exp(chosen - jnp.max(chosen, axis=1, keepdims=True)), 0.0)
-        gates = raw / jnp.sum(raw, axis=1, keepdims=True)
-        gates_ref[rows, :] = gates
-        gates = jnp.where(lanes == EXPERTS, 1.0, gates)
-        gate_ref[rows, :] = jnp.sum(jnp.where(lanes == me, gates, 0.0), axis=1, keepdims=True)
-
-
-def attn_forward(length, u, routes, pack, table):
+
+
+def attn_forward(length, u, pack, table):
     sems = pltpu.SemaphoreType.DMA
     return pl.pallas_call(
         attn_forward_kernel,
@@ -754,34 +779,28 @@
             jax.ShapeDtypeStruct((HEADS_DEV, SEQ, 1), F32),
             jax.ShapeDtypeStruct((CTX, ROWS, COLS), BF16),
             jax.ShapeDtypeStruct((ROWS, D), F32),
-            jax.ShapeDtypeStruct((SEQ, D), BF16),
-            jax.ShapeDtypeStruct((SEQ, LANES), F32),
-            jax.ShapeDtypeStruct((SEQ, 1), F32),
+            jax.ShapeDtypeStruct((ROWS, D), BF16),
             jax.ShapeDtypeStruct((8, D), F32),
             jax.ShapeDtypeStruct((D, LANES), BF16),
             jax.ShapeDtypeStruct((D, EXT), BF16),
             jax.ShapeDtypeStruct((D, D), BF16),
         ),
-        in_specs=[SMEM] + [VMEM] * 4,
-        out_specs=[VMEM] * 12,
+        in_specs=[SMEM] + [VMEM] * 3,
+        out_specs=[VMEM] * 10,
         scratch_shapes=[pltpu.VMEM((CTX, ROWS, COLS), BF16), pltpu.VMEM((D, D), BF16)]
-        + [sems((6,)), sems((6,)), sems((CTX,)), sems((CTX,)), sems((6,)), sems((6,))],
+        + [sems((6,)), sems((6,)), sems((CTX,)), sems((CTX,))],
         compiler_params=params(1),
         name="attn_forward",
-    )(length, u, routes, pack, table)
+    )(length, u, pack, table)
 
 
 def attn_backward_kernel(
-    last, length_ref, u_ref, gains_ref, router_ref, w_ref, back_ref, table_ref,
+    length_ref, u_ref, gains_ref, router_ref, w_ref, back_ref, table_ref,
     a_ref, qkv_ref, mass_ref, attended_ref, residual_ref, second_ref, gates_ref,
     delta_ref, db_ref, gate_grad_ref, *rest,
 ):
-    if last:
-        input_ref, pack_ref = rest[:2]
-        rest = rest[2:]
-    else:
-        input_ref, pack_ref, lower_ref = rest[:3]
-        rest = rest[3:]
+    input_ref, pack_ref, lower_ref = rest[:3]
+    rest = rest[3:]
     dheads_ref, dback_ref = rest[:2]
     rest = rest[2:]
     key_acc, value_acc, dz, grads_out, grads_in, send_o, recv_o = rest[:7]
@@ -921,19 +940,16 @@
         jnp.where(small_lanes == EXPERTS + 1, gain_two_column, router_terms),
     ).astype(BF16)
     repack(dback_ref, dheads_ref, pack_ref)
-    if not last:
-        lower_ref[rows_of(me), :] = input_grad.astype(BF16)
-        gather_rows(lower_ref, *rest[13:])
-
-
-def attn_backward(last, length, *arrays):
+    lower_ref[...] = input_grad.astype(BF16)
+
+
+def attn_backward(length, *arrays):
     sems = pltpu.SemaphoreType.DMA
     out_shape = [
         jax.ShapeDtypeStruct((ROWS, D), F32),
         jax.ShapeDtypeStruct((16, ATTN_ROWS, UNIT), BF16),
+        jax.ShapeDtypeStruct((ROWS, D), BF16),
     ]
-    if not last:
-        out_shape.append(jax.ShapeDtypeStruct((SEQ, D), BF16))
     scratch = [
         pltpu.VMEM((D, D), BF16),
         pltpu.VMEM((D, D), BF16),
@@ -945,262 +961,336 @@
         sems((CTX,)),
         sems((CTX,)),
     ] + REDUCE_SCRATCH
-    if not last:
-        scratch += [sems((6,)), sems((6,))]
     return pl.pallas_call(
-        functools.partial(attn_backward_kernel, last),
+        attn_backward_kernel,
         out_shape=tuple(out_shape),
         in_specs=[SMEM] + [VMEM] * len(arrays),
         out_specs=[VMEM] * len(out_shape),
         scratch_shapes=scratch,
-        compiler_params=params(3 if last else 4),
+        compiler_params=params(3),
         name="attn_backward",
     )(length, *arrays)
 
 
-SHARDS_STEP = 4
-IN_ROWS = D
-HALF_ROWS = (D + D * 128 // 256) // 2
-
-
-def assemble(w_ref, win, wout):
-    shards, units = win.shape[0], LANES
-    width = 2 * units
-    split = HALF_ROWS
-    for shard in range(shards):
-        win[shard, :split, :] = w_ref[0, shard]
-        win[shard, split:, :] = w_ref[1, shard, : D - split, :]
-        for piece in range(D // width):
-            at = D - split + piece * units
-            wout[shard * units : (shard + 1) * units, piece * width : (piece + 1) * width] = w_ref[
-                1, shard, at : at + units, :
+GROUP = 4
+GROUPS = 16 // GROUP
+GROUP_UNITS = GROUP * LANES
+SPLIT = EXPERT_ROWS // 2
+ANY = pl.BlockSpec(memory_space=pl.ANY)
+SUM_SCRATCH = [
+    pltpu.VMEM((CTX, ROWS, D), BF16),
+    pltpu.VMEM((HALF, D), BF16),
+    pltpu.VMEM((HALF, D), BF16),
+    pltpu.VMEM((ROWS, D), BF16),
+    pltpu.VMEM((ROWS, D), BF16),
+    SEMS((6,)),
+    SEMS((6,)),
+]
+
+
+def weight_copies(w_ref, win, wout, sem):
+    groups = []
+    for group in range(GROUPS):
+        shards = pl.ds(group * GROUP, GROUP)
+        pairs = [
+            (w_ref.at[0, shards], win.at[shards, pl.ds(0, SPLIT), :]),
+            (w_ref.at[1, shards, pl.ds(0, D - SPLIT), :], win.at[shards, pl.ds(SPLIT, D - SPLIT), :]),
+        ]
+        for piece in range(D // UNIT):
+            pairs.append(
+                (
+                    w_ref.at[1, shards, pl.ds(D - SPLIT + piece * LANES, LANES), :],
+                    wout.at[shards, :, pl.ds(piece * UNIT, UNIT)],
+                )
+            )
+        groups.append(
+            [
+                pltpu.make_async_copy(source, target, sem.at[group * 5 + index])
+                for index, (source, target) in enumerate(pairs)
             ]
+        )
+    return groups
+
+
+def wout_group(wout, group):
+    return wout[group * GROUP : (group + 1) * GROUP].reshape(GROUP_UNITS, D)
 
 
 def ffn_forward_kernel(
-    b_ref, gate_ref, residual_ref, w_ref, y_ref, kept_ref, acc, win, wout,
-    part, across_in, from_left, from_right, send, recv,
+    b_own_ref, residual_ref, codes_ref, router_ref, w_ref,
+    y_ref, b_ref, gates_ref, gate_ref, kept_ref,
+    win, wout, kept_out, acc, w_sem, kept_sem, send_b, recv_b,
+    part, top_in, bottom_in, from_left, from_right, send, recv,
 ):
-    step = pl.program_id(0)
-    final = pl.num_programs(0) - 1
-    shards, units = win.shape[0], LANES
-
-    @pl.when(step == 0)
-    def _():
-        _, right, left, _ = ring()
-        greet((right, left))
-        acc[...] = jnp.zeros_like(acc)
-
-    assemble(w_ref, win, wout)
-
-    def terms(block):
-        rows = rows_of(block)
-        b_rows = b_ref[rows, :]
-        acted = []
-        for shard in range(shards):
+    ring = Ring("x")
+    greet_ids(ring.near())
+    loads = weight_copies(w_ref, win, wout, w_sem)
+    for group in loads:
+        for copy in group:
+            copy.start()
+    b_ref[ring.me] = b_own_ref[...]
+    met(2)
+    halves = (pl.ds(0, HALF), pl.ds(HALF, HALF))
+    rows = RingGather(ring, lambda b, h: b_ref.at[b, halves[h]], send_b, recv_b)
+    rows.start()
+    section = lax.axis_index("section")
+    lanes = lax.broadcasted_iota(jnp.int32, (ROWS, LANES), 1)
+    picker = jnp.where(lax.broadcasted_iota(jnp.int32, (8, LANES), 0) == section, 1.0, 0.0)
+    stores = []
+
+    def make(index, block):
+        b_rows = b_ref[block]
+        slot = index % 2
+        for shard in range(16):
+            if index == 0 and shard % GROUP == 0:
+                for copy in loads[shard // GROUP]:
+                    copy.wait()
+            if index >= 2 and shard == 0:
+                stores[index - 2].wait()
             hidden = dot(b_rows, win[shard])
-            kept_ref[shard, rows, :] = hidden.astype(BF16)
-            gate_part = hidden[:, :units]
-            acted.append(
-                (gate_part / (1.0 + jnp.exp(-gate_part)) * hidden[:, units:]).astype(BF16)
-            )
-        return acc[rows, :] + dot(jnp.concatenate(acted, axis=1), wout[...])
-
-    @pl.when(step < final)
-    def _():
-        for block in range(CTX):
-            acc[pl.ds(block * ROWS, ROWS), :] = terms(block)
-
-    @pl.when(step == final)
-    def _():
-        met(2)
-
-        def make(block):
-            rows = rows_of(block)
-            part[rows, :] = (terms(block) * gate_ref[rows, :]).astype(BF16)
-
-        total = reduce_rows(make, part, across_in, from_left, from_right, send, recv)
-        y_ref[...] = (residual_ref[...] + total).astype(BF16)
-
-
-def ffn_forward(b_all, gate_col, residual, weights):
-    _, count, half_rows, double = weights.shape
-    shards = SHARDS_STEP
+            kept_out[slot, shard] = hidden.astype(BF16)
+            gate_part = hidden[:, :LANES]
+            at = shard % GROUP * LANES
+            acc_act = (gate_part / (1.0 + jnp.exp(-gate_part)) * hidden[:, LANES:]).astype(BF16)
+            if shard % GROUP == 0:
+                acted = []
+            acted.append(acc_act)
+            if shard % GROUP == GROUP - 1:
+                terms = dot(jnp.concatenate(acted, axis=1), wout_group(wout, shard // GROUP))
+                acc[...] = terms if shard < GROUP else acc[...] + terms
+        stores.append(pltpu.make_async_copy(kept_out.at[slot], kept_ref.at[block], kept_sem.at[slot]))
+        stores[-1].start()
+        logits = dot(b_rows, router_ref[...])
+        codes = lax.dot_general(
+            codes_ref[block], picker, TN, precision=EXACT, preferred_element_type=F32
+        )
+        named = (lanes < EXPERTS) & (lanes != jnp.round(codes).astype(jnp.int32))
+        chosen = jnp.where(named, logits, MASK_VALUE)
+        raw = jnp.where(named, jnp.exp(chosen - jnp.max(chosen, axis=1, keepdims=True)), 0.0)
+        gates = raw / jnp.sum(raw, axis=1, keepdims=True)
+        if index == 0:
+            gates_ref[...] = gates
+        gates = jnp.where(lanes == EXPERTS, 1.0, gates)
+        gate = jnp.sum(jnp.where(lanes == ring.me, gates, 0.0), axis=1, keepdims=True)
+        gate_ref[block] = gate
+        part[block] = (acc[...] * gate).astype(BF16)
+
+    order = {ring_index: number for number, ring_index in enumerate(("me", "right", "left", "across"))}
+
+    def from_sum(position, block):
+        make({0: order["across"], 1: order["right"], 2: order["left"], 3: order["me"]}[position], block)
+
+    sums = RingSum(
+        ring, part, (top_in, bottom_in), from_left, from_right, send, recv, HALF, from_sum
+    )
+    sums.stage(4)
+    rows.forward()
+    rows.near()
+    sums.stage(1)
+    sums.stage(2)
+    rows.far()
+    sums.stage(0)
+    sums.stage(3)
+    sums.stage(5)
+    y_ref[...] = (residual_ref[...] + sums.total()).astype(BF16)
+    rows.sent()
+    stores[2].wait()
+    stores[3].wait()
+
+
+def ffn_forward(b_own, residual, codes, router, weights):
     return pl.pallas_call(
         ffn_forward_kernel,
-        grid=(count // shards,),
         out_shape=(
             jax.ShapeDtypeStruct((ROWS, D), BF16),
-            jax.ShapeDtypeStruct((count, SEQ, double), BF16),
+            jax.ShapeDtypeStruct((CTX, ROWS, D), BF16),
+            jax.ShapeDtypeStruct((ROWS, LANES), F32),
+            jax.ShapeDtypeStruct((CTX, ROWS, 1), F32),
+            jax.ShapeDtypeStruct((CTX, 16, ROWS, UNIT), BF16),
         ),
-        in_specs=[
-            whole((SEQ, D)),
-            whole((SEQ, 1)),
-            whole((ROWS, D)),
-            pl.BlockSpec((2, shards, half_rows, double), lambda i: (0, i, 0, 0)),
-        ],
-        out_specs=[whole((ROWS, D)), pl.BlockSpec((shards, SEQ, double), lambda i: (i, 0, 0))],
+        in_specs=[VMEM] * 4 + [ANY],
+        out_specs=[VMEM] * 4 + [ANY],
         scratch_shapes=[
-            pltpu.VMEM((SEQ, D), F32),
-            pltpu.VMEM((shards, D, double), BF16),
-            pltpu.VMEM((shards * double // 2, D), BF16),
+            pltpu.VMEM((16, D, UNIT), BF16),
+            pltpu.VMEM((16, LANES, D), BF16),
+            pltpu.VMEM((2, 16, ROWS, UNIT), BF16),
+            pltpu.VMEM((ROWS, D), F32),
+            SEMS((5 * GROUPS,)),
+            SEMS((2,)),
+            SEMS((6,)),
+            SEMS((6,)),
         ]
-        + REDUCE_SCRATCH,
+        + SUM_SCRATCH,
         compiler_params=params(5),
         name="ffn_forward",
-    )(b_all, gate_col, residual, weights)
+    )(b_own, residual, codes, router, weights)
 
 
 def ffn_backward_kernel(
-    b_ref, gate_ref, delta_ref, kept_ref, w_ref, db_ref, gate_grad_ref, dw_ref,
-    acc, gate_acc, b_turned, slot_grad, hidden_grad, acted, win, wout, rows_out, rows_in, send_g, recv_g,
-    part, across_in, from_left, from_right, send, recv,
+    b_ref, gate_ref, delta_own_ref, kept_ref, w_ref, db_ref, gate_grad_ref, dw_ref,
+    delta, acc, gate_acc, slot_grad, hidden, acted, win, wout, staged, rows_out, rows_in,
+    w_sem, kept_sem, dw_sem, send_d, recv_d, send_g, recv_g,
+    part, top_in, bottom_in, from_left, from_right, send, recv,
 ):
-    step = pl.program_id(0)
-    final = pl.num_programs(0) - 1
-    shards, units = win.shape[0], LANES
-    width = 2 * units
-
-    @pl.when(step == 0)
-    def _():
-        _, right, left, across = ring()
-        greet((right, left, across))
-        acc[...] = jnp.zeros_like(acc)
-        gate_acc[...] = jnp.zeros_like(gate_acc)
-        b_turned[...] = b_ref[...].T
-        slot_grad[...] = (delta_ref[...].astype(F32) * gate_ref[...]).astype(BF16)
-
-    assemble(w_ref, win, wout)
-
-    def terms(block):
-        rows = rows_of(block)
-        gate = gate_ref[rows, :]
-        act_grad_all = dot_nt(delta_ref[rows, :], wout[...])
-        gate_sum = gate_acc[rows, :]
-        second_grad = acc[rows, :]
-        for shard in range(shards):
-            hidden = kept_ref[shard, rows, :].astype(F32)
-            gate_part = hidden[:, :units]
-            up_part = hidden[:, units:]
-            act_grad = act_grad_all[:, shard * units : (shard + 1) * units]
-            sigmoid = 1.0 / (1.0 + jnp.exp(-gate_part))
-            silu = gate_part * sigmoid
-            act = (silu * up_part).astype(BF16)
-            acted[rows, shard * units : (shard + 1) * units] = act
-            gate_sum += act.astype(F32) * act_grad
-            act_grad = act_grad * gate
-            gate_grad = act_grad * up_part * (sigmoid * (1.0 + gate_part * (1.0 - sigmoid)))
-            pair = jnp.concatenate([gate_grad, act_grad * silu], axis=1).astype(BF16)
-            hidden_grad[shard, rows, :] = pair
-            second_grad += dot_nt(pair, win[shard])
-        gate_acc[rows, :] = gate_sum
-        return second_grad
-
-    def weight_terms():
-        for shard in range(shards):
-            dw_ref[shard, :D, :] = dot(b_turned[...], hidden_grad[shard]).astype(BF16)
-        whole_out = dot_tn(acted[...], slot_grad[...]).astype(BF16)
-        for shard in range(shards):
-            for piece in range(D // width):
-                at = D + piece * units
-                dw_ref[shard, at : at + units, :] = whole_out[
-                    shard * units : (shard + 1) * units, piece * width : (piece + 1) * width
+    ring = Ring("x")
+    peers = (ring.right, ring.left, ring.across)
+    greet_ids([ring.place(peer) for peer in peers])
+    blocks = (ring.me, ring.right, ring.left, ring.across)
+    kept_loads = [
+        pltpu.make_async_copy(
+            kept_ref.at[block], hidden.at[:, rows_of(block), :], kept_sem.at[index]
+        )
+        for index, block in enumerate(blocks)
+    ]
+    loads = weight_copies(w_ref, win, wout, w_sem)
+    kept_loads[0].start()
+    for group in loads:
+        for copy in group:
+            copy.start()
+    for copy in kept_loads[1:]:
+        copy.start()
+    delta[ring.me] = delta_own_ref[...]
+    met(3)
+    halves = (pl.ds(0, HALF), pl.ds(HALF, HALF))
+    rows = RingGather(ring, lambda b, h: delta.at[b, halves[h]], send_d, recv_d)
+    rows.start()
+    own_row = lax.broadcasted_iota(jnp.int32, (8, LANES), 0) == ring.me
+    picker = jnp.where(own_row, 1.0, 0.0)
+    handed = [
+        ring.copy(rows_out.at[peer], rows_in.at[index], send_g.at[index], recv_g.at[index], peer)
+        for index, peer in enumerate(peers)
+    ]
+
+    def make(index, block):
+        kept_loads[index].wait()
+        at = rows_of(block)
+        gate = gate_ref[block]
+        delta_rows = delta[block]
+        slot_grad[at, :] = (delta_rows.astype(F32) * gate).astype(BF16)
+        gate_sum = jnp.zeros((ROWS, LANES), F32)
+        for group in range(GROUPS):
+            if index == 0:
+                for copy in loads[group]:
+                    copy.wait()
+            act_grad_all = dot_nt(delta_rows, wout_group(wout, group))
+            second_grad = None
+            for inner in range(GROUP):
+                shard = group * GROUP + inner
+                values = hidden[shard, at, :].astype(F32)
+                gate_part = values[:, :LANES]
+                up_part = values[:, LANES:]
+                act_grad = act_grad_all[:, inner * LANES : (inner + 1) * LANES]
+                sigmoid = 1.0 / (1.0 + jnp.exp(-gate_part))
+                silu = gate_part * sigmoid
+                act = (silu * up_part).astype(BF16)
+                acted[at, shard * LANES : (shard + 1) * LANES] = act
+                gate_sum += act.astype(F32) * act_grad
+                act_grad = act_grad * gate
+                gate_grad = act_grad * up_part * (sigmoid * (1.0 + gate_part * (1.0 - sigmoid)))
+                pair = jnp.concatenate([gate_grad, act_grad * silu], axis=1).astype(BF16)
+                hidden[shard, at, :] = pair
+                term = dot_nt(pair, win[shard])
+                second_grad = term if second_grad is None else second_grad + term
+            acc[...] = second_grad if group == 0 else acc[...] + second_grad
+        part[block] = acc[...].astype(BF16)
+        rows_out[block] = lax.dot_general(
+            picker, gate_sum, NT, precision=EXACT, preferred_element_type=F32
+        )
+        if index > 0:
+            handed[index - 1].start()
+
+    def from_sum(position, block):
+        make((3, 1, 2, 0)[position], block)
+
+    sums = RingSum(
+        ring, part, (top_in, bottom_in), from_left, from_right, send, recv, HALF, from_sum
+    )
+    sums.stage(4)
+    rows.forward()
+    rows.near()
+    sums.stage(1)
+    sums.stage(2)
+    rows.far()
+    sums.stage(0)
+    stores = []
+    b_all = b_ref[...].reshape(SEQ, D)
+    for group in range(GROUPS):
+        slot = group % 2
+        if group == 1:
+            sums.stage(3)
+        if group >= 2:
+            stores[group - 2].wait()
+        for inner in range(GROUP):
+            staged[slot, inner, :D, :] = dot_tn(b_all, hidden[group * GROUP + inner]).astype(BF16)
+        whole_out = dot_tn(
+            acted[:, group * GROUP_UNITS : (group + 1) * GROUP_UNITS], slot_grad[...]
+        ).astype(BF16)
+        for inner in range(GROUP):
+            for piece in range(D // UNIT):
+                at = D + piece * LANES
+                staged[slot, inner, at : at + LANES, :] = whole_out[
+                    inner * LANES : (inner + 1) * LANES, piece * UNIT : (piece + 1) * UNIT
                 ]
-
-    @pl.when(step < final)
-    def _():
-        for block in range(CTX):
-            acc[pl.ds(block * ROWS, ROWS), :] = terms(block)
-        weight_terms()
-
-    @pl.when(step == final)
-    def _():
-        met(3)
-        me, right, left, across = ring()
-
-        def make(block):
-            part[rows_of(block), :] = terms(block).astype(BF16)
-
-        def handed(step_to, peer):
-            return remote(
-                rows_out.at[peer], rows_in.at[step_to], send_g.at[step_to], recv_g.at[step_to], peer
+        stores.append(
+            pltpu.make_async_copy(
+                staged.at[slot], dw_ref.at[pl.ds(group * GROUP, GROUP)], dw_sem.at[slot]
             )
-
-        def beside():
-            own_row = lax.broadcasted_iota(jnp.int32, (8, LANES), 0) == me
-            picker = jnp.where(own_row, 1.0, 0.0)
-            for block in range(CTX):
-                rows_out[block] = lax.dot_general(
-                    picker,
-                    gate_acc[pl.ds(block * ROWS, ROWS), :],
-                    NT,
-                    precision=EXACT,
-                    preferred_element_type=F32,
-                )
-            for step_to, peer in ((0, right), (1, left), (2, across)):
-                handed(step_to, peer).start()
-            weight_terms()
-
-        db_ref[...] = reduce_rows(
-            make, part, across_in, from_left, from_right, send, recv, beside
         )
-        for step_to, peer in ((0, right), (1, left), (2, across)):
-            handed(step_to, peer).wait()
-        rows_all = rows_out[me] + rows_in[0] + rows_in[1] + rows_in[2]
-        picker = jnp.where(
-            lax.broadcasted_iota(jnp.int32, (8, LANES), 0)
-            == lax.broadcasted_iota(jnp.int32, (8, LANES), 1),
-            1.0,
-            0.0,
-        )
-        gate_grad_ref[...] = lax.dot_general(
-            rows_all, picker, TN, precision=EXACT, preferred_element_type=F32
-        )
-
-
-def ffn_backward(b_all, gate_col, delta_all, kept, weights):
-    _, count, half_rows, double = weights.shape
-    shards = SHARDS_STEP
-    units = double // 2
-    sems = pltpu.SemaphoreType.DMA
+        stores[-1].start()
+    sums.stage(5)
+    db_ref[...] = sums.total()
+    for copy in handed:
+        copy.wait()
+    rows_all = rows_out[ring.me] + rows_in[0] + rows_in[1] + rows_in[2]
+    diagonal = jnp.where(
+        lax.broadcasted_iota(jnp.int32, (8, LANES), 0)
+        == lax.broadcasted_iota(jnp.int32, (8, LANES), 1),
+        1.0,
+        0.0,
+    )
+    gate_grad_ref[...] = lax.dot_general(
+        rows_all, diagonal, TN, precision=EXACT, preferred_element_type=F32
+    )
+    rows.sent()
+    stores[2].wait()
+    stores[3].wait()
+
+
+def ffn_backward(b_all, gate_col, delta_own, kept, weights):
     return pl.pallas_call(
         ffn_backward_kernel,
-        grid=(count // shards,),
         out_shape=(
             jax.ShapeDtypeStruct((ROWS, D), F32),
             jax.ShapeDtypeStruct((ROWS, LANES), F32),
-            jax.ShapeDtypeStruct((count, 2 * half_rows, double), BF16),
+            jax.ShapeDtypeStruct((16, EXPERT_ROWS, UNIT), BF16),
         ),
-        in_specs=[
-            whole((SEQ, D)),
-            whole((SEQ, 1)),
-            whole((SEQ, D)),
-            pl.BlockSpec((shards, SEQ, double), lambda i: (i, 0, 0)),
-            pl.BlockSpec((2, shards, half_rows, double), lambda i: (0, i, 0, 0)),
-        ],
-        out_specs=[
-            whole((ROWS, D)),
-            whole((ROWS, LANES)),
-            pl.BlockSpec((shards, 2 * half_rows, double), lambda i: (i, 0, 0)),
-        ],
+        in_specs=[VMEM] * 3 + [ANY] * 2,
+        out_specs=[VMEM] * 2 + [ANY],
         scratch_shapes=[
-            pltpu.VMEM((SEQ, D), F32),
-            pltpu.VMEM((SEQ, units), F32),
-            pltpu.VMEM((D, SEQ), BF16),
+            pltpu.VMEM((CTX, ROWS, D), BF16),
+            pltpu.VMEM((ROWS, D), F32),
+            pltpu.VMEM((8, LANES), F32),
             pltpu.VMEM((SEQ, D), BF16),
-            pltpu.VMEM((shards, SEQ, double), BF16),
-            pltpu.VMEM((SEQ, shards * units), BF16),
-            pltpu.VMEM((shards, D, double), BF16),
-            pltpu.VMEM((shards * units, D), BF16),
+            pltpu.VMEM((16, SEQ, UNIT), BF16),
+            pltpu.VMEM((SEQ, FFN), BF16),
+            pltpu.VMEM((16, D, UNIT), BF16),
+            pltpu.VMEM((16, LANES, D), BF16),
+            pltpu.VMEM((2, GROUP, EXPERT_ROWS, UNIT), BF16),
             pltpu.VMEM((CTX, 8, ROWS), F32),
             pltpu.VMEM((3, 8, ROWS), F32),
-            sems((3,)),
-            sems((3,)),
+            SEMS((5 * GROUPS,)),
+            SEMS((CTX,)),
+            SEMS((2,)),
+            SEMS((6,)),
+            SEMS((6,)),
+            SEMS((3,)),
+            SEMS((3,)),
         ]
-        + REDUCE_SCRATCH,
+        + SUM_SCRATCH,
         compiler_params=params(6),
         name="ffn_backward",
-    )(b_all, gate_col, delta_all, kept, weights)
+    )(b_all, gate_col, delta_own, kept, weights)
+
 
 def rotary_table():
     half_dim = HEAD_DIM // 2
@@ -1212,28 +1302,30 @@
     return jnp.concatenate([cosine, cosine, sine, sine], axis=1)
 
 
-def layer_forward(weights, tokens_in, length, routes_all, table):
+def layer_forward(weights, tokens_in, length, codes, table):
     pack, experts = weights
-    a_all, qkv, mass, attended, residual, b_all, gates, gate_col, *unpacked = attn_forward(
-        length, tokens_in, routes_all, pack, table
-    )
-    output, kept = ffn_forward(b_all, gate_col, residual, experts)
+    a_all, qkv, mass, attended, residual, second, *unpacked = attn_forward(
+        length, tokens_in, pack, table
+    )
+    output, b_all, gates, gate_col, kept = ffn_forward(
+        second, residual, codes, unpacked[1], experts
+    )
     return output, (
-        tokens_in, a_all, qkv, mass, attended, residual, b_all, gates, gate_col, kept, unpacked,
-    )
-
-
-def layer_backward(weights, saved, delta_all, delta_own, length, table, ctx_index, last):
+        tokens_in, a_all, qkv, mass, attended, residual, second, b_all, gates, gate_col, kept, unpacked,
+    )
+
+
+def layer_backward(weights, saved, delta_own, length, table):
     _, experts = weights
-    tokens_in, a_all, qkv, mass, attended, residual, b_all, gates, gate_col, kept, unpacked = saved
-    db, gate_grads, dexperts = ffn_backward(b_all, gate_col, delta_all, kept, experts)
-    second = lax.dynamic_slice_in_dim(b_all, ctx_index * ROWS, ROWS, 0)
-    own_gates = lax.dynamic_slice_in_dim(gates, ctx_index * ROWS, ROWS, 0)
-    results = attn_backward(
-        last, length, tokens_in, *unpacked, table, a_all, qkv, mass,
-        attended, residual, second, own_gates, delta_own, db, gate_grads,
-    )
-    return dexperts, results
+    (
+        tokens_in, a_all, qkv, mass, attended, residual, second, b_all, gates, gate_col, kept, unpacked,
+    ) = saved
+    db, gate_grads, dexperts = ffn_backward(b_all, gate_col, delta_own, kept, experts)
+    return dexperts, attn_backward(
+        length, tokens_in, *unpacked, table, a_all, qkv, mass,
+        attended, residual, second, gates, delta_own, db, gate_grads,
+    )
+
 
 def adam_update(gradient, clipped, master, mean_old, square_old, step_value, learn_rate):
     mean_new = BETA_ONE * mean_old + (1.0 - BETA_ONE) * clipped
@@ -1244,6 +1336,120 @@
         mean_new / fix_one / (jnp.sqrt(square_new / fix_two) + ADAM_EPS) + DECAY_RATE * master
     )
     return (gradient, mean_new, square_new, master_new, master_new.astype(BF16))
+
+
+def factor_of(squares_ref, index):
+    return jnp.minimum(1.0, CLIP_LIMIT / jnp.sqrt(squares_ref[0:1, index : index + 1]))
+
+
+def updated(fixes_ref, gradient, factor, old, new, learn_rate, at=...):
+    master_ref, mean_ref, square_ref = old
+    gradient_ref, mean_new_ref, square_new_ref, master_new_ref, copy_ref = new
+    clipped = gradient * factor
+    master = master_ref[at]
+    mean_new = BETA_ONE * mean_ref[at] + (1.0 - BETA_ONE) * clipped
+    square_new = BETA_TWO * square_ref[at] + (1.0 - BETA_TWO) * clipped * clipped
+    master_new = master - learn_rate * (
+        mean_new / fixes_ref[0] / (jnp.sqrt(square_new / fixes_ref[1]) + ADAM_EPS) + DECAY_RATE * master
+    )
+    gradient_ref[at] = gradient
+    mean_new_ref[at] = mean_new
+    square_new_ref[at] = square_new
+    master_new_ref[at] = master_new
+    copy_ref[at] = master_new.astype(BF16)
+
+
+def update_kernel(
+    fixes_ref, squares_ref, in_sum_ref, out_sum_ref, attn_sum_ref, *refs,
+):
+    in_old, out_old, attn_old = refs[0:3], refs[3:6], refs[6:9]
+    in_new, out_new, attn_new = refs[9:14], refs[14:19], refs[19:24]
+    small_ref, turned, wide = refs[24:]
+    turned[pl.ds(0, D, 2), :] = in_sum_ref[0, :, :LANES].astype(F32)
+    turned[pl.ds(1, D, 2), :] = in_sum_ref[0, :, LANES:].astype(F32)
+    updated(
+        fixes_ref, turned[...], factor_of(squares_ref, 3), in_old, in_new, RATE_FACTOR / D**0.5
+    )
+    pieces = [
+        out_sum_ref[0, piece * LANES : (piece + 1) * LANES, :].astype(F32)
+        for piece in range(D // UNIT)
+    ]
+    updated(
+        fixes_ref,
+        jnp.concatenate(pieces, axis=1),
+        factor_of(squares_ref, 4),
+        out_old,
+        out_new,
+        RATE_FACTOR / FFN**0.5,
+        0,
+    )
+
+    @pl.when(pl.program_id(0) == 0)
+    def _():
+        back = [jnp.zeros((48, UNIT), F32) for _ in range(3)]
+        small = jnp.zeros((48, UNIT), F32)
+        for block in range(CTX):
+            rows = [
+                attn_sum_ref[block, piece * 48 : (piece + 1) * 48, :].astype(F32) for piece in range(6)
+            ]
+            back = [left + right for left, right in zip(back, rows[:3])]
+            small = small + rows[5]
+            heads = jnp.concatenate(rows[3:], axis=1)
+            for part in range(3):
+                at = part * D + block * COLS
+                wide[:, at : at + COLS] = heads[:, part * COLS : (part + 1) * COLS]
+        wide[:, 3 * D :] = jnp.concatenate(back, axis=1)
+        small_ref[...] = small[:, LANES:]
+        for part in range(4):
+            lanes = (slice(None), slice(part * D, (part + 1) * D))
+            updated(
+                fixes_ref,
+                wide[lanes],
+                factor_of(squares_ref, 1),
+                attn_old,
+                attn_new,
+                RATE_FACTOR / D**0.5,
+                lanes,
+            )
+
+
+def update(fixes, squares, sums_all, in_old, out_old, attn_old):
+    in_rows, units = 2 * D, LANES
+    in_shape, out_shape, attn_shape = (CTX * in_rows, units), (CTX, units, D), (48, 4 * D)
+    in_spec = pl.BlockSpec((in_rows, units), lambda i: (i, 0))
+    out_spec = pl.BlockSpec((1, units, D), lambda i: (i, 0, 0))
+    attn_spec = whole(attn_shape)
+
+    def five(shape):
+        return [jax.ShapeDtypeStruct(shape, F32)] * 4 + [jax.ShapeDtypeStruct(shape, BF16)]
+
+    return pl.pallas_call(
+        update_kernel,
+        grid=(CTX,),
+        out_shape=five(in_shape)
+        + five(out_shape)
+        + five(attn_shape)
+        + [jax.ShapeDtypeStruct((48, LANES), F32)],
+        in_specs=[
+            SMEM,
+            whole((8, LANES)),
+            pl.BlockSpec((1, D, UNIT), lambda i: (i, 0, 0)),
+            pl.BlockSpec((1, D // 2, UNIT), lambda i: (i, 2, 0)),
+            pl.BlockSpec((CTX, ATTN_ROWS, UNIT), lambda i: (0, EXPERT_ROWS // ATTN_ROWS, 0)),
+        ]
+        + [in_spec] * 3
+        + [out_spec] * 3
+        + [attn_spec] * 3,
+        out_specs=[in_spec] * 5 + [out_spec] * 5 + [attn_spec] * 5 + [whole((48, LANES))],
+        scratch_shapes=[pltpu.VMEM((in_rows, units), F32), pltpu.VMEM(attn_shape, F32)],
+        compiler_params=pltpu.CompilerParams(vmem_limit_bytes=VMEM_LIMIT),
+        name="update",
+    )(
+        fixes, squares, sums_all, sums_all, sums_all,
+        *(array.reshape(in_shape) for array in in_old),
+        *(array.reshape(out_shape) for array in out_old),
+        *(array.reshape(attn_shape) for array in attn_old),
+    )
 
 
 def on_device(
@@ -1276,7 +1482,9 @@
         axis=1,
     ).astype(BF16)
     attn_shard = attn_shard.reshape(shard_rows, 6, UNIT).transpose(1, 0, 2).reshape(-1, UNIT)
-    packs = gather_shards(attn_shard).reshape(2, fsdp, ATTN_ROWS, UNIT)
+    left_out = (3 - routes[0, :, :, 0] - routes[0, :, :, 1]).astype(F32)
+    packs, codes = gather_shards(attn_shard, jnp.pad(left_out, ((0, 8 - left_out.shape[0]), (0, 0))))
+    packs = packs.reshape(2, fsdp, ATTN_ROWS, UNIT)
     in_shard = (
         lax.dynamic_index_in_dim(expert_in[0], ctx_index, 0, keepdims=False)
         .astype(BF16)
@@ -1285,32 +1493,28 @@
     out_shard = lax.dynamic_index_in_dim(expert_out[0], ctx_index, 0, keepdims=False).astype(BF16)
     halves = jnp.concatenate(
         [in_shard] + [out_shard[:, at : at + 2 * units] for at in range(0, D, 2 * units)], axis=0
-    ).reshape(2, HALF_ROWS, 2 * units)
+    ).reshape(2, SPLIT, 2 * units)
     other = swap(jnp.where(first_core, halves[1], halves[0]))
     pieces = (jnp.where(first_core, halves[0], other), jnp.where(first_core, other, halves[1]))
     experts = [
-        lax.all_gather(piece, everyone).reshape(2, fsdp, HALF_ROWS, 2 * units) for piece in pieces
+        lax.all_gather(piece, everyone).reshape(2, fsdp, SPLIT, 2 * units) for piece in pieces
     ]
-    routes_all = lax.all_gather(routes[0], ("section", "ctx")).reshape((2, CTX) + routes.shape[1:])
-    routes_all = lax.dynamic_index_in_dim(routes_all, section, 2, keepdims=False).reshape(2, SEQ, 2)
     length = lax.dynamic_slice_in_dim(lengths, section, 1, 0)
     tokens = lax.dynamic_index_in_dim(inputs, section, 0, keepdims=False)
     positions = ctx_index * ROWS + jnp.arange(ROWS, dtype=jnp.int32)
     seed = lax.dynamic_index_in_dim(cotangent, section, 0, keepdims=False)
     seed = jnp.where((positions < length[0])[:, None], seed, jnp.zeros_like(seed))
-    seed_all = lax.all_gather(seed, "ctx", tiled=True)
     table = rotary_table()
 
     layers = [(packs[layer], experts[layer]) for layer in range(2)]
-    lower_out, lower_saved = layer_forward(layers[0], tokens, length, routes_all[0], table)
-    upper_out, upper_saved = layer_forward(layers[1], lower_out, length, routes_all[1], table)
+    lower_out, lower_saved = layer_forward(layers[0], tokens, length, codes[0], table)
+    upper_out, upper_saved = layer_forward(layers[1], lower_out, length, codes[1], table)
 
     upper_experts, (upper_grad, upper_attn, lower_seed) = layer_backward(
-        layers[1], upper_saved, seed_all, seed, length, table, ctx_index, False
-    )
-    own_seed = upper_grad.astype(BF16)
-    lower_experts, (lower_grad, lower_attn) = layer_backward(
-        layers[0], lower_saved, lower_seed, own_seed, length, table, ctx_index, True
+        layers[1], upper_saved, seed, length, table
+    )
+    lower_experts, (lower_grad, lower_attn, _) = layer_backward(
+        layers[0], lower_saved, lower_seed, length, table
     )
 
     def paired(first, second):
@@ -1324,39 +1528,42 @@
     input_grads = paired(lower_grad, upper_grad)[None]
     shard_sum = sum_shards(lower_experts, lower_attn, upper_experts, upper_attn)
     sums_all, squares = spread_sums(shard_sum)
-    in_sum = sums_all[:, :D].astype(F32).reshape(1, CTX, D, 2, units)
-    out_sum = jnp.concatenate(
-        [sums_all[:, at : at + units] for at in range(D, EXPERT_ROWS, units)], axis=2
-    ).astype(F32)[None]
-    attn_all = sums_all[:, EXPERT_ROWS:].astype(F32).reshape(CTX, 6, shard_rows, UNIT)
-    back_sum = jnp.sum(attn_all[:, :3], axis=0).transpose(1, 0, 2).reshape(shard_rows, D)
-    heads_sum = attn_all[:, 3:].transpose(0, 2, 1, 3).reshape(CTX, shard_rows, D)
-    small_sum = jnp.sum(heads_sum[:, :, D - LANES :], axis=0)
-    heads_sum = heads_sum[:, :, : 3 * COLS].reshape(CTX, shard_rows, 3, COLS)
-    heads_sum = heads_sum.transpose(1, 2, 0, 3).reshape(shard_rows, 3 * D)
-    attn_sum = jnp.concatenate([heads_sum, back_sum], axis=1)[None]
+    step_value = step_count[0].astype(F32)
+    fixes = jnp.stack([1.0 - BETA_ONE**step_value, 1.0 - BETA_TWO**step_value])
+    changed = update(
+        fixes,
+        squares,
+        sums_all,
+        (expert_in, in_mean, in_square),
+        (expert_out, out_mean, out_square),
+        (attn_weight, attn_mean, attn_square),
+    )
+    small_sum = changed[15]
+    norms = jnp.sqrt(squares[0, :5])
+    factors = jnp.minimum(1.0, CLIP_LIMIT / norms)
     router_sum = small_sum[:, :EXPERTS][None]
     gain_sum = small_sum[:, EXPERTS : EXPERTS + 2].T[None]
-    sums = (gain_sum, attn_sum, router_sum, in_sum, out_sum)
-    norms = jnp.sqrt(squares[0, : len(sums)])
-    factors = jnp.minimum(1.0, CLIP_LIMIT / norms)
-    step_value = step_count[0].astype(F32)
-    wide_rate = RATE_FACTOR / D**0.5
-    router_rate = RATE_FACTOR / (D // 4) ** 0.5
-    down_rate = RATE_FACTOR / FFN**0.5
-    olds = (
-        (norm_gains, gains_mean, gains_square, GAIN_RATE),
-        (attn_weight, attn_mean, attn_square, wide_rate),
-        (router_weight, router_mean, router_square, router_rate),
-        (expert_in, in_mean, in_square, wide_rate),
-        (expert_out, out_mean, out_square, down_rate),
-    )
-    results = [layer_outputs, input_grads]
-    for index, (total, (master, mean_old, square_old, rate)) in enumerate(zip(sums, olds)):
-        results.extend(
-            adam_update(total, total * factors[index], master, mean_old, square_old, step_value, rate)
-        )
-    return tuple(results) + (norms[None],)
+    gains_new = adam_update(
+        gain_sum, gain_sum * factors[0], norm_gains, gains_mean, gains_square, step_value, GAIN_RATE
+    )
+    router_new = adam_update(
+        router_sum,
+        router_sum * factors[2],
+        router_weight,
+        router_mean,
+        router_square,
+        step_value,
+        RATE_FACTOR / (D // 4) ** 0.5,
+    )
+    return (
+        (layer_outputs, input_grads)
+        + gains_new
+        + tuple(array.reshape(attn_weight.shape) for array in changed[10:15])
+        + router_new
+        + tuple(array.reshape(expert_in.shape) for array in changed[:5])
+        + tuple(array.reshape(expert_out.shape) for array in changed[5:10])
+        + (norms[None],)
+    )
 
 
 def solution(mesh):

time: 631 us -> 539 us (0.85)
  other arithmetic: 46 us -> 16.5 us
  blocking collectives: 22.8 us -> 0 us
  Pallas kernels: 499 us -> 478 us
  local copies, waits for them, and re-layouts: 38.1 us -> 19.5 us
    pallas_call x2, Pallas kernels: 106 us -> 76.1 us  [attn_forward(): pl.pallas_call(attn_forward_kernel, out_shape=(jax.ShapeDtypeStruct((SEQ,...]
    convert_element_type x5 -> x2, other arithmetic: 23.4 us -> 0.6 us  [adam_update(): return (gradient, mean_new, square_new, master_new, master_new.astype(BF16))]
    all_gather x1 -> x0, blocking collectives: 22.8 us -> none  [on_device(): lax.all_gather(routes[0], ('section', 'ctx'))]
    pallas_call x7 -> x8, Pallas kernels: 279 us -> 290 us  [the longest x2 83.1 us: ffn_backward(): pl.pallas_call(ffn_backward_kernel, out_shape=(jax.ShapeDtypeStruct((ROWS...]
    reshape x5 -> x0, local copies, waits for them, and re-layouts: 7.11 us -> none  [the longest x1 3.02 us: on_device(): in_sum = sums_all[:, :D].astype(F32).reshape(1, CTX, D, 2, units)]
  transfers between devices with their start and end apart: 6 -> 5, of which waited for: 1 -> 2; matrix products, arithmetic and copies ran while one was open for 8% -> 4% of each run, Pallas kernels for 35% -> 28%
where the time goes in v3:
time: 539 us; the launch traced here: 533 us
  Pallas kernels  478 us (89%)
  local copies, waits for them, and re-layouts  19.5 us (4%)
  other arithmetic  16.5 us (3%)
  between operations  15.4 us (3%)
    pallas_call x2, Pallas kernels, ffn_backward(): pl.pallas_call(ffn_backward_kernel, out_shape=(jax.ShapeDtypeStruct((ROWS...  83.1 us
    pallas_call x2, Pallas kernels, attn_backward(): pl.pallas_call(attn_backward_kernel, out_shape=tuple(out_shape), in_specs...  82 us
    pallas_call x2, Pallas kernels, attn_forward(): pl.pallas_call(attn_forward_kernel, out_shape=(jax.ShapeDtypeStruct((SEQ,...  76.1 us
    pallas_call x1, Pallas kernels, sum_shards(): pl.pallas_call(sum_shards_kernel, out_shape=jax.ShapeDtypeStruct((SHARD_R...  72.3 us
    pallas_call x2, Pallas kernels, ffn_forward(): pl.pallas_call(ffn_forward_kernel, out_shape=(jax.ShapeDtypeStruct((ROWS,...  72.2 us
    pallas_call x1, Pallas kernels, spread_sums(): pl.pallas_call(spread_sums_kernel, out_shape=(jax.ShapeDtypeStruct((CTX,...  39.1 us
    pallas_call x1, Pallas kernels, gather_shards(): pl.pallas_call(gather_shards_kernel, out_shape=(jax.ShapeDtypeStruct((2,...  35.5 us
    pallas_call x1, Pallas kernels, update(): pl.pallas_call(update_kernel, grid=(CTX,), out_shape=five(in_shape) + fiv...  17.6 us
  transfers between devices with their start and end apart: 5, of which 2 were waited for; matrix products, arithmetic and copies ran while one was open for 4% of the time, Pallas kernels for 28%

profile of v3, /device:TPU:0, one launch (start us, length us, event | category | flops | bytes accessed | tf_op | source)
XLA Modules:
  0.0 532.7 jit_solution(13614834103425045047)
XLA Ops:
  7.3 1.1 fusion
  8.4 1.4 dynamic-slice_convert_fusion
  9.8 0.2 slice.83
  10.2 0.1 bitcast_select_fusion.2
  10.2 0.1 collective-permute-start
  10.3 1.6 collective-permute-done
  11.9 0.9 broadcast_select_fusion.4
  12.9 0.7 all-gather.7.cloned.1.call-update
  13.6 0.9 slice.100
  14.5 0.1 copy.92
  14.6 0.1 copy.93
  14.8 1.0 fusion.5
  15.8 0.1 concatenate.10
  16.0 0.2 convert_element_type.49
  16.1 0.7 copy.94
  17.6 0.1 copy.102
  17.7 0.1 copy.103
  17.8 0.6 pad.4.code_ref
  18.4 35.5 %gather_shards.1 = (bf16[2,4,4,288,256]{4,3,2,1,0:T(8,128)(2,1)}, f32[2,4,8,256]{3,2,1,0:T(8,128)}) custom-call(bf16[288,256]{1,0:T(8,128)(2,1)} %bitcast.133, f32[8,256]{1,0:T(8,128)} %pad.4.code_ref), custom_call_target="tpu_custom_call" | custom-call | tf_op jit(solution)/shard_map/gather_shards/pallas_call | solution.py:420
  53.9 0.6 dynamic_slice.33.length_ref
  54.5 0.8 dynamic-slice_bitcast_fusion.u_ref
  55.3 1.9 multiply_cosine_fusion
  57.2 1.3 pad_maximum_fusion.table_ref
  58.4 5.1 fusion.11
  63.5 39.6 %attn_forward.2 = (bf16[1024,768]{1,0:T(8,128)(2,1)}, bf16[1024,1152]{1,0:T(8,128)(2,1)}, f32[3,1024,1]{2,1,0:T(8,128)}, bf16[4,256,192]{2,1,0:T(8,128)(2,1)}, f...) custom-call(s32[1]{0:T(128)} %dynamic_slice.33.length_ref, ...), custom_call_target="tpu_custom_call" | custom-call | tf_op jit(solution)/shard_map/attn_forward/pallas_call | solution.py:774
  103.2 0.7 add_compare_fusion
  103.8 0.6 pad_maximum_fusion.4.fixes_ref
  104.4 0.6 slice_bitcast_fusion
  105.0 0.9 bitcast_select_fusion.delta_own_ref.delta_ref
  105.9 37.2 %ffn_forward.2 = (bf16[256,768]{1,0:T(8,128)(2,1)}, bf16[4,256,768]{2,1,0:T(8,128)(2,1)}, f32[256,128]{1,0:T(8,128)}, f32[4,256,1]{2,1,0:T(8,128)}, bf16[4,16,256,256]{3,2,1,0:T(8,128)(2,1)}) custom-call(bf16[256,768]{1,0:T(8,128)(2,1)} %get-tuple-element.90.b_own_ref.second_ref, f32[256,768]{1,0:T(8,128)} %get-tuple-element.91.residual_ref, ...), custom_call_target="tpu_custom_call" | custom-call | tf_op jit(solution)/shard_map/ffn_forward/pallas_call | solution.py:1102
  143.1 36.5 %attn_forward.3 = (bf16[1024,768]{1,0:T(8,128)(2,1)}, bf16[1024,1152]{1,0:T(8,128)(2,1)}, f32[3,1024,1]{2,1,0:T(8,128)}, bf16[4,256,192]{2,1,0:T(8,128)(2,1)}, f...) custom-call(s32[1]{0:T(128)} %dynamic_slice.33.length_ref, ...), custom_call_target="tpu_custom_call" | custom-call | tf_op jit(solution)/shard_map/attn_forward/pallas_call | solution.py:774
  179.6 35.0 %ffn_forward.3 = (bf16[256,768]{1,0:T(8,128)(2,1)}, bf16[4,256,768]{2,1,0:T(8,128)(2,1)}, f32[256,128]{1,0:T(8,128)}, f32[4,256,1]{2,1,0:T(8,128)}, bf16[4,16,256,256]{3,2,1,0:T(8,128)(2,1)}) custom-call(bf16[256,768]{1,0:T(8,128)(2,1)} %get-tuple-element.95.b_own_ref.second_ref, f32[256,768]{1,0:T(8,128)} %get-tuple-element.96.residual_ref, ...), custom_call_target="tpu_custom_call" | custom-call | tf_op jit(solution)/shard_map/ffn_forward/pallas_call | solution.py:1102
  214.6 41.6 %ffn_backward.2 = (f32[256,768]{1,0:T(8,128)}, f32[256,128]{1,0:T(8,128)}, bf16[16,1152,256]{2,1,0:T(8,128)(2,1)}) custom-call(bf16[4,256,768]{2,1,0:T(8,128)(2,1)} %get-tuple-element.115.b_ref, f32[4,256,1]{2,1,0:T(8,128)} %get-tuple-element.116.gate_ref, bf16[256,768]{1,0:T(8,128)(2,1)} %bitcast_select_fusion.delta_own_ref.delta_ref, ...), custom_call_target="tpu_custom_call" | custom-call | tf_op jit(solution)/shard_map/ffn_backward/pallas_call | solution.py:1260
  256.2 41.9 %attn_backward.2 = (f32[256,768]{1,0:T(8,128)}, bf16[16,288,256]{2,1,0:T(8,128)(2,1)}, bf16[256,768]{1,0:T(8,128)(2,1)}) custom-call(s32[1]{0:T(128)} %dynamic_slice.33.length_ref, bf16[256,768]{1,0:T(8,128)(2,1)} %get-tuple-element.94.u_ref, f32[8,768]{1,0:T(8,128)} %get-tuple-element.107.gains_ref, bf16[768,128]{1,0:T(8,128)(2,1)} %get-tuple-element.97.router_ref, ...), custom_call_target="tpu_custom_call" | custom-call | tf_op jit(solution)/shard_map/attn_backward/pallas_call | solution.py:964
  298.1 41.5 %ffn_backward.3 = (f32[256,768]{1,0:T(8,128)}, f32[256,128]{1,0:T(8,128)}, bf16[16,1152,256]{2,1,0:T(8,128)(2,1)}) custom-call(bf16[4,256,768]{2,1,0:T(8,128)(2,1)} %get-tuple-element.121.b_ref, f32[4,256,1]{2,1,0:T(8,128)} %get-tuple-element.122.gate_ref, bf16[256,768]{1,0:T(8,128)(2,1)} %get-tuple-element.120.delta_own_ref.delta_ref, ...), custom_call_target="tpu_custom_call" | custom-call | tf_op jit(solution)/shard_map/ffn_backward/pallas_call | solution.py:1260
  339.6 40.1 %attn_backward.3 = (f32[256,768]{1,0:T(8,128)}, bf16[16,288,256]{2,1,0:T(8,128)(2,1)}, bf16[256,768]{1,0:T(8,128)(2,1)}) custom-call(s32[1]{0:T(128)} %dynamic_slice.33.length_ref, bf16[256,768]{1,0:T(8,128)(2,1)} %dynamic-slice_bitcast_fusion.u_ref, f32[8,768]{1,0:T(8,128)} %get-tuple-element.99.gains_ref, bf16[768,128]{1,0:T(8,128)(2,1)} %get-tuple-element.93.router_ref, ...), custom_call_target="tpu_custom_call" | custom-call | tf_op jit(solution)/shard_map/attn_backward/pallas_call | solution.py:964
  379.7 72.3 %sum_shards.1.shard_ref = bf16[1440,256]{1,0:T(8,128)(2,1)} custom-call(bf16[4,4,1152,256]{3,2,1,0:T(8,128)(2,1)} %bitcast.114, bf16[4,4,288,256]{3,2,1,0:T(8,128)(2,1)} %bitcast.124, bf16[4,4,1152,256]{3,2,1,0:T(8,128)(2,1)} %bitcast.113, bf16[4,4,288,256]{3,2,1,0:T(8,128)(2,1)} %bitcast.123), custom_call_target="tpu_custom_call" | custom-call | tf_op jit(solution)/shard_map/sum_shards/pallas_call | solution.py:551
  452.0 39.1 %spread_sums.1 = (bf16[4,1440,256]{2,1,0:T(8,128)(2,1)}, f32[8,128]{1,0:T(8,128)}) custom-call(bf16[1440,256]{1,0:T(8,128)(2,1)} %sum_shards.1.shard_ref), custom_call_target="tpu_custom_call" | custom-call | tf_op jit(solution)/shard_map/spread_sums/pallas_call | solution.py:638
  491.1 1.2 slice_sqrt_fusion
  492.3 0.6 fusion.14
  492.9 17.6 %update.1 = (f32[6144,128]{1,0:T(8,128)}, f32[6144,128]{1,0:T(8,128)}, f32[6144,128]{1,0:T(8,128)}, f32[6144,128]{1,0:T(8,128)}, bf16[6144,128]{1,0:T(8,128)(2,1...) custom-call(f32[2]{0:T(128)} %pad_maximum_fusion.4.fixes_ref, ...), custom_call_target="tpu_custom_call" | custom-call | tf_op jit(solution)/shard_map/update/pallas_call | solution.py:1426
  510.5 0.8 slice_bitcast_fusion.3
  511.3 1.4 multiply_divide_fusion
  512.7 0.1 copy.104
  512.8 0.1 copy.106
  512.9 0.6 copy.110
  513.5 0.6 copy.111
  514.2 0.6 copy.108
  514.8 0.6 copy.109
  515.5 1.5 multiply_multiply_fusion.2
  516.9 0.1 copy.100
  517.0 0.1 copy.101
  517.1 0.7 copy.107
  517.7 0.1 broadcast_select_fusion
  517.8 0.1 collective-permute-start.2
  517.9 0.8 broadcast_select_fusion.2
  518.7 0.5 collective-permute-start.1
  519.3 0.6 copy.98
  519.9 0.6 fusion.10
  520.5 0.6 collective-permute-done.1
  521.1 1.1 select_bitcast_fusion.3
  522.2 0.9 maximum_bitcast_fusion.1
  523.1 1.4 select_bitcast_fusion.1
  524.5 1.2 maximum_bitcast_fusion
  (55 shorter events, 0.4 us)
Async XLA Ops:
  7.2 47.3 %copy-start = (bf16[2,256,768]{2,1,0:T(8,128)(2,1)S(1)}, bf16[2,256,768]{2,1,0:T(8,128)(2,1)}, u32[]{:S(2)}) copy-start(bf16[2,256,768]{2,1,0:T(8,128)(2,1)} %param.20) | copy-start | bytes 2359300
  7.2 98.7 %all-gather.5.cloned.1.call-start = ((), (), s32[]{:S(2)}) async-start(), calls=%async_computation | async-start | bytes 9732096 | tf_op jit(solution)/shard_map/all_gather | solution.py:1500
  10.0 4.5 copy-start.9
  10.0 4.6 copy-start.13
  10.1 7.5 %copy-start.11 = (f32[1,48,3]{1,0,2:T(1,128)S(1)}, f32[1,48,3]{1,0,2:T(1,128)}, u32[]{:S(2)}) copy-start(f32[1,48,3]{1,0,2:T(1,128)} %param.32) | copy-start | bytes 1732
  10.1 7.6 %copy-start.12 = (f32[1,48,3]{1,0,2:T(1,128)S(1)}, f32[1,48,3]{1,0,2:T(1,128)}, u32[]{:S(2)}) copy-start(f32[1,48,3]{1,0,2:T(1,128)} %param.33) | copy-start | bytes 1732
  10.1 7.7 %copy-start.10 = (s32[1,2,256,2]{2,3,1,0:T(2,128)S(1)}, s32[1,2,256,2]{2,3,1,0:T(2,128)}, u32[]{:S(2)}) copy-start(s32[1,2,256,2]{2,3,1,0:T(2,128)} %param.23) | copy-start | bytes 12292
  10.1 43.7 %copy-start.16 = (s32[2]{0:T(128)S(1)}, s32[2]{0:T(128)}, u32[]{:S(2)}) copy-start(s32[2]{0:T(128)} %param.22) | copy-start | bytes 28
  10.2 1.7 collective-permute-start
  12.9 166.7 %all-gather.7.cloned.1.call-start = ((), (), s32[]{:S(2)}) async-start(), calls=%async_computation.1 | async-start | bytes 9732096 | tf_op jit(solution)/shard_map/all_gather | solution.py:1500
  63.5 40.9 %copy-start.8 = (f32[2,4,8,256]{3,2,1,0:T(8,128)S(1)}, f32[2,4,8,256]{3,2,1,0:T(8,128)}, u32[]{:S(2)}) copy-start(f32[2,4,8,256]{3,2,1,0:T(8,128)} %get-tuple-element.92) | copy-start | bytes 196612
  63.5 41.5 %copy-start.7 = (bf16[2,256,768]{2,1,0:T(8,128)(2,1)S(1)}, bf16[2,256,768]{2,1,0:T(8,128)(2,1)}, u32[]{:S(2)}) copy-start(bf16[2,256,768]{2,1,0:T(8,128)(2,1)} %param.21) | copy-start | bytes 2359300
  492.9 24.9 %copy-start.3 = (f32[256,768]{1,0:T(8,128)S(1)}, f32[256,768]{1,0:T(8,128)}, u32[]{:S(2)}) copy-start(f32[256,768]{1,0:T(8,128)} %get-tuple-element.127) | copy-start | bytes 2359300
  492.9 24.9 %copy-start.4 = (f32[256,768]{1,0:T(8,128)S(1)}, f32[256,768]{1,0:T(8,128)}, u32[]{:S(2)}) copy-start(f32[256,768]{1,0:T(8,128)} %get-tuple-element.126) | copy-start | bytes 2359300
  510.4 7.5 %copy-start.2 = (bf16[256,768]{1,0:T(8,128)(2,1)S(1)}, bf16[256,768]{1,0:T(8,128)(2,1)}, u32[]{:S(2)}) copy-start(bf16[256,768]{1,0:T(8,128)(2,1)} %get-tuple-element.94.u_ref) | copy-start | bytes 1179652
  510.4 7.5 %copy-start.5 = (bf16[256,768]{1,0:T(8,128)(2,1)S(1)}, bf16[256,768]{1,0:T(8,128)(2,1)}, u32[]{:S(2)}) copy-start(bf16[256,768]{1,0:T(8,128)(2,1)} %get-tuple-element.98) | copy-start | bytes 1179652
  510.4 8.8 %copy-start.6 = (f32[48,128]{1,0:T(8,128)S(1)}, f32[48,128]{1,0:T(8,128)}, u32[]{:S(2)}) copy-start(f32[48,128]{1,0:T(8,128)} %get-tuple-element.134) | copy-start | bytes 73732
  510.5 9.5 %copy-start.14 = (f32[1,2,48]{2,1,0:T(2,128)S(1)}, f32[1,2,48]{2,1,0:T(2,128)}, u32[]{:S(2)}) copy-start(f32[1,2,48]{2,1,0:T(2,128)} %param.27) | copy-start | bytes 1156
  510.5 9.5 %copy-start.15 = (f32[1,2,48]{2,1,0:T(2,128)S(1)}, f32[1,2,48]{2,1,0:T(2,128)}, u32[]{:S(2)}) copy-start(f32[1,2,48]{2,1,0:T(2,128)} %param.26) | copy-start | bytes 1156
  517.8 5.3 collective-permute-start.2
  518.7 2.4 collective-permute-start.1
  523.1 2.6 copy-start.1
Sparse Core Ops, SparseCore 0:
  13.0 60.4 all-gather.4
  76.2 54.9 all-gather.6

commit v4 on v3

--- a/solution.py
+++ b/solution.py
@@ -2,6 +2,7 @@
 
 import jax
 import jax.numpy as jnp
+import numpy as np
 from jax import lax
 from jax.experimental import pallas as pl
 from jax.experimental.pallas import tpu as pltpu
@@ -71,6 +72,7 @@
 
 VMEM = pl.BlockSpec(memory_space=pltpu.VMEM)
 SMEM = pl.BlockSpec(memory_space=pltpu.SMEM)
+ANY = pl.BlockSpec(memory_space=pl.ANY)
 
 
 def ring():
@@ -431,140 +433,235 @@
     )(shard, codes)
 
 
+HALF_SHARD = SHARD_ROWS // 2
+Y_ROWS, Z_ROWS = 352, 368
+Z_CUT = Z_ROWS - ATTN_ROWS
+
+
+def half_sources(half, experts, attn):
+    if half == 0:
+        return (
+            experts.at[:, :, pl.ds(0, Y_ROWS), :],
+            experts.at[:, :, pl.ds(Y_ROWS, Z_CUT), :],
+            experts.at[:, :, pl.ds(Y_ROWS + Z_CUT, ATTN_ROWS), :],
+        )
+    return (
+        experts.at[:, :, pl.ds(HALF_SHARD, Y_ROWS), :],
+        experts.at[:, :, pl.ds(HALF_SHARD + Y_ROWS, Z_CUT), :],
+        attn,
+    )
+
+
+class HalfSums:
+    def __init__(self, refs, sems, make_y, make_z):
+        (
+            self.part_y, self.part_z, top_y, bottom_y, left_y, right_y, top_z, bottom_z, left_z, right_z,
+            more_z, more_y, top_zz, bottom_zz, left_zz, right_zz, top_yy, bottom_yy, left_yy, right_yy,
+        ) = refs
+        ring_y, ring_z = Ring("y"), Ring("z")
+        self.ring_y, self.ring_z = ring_y, ring_z
+        self.first_y = RingSum(
+            ring_y, self.part_y, (top_y, bottom_y), left_y, right_y, sems[0], sems[1], 2, make_y
+        )
+        self.first_z = RingSum(
+            ring_z, self.part_z, (top_z, bottom_z), left_z, right_z, sems[2], sems[3], 2, make_z
+        )
+
+        def make_zz(index, block):
+            more_z[block] = self.first_y.total(block).astype(BF16)
+
+        def make_yy(index, block):
+            more_y[block] = self.first_z.total(block).astype(BF16)
+
+        self.then_z = RingSum(
+            ring_z, more_z, (top_zz, bottom_zz), left_zz, right_zz, sems[4], sems[5], Y_ROWS // 2, make_zz
+        )
+        self.then_y = RingSum(
+            ring_y, more_y, (top_yy, bottom_yy), left_yy, right_yy, sems[6], sems[7], 176, make_yy
+        )
+
+    def first(self, number):
+        self.first_y.stage(number)
+        self.first_z.stage(number)
+
+    def then(self, number):
+        self.then_z.stage(number)
+        self.then_y.stage(number)
+
+    def result(self, out_ref):
+        out_ref[pl.ds(0, Y_ROWS), :] = self.then_z.total().astype(BF16)
+        out_ref[pl.ds(Y_ROWS, Z_ROWS), :] = self.then_y.total().astype(BF16)
+
+
+def half_scratch():
+    shapes = [(CTX, CTX, Y_ROWS, UNIT), (CTX, CTX, Z_ROWS, UNIT)]
+    for rows in (Y_ROWS, Z_ROWS):
+        shapes += [(2, rows, UNIT)] * 2 + [(CTX, rows, UNIT)] * 2
+    shapes += [(CTX, Y_ROWS, UNIT), (CTX, Z_ROWS, UNIT)]
+    for rows in (Y_ROWS, Z_ROWS):
+        shapes += [(176, UNIT), (rows - 176, UNIT)] + [(rows, UNIT)] * 2
+    return [pltpu.VMEM(shape, BF16) for shape in shapes]
+
+
+HALF_REFS = 20
+
+
+def add_block(part, incoming, block):
+    for other in range(CTX):
+        part[block, other] = (part[block, other].astype(F32) + incoming[block, other].astype(F32)).astype(
+            BF16
+        )
+
+
 def sum_shards_kernel(
-    lower_e, lower_a, upper_e, upper_a, out_ref,
-    part_y, in_y, part_z, in_z, top_y, bottom_y, left_y, right_y, top_z, bottom_z, left_z, right_z,
-    more_z, more_y, top_zz, bottom_zz, left_zz, right_zz, top_yy, bottom_yy, left_yy, right_yy, *sems,
+    experts, attn, upper_half_ref, lower_out_ref, upper_out_ref, lower_grad_ref, upper_grad_ref,
+    out_ref, outputs_ref, grads_ref, *rest,
 ):
+    halves, rest = rest[:HALF_REFS], rest[HALF_REFS:]
+    in_y, in_z, sent_out, sent_grad, local, send_s, recv_s, send_w, recv_w = rest[:9]
     section = lax.axis_index("section")
     sibling = {"section": 1 - section}
-    ring_y, ring_z = Ring("y"), Ring("z")
+    first_core = section == 0
+    part_y, part_z = halves[:2]
+
+    def make_y(index, block):
+        ready(index, 0)
+        add_block(part_y, in_y, block)
+
+    def make_z(index, block):
+        ready(index, 1)
+        ready(index, 2)
+        add_block(part_z, in_z, block)
+
+    sums = HalfSums(halves, rest[9:], make_y, make_z)
+    ring_y, ring_z = sums.ring_y, sums.ring_z
     greet_ids([sibling] + ring_y.near() + ring_z.near())
-    local, send_s, recv_s = sems[:3]
-
-    def pieces(index, experts, attn, target_y, target_z):
+
+    def pieces(index, half, target_y, target_z):
         b_y, b_z = ring_y.order()[index], ring_z.order()[index]
+        sources = half_sources(half, experts, attn)
         return (
-            (experts.at[:, b_y, pl.ds(0, FIRST), :], target_y.at[b_y]),
-            (experts.at[b_z, :, pl.ds(FIRST, KEPT), :], target_z.at[b_z, :, pl.ds(0, KEPT), :]),
-            (attn.at[b_z], target_z.at[b_z, :, pl.ds(KEPT, ATTN_ROWS), :]),
+            (sources[0].at[:, b_y], target_y.at[b_y]),
+            (sources[1].at[b_z], target_z.at[b_z, :, pl.ds(0, Z_CUT), :]),
+            (sources[2].at[b_z], target_z.at[b_z, :, pl.ds(Z_CUT, ATTN_ROWS), :]),
         )
 
     def fetch(index, number, source, target):
         return pltpu.make_async_copy(source, target, local.at[index * 3 + number])
 
-    def pass_on(index, number, source, target):
-        at = index * 3 + number
+    def pass_on(source, target, send, recv):
         return pltpu.make_async_remote_copy(
             src_ref=source,
             dst_ref=target,
-            send_sem=send_s.at[at],
-            recv_sem=recv_s.at[at],
+            send_sem=send,
+            recv_sem=recv,
             device_id=sibling,
             device_id_type=MESH,
         )
 
-    def begin(own_e, own_a, other_e, other_a):
+    def lend(index, number, source, target):
+        at = index * 3 + number
+        return pass_on(source, target, send_s.at[at], recv_s.at[at])
+
+    def ready(index, number):
+        source, target = pieces(index, 0, part_y, part_z)[number]
+        fetch(index, number, source, target).wait()
+        source, target = pieces(index, 0, in_y, in_z)[number]
+        lend(index, number, source, target).wait_recv()
+
+    def start(kept):
         for index in range(CTX):
-            for number, (source, target) in enumerate(pieces(index, own_e, own_a, part_y, part_z)):
-                fetch(index, number, source, target).start()
-
-    def lend(other_e, other_a):
+            for number, pair in enumerate(pieces(index, kept, part_y, part_z)):
+                fetch(index, number, *pair).start()
+
+    def hand(given):
         for index in range(CTX):
-            for number, (source, target) in enumerate(pieces(index, other_e, other_a, in_y, in_z)):
-                pass_on(index, number, source, target).start()
-
-    @pl.when(section == 0)
+            for number, pair in enumerate(pieces(index, given, in_y, in_z)):
+                lend(index, number, *pair).start()
+
+    for core in range(2):
+
+        @pl.when(section == core)
+        def _():
+            start(core)
+
+    met(5)
+    for core in range(2):
+
+        @pl.when(section == core)
+        def _():
+            hand(1 - core)
+
+    lower_out, upper_out = lower_out_ref[...], upper_out_ref[...]
+    outputs_ref[section] = jnp.where(first_core, lower_out, upper_out)
+    sent_out[...] = jnp.where(first_core, upper_out, lower_out)
+    lower_grad, upper_grad = lower_grad_ref[...], upper_grad_ref[...]
+    grads_ref[section] = jnp.where(first_core, lower_grad, upper_grad)
+    sent_grad[...] = jnp.where(first_core, upper_grad, lower_grad)
+    swaps = [
+        pass_on(sent_out, outputs_ref.at[section], send_w.at[0], recv_w.at[0]),
+        pass_on(sent_grad, grads_ref.at[section], send_w.at[1], recv_w.at[1]),
+    ]
+    for number in range(3):
+        sums.first(number)
+    for copy in swaps:
+        copy.start()
+    for number in range(3, 6):
+        sums.first(number)
+    for number in range(6):
+        sums.then(number)
+    own = out_ref.at[pl.ds(pl.multiple_of(section * HALF_SHARD, HALF_SHARD), HALF_SHARD)]
+
+    @pl.when(first_core)
     def _():
-        begin(lower_e, lower_a, upper_e, upper_a)
+        sums.result(own)
+        copy = pass_on(upper_half_ref, own, send_w.at[2], recv_w.at[2])
+        copy.start()
+        copy.wait()
 
     @pl.when(section == 1)
     def _():
-        begin(upper_e, upper_a, lower_e, lower_a)
-
-    met(5)
-
-    @pl.when(section == 0)
-    def _():
-        lend(upper_e, upper_a)
-
-    @pl.when(section == 1)
-    def _():
-        lend(lower_e, lower_a)
-
-    def ready(index, number):
-        source, target = pieces(index, lower_e, lower_a, part_y, part_z)[number]
-        fetch(index, number, source, target).wait()
-        source, target = pieces(index, lower_e, lower_a, in_y, in_z)[number]
-        pass_on(index, number, source, target).wait_recv()
-
-    def make_y(index, block):
-        ready(index, 0)
-        for other in range(CTX):
-            part_y[block, other] = (
-                part_y[block, other].astype(F32) + in_y[block, other].astype(F32)
-            ).astype(BF16)
-
-    def make_z(index, block):
-        ready(index, 1)
-        ready(index, 2)
-        for other in range(CTX):
-            part_z[block, other] = (
-                part_z[block, other].astype(F32) + in_z[block, other].astype(F32)
-            ).astype(BF16)
-
-    first_y = RingSum(ring_y, part_y, (top_y, bottom_y), left_y, right_y, sems[3], sems[4], 2, make_y)
-    first_z = RingSum(ring_z, part_z, (top_z, bottom_z), left_z, right_z, sems[5], sems[6], 2, make_z)
-
-    def make_zz(index, block):
-        more_z[block] = first_y.total(block).astype(BF16)
-
-    def make_yy(index, block):
-        more_y[block] = first_z.total(block).astype(BF16)
-
-    then_z = RingSum(
-        ring_z, more_z, (top_zz, bottom_zz), left_zz, right_zz, sems[7], sems[8], CUT, make_zz
-    )
-    then_y = RingSum(
-        ring_y, more_y, (top_yy, bottom_yy), left_yy, right_yy, sems[9], sems[10], CUT, make_yy
-    )
-    for number in range(6):
-        first_y.stage(number)
-        first_z.stage(number)
-    for number in range(6):
-        then_z.stage(number)
-        then_y.stage(number)
-    out_ref[:FIRST, :] = then_z.total().astype(BF16)
-    out_ref[FIRST:, :] = then_y.total().astype(BF16)
+        sums.result(sent_half := rest[8 + 9])
+        own[...] = upper_half_ref[...]
+        copy = pass_on(sent_half, own, send_w.at[2], recv_w.at[2])
+        copy.start()
+        copy.wait()
+
+    for copy in swaps:
+        copy.wait()
     for index in range(CTX):
-        for number, (source, target) in enumerate(pieces(index, lower_e, lower_a, in_y, in_z)):
-            pass_on(index, number, source, target).wait_send()
-
-
-def sum_shards(lower_e, lower_a, upper_e, upper_a):
-    block = pltpu.VMEM((CTX, FIRST, UNIT), BF16)
-    pair = pltpu.VMEM((2, FIRST, UNIT), BF16)
-    one = pltpu.VMEM((FIRST, UNIT), BF16)
-    top, bottom = pltpu.VMEM((CUT, UNIT), BF16), pltpu.VMEM((FIRST - CUT, UNIT), BF16)
-    full = pltpu.VMEM((CTX, CTX, FIRST, UNIT), BF16)
-    anywhere = pl.BlockSpec(memory_space=pl.ANY)
+        for number, pair in enumerate(pieces(index, 0, in_y, in_z)):
+            lend(index, number, *pair).wait_send()
+
+
+def by_place(array):
+    return array.reshape((CTX, CTX) + array.shape[1:])
+
+
+def sum_shards(lower_e, lower_a, upper_half, lower_out, upper_out, lower_grad, upper_grad):
     return pl.pallas_call(
         sum_shards_kernel,
-        out_shape=jax.ShapeDtypeStruct((SHARD_ROWS, UNIT), BF16),
-        in_specs=[anywhere] * 4,
-        out_specs=VMEM,
-        scratch_shapes=[full] * 4
-        + [pair, pair, block, block] * 2
-        + [block, block]
-        + [top, bottom, one, one] * 2
+        out_shape=(
+            jax.ShapeDtypeStruct((SHARD_ROWS, UNIT), BF16),
+            jax.ShapeDtypeStruct((2, ROWS, D), BF16),
+            jax.ShapeDtypeStruct((2, ROWS, D), F32),
+        ),
+        in_specs=[ANY] * 2 + [VMEM] * 5,
+        out_specs=[VMEM] * 3,
+        scratch_shapes=half_scratch()
+        + [
+            pltpu.VMEM((CTX, CTX, Y_ROWS, UNIT), BF16),
+            pltpu.VMEM((CTX, CTX, Z_ROWS, UNIT), BF16),
+            pltpu.VMEM((ROWS, D), BF16),
+            pltpu.VMEM((ROWS, D), F32),
+        ]
         + [SEMS((12,))] * 3
-        + [SEMS((6,))] * 8,
+        + [SEMS((3,))] * 2
+        + [SEMS((6,))] * 8
+        + [pltpu.VMEM((HALF_SHARD, UNIT), BF16)],
         compiler_params=params(8),
         name="sum_shards",
-    )(*(
-        array.reshape((CTX, CTX) + array.shape[1:])
-        for array in (lower_e, lower_a, upper_e, upper_a)
-    ))
+    )(by_place(lower_e), by_place(lower_a), upper_half, lower_out, upper_out, lower_grad, upper_grad)
 
 
 def spread_sums_kernel(shard_ref, all_ref, squares_ref, from_y, from_z, *sems):
@@ -696,15 +793,18 @@
 
 
 def attn_forward_kernel(
-    length_ref, u_ref, pack_ref, table_ref,
+    layer, length_ref, u_ref, packs_ref, table_ref,
     a_ref, qkv_ref, mass_ref, attended_ref, residual_ref, b_ref,
     gains_ref, router_ref, w_ref, back_ref,
-    heads_out, heads_w, send_a, recv_a, send_o, recv_o,
+    heads_out, heads_w, pack_ref, pack_sem, send_a, recv_a, send_o, recv_o,
 ):
     me, right, left, across = ring()
+    load = pltpu.make_async_copy(packs_ref.at[layer], pack_ref, pack_sem)
+    load.start()
     greet((right, left, across))
     length = length_ref[0]
     tokens = u_ref[...].astype(F32)
+    load.wait()
     unpack(pack_ref, back_ref, heads_w)
     router_ref[...] = heads_w[:, D - LANES :]
     places = lax.broadcasted_iota(jnp.int32, (8, LANES), 0) + EXPERTS
@@ -769,10 +869,10 @@
         pltpu.make_async_copy(heads_out.at[0], attended_ref.at[0], send_o.at[step]).wait()
 
 
-def attn_forward(length, u, pack, table):
+def attn_forward(layer, length, u, packs, table):
     sems = pltpu.SemaphoreType.DMA
     return pl.pallas_call(
-        attn_forward_kernel,
+        functools.partial(attn_forward_kernel, layer),
         out_shape=(
             jax.ShapeDtypeStruct((SEQ, D), BF16),
             jax.ShapeDtypeStruct((SEQ, EXT), BF16),
@@ -785,28 +885,77 @@
             jax.ShapeDtypeStruct((D, EXT), BF16),
             jax.ShapeDtypeStruct((D, D), BF16),
         ),
-        in_specs=[SMEM] + [VMEM] * 3,
+        in_specs=[
+            SMEM,
+            VMEM,
+            ANY,
+            VMEM,
+        ],
         out_specs=[VMEM] * 10,
-        scratch_shapes=[pltpu.VMEM((CTX, ROWS, COLS), BF16), pltpu.VMEM((D, D), BF16)]
+        scratch_shapes=[
+            pltpu.VMEM((CTX, ROWS, COLS), BF16),
+            pltpu.VMEM((D, D), BF16),
+            pltpu.VMEM((16, ATTN_ROWS, UNIT), BF16),
+            sems,
+        ]
         + [sems((6,)), sems((6,)), sems((CTX,)), sems((CTX,))],
-        compiler_params=params(1),
+        compiler_params=params(1 + 10 * layer),
         name="attn_forward",
-    )(length, u, pack, table)
+    )(length, u, packs, table)
 
 
 def attn_backward_kernel(
-    length_ref, u_ref, gains_ref, router_ref, w_ref, back_ref, table_ref,
+    hosting, length_ref, u_ref, gains_ref, router_ref, w_ref, back_ref, table_ref,
     a_ref, qkv_ref, mass_ref, attended_ref, residual_ref, second_ref, gates_ref,
     delta_ref, db_ref, gate_grad_ref, *rest,
 ):
+    if hosting:
+        upper_e, upper_a, lent, *rest = rest
     input_ref, pack_ref, lower_ref = rest[:3]
     rest = rest[3:]
+    if hosting:
+        half_ref, *rest = rest
+        rest, hosted = rest[:15], rest[15:]
     dheads_ref, dback_ref = rest[:2]
     rest = rest[2:]
     key_acc, value_acc, dz, grads_out, grads_in, send_o, recv_o = rest[:7]
     part, across_in, from_left, from_right, send_r, recv_r = rest[7:13]
     me, right, left, across = ring()
     greet((right, left, across))
+    if hosting:
+        refs, (in_y, in_z, local, *sems) = hosted[:HALF_REFS], hosted[HALF_REFS:]
+        part_y, part_z = refs[:2]
+        section = lax.axis_index("section")
+        sums = HalfSums(
+            refs,
+            sems,
+            lambda index, block: add_block(part_y, in_y, block),
+            lambda index, block: add_block(part_z, in_z, block),
+        )
+        greet_ids(sums.ring_y.near() + sums.ring_z.near())
+
+        def loads(half):
+            sources = half_sources(half, upper_e, upper_a)
+            pairs = [
+                (sources[1], part_z.at[:, :, pl.ds(0, Z_CUT), :]),
+                (sources[2], part_z.at[:, :, pl.ds(Z_CUT, ATTN_ROWS), :]),
+                (lent.at[:, :, pl.ds(Y_ROWS, Z_ROWS), :], in_z),
+            ]
+            for block in range(CTX):
+                pairs.append((sources[0].at[:, block], part_y.at[block]))
+                pairs.append((lent.at[:, block, pl.ds(0, Y_ROWS), :], in_y.at[block]))
+            return [
+                pltpu.make_async_copy(source, target, local.at[index])
+                for index, (source, target) in enumerate(pairs)
+            ]
+
+        for core in range(2):
+
+            @pl.when(section == core)
+            def _():
+                for copy in loads(core):
+                    copy.start()
+
     length = length_ref[0]
     lanes = lax.broadcasted_iota(jnp.int32, (ROWS, LANES), 1)
     gates = gates_ref[...]
@@ -824,7 +973,7 @@
     )
     input_ref[...] = residual_grad
     branch_grad = residual_grad.astype(BF16)
-    met(3)
+    met(7 if hosting else 3)
 
     for block in range(CTX):
         grads_out[block] = dot_nt(branch_grad, back_ref[block * COLS : (block + 1) * COLS, :]).astype(
@@ -839,6 +988,11 @@
             ).start()
 
     grads_in[me] = grads_out[me]
+    if hosting:
+        for copy in loads(0):
+            copy.wait()
+        for number in range(3):
+            sums.first(number)
     for block in range(CTX):
         dback_ref[block * COLS : (block + 1) * COLS, :] = dot_tn(
             attended_ref[block], branch_grad
@@ -882,6 +1036,9 @@
             spot = slice(head * WIDE, (head + 1) * WIDE)
             key_acc[:keys, spot] += dot_tn(score_grad, queries)
             value_acc[:keys, spot] += dot_tn(probs.astype(BF16), grads)
+        if hosting and block == 2:
+            sums.first(3)
+            sums.first(4)
     for block in range(CTX):
         rows = pl.ds(block * ROWS, ROWS)
         table = table_ref[rows, :] * (HEAD_DIM**-0.5)
@@ -891,6 +1048,11 @@
             dz[rows, at : at + WIDE] = (key_acc[rows, spot] * table).astype(BF16)
             at = (2 * HEADS_DEV + head) * WIDE
             dz[rows, at : at + WIDE] = value_acc[rows, spot].astype(BF16)
+
+    if hosting:
+        sums.first(5)
+        for number in range(3):
+            sums.then(number)
 
     def make(block):
         part[rows_of(block), :] = dot_nt(dz[rows_of(block), :], w_ref[...]).astype(BF16)
@@ -920,6 +1082,9 @@
         dheads_ref[:, 4 * WIDE : 5 * WIDE] = jnp.where(
             wide_lanes < HEAD_DIM, pieces[8], 0.0
         ).astype(BF16)
+        if hosting:
+            sums.then(3)
+            sums.then(4)
 
     normed_grad = reduce_rows(make, part, across_in, from_left, from_right, send_r, recv_r, beside)
     tokens = u_ref[...].astype(F32)
@@ -941,15 +1106,20 @@
     ).astype(BF16)
     repack(dback_ref, dheads_ref, pack_ref)
     lower_ref[...] = input_grad.astype(BF16)
-
-
-def attn_backward(length, *arrays):
+    if hosting:
+        sums.then(5)
+        sums.result(half_ref)
+
+
+def attn_backward(length, arrays, upper=()):
     sems = pltpu.SemaphoreType.DMA
     out_shape = [
         jax.ShapeDtypeStruct((ROWS, D), F32),
         jax.ShapeDtypeStruct((16, ATTN_ROWS, UNIT), BF16),
         jax.ShapeDtypeStruct((ROWS, D), BF16),
     ]
+    if upper:
+        out_shape.append(jax.ShapeDtypeStruct((HALF_SHARD, UNIT), BF16))
     scratch = [
         pltpu.VMEM((D, D), BF16),
         pltpu.VMEM((D, D), BF16),
@@ -961,22 +1131,28 @@
         sems((CTX,)),
         sems((CTX,)),
     ] + REDUCE_SCRATCH
+    if upper:
+        scratch += half_scratch()
+        scratch += [
+            pltpu.VMEM((CTX, CTX, Y_ROWS, UNIT), BF16),
+            pltpu.VMEM((CTX, CTX, Z_ROWS, UNIT), BF16),
+            sems((11,)),
+        ] + [sems((6,))] * 8
     return pl.pallas_call(
-        attn_backward_kernel,
+        functools.partial(attn_backward_kernel, bool(upper)),
         out_shape=tuple(out_shape),
-        in_specs=[SMEM] + [VMEM] * len(arrays),
+        in_specs=[SMEM] + [VMEM] * len(arrays) + [ANY] * len(upper),
         out_specs=[VMEM] * len(out_shape),
         scratch_shapes=scratch,
-        compiler_params=params(3),
+        compiler_params=params(4 if upper else 3),
         name="attn_backward",
-    )(length, *arrays)
+    )(length, *arrays, *(by_place(array) for array in upper))
 
 
 GROUP = 4
 GROUPS = 16 // GROUP
 GROUP_UNITS = GROUP * LANES
 SPLIT = EXPERT_ROWS // 2
-ANY = pl.BlockSpec(memory_space=pl.ANY)
 SUM_SCRATCH = [
     pltpu.VMEM((CTX, ROWS, D), BF16),
     pltpu.VMEM((HALF, D), BF16),
@@ -1127,14 +1303,23 @@
 
 
 def ffn_backward_kernel(
-    b_ref, gate_ref, delta_own_ref, kept_ref, w_ref, db_ref, gate_grad_ref, dw_ref,
+    lending, b_ref, gate_ref, delta_own_ref, kept_ref, w_ref, *rest,
+):
+    if lending:
+        upper_e, upper_a, db_ref, gate_grad_ref, dw_ref, lent_ref, *rest = rest
+        *rest, send_l, recv_l = rest
+    else:
+        db_ref, gate_grad_ref, dw_ref, *rest = rest
+    (
     delta, acc, gate_acc, slot_grad, hidden, acted, win, wout, staged, rows_out, rows_in,
     w_sem, kept_sem, dw_sem, send_d, recv_d, send_g, recv_g,
     part, top_in, bottom_in, from_left, from_right, send, recv,
-):
+    ) = rest
     ring = Ring("x")
     peers = (ring.right, ring.left, ring.across)
-    greet_ids([ring.place(peer) for peer in peers])
+    section = lax.axis_index("section")
+    sibling = {"section": 1 - section}
+    greet_ids([ring.place(peer) for peer in peers] + ([sibling] if lending else []))
     blocks = (ring.me, ring.right, ring.left, ring.across)
     kept_loads = [
         pltpu.make_async_copy(
@@ -1150,7 +1335,36 @@
     for copy in kept_loads[1:]:
         copy.start()
     delta[ring.me] = delta_own_ref[...]
-    met(3)
+    met(4 if lending else 3)
+    if lending:
+        first_rows = pl.ds(0, KEPT)
+        last_rows = pl.ds(KEPT, ATTN_ROWS)
+
+        def lends(given):
+            sources = (
+                (upper_e.at[:, first_rows, :], upper_e.at[:, last_rows, :])
+                if given == 0
+                else (upper_e.at[:, pl.ds(HALF_SHARD, KEPT), :], upper_a)
+            )
+            return [
+                pltpu.make_async_remote_copy(
+                    src_ref=source,
+                    dst_ref=lent_ref.at[:, target, :],
+                    send_sem=send_l.at[index],
+                    recv_sem=recv_l.at[index],
+                    device_id=sibling,
+                    device_id_type=MESH,
+                )
+                for index, (source, target) in enumerate(zip(sources, (first_rows, last_rows)))
+            ]
+
+        for core in range(2):
+
+            @pl.when(section == core)
+            def _():
+                for copy in lends(1 - core):
+                    copy.start()
+
     halves = (pl.ds(0, HALF), pl.ds(HALF, HALF))
     rows = RingGather(ring, lambda b, h: delta.at[b, halves[h]], send_d, recv_d)
     rows.start()
@@ -1254,18 +1468,24 @@
     rows.sent()
     stores[2].wait()
     stores[3].wait()
-
-
-def ffn_backward(b_all, gate_col, delta_own, kept, weights):
+    if lending:
+        for copy in lends(0):
+            copy.wait()
+
+
+def ffn_backward(b_all, gate_col, delta_own, kept, weights, upper=()):
+    out_shape = [
+        jax.ShapeDtypeStruct((ROWS, D), F32),
+        jax.ShapeDtypeStruct((ROWS, LANES), F32),
+        jax.ShapeDtypeStruct((16, EXPERT_ROWS, UNIT), BF16),
+    ]
+    if upper:
+        out_shape.append(jax.ShapeDtypeStruct((16, HALF_SHARD, UNIT), BF16))
     return pl.pallas_call(
-        ffn_backward_kernel,
-        out_shape=(
-            jax.ShapeDtypeStruct((ROWS, D), F32),
-            jax.ShapeDtypeStruct((ROWS, LANES), F32),
-            jax.ShapeDtypeStruct((16, EXPERT_ROWS, UNIT), BF16),
-        ),
-        in_specs=[VMEM] * 3 + [ANY] * 2,
-        out_specs=[VMEM] * 2 + [ANY],
+        functools.partial(ffn_backward_kernel, bool(upper)),
+        out_shape=out_shape,
+        in_specs=[VMEM] * 3 + [ANY] * (2 + len(upper)),
+        out_specs=[VMEM] * 2 + [ANY] * (len(out_shape) - 2),
         scratch_shapes=[
             pltpu.VMEM((CTX, ROWS, D), BF16),
             pltpu.VMEM((ROWS, D), F32),
@@ -1286,26 +1506,25 @@
             SEMS((3,)),
             SEMS((3,)),
         ]
-        + SUM_SCRATCH,
-        compiler_params=params(6),
+        + SUM_SCRATCH
+        + ([SEMS((2,)), SEMS((2,))] if upper else []),
+        compiler_params=params(10 if upper else 6),
         name="ffn_backward",
-    )(b_all, gate_col, delta_own, kept, weights)
+    )(b_all, gate_col, delta_own, kept, weights, *upper)
 
 
 def rotary_table():
     half_dim = HEAD_DIM // 2
-    frequency = jnp.exp(
-        -jnp.log(10000.0) * (2.0 * jnp.arange(half_dim, dtype=F32) / HEAD_DIM)
-    )
-    angles = jnp.arange(SEQ, dtype=jnp.int32).astype(F32)[:, None] * frequency[None, :]
-    cosine, sine = jnp.cos(angles), jnp.sin(angles)
-    return jnp.concatenate([cosine, cosine, sine, sine], axis=1)
-
-
-def layer_forward(weights, tokens_in, length, codes, table):
-    pack, experts = weights
+    steps = 2.0 * np.arange(half_dim, dtype=np.float32) / np.float32(HEAD_DIM)
+    frequency = np.exp(-np.log(np.float32(10000.0)) * steps)
+    angles = np.arange(SEQ, dtype=np.float32)[:, None] * frequency[None, :]
+    cosine, sine = np.cos(angles), np.sin(angles)
+    return jnp.asarray(np.concatenate([cosine, cosine, sine, sine], axis=1), F32)
+
+
+def layer_forward(layer, packs, experts, tokens_in, length, codes, table):
     a_all, qkv, mass, attended, residual, second, *unpacked = attn_forward(
-        length, tokens_in, pack, table
+        layer, length, tokens_in, packs, table
     )
     output, b_all, gates, gate_col, kept = ffn_forward(
         second, residual, codes, unpacked[1], experts
@@ -1315,27 +1534,20 @@
     )
 
 
-def layer_backward(weights, saved, delta_own, length, table):
-    _, experts = weights
+def layer_backward(experts, saved, delta_own, length, table, upper=()):
     (
         tokens_in, a_all, qkv, mass, attended, residual, second, b_all, gates, gate_col, kept, unpacked,
     ) = saved
-    db, gate_grads, dexperts = ffn_backward(b_all, gate_col, delta_own, kept, experts)
-    return dexperts, attn_backward(
-        length, tokens_in, *unpacked, table, a_all, qkv, mass,
-        attended, residual, second, gates, delta_own, db, gate_grads,
-    )
-
-
-def adam_update(gradient, clipped, master, mean_old, square_old, step_value, learn_rate):
-    mean_new = BETA_ONE * mean_old + (1.0 - BETA_ONE) * clipped
-    square_new = BETA_TWO * square_old + (1.0 - BETA_TWO) * clipped * clipped
-    fix_one = 1.0 - BETA_ONE**step_value
-    fix_two = 1.0 - BETA_TWO**step_value
-    master_new = master - learn_rate * (
-        mean_new / fix_one / (jnp.sqrt(square_new / fix_two) + ADAM_EPS) + DECAY_RATE * master
-    )
-    return (gradient, mean_new, square_new, master_new, master_new.astype(BF16))
+    db, gate_grads, dexperts, *lent = ffn_backward(b_all, gate_col, delta_own, kept, experts, upper)
+    results = attn_backward(
+        length,
+        (
+            tokens_in, *unpacked, table, a_all, qkv, mass,
+            attended, residual, second, gates, delta_own, db, gate_grads,
+        ),
+        tuple(upper) + tuple(lent),
+    )
+    return dexperts, results
 
 
 def factor_of(squares_ref, index):
@@ -1362,9 +1574,9 @@
 def update_kernel(
     fixes_ref, squares_ref, in_sum_ref, out_sum_ref, attn_sum_ref, *refs,
 ):
-    in_old, out_old, attn_old = refs[0:3], refs[3:6], refs[6:9]
-    in_new, out_new, attn_new = refs[9:14], refs[14:19], refs[19:24]
-    small_ref, turned, wide = refs[24:]
+    in_old, out_old, attn_old, gain_old, router_old = (refs[at : at + 3] for at in range(0, 15, 3))
+    in_new, out_new, attn_new, gain_new, router_new = (refs[at : at + 5] for at in range(15, 40, 5))
+    norms_ref, turned, wide = refs[40:]
     turned[pl.ds(0, D, 2), :] = in_sum_ref[0, :, :LANES].astype(F32)
     turned[pl.ds(1, D, 2), :] = in_sum_ref[0, :, LANES:].astype(F32)
     updated(
@@ -1399,7 +1611,22 @@
                 at = part * D + block * COLS
                 wide[:, at : at + COLS] = heads[:, part * COLS : (part + 1) * COLS]
         wide[:, 3 * D :] = jnp.concatenate(back, axis=1)
-        small_ref[...] = small[:, LANES:]
+        small = small[:, LANES:]
+        places = lax.broadcasted_iota(jnp.int32, (8, LANES), 0) + EXPERTS
+        picker = jnp.where(places == lax.broadcasted_iota(jnp.int32, (8, LANES), 1), 1.0, 0.0)
+        gain_rows = lax.dot_general(
+            picker, small, NT, precision=EXACT, preferred_element_type=F32
+        )
+        updated(fixes_ref, gain_rows[:2], factor_of(squares_ref, 0), gain_old, gain_new, GAIN_RATE)
+        updated(
+            fixes_ref,
+            small[:, :EXPERTS],
+            factor_of(squares_ref, 2),
+            router_old,
+            router_new,
+            RATE_FACTOR / (D // 4) ** 0.5,
+        )
+        norms_ref[...] = jnp.sqrt(squares_ref[...])
         for part in range(4):
             lanes = (slice(None), slice(part * D, (part + 1) * D))
             updated(
@@ -1413,12 +1640,13 @@
             )
 
 
-def update(fixes, squares, sums_all, in_old, out_old, attn_old):
+def update(fixes, squares, sums_all, in_old, out_old, attn_old, gain_old, router_old):
     in_rows, units = 2 * D, LANES
     in_shape, out_shape, attn_shape = (CTX * in_rows, units), (CTX, units, D), (48, 4 * D)
     in_spec = pl.BlockSpec((in_rows, units), lambda i: (i, 0))
     out_spec = pl.BlockSpec((1, units, D), lambda i: (i, 0, 0))
     attn_spec = whole(attn_shape)
+    gain_shape, router_shape = (2, 48), (48, EXPERTS)
 
     def five(shape):
         return [jax.ShapeDtypeStruct(shape, F32)] * 4 + [jax.ShapeDtypeStruct(shape, BF16)]
@@ -1429,7 +1657,9 @@
         out_shape=five(in_shape)
         + five(out_shape)
         + five(attn_shape)
-        + [jax.ShapeDtypeStruct((48, LANES), F32)],
+        + five(gain_shape)
+        + five(router_shape)
+        + [jax.ShapeDtypeStruct((8, LANES), F32)],
         in_specs=[
             SMEM,
             whole((8, LANES)),
@@ -1439,8 +1669,15 @@
         ]
         + [in_spec] * 3
         + [out_spec] * 3
-        + [attn_spec] * 3,
-        out_specs=[in_spec] * 5 + [out_spec] * 5 + [attn_spec] * 5 + [whole((48, LANES))],
+        + [attn_spec] * 3
+        + [whole(gain_shape)] * 3
+        + [whole(router_shape)] * 3,
+        out_specs=[in_spec] * 5
+        + [out_spec] * 5
+        + [attn_spec] * 5
+        + [whole(gain_shape)] * 5
+        + [whole(router_shape)] * 5
+        + [whole((8, LANES))],
         scratch_shapes=[pltpu.VMEM((in_rows, units), F32), pltpu.VMEM(attn_shape, F32)],
         compiler_params=pltpu.CompilerParams(vmem_limit_bytes=VMEM_LIMIT),
         name="update",
@@ -1449,6 +1686,8 @@
         *(array.reshape(in_shape) for array in in_old),
         *(array.reshape(out_shape) for array in out_old),
         *(array.reshape(attn_shape) for array in attn_old),
+        *(array.reshape(gain_shape) for array in gain_old),
+        *(array.reshape(router_shape) for array in router_old),
     )
 
 
@@ -1506,27 +1745,17 @@
     seed = jnp.where((positions < length[0])[:, None], seed, jnp.zeros_like(seed))
     table = rotary_table()
 
-    layers = [(packs[layer], experts[layer]) for layer in range(2)]
-    lower_out, lower_saved = layer_forward(layers[0], tokens, length, codes[0], table)
-    upper_out, upper_saved = layer_forward(layers[1], lower_out, length, codes[1], table)
-
+    lower_out, lower_saved = layer_forward(0, packs, experts[0], tokens, length, codes[0], table)
+    upper_out, upper_saved = layer_forward(1, packs, experts[1], lower_out, length, codes[1], table)
     upper_experts, (upper_grad, upper_attn, lower_seed) = layer_backward(
-        layers[1], upper_saved, seed, length, table
-    )
-    lower_experts, (lower_grad, lower_attn, _) = layer_backward(
-        layers[0], lower_saved, lower_seed, length, table
-    )
-
-    def paired(first, second):
-        kept = jnp.where(first_core, first, second)
-        other = swap(jnp.where(first_core, second, first))
-        return jnp.stack(
-            [jnp.where(first_core, kept, other), jnp.where(first_core, other, kept)]
-        )
-
-    layer_outputs = paired(lower_out, upper_out)[None]
-    input_grads = paired(lower_grad, upper_grad)[None]
-    shard_sum = sum_shards(lower_experts, lower_attn, upper_experts, upper_attn)
+        experts[1], upper_saved, seed, length, table
+    )
+    lower_experts, (lower_grad, lower_attn, _, upper_half) = layer_backward(
+        experts[0], lower_saved, lower_seed, length, table, (upper_experts, upper_attn)
+    )
+    shard_sum, layer_outputs, input_grads = sum_shards(
+        lower_experts, lower_attn, upper_half, lower_out, upper_out, lower_grad, upper_grad
+    )
     sums_all, squares = spread_sums(shard_sum)
     step_value = step_count[0].astype(F32)
     fixes = jnp.stack([1.0 - BETA_ONE**step_value, 1.0 - BETA_TWO**step_value])
@@ -1537,32 +1766,21 @@
         (expert_in, in_mean, in_square),
         (expert_out, out_mean, out_square),
         (attn_weight, attn_mean, attn_square),
-    )
-    small_sum = changed[15]
-    norms = jnp.sqrt(squares[0, :5])
-    factors = jnp.minimum(1.0, CLIP_LIMIT / norms)
-    router_sum = small_sum[:, :EXPERTS][None]
-    gain_sum = small_sum[:, EXPERTS : EXPERTS + 2].T[None]
-    gains_new = adam_update(
-        gain_sum, gain_sum * factors[0], norm_gains, gains_mean, gains_square, step_value, GAIN_RATE
-    )
-    router_new = adam_update(
-        router_sum,
-        router_sum * factors[2],
-        router_weight,
-        router_mean,
-        router_square,
-        step_value,
-        RATE_FACTOR / (D // 4) ** 0.5,
-    )
+        (norm_gains, gains_mean, gains_square),
+        (router_weight, router_mean, router_square),
+    )
+
+    def shaped(first, like):
+        return tuple(array.reshape(like.shape) for array in changed[first : first + 5])
+
     return (
-        (layer_outputs, input_grads)
-        + gains_new
-        + tuple(array.reshape(attn_weight.shape) for array in changed[10:15])
-        + router_new
-        + tuple(array.reshape(expert_in.shape) for array in changed[:5])
-        + tuple(array.reshape(expert_out.shape) for array in changed[5:10])
-        + (norms[None],)
+        (layer_outputs[None], input_grads[None])
+        + shaped(15, norm_gains)
+        + shaped(10, attn_weight)
+        + shaped(20, router_weight)
+        + shaped(0, expert_in)
+        + shaped(5, expert_out)
+        + (changed[25][:1, :5],)
     )
 
 

time: 539 us -> 508 us (0.942)
  Pallas kernels: 478 us -> 464 us
  other arithmetic: 16.5 us -> 3.11 us
    pallas_call x7, Pallas kernels: 313 us -> 296 us  [the longest x2 92.6 us: attn_backward(): pl.pallas_call(functools.partial(attn_backward_kernel, bool(upper)), out_...]
    unnamed x41 -> x37, local copies, waits for them, and re-layouts: 3.46 us -> 10.6 us
  transfers between devices with their start and end apart: 5 -> 3, of which waited for: 2 -> 1; matrix products, arithmetic and copies ran while one was open for 4% -> 2% of each run, Pallas kernels for 28% -> 30%
where the time goes in v4:
time: 508 us; the launch traced here: 505 us
  Pallas kernels  464 us (91%)
  local copies, waits for them, and re-layouts  20.2 us (4%)
  between operations  15.4 us (3%)
    pallas_call x2, Pallas kernels, attn_backward(): pl.pallas_call(functools.partial(attn_backward_kernel, bool(upper)), out_...  92.6 us
    pallas_call x2, Pallas kernels, ffn_backward(): pl.pallas_call(functools.partial(ffn_backward_kernel, bool(upper)), out_s...  84.7 us
    pallas_call x2, Pallas kernels, attn_forward(): pl.pallas_call(functools.partial(attn_forward_kernel, layer), out_shape=(...  74.2 us
    pallas_call x2, Pallas kernels, ffn_forward(): pl.pallas_call(ffn_forward_kernel, out_shape=(jax.ShapeDtypeStruct((ROWS,...  73.7 us
    pallas_call x1, Pallas kernels, sum_shards(): pl.pallas_call(sum_shards_kernel, out_shape=(jax.ShapeDtypeStruct((SHARD_...  45 us
    pallas_call x1, Pallas kernels, spread_sums(): pl.pallas_call(spread_sums_kernel, out_shape=(jax.ShapeDtypeStruct((CTX,...  38.7 us
    pallas_call x1, Pallas kernels, gather_shards(): pl.pallas_call(gather_shards_kernel, out_shape=(jax.ShapeDtypeStruct((2,...  36.6 us
    pallas_call x1, Pallas kernels, update(): pl.pallas_call(update_kernel, grid=(CTX,), out_shape=five(in_shape) + fiv...  18 us
  transfers between devices with their start and end apart: 3, of which 1 were waited for; matrix products, arithmetic and copies ran while one was open for 2% of the time, Pallas kernels for 30%

profile of v4, /device:TPU:0, one launch (start us, length us, event | category | flops | bytes accessed | tf_op | source)
XLA Modules:
  0.0 504.7 jit_solution(11336352841873887422)
XLA Ops:
  7.2 0.0 copy-start
  7.2 0.0 all-gather.5.cloned.1.call-start
  7.3 1.5 dynamic-slice_convert_fusion
  8.7 0.2 slice.55
  9.0 1.0 fusion
  10.0 0.0 copy-start.8
  10.0 0.0 copy-start.11
  10.0 0.1 copy.100
  10.1 0.0 copy-start.9
  10.1 0.0 copy-start.10
  10.1 0.0 copy-start.12
  10.1 0.0 copy-start.7
  10.2 0.1 bitcast_select_fusion.2
  10.2 0.1 collective-permute-start
  10.3 1.6 collective-permute-done
  11.9 0.9 broadcast_select_fusion
  12.8 0.0 all-gather.5.cloned.1.call-update
  12.8 0.0 all-gather.7.cloned.1.call-start
  12.9 0.7 all-gather.7.cloned.1.call-update
  13.6 0.9 slice.62
  14.5 0.0 copy-done.8
  14.5 0.1 copy.73
  14.7 0.1 copy.74
  14.8 1.0 fusion.3
  15.8 0.1 concatenate.7
  16.0 0.2 convert_element_type.30
  16.1 0.7 copy.75
  17.6 0.7 copy.78
  18.3 0.0 copy-done.10
  18.3 0.7 copy.79
  19.0 0.0 copy-done.12
  19.0 0.6 dynamic_slice.33.length_ref
  19.6 0.6 pad.4.code_ref
  20.2 36.6 %gather_shards.1 = (bf16[2,4,4,288,256]{4,3,2,1,0:T(8,128)(2,1)}, f32[2,4,8,256]{3,2,1,0:T(8,128)}) custom-call(bf16[288,256]{1,0:T(8,128)(2,1)} %bitcast.113, f32[8,256]{1,0:T(8,128)} %pad.4.code_ref), custom_call_target="tpu_custom_call" | custom-call | tf_op jit(solution)/shard_map/gather_shards/pallas_call | solution.py:422
  56.8 0.0 copy-done
  56.9 0.8 dynamic-slice_bitcast_fusion.u_ref
  57.6 39.0 %attn_forward.2 = (bf16[1024,768]{1,0:T(8,128)(2,1)}, bf16[1024,1152]{1,0:T(8,128)(2,1)}, f32[3,1024,1]{2,1,0:T(8,128)}, bf16[4,256,192]{2,1,0:T(8,128)(2,1)}, f...) custom-call(s32[1]{0:T(128)} %dynamic_slice.33.length_ref, ...), custom_call_target="tpu_custom_call" | custom-call | tf_op jit(solution)/shard_map/attn_forward/pallas_call | solution.py:874
  96.7 0.7 add_compare_fusion
  97.4 0.6 pad_maximum_fusion.3.fixes_ref
  98.0 0.6 slice_bitcast_fusion
  98.6 0.0 copy-done.5
  98.6 0.9 bitcast_select_fusion.delta_own_ref.delta_ref
  99.4 38.1 %ffn_forward.2 = (bf16[256,768]{1,0:T(8,128)(2,1)}, bf16[4,256,768]{2,1,0:T(8,128)(2,1)}, f32[256,128]{1,0:T(8,128)}, f32[4,256,1]{2,1,0:T(8,128)}, bf16[4,16,256,256]{3,2,1,0:T(8,128)(2,1)}) custom-call(bf16[256,768]{1,0:T(8,128)(2,1)} %get-tuple-element.105.b_own_ref.second_ref, f32[256,768]{1,0:T(8,128)} %get-tuple-element.106.residual_ref, ...), custom_call_target="tpu_custom_call" | custom-call | tf_op jit(solution)/shard_map/ffn_forward/pallas_call | solution.py:1278
  137.6 35.2 %attn_forward.3 = (bf16[1024,768]{1,0:T(8,128)(2,1)}, bf16[1024,1152]{1,0:T(8,128)(2,1)}, f32[3,1024,1]{2,1,0:T(8,128)}, bf16[4,256,192]{2,1,0:T(8,128)(2,1)}, f...) custom-call(s32[1]{0:T(128)} %dynamic_slice.33.length_ref, ...), custom_call_target="tpu_custom_call" | custom-call | tf_op jit(solution)/shard_map/attn_forward/pallas_call | solution.py:874
  172.8 0.0 all-gather.7.cloned.1.call-done
  172.8 35.6 %ffn_forward.3 = (bf16[256,768]{1,0:T(8,128)(2,1)}, bf16[4,256,768]{2,1,0:T(8,128)(2,1)}, f32[256,128]{1,0:T(8,128)}, f32[4,256,1]{2,1,0:T(8,128)}, bf16[4,16,256,256]{3,2,1,0:T(8,128)(2,1)}) custom-call(bf16[256,768]{1,0:T(8,128)(2,1)} %get-tuple-element.121.b_own_ref.second_ref, f32[256,768]{1,0:T(8,128)} %get-tuple-element.120.residual_ref, ...), custom_call_target="tpu_custom_call" | custom-call | tf_op jit(solution)/shard_map/ffn_forward/pallas_call | solution.py:1278
  208.4 40.6 %ffn_backward.2 = (f32[256,768]{1,0:T(8,128)}, f32[256,128]{1,0:T(8,128)}, bf16[16,1152,256]{2,1,0:T(8,128)(2,1)}) custom-call(bf16[4,256,768]{2,1,0:T(8,128)(2,1)} %get-tuple-element.123.b_ref, f32[4,256,1]{2,1,0:T(8,128)} %get-tuple-element.124.gate_ref, bf16[256,768]{1,0:T(8,128)(2,1)} %bitcast_select_fusion.delta_own_ref.delta_ref, ...), custom_call_target="tpu_custom_call" | custom-call | tf_op jit(solution)/shard_map/ffn_backward/pallas_call | solution.py:1484
  249.0 39.3 %attn_backward.2 = (f32[256,768]{1,0:T(8,128)}, bf16[16,288,256]{2,1,0:T(8,128)(2,1)}, bf16[256,768]{1,0:T(8,128)(2,1)}) custom-call(s32[1]{0:T(128)} %dynamic_slice.33.length_ref, bf16[256,768]{1,0:T(8,128)(2,1)} %get-tuple-element.111.u_ref.lower_out_ref, f32[8,768]{1,0:T(8,128)} %get-tuple-element.112.gains_ref, ...), custom_call_target="tpu_custom_call" | custom-call | tf_op jit(solution)/shard_map/attn_backward/pallas_call | solution.py:1141
  288.3 44.0 %ffn_backward.3 = (f32[256,768]{1,0:T(8,128)}, f32[256,128]{1,0:T(8,128)}, bf16[16,1152,256]{2,1,0:T(8,128)(2,1)}, bf16[16,720,256]{2,1,0:T(8,128)(2,1)}) custom-call(bf16[4,256,768]{2,1,0:T(8,128)(2,1)} %get-tuple-element.109.b_ref, f32[4,256,1]{2,1,0:T(8,128)} %get-tuple-element.110.gate_ref, bf16[256,768]{1,0:T(8,128)(2,1)} %get-tuple-element.128.delta_own_ref.delta_ref, ...), custom_call_target="tpu_custom_call" | custom-call | tf_op jit(solution)/shard_map/ffn_backward/pallas_call | solution.py:1484
  332.3 53.3 %attn_backward.3 = (f32[256,768]{1,0:T(8,128)}, bf16[16,288,256]{2,1,0:T(8,128)(2,1)}, bf16[256,768]{1,0:T(8,128)(2,1)}, bf16[720,256]{1,0:T(8,128)(2,1)}) custom-call(s32[1]{0:T(128)} %dynamic_slice.33.length_ref, bf16[256,768]{1,0:T(8,128)(2,1)} %dynamic-slice_bitcast_fusion.u_ref, f32[8,768]{1,0:T(8,128)} %get-tuple-element.133.gains_ref, ...), custom_call_target="tpu_custom_call" | custom-call | tf_op jit(solution)/shard_map/attn_backward/pallas_call | solution.py:1141
  385.7 45.0 %sum_shards.1 = (bf16[1440,256]{1,0:T(8,128)(2,1)}, bf16[2,256,768]{2,1,0:T(8,128)(2,1)}, f32[2,256,768]{2,1,0:T(8,128)}) custom-call(bf16[4,4,1152,256]{3,2,1,0:T(8,128)(2,1)} %bitcast.91, bf16[4,4,288,256]{3,2,1,0:T(8,128)(2,1)} %bitcast.102, bf16[720,256]{1,0:T(8,128)(2,1)} %get-tuple-element.145.upper_half_ref, ...), custom_call_target="tpu_custom_call" | custom-call | tf_op jit(solution)/shard_map/sum_shards/pallas_call | solution.py:642
  430.7 38.7 %spread_sums.1 = (bf16[4,1440,256]{2,1,0:T(8,128)(2,1)}, f32[8,128]{1,0:T(8,128)}) custom-call(bf16[1440,256]{1,0:T(8,128)(2,1)} %get-tuple-element.151.shard_ref), custom_call_target="tpu_custom_call" | custom-call | tf_op jit(solution)/shard_map/spread_sums/pallas_call | solution.py:735
  469.3 18.0 %update.1 = (f32[6144,128]{1,0:T(8,128)}, f32[6144,128]{1,0:T(8,128)}, f32[6144,128]{1,0:T(8,128)}, f32[6144,128]{1,0:T(8,128)}, bf16[6144,128]{1,0:T(8,128)(2,1...) custom-call(f32[2]{0:T(128)} %pad_maximum_fusion.3.fixes_ref, ...), custom_call_target="tpu_custom_call" | custom-call | tf_op jit(solution)/shard_map/update/pallas_call | solution.py:1654
  487.4 0.0 copy-start.2
  487.4 1.5 copy.80
  488.9 1.4 copy.81
  490.2 1.4 copy.82
  491.6 1.4 copy.83
  493.0 1.3 copy.84
  494.3 1.2 slice.53
  495.5 0.0 copy-done.3
  495.5 0.9 copy.104
  496.4 1.1 copy.105
  497.6 0.0 copy-done.1
  (19 shorter events, 0.1 us)
Async XLA Ops:
  7.2 49.6 %copy-start = (bf16[2,256,768]{2,1,0:T(8,128)(2,1)S(1)}, bf16[2,256,768]{2,1,0:T(8,128)(2,1)}, u32[]{:S(2)}) copy-start(bf16[2,256,768]{2,1,0:T(8,128)(2,1)} %param.21) | copy-start | bytes 2359300
  7.2 92.2 %all-gather.5.cloned.1.call-start = ((), (), s32[]{:S(2)}) async-start(), calls=%async_computation | async-start | bytes 9732096 | tf_op jit(solution)/shard_map/all_gather | solution.py:1739
  10.0 4.5 copy-start.8
  10.0 4.6 copy-start.11
  10.1 7.5 %copy-start.9 = (f32[1,48,3]{1,0,2:T(1,128)S(1)}, f32[1,48,3]{1,0,2:T(1,128)}, u32[]{:S(2)}) copy-start(f32[1,48,3]{1,0,2:T(1,128)} %param.33) | copy-start | bytes 1732
  10.1 8.2 %copy-start.10 = (f32[1,48,3]{1,0,2:T(1,128)S(1)}, f32[1,48,3]{1,0,2:T(1,128)}, u32[]{:S(2)}) copy-start(f32[1,48,3]{1,0,2:T(1,128)} %param.34) | copy-start | bytes 1732
  10.1 8.9 %copy-start.12 = (s32[2]{0:T(128)S(1)}, s32[2]{0:T(128)}, u32[]{:S(2)}) copy-start(s32[2]{0:T(128)} %param.23) | copy-start | bytes 28
  10.1 9.4 %copy-start.7 = (s32[1,2,256,2]{2,3,1,0:T(2,128)S(1)}, s32[1,2,256,2]{2,3,1,0:T(2,128)}, u32[]{:S(2)}) copy-start(s32[1,2,256,2]{2,3,1,0:T(2,128)} %param.24) | copy-start | bytes 12292
  10.2 1.7 collective-permute-start
  12.8 159.9 %all-gather.7.cloned.1.call-start = ((), (), s32[]{:S(2)}) async-start(), calls=%async_computation.1 | async-start | bytes 9732096 | tf_op jit(solution)/shard_map/all_gather | solution.py:1739
  14.6 82.1 %copy-start.4 = (f32[1,48,3]{2,1,0:T(8,128)}, f32[1,48,3]{2,1,0:T(8,128)S(1)}, u32[]{:S(2)}) copy-start(f32[1,48,3]{2,1,0:T(8,128)S(1)} %copy.73) | copy-start | bytes 1732
  57.6 40.3 %copy-start.6 = (f32[2,4,8,256]{3,2,1,0:T(8,128)S(1)}, f32[2,4,8,256]{3,2,1,0:T(8,128)}, u32[]{:S(2)}) copy-start(f32[2,4,8,256]{3,2,1,0:T(8,128)} %get-tuple-element.107) | copy-start | bytes 196612
  57.6 41.0 %copy-start.5 = (bf16[2,256,768]{2,1,0:T(8,128)(2,1)S(1)}, bf16[2,256,768]{2,1,0:T(8,128)(2,1)}, u32[]{:S(2)}) copy-start(bf16[2,256,768]{2,1,0:T(8,128)(2,1)} %param.22) | copy-start | bytes 2359300
  469.3 26.2 %copy-start.3 = (bf16[2,256,768]{2,1,0:T(8,128)(2,1)S(1)}, bf16[2,256,768]{2,1,0:T(8,128)(2,1)}, u32[]{:S(2)}) copy-start(bf16[2,256,768]{2,1,0:T(8,128)(2,1)} %get-tuple-element.149) | copy-start | bytes 2359300
  487.4 9.0 %copy-start.2 = (f32[2,256,768]{2,1,0:T(8,128)S(1)}, f32[2,256,768]{2,1,0:T(8,128)}, u32[]{:S(2)}) copy-start(f32[2,256,768]{2,1,0:T(8,128)} %get-tuple-element.150) | copy-start | bytes 4718596
  495.5 2.0 copy-start.1
Sparse Core Ops, SparseCore 0:
  13.0 60.1 all-gather.4
  76.0 55.0 all-gather.6

commit v5 on v4

--- a/solution.py
+++ b/solution.py
@@ -232,37 +232,34 @@
 class RingGather:
     def __init__(self, ring, at, send, recv):
         self.ring, self.at, self.send, self.recv = ring, at, send, recv
-        self.copies = []
-
-    def go(self, block, half, to):
+        self.sends = (
+            (ring.me, 0, ring.right),
+            (ring.me, 1, ring.left),
+            (ring.me, 1, ring.right),
+            (ring.me, 0, ring.left),
+            (ring.left, 0, ring.right),
+            (ring.right, 1, ring.left),
+        )
+
+    def piece(self, index, block, half, to):
         spot = self.at(block, half)
-        index = len(self.copies)
-        self.copies.append(
-            self.ring.copy(spot, spot, self.send.at[index], self.recv.at[index], to)
-        )
-        self.copies[-1].start()
+        return self.ring.copy(spot, spot, self.send.at[index], self.recv.at[index], to)
+
+    def go(self, index):
+        self.piece(index, *self.sends[index]).start()
+
+    def landed(self, index, block, half):
+        self.piece(index, block, half, self.ring.right).wait_recv()
 
     def start(self):
-        ring = self.ring
-        self.go(ring.me, 0, ring.right)
-        self.go(ring.me, 1, ring.left)
-        self.go(ring.me, 1, ring.right)
-        self.go(ring.me, 0, ring.left)
+        for index in range(4):
+            self.go(index)
 
     def forward(self):
-        ring = self.ring
-        spot = self.at(ring.left, 0)
-        ring.copy(spot, spot, self.send.at[0], self.recv.at[0], ring.right).wait_recv()
-        self.go(ring.left, 0, ring.right)
-        spot = self.at(ring.right, 1)
-        ring.copy(spot, spot, self.send.at[1], self.recv.at[1], ring.left).wait_recv()
-        self.go(ring.right, 1, ring.left)
-
-    def landed(self, index, block, half):
-        spot = self.at(block, half)
-        self.ring.copy(
-            spot, spot, self.send.at[index], self.recv.at[index], self.ring.right
-        ).wait_recv()
+        self.landed(0, self.ring.left, 0)
+        self.go(4)
+        self.landed(1, self.ring.right, 1)
+        self.go(5)
 
     def near(self):
         self.landed(2, self.ring.left, 1)
@@ -273,8 +270,8 @@
         self.landed(5, self.ring.across, 1)
 
     def sent(self):
-        for copy in self.copies:
-            copy.wait_send()
+        for index in range(6):
+            self.piece(index, *self.sends[index]).wait_send()
 
     def finish(self):
         self.near()
@@ -513,172 +510,8 @@
         )
 
 
-def sum_shards_kernel(
-    experts, attn, upper_half_ref, lower_out_ref, upper_out_ref, lower_grad_ref, upper_grad_ref,
-    out_ref, outputs_ref, grads_ref, *rest,
-):
-    halves, rest = rest[:HALF_REFS], rest[HALF_REFS:]
-    in_y, in_z, sent_out, sent_grad, local, send_s, recv_s, send_w, recv_w = rest[:9]
-    section = lax.axis_index("section")
-    sibling = {"section": 1 - section}
-    first_core = section == 0
-    part_y, part_z = halves[:2]
-
-    def make_y(index, block):
-        ready(index, 0)
-        add_block(part_y, in_y, block)
-
-    def make_z(index, block):
-        ready(index, 1)
-        ready(index, 2)
-        add_block(part_z, in_z, block)
-
-    sums = HalfSums(halves, rest[9:], make_y, make_z)
-    ring_y, ring_z = sums.ring_y, sums.ring_z
-    greet_ids([sibling] + ring_y.near() + ring_z.near())
-
-    def pieces(index, half, target_y, target_z):
-        b_y, b_z = ring_y.order()[index], ring_z.order()[index]
-        sources = half_sources(half, experts, attn)
-        return (
-            (sources[0].at[:, b_y], target_y.at[b_y]),
-            (sources[1].at[b_z], target_z.at[b_z, :, pl.ds(0, Z_CUT), :]),
-            (sources[2].at[b_z], target_z.at[b_z, :, pl.ds(Z_CUT, ATTN_ROWS), :]),
-        )
-
-    def fetch(index, number, source, target):
-        return pltpu.make_async_copy(source, target, local.at[index * 3 + number])
-
-    def pass_on(source, target, send, recv):
-        return pltpu.make_async_remote_copy(
-            src_ref=source,
-            dst_ref=target,
-            send_sem=send,
-            recv_sem=recv,
-            device_id=sibling,
-            device_id_type=MESH,
-        )
-
-    def lend(index, number, source, target):
-        at = index * 3 + number
-        return pass_on(source, target, send_s.at[at], recv_s.at[at])
-
-    def ready(index, number):
-        source, target = pieces(index, 0, part_y, part_z)[number]
-        fetch(index, number, source, target).wait()
-        source, target = pieces(index, 0, in_y, in_z)[number]
-        lend(index, number, source, target).wait_recv()
-
-    def start(kept):
-        for index in range(CTX):
-            for number, pair in enumerate(pieces(index, kept, part_y, part_z)):
-                fetch(index, number, *pair).start()
-
-    def hand(given):
-        for index in range(CTX):
-            for number, pair in enumerate(pieces(index, given, in_y, in_z)):
-                lend(index, number, *pair).start()
-
-    for core in range(2):
-
-        @pl.when(section == core)
-        def _():
-            start(core)
-
-    met(5)
-    for core in range(2):
-
-        @pl.when(section == core)
-        def _():
-            hand(1 - core)
-
-    lower_out, upper_out = lower_out_ref[...], upper_out_ref[...]
-    outputs_ref[section] = jnp.where(first_core, lower_out, upper_out)
-    sent_out[...] = jnp.where(first_core, upper_out, lower_out)
-    lower_grad, upper_grad = lower_grad_ref[...], upper_grad_ref[...]
-    grads_ref[section] = jnp.where(first_core, lower_grad, upper_grad)
-    sent_grad[...] = jnp.where(first_core, upper_grad, lower_grad)
-    swaps = [
-        pass_on(sent_out, outputs_ref.at[section], send_w.at[0], recv_w.at[0]),
-        pass_on(sent_grad, grads_ref.at[section], send_w.at[1], recv_w.at[1]),
-    ]
-    for number in range(3):
-        sums.first(number)
-    for copy in swaps:
-        copy.start()
-    for number in range(3, 6):
-        sums.first(number)
-    for number in range(6):
-        sums.then(number)
-    own = out_ref.at[pl.ds(pl.multiple_of(section * HALF_SHARD, HALF_SHARD), HALF_SHARD)]
-
-    @pl.when(first_core)
-    def _():
-        sums.result(own)
-        copy = pass_on(upper_half_ref, own, send_w.at[2], recv_w.at[2])
-        copy.start()
-        copy.wait()
-
-    @pl.when(section == 1)
-    def _():
-        sums.result(sent_half := rest[8 + 9])
-        own[...] = upper_half_ref[...]
-        copy = pass_on(sent_half, own, send_w.at[2], recv_w.at[2])
-        copy.start()
-        copy.wait()
-
-    for copy in swaps:
-        copy.wait()
-    for index in range(CTX):
-        for number, pair in enumerate(pieces(index, 0, in_y, in_z)):
-            lend(index, number, *pair).wait_send()
-
-
-def by_place(array):
-    return array.reshape((CTX, CTX) + array.shape[1:])
-
-
-def sum_shards(lower_e, lower_a, upper_half, lower_out, upper_out, lower_grad, upper_grad):
-    return pl.pallas_call(
-        sum_shards_kernel,
-        out_shape=(
-            jax.ShapeDtypeStruct((SHARD_ROWS, UNIT), BF16),
-            jax.ShapeDtypeStruct((2, ROWS, D), BF16),
-            jax.ShapeDtypeStruct((2, ROWS, D), F32),
-        ),
-        in_specs=[ANY] * 2 + [VMEM] * 5,
-        out_specs=[VMEM] * 3,
-        scratch_shapes=half_scratch()
-        + [
-            pltpu.VMEM((CTX, CTX, Y_ROWS, UNIT), BF16),
-            pltpu.VMEM((CTX, CTX, Z_ROWS, UNIT), BF16),
-            pltpu.VMEM((ROWS, D), BF16),
-            pltpu.VMEM((ROWS, D), F32),
-        ]
-        + [SEMS((12,))] * 3
-        + [SEMS((3,))] * 2
-        + [SEMS((6,))] * 8
-        + [pltpu.VMEM((HALF_SHARD, UNIT), BF16)],
-        compiler_params=params(8),
-        name="sum_shards",
-    )(by_place(lower_e), by_place(lower_a), upper_half, lower_out, upper_out, lower_grad, upper_grad)
-
-
-def spread_sums_kernel(shard_ref, all_ref, squares_ref, from_y, from_z, *sems):
-    ring_x, ring_y, ring_z = Ring("x"), Ring("y"), Ring("z")
-    far = [
-        one.place(index)
-        for one in (ring_y, ring_z)
-        for index in (one.right, one.left, one.across)
-    ]
-    greet_ids(ring_x.near() + far)
-    all_ref[ring_x.me] = shard_ref[...]
-    met(8)
-    halves = (pl.ds(0, FIRST), pl.ds(FIRST, FIRST))
-    rows = RingGather(ring_x, lambda b, h: all_ref.at[b, halves[h]], sems[0], sems[1])
-    rows.start()
-    rows.forward()
-    rows.finish()
+def shared_squares(all_ref, ring_y, ring_z, spread):
+    from_y, from_z, *sems = spread
 
     def folded(values):
         squared = values * values
@@ -726,24 +559,193 @@
             copy.wait()
         return (slots[0] + slots[1]) + (slots[2] + slots[3])
 
-    tile = shared(ring_y, from_y, sems[2], sems[3], tile)
-    squares_ref[...] = shared(ring_z, from_z, sems[4], sems[5], tile)
-
-
-def spread_sums(shard):
-    slots = pltpu.VMEM((CTX, 8, LANES), F32)
+    tile = shared(ring_y, from_y, sems[0], sems[1], tile)
+    return shared(ring_z, from_z, sems[2], sems[3], tile)
+
+
+def sum_shards_kernel(
+    experts, attn, upper_half_ref, lower_out_ref, upper_out_ref, lower_grad_ref, upper_grad_ref,
+    all_ref, squares_ref, outputs_ref, grads_ref, *rest,
+):
+    halves, rest = rest[:HALF_REFS], rest[HALF_REFS:]
+    in_y, in_z, sent_out, sent_grad, sent_half, local, send_s, recv_s, send_w, recv_w, *rest = rest
+    spread, rest = rest[:8], rest[8:]
+    ring_x = Ring("x")
+    section = lax.axis_index("section")
+    sibling = {"section": 1 - section}
+    first_core = section == 0
+    part_y, part_z = halves[:2]
+
+    def make_y(index, block):
+        ready(index, 0)
+        add_block(part_y, in_y, block)
+
+    def make_z(index, block):
+        ready(index, 1)
+        ready(index, 2)
+        add_block(part_z, in_z, block)
+
+    sums = HalfSums(halves, rest, make_y, make_z)
+    ring_y, ring_z = sums.ring_y, sums.ring_z
+    far = [one.place(one.across) for one in (ring_y, ring_z)]
+    greet_ids([sibling] + ring_x.near() + ring_y.near() + ring_z.near() + far)
+
+    def pieces(index, half, target_y, target_z):
+        b_y, b_z = ring_y.order()[index], ring_z.order()[index]
+        sources = half_sources(half, experts, attn)
+        return (
+            (sources[0].at[:, b_y], target_y.at[b_y]),
+            (sources[1].at[b_z], target_z.at[b_z, :, pl.ds(0, Z_CUT), :]),
+            (sources[2].at[b_z], target_z.at[b_z, :, pl.ds(Z_CUT, ATTN_ROWS), :]),
+        )
+
+    def fetch(index, number, source, target):
+        return pltpu.make_async_copy(source, target, local.at[index * 3 + number])
+
+    def pass_on(source, target, send, recv):
+        return pltpu.make_async_remote_copy(
+            src_ref=source,
+            dst_ref=target,
+            send_sem=send,
+            recv_sem=recv,
+            device_id=sibling,
+            device_id_type=MESH,
+        )
+
+    def lend(index, number, source, target):
+        at = index * 3 + number
+        return pass_on(source, target, send_s.at[at], recv_s.at[at])
+
+    def ready(index, number):
+        source, target = pieces(index, 0, part_y, part_z)[number]
+        fetch(index, number, source, target).wait()
+        source, target = pieces(index, 0, in_y, in_z)[number]
+        lend(index, number, source, target).wait_recv()
+
+    def start(kept):
+        for index in range(CTX):
+            for number, pair in enumerate(pieces(index, kept, part_y, part_z)):
+                fetch(index, number, *pair).start()
+
+    def hand(given):
+        for index in range(CTX):
+            for number, pair in enumerate(pieces(index, given, in_y, in_z)):
+                lend(index, number, *pair).start()
+
+    for core in range(2):
+
+        @pl.when(section == core)
+        def _():
+            start(core)
+
+    met(9)
+    own_at = pl.ds(pl.multiple_of(section * HALF_SHARD, HALF_SHARD), HALF_SHARD)
+    own = all_ref.at[ring_x.me, own_at]
+    cuts = (pl.ds(0, HALF_SHARD), pl.ds(HALF_SHARD, HALF_SHARD))
+    rows = RingGather(ring_x, lambda b, h: all_ref.at[b, cuts[h]], spread[0], spread[1])
+
+    @pl.when(first_core)
+    def _():
+        pass_on(upper_half_ref, own, send_w.at[2], recv_w.at[2]).start()
+
+    @pl.when(section == 1)
+    def _():
+        own[...] = upper_half_ref[...]
+
+    for core in range(2):
+
+        @pl.when(section == core)
+        def _():
+            hand(1 - core)
+
+    lower_out, upper_out = lower_out_ref[...], upper_out_ref[...]
+    outputs_ref[section] = jnp.where(first_core, lower_out, upper_out)
+    sent_out[...] = jnp.where(first_core, upper_out, lower_out)
+    lower_grad, upper_grad = lower_grad_ref[...], upper_grad_ref[...]
+    grads_ref[section] = jnp.where(first_core, lower_grad, upper_grad)
+    sent_grad[...] = jnp.where(first_core, upper_grad, lower_grad)
+    swaps = [
+        pass_on(sent_out, outputs_ref.at[section], send_w.at[0], recv_w.at[0]),
+        pass_on(sent_grad, grads_ref.at[section], send_w.at[1], recv_w.at[1]),
+    ]
+    for number in range(3):
+        sums.first(number)
+
+    @pl.when(section == 1)
+    def _():
+        pass_on(sent_half, own, send_w.at[2], recv_w.at[2]).wait_recv()
+        rows.start()
+
+    for copy in swaps:
+        copy.start()
+    sums.first(3)
+    sums.first(4)
+
+    @pl.when(section == 1)
+    def _():
+        rows.forward()
+
+    sums.first(5)
+    for number in range(6):
+        sums.then(number)
+
+    @pl.when(first_core)
+    def _():
+        sums.result(own)
+        pass_on(upper_half_ref, own, send_w.at[2], recv_w.at[2]).wait()
+        rows.start()
+        rows.forward()
+
+    @pl.when(section == 1)
+    def _():
+        sums.result(sent_half)
+        back = pass_on(sent_half, own, send_w.at[2], recv_w.at[2])
+        back.start()
+        back.wait_send()
+
+    rows.near()
+    rows.far()
+    squares_ref[...] = shared_squares(all_ref, ring_y, ring_z, spread[2:])
+    rows.sent()
+    for copy in swaps:
+        copy.wait()
+    for index in range(CTX):
+        for number, pair in enumerate(pieces(index, 0, in_y, in_z)):
+            lend(index, number, *pair).wait_send()
+
+
+def by_place(array):
+    return array.reshape((CTX, CTX) + array.shape[1:])
+
+
+def sum_shards(lower_e, lower_a, upper_half, lower_out, upper_out, lower_grad, upper_grad):
     return pl.pallas_call(
-        spread_sums_kernel,
+        sum_shards_kernel,
         out_shape=(
             jax.ShapeDtypeStruct((CTX, SHARD_ROWS, UNIT), BF16),
             jax.ShapeDtypeStruct((8, LANES), F32),
+            jax.ShapeDtypeStruct((2, ROWS, D), BF16),
+            jax.ShapeDtypeStruct((2, ROWS, D), F32),
         ),
-        in_specs=[VMEM],
-        out_specs=[VMEM, VMEM],
-        scratch_shapes=[slots, slots, SEMS((6,)), SEMS((6,))] + [SEMS((3,))] * 4,
-        compiler_params=params(9),
-        name="spread_sums",
-    )(shard)
+        in_specs=[ANY] * 2 + [VMEM] * 5,
+        out_specs=[VMEM] * 4,
+        scratch_shapes=half_scratch()
+        + [
+            pltpu.VMEM((CTX, CTX, Y_ROWS, UNIT), BF16),
+            pltpu.VMEM((CTX, CTX, Z_ROWS, UNIT), BF16),
+            pltpu.VMEM((ROWS, D), BF16),
+            pltpu.VMEM((ROWS, D), F32),
+            pltpu.VMEM((HALF_SHARD, UNIT), BF16),
+        ]
+        + [SEMS((12,))] * 3
+        + [SEMS((3,))] * 2
+        + [SEMS((6,))] * 2
+        + [pltpu.VMEM((CTX, 8, LANES), F32)] * 2
+        + [SEMS((3,))] * 4
+        + [SEMS((6,))] * 8,
+        compiler_params=params(8),
+        name="sum_shards",
+    )(by_place(lower_e), by_place(lower_a), upper_half, lower_out, upper_out, lower_grad, upper_grad)
 
 
 def inverse_size(values):
@@ -794,8 +796,9 @@
 
 def attn_forward_kernel(
     layer, length_ref, u_ref, packs_ref, table_ref,
-    a_ref, qkv_ref, mass_ref, attended_ref, residual_ref, b_ref,
-    gains_ref, router_ref, w_ref, back_ref,
+    a_out, qkv_out, mass_out, attended_ref, residual_ref, b_ref,
+    gains_ref, router_ref, w_out, back_out,
+    a_ref, qkv_ref, mass_ref, w_ref, back_ref, out_sem,
     heads_out, heads_w, pack_ref, pack_sem, send_a, recv_a, send_o, recv_o,
 ):
     me, right, left, across = ring()
@@ -806,6 +809,13 @@
     tokens = u_ref[...].astype(F32)
     load.wait()
     unpack(pack_ref, back_ref, heads_w)
+    leaving = [
+        pltpu.make_async_copy(source, target, out_sem.at[index])
+        for index, (source, target) in enumerate(
+            ((back_ref, back_out), (w_ref, w_out), (a_ref, a_out), (qkv_ref, qkv_out), (mass_ref, mass_out))
+        )
+    ]
+    leaving[0].start()
     router_ref[...] = heads_w[:, D - LANES :]
     places = lax.broadcasted_iota(jnp.int32, (8, LANES), 0) + EXPERTS
     picker = jnp.where(places == lax.broadcasted_iota(jnp.int32, (8, LANES), 1), 1.0, 0.0)
@@ -813,6 +823,8 @@
     a_ref[rows_of(me), :] = (tokens * inverse_size(tokens) * gains_ref[0:1, :]).astype(BF16)
     met(3)
     gather_rows(a_ref, send_a, recv_a, lambda: extend(heads_w, w_ref))
+    leaving[1].start()
+    leaving[2].start()
     for block in range(CTX):
         rows = pl.ds(block * ROWS, ROWS)
         table = table_ref[rows, :]
@@ -824,6 +836,7 @@
                 turned = piece * table
                 piece = turned + pltpu.roll(turned, WIDE // 2, 1)
             qkv_ref[rows, lanes] = piece.astype(BF16)
+    leaving[3].start()
 
     def handed(block):
         step = lax.rem(block - me + CTX, CTX)
@@ -857,6 +870,7 @@
         def _():
             handed(block).start()
 
+    leaving[4].start()
     attended_ref[me] = heads_out[me]
     for step in range(1, CTX):
         pltpu.make_async_copy(heads_out.at[0], attended_ref.at[0], recv_o.at[step]).wait()
@@ -867,6 +881,8 @@
     b_ref[...] = (residual * inverse_size(residual) * gains_ref[1:2, :]).astype(BF16)
     for step in range(1, CTX):
         pltpu.make_async_copy(heads_out.at[0], attended_ref.at[0], send_o.at[step]).wait()
+    for copy in leaving:
+        copy.wait()
 
 
 def attn_forward(layer, length, u, packs, table):
@@ -891,8 +907,14 @@
             ANY,
             VMEM,
         ],
-        out_specs=[VMEM] * 10,
+        out_specs=[ANY] * 3 + [VMEM] * 5 + [ANY] * 2,
         scratch_shapes=[
+            pltpu.VMEM((SEQ, D), BF16),
+            pltpu.VMEM((SEQ, EXT), BF16),
+            pltpu.VMEM((HEADS_DEV, SEQ, 1), F32),
+            pltpu.VMEM((D, EXT), BF16),
+            pltpu.VMEM((D, D), BF16),
+            sems((5,)),
             pltpu.VMEM((CTX, ROWS, COLS), BF16),
             pltpu.VMEM((D, D), BF16),
             pltpu.VMEM((16, ATTN_ROWS, UNIT), BF16),
@@ -905,10 +927,24 @@
 
 
 def attn_backward_kernel(
-    hosting, length_ref, u_ref, gains_ref, router_ref, w_ref, back_ref, table_ref,
-    a_ref, qkv_ref, mass_ref, attended_ref, residual_ref, second_ref, gates_ref,
+    hosting, length_ref, u_ref, gains_ref, router_ref, w_in, back_in, table_in,
+    a_in, qkv_in, mass_in, attended_in, residual_ref, second_in, gates_ref,
     delta_ref, db_ref, gate_grad_ref, *rest,
 ):
+    (
+        w_ref, back_ref, table_ref, a_ref, qkv_ref, mass_ref, attended_ref, second_ref, in_sem, *rest,
+    ) = rest[-9:] + rest[:-9]
+    coming = [
+        pltpu.make_async_copy(source, target, in_sem.at[index])
+        for index, (source, target) in enumerate(
+            (
+                (back_in, back_ref), (attended_in, attended_ref), (second_in, second_ref),
+                (qkv_in, qkv_ref), (mass_in, mass_ref), (table_in, table_ref), (w_in, w_ref), (a_in, a_ref),
+            )
+        )
+    ]
+    for copy in coming:
+        copy.start()
     if hosting:
         upper_e, upper_a, lent, *rest = rest
     input_ref, pack_ref, lower_ref = rest[:3]
@@ -974,6 +1010,7 @@
     input_ref[...] = residual_grad
     branch_grad = residual_grad.astype(BF16)
     met(7 if hosting else 3)
+    coming[0].wait()
 
     for block in range(CTX):
         grads_out[block] = dot_nt(branch_grad, back_ref[block * COLS : (block + 1) * COLS, :]).astype(
@@ -993,6 +1030,8 @@
             copy.wait()
         for number in range(3):
             sums.first(number)
+    coming[1].wait()
+    coming[2].wait()
     for block in range(CTX):
         dback_ref[block * COLS : (block + 1) * COLS, :] = dot_tn(
             attended_ref[block], branch_grad
@@ -1004,6 +1043,8 @@
     )
     key_acc[...] = jnp.zeros_like(key_acc)
     value_acc[...] = jnp.zeros_like(value_acc)
+    for copy in coming[3:]:
+        copy.wait()
     for step in range(1, CTX):
         pltpu.make_async_copy(grads_out.at[0], grads_in.at[0], recv_o.at[step]).wait()
     for step in range(1, CTX):
@@ -1138,10 +1179,15 @@
             pltpu.VMEM((CTX, CTX, Z_ROWS, UNIT), BF16),
             sems((11,)),
         ] + [sems((6,))] * 8
+    late = (3, 4, 5, 6, 7, 8, 9, 11)
+    specs = [ANY if index in late else VMEM for index in range(len(arrays))]
+    for index in late:
+        scratch.append(pltpu.VMEM(arrays[index].shape, arrays[index].dtype))
+    scratch.append(sems((len(late),)))
     return pl.pallas_call(
         functools.partial(attn_backward_kernel, bool(upper)),
         out_shape=tuple(out_shape),
-        in_specs=[SMEM] + [VMEM] * len(arrays) + [ANY] * len(upper),
+        in_specs=[SMEM] + specs + [ANY] * len(upper),
         out_specs=[VMEM] * len(out_shape),
         scratch_shapes=scratch,
         compiler_params=params(4 if upper else 3),
@@ -1311,7 +1357,7 @@
     else:
         db_ref, gate_grad_ref, dw_ref, *rest = rest
     (
-    delta, acc, gate_acc, slot_grad, hidden, acted, win, wout, staged, rows_out, rows_in,
+    delta, acc, gate_acc, slot_grad, hidden, acted, win, wout, staged, rows_out, rows_in, b_turned,
     w_sem, kept_sem, dw_sem, send_d, recv_d, send_g, recv_g,
     part, top_in, bottom_in, from_left, from_right, send, recv,
     ) = rest
@@ -1420,6 +1466,7 @@
         ring, part, (top_in, bottom_in), from_left, from_right, send, recv, HALF, from_sum
     )
     sums.stage(4)
+    b_turned[...] = b_ref[...].reshape(SEQ, D).T
     rows.forward()
     rows.near()
     sums.stage(1)
@@ -1427,7 +1474,6 @@
     rows.far()
     sums.stage(0)
     stores = []
-    b_all = b_ref[...].reshape(SEQ, D)
     for group in range(GROUPS):
         slot = group % 2
         if group == 1:
@@ -1435,7 +1481,7 @@
         if group >= 2:
             stores[group - 2].wait()
         for inner in range(GROUP):
-            staged[slot, inner, :D, :] = dot_tn(b_all, hidden[group * GROUP + inner]).astype(BF16)
+            staged[slot, inner, :D, :] = dot(b_turned[...], hidden[group * GROUP + inner]).astype(BF16)
         whole_out = dot_tn(
             acted[:, group * GROUP_UNITS : (group + 1) * GROUP_UNITS], slot_grad[...]
         ).astype(BF16)
@@ -1498,6 +1544,7 @@
             pltpu.VMEM((2, GROUP, EXPERT_ROWS, UNIT), BF16),
             pltpu.VMEM((CTX, 8, ROWS), F32),
             pltpu.VMEM((3, 8, ROWS), F32),
+            pltpu.VMEM((D, SEQ), BF16),
             SEMS((5 * GROUPS,)),
             SEMS((CTX,)),
             SEMS((2,)),
@@ -1612,20 +1659,23 @@
                 wide[:, at : at + COLS] = heads[:, part * COLS : (part + 1) * COLS]
         wide[:, 3 * D :] = jnp.concatenate(back, axis=1)
         small = small[:, LANES:]
-        places = lax.broadcasted_iota(jnp.int32, (8, LANES), 0) + EXPERTS
+        places = lax.broadcasted_iota(jnp.int32, (8, LANES), 0)
         picker = jnp.where(places == lax.broadcasted_iota(jnp.int32, (8, LANES), 1), 1.0, 0.0)
-        gain_rows = lax.dot_general(
+        turned_rows = lax.dot_general(
             picker, small, NT, precision=EXACT, preferred_element_type=F32
         )
-        updated(fixes_ref, gain_rows[:2], factor_of(squares_ref, 0), gain_old, gain_new, GAIN_RATE)
-        updated(
-            fixes_ref,
-            small[:, :EXPERTS],
-            factor_of(squares_ref, 2),
-            router_old,
-            router_new,
-            RATE_FACTOR / (D // 4) ** 0.5,
-        )
+        gain_rows = turned_rows[EXPERTS : EXPERTS + 2]
+        updated(fixes_ref, gain_rows, factor_of(squares_ref, 0), gain_old, gain_new, GAIN_RATE)
+        for expert in range(EXPERTS):
+            updated(
+                fixes_ref,
+                turned_rows[expert : expert + 1],
+                factor_of(squares_ref, 2),
+                router_old,
+                router_new,
+                RATE_FACTOR / (D // 4) ** 0.5,
+                expert,
+            )
         norms_ref[...] = jnp.sqrt(squares_ref[...])
         for part in range(4):
             lanes = (slice(None), slice(part * D, (part + 1) * D))
@@ -1646,7 +1696,7 @@
     in_spec = pl.BlockSpec((in_rows, units), lambda i: (i, 0))
     out_spec = pl.BlockSpec((1, units, D), lambda i: (i, 0, 0))
     attn_spec = whole(attn_shape)
-    gain_shape, router_shape = (2, 48), (48, EXPERTS)
+    gain_shape, router_shape = (2, 48), (EXPERTS, 1, 48)
 
     def five(shape):
         return [jax.ShapeDtypeStruct(shape, F32)] * 4 + [jax.ShapeDtypeStruct(shape, BF16)]
@@ -1687,7 +1737,7 @@
         *(array.reshape(out_shape) for array in out_old),
         *(array.reshape(attn_shape) for array in attn_old),
         *(array.reshape(gain_shape) for array in gain_old),
-        *(array.reshape(router_shape) for array in router_old),
+        *(array.transpose(2, 0, 1) for array in router_old),
     )
 
 
@@ -1753,10 +1803,9 @@
     lower_experts, (lower_grad, lower_attn, _, upper_half) = layer_backward(
         experts[0], lower_saved, lower_seed, length, table, (upper_experts, upper_attn)
     )
-    shard_sum, layer_outputs, input_grads = sum_shards(
+    sums_all, squares, layer_outputs, input_grads = sum_shards(
         lower_experts, lower_attn, upper_half, lower_out, upper_out, lower_grad, upper_grad
     )
-    sums_all, squares = spread_sums(shard_sum)
     step_value = step_count[0].astype(F32)
     fixes = jnp.stack([1.0 - BETA_ONE**step_value, 1.0 - BETA_TWO**step_value])
     changed = update(
@@ -1777,7 +1826,7 @@
         (layer_outputs[None], input_grads[None])
         + shaped(15, norm_gains)
         + shaped(10, attn_weight)
-        + shaped(20, router_weight)
+        + tuple(array.transpose(1, 2, 0) for array in changed[20:25])
         + shaped(0, expert_in)
         + shaped(5, expert_out)
         + (changed[25][:1, :5],)

time: 508 us -> 476 us (0.937)
  Pallas kernels: 464 us -> 439 us
  local copies, waits for them, and re-layouts: 20.2 us -> 13.2 us
    pallas_call x2 -> x1, Pallas kernels: 83.6 us -> 67.6 us  [sum_shards(): pl.pallas_call(sum_shards_kernel, out_shape=(jax.ShapeDtypeStruct((CTX, S...]
    unnamed x37 -> x25, local copies, waits for them, and re-layouts: 10.6 us -> 3.6 us
where the time goes in v5:
time: 476 us; the launch traced here: 473 us
  Pallas kernels  439 us (92%)
  between operations  15.4 us (3%)
  local copies, waits for them, and re-layouts  13.2 us (3%)
    pallas_call x2, Pallas kernels, attn_backward(): pl.pallas_call(functools.partial(attn_backward_kernel, bool(upper)), out_...  89.3 us
    pallas_call x2, Pallas kernels, ffn_backward(): pl.pallas_call(functools.partial(ffn_backward_kernel, bool(upper)), out_s...  85.2 us
    pallas_call x2, Pallas kernels, ffn_forward(): pl.pallas_call(ffn_forward_kernel, out_shape=(jax.ShapeDtypeStruct((ROWS,...  72 us
    pallas_call x2, Pallas kernels, attn_forward(): pl.pallas_call(functools.partial(attn_forward_kernel, layer), out_shape=(...  71.8 us
    pallas_call x1, Pallas kernels, sum_shards(): pl.pallas_call(sum_shards_kernel, out_shape=(jax.ShapeDtypeStruct((CTX, S...  67.6 us
    pallas_call x1, Pallas kernels, gather_shards(): pl.pallas_call(gather_shards_kernel, out_shape=(jax.ShapeDtypeStruct((2,...  35.2 us
    pallas_call x1, Pallas kernels, update(): pl.pallas_call(update_kernel, grid=(CTX,), out_shape=five(in_shape) + fiv...  18 us
  transfers between devices with their start and end apart: 3, of which 1 were waited for; matrix products, arithmetic and copies ran while one was open for 2% of the time, Pallas kernels for 30%

profile of v5, /device:TPU:0, one launch (start us, length us, event | category | flops | bytes accessed | tf_op | source)
XLA Modules:
  0.0 473.2 jit_solution(6558963776830002516)
XLA Ops:
  7.2 0.0 copy-start
  7.2 0.0 all-gather.5.cloned.1.call-start
  7.3 1.5 dynamic-slice_convert_fusion
  8.8 0.2 slice.55
  9.0 1.0 fusion
  10.0 0.0 copy-start.6
  10.0 0.0 copy-start.8
  10.0 0.1 copy.82
  10.1 0.0 copy-start.9
  10.1 0.0 copy-start.7
  10.1 0.1 bitcast_select_fusion.2
  10.2 0.1 collective-permute-start
  10.3 1.6 collective-permute-done
  11.9 0.9 broadcast_select_fusion
  12.8 0.0 all-gather.5.cloned.1.call-update
  12.8 0.0 all-gather.7.cloned.1.call-start
  12.9 0.7 all-gather.7.cloned.1.call-update
  13.6 0.9 slice.62
  14.5 0.0 copy-done.6
  14.5 0.1 copy.61
  14.6 0.0 copy-done.8
  14.6 0.1 copy.62
  14.7 1.0 fusion.3
  15.8 0.1 concatenate.7
  15.9 0.2 convert_element_type.30
  16.1 0.7 copy.63
  17.5 0.0 copy-done.9
  17.5 0.6 dynamic_slice.33.length_ref
  18.1 0.0 copy-done.7
  18.1 0.6 pad.4.code_ref
  18.8 35.2 %gather_shards.1 = (bf16[2,4,4,288,256]{4,3,2,1,0:T(8,128)(2,1)}, f32[2,4,8,256]{3,2,1,0:T(8,128)}) custom-call(bf16[288,256]{1,0:T(8,128)(2,1)} %bitcast.115, f32[8,256]{1,0:T(8,128)} %pad.4.code_ref), custom_call_target="tpu_custom_call" | custom-call | tf_op jit(solution)/shard_map/gather_shards/pallas_call | solution.py:419
  54.0 0.0 copy-done
  54.0 0.8 dynamic-slice_bitcast_fusion.u_ref
  54.8 0.0 copy-start.5
  54.8 0.0 copy-start.4
  54.8 37.6 %attn_forward.2 = (bf16[1024,768]{1,0:T(8,128)(2,1)}, bf16[1024,1152]{1,0:T(8,128)(2,1)}, f32[3,1024,1]{2,1,0:T(8,128)}, bf16[4,256,192]{2,1,0:T(8,128)(2,1)}, f...) custom-call(s32[1]{0:T(128)} %dynamic_slice.33.length_ref, ...), custom_call_target="tpu_custom_call" | custom-call | tf_op jit(solution)/shard_map/attn_forward/pallas_call | solution.py:890
  92.4 0.7 add_compare_fusion
  93.1 0.6 pad_maximum_fusion.3.fixes_ref
  93.7 0.0 copy-done.5
  93.7 0.6 slice_bitcast_fusion
  94.3 0.0 copy-done.4
  94.3 0.9 bitcast_select_fusion.delta_own_ref.delta_ref
  95.2 0.0 all-gather.5.cloned.1.call-done
  95.2 36.6 %ffn_forward.2 = (bf16[256,768]{1,0:T(8,128)(2,1)}, bf16[4,256,768]{2,1,0:T(8,128)(2,1)}, f32[256,128]{1,0:T(8,128)}, f32[4,256,1]{2,1,0:T(8,128)}, bf16[4,16,256,256]{3,2,1,0:T(8,128)(2,1)}) custom-call(bf16[256,768]{1,0:T(8,128)(2,1)} %get-tuple-element.104.b_own_ref.second_in, f32[256,768]{1,0:T(8,128)} %get-tuple-element.105.residual_ref, ...), custom_call_target="tpu_custom_call" | custom-call | tf_op jit(solution)/shard_map/ffn_forward/pallas_call | solution.py:1324
  131.8 34.1 %attn_forward.3 = (bf16[1024,768]{1,0:T(8,128)(2,1)}, bf16[1024,1152]{1,0:T(8,128)(2,1)}, f32[3,1024,1]{2,1,0:T(8,128)}, bf16[4,256,192]{2,1,0:T(8,128)(2,1)}, f...) custom-call(s32[1]{0:T(128)} %dynamic_slice.33.length_ref, ...), custom_call_target="tpu_custom_call" | custom-call | tf_op jit(solution)/shard_map/attn_forward/pallas_call | solution.py:890
  166.0 0.0 all-gather.7.cloned.1.call-done
  166.0 35.4 %ffn_forward.3 = (bf16[256,768]{1,0:T(8,128)(2,1)}, bf16[4,256,768]{2,1,0:T(8,128)(2,1)}, f32[256,128]{1,0:T(8,128)}, f32[4,256,1]{2,1,0:T(8,128)}, bf16[4,16,256,256]{3,2,1,0:T(8,128)(2,1)}) custom-call(bf16[256,768]{1,0:T(8,128)(2,1)} %get-tuple-element.120.b_own_ref.second_in, f32[256,768]{1,0:T(8,128)} %get-tuple-element.119.residual_ref, ...), custom_call_target="tpu_custom_call" | custom-call | tf_op jit(solution)/shard_map/ffn_forward/pallas_call | solution.py:1324
  201.4 41.2 %ffn_backward.2 = (f32[256,768]{1,0:T(8,128)}, f32[256,128]{1,0:T(8,128)}, bf16[16,1152,256]{2,1,0:T(8,128)(2,1)}) custom-call(bf16[4,256,768]{2,1,0:T(8,128)(2,1)} %get-tuple-element.122.b_ref, f32[4,256,1]{2,1,0:T(8,128)} %get-tuple-element.123.gate_ref, bf16[256,768]{1,0:T(8,128)(2,1)} %bitcast_select_fusion.delta_own_ref.delta_ref, ...), custom_call_target="tpu_custom_call" | custom-call | tf_op jit(solution)/shard_map/ffn_backward/pallas_call | solution.py:1530
  242.6 35.6 %attn_backward.2 = (f32[256,768]{1,0:T(8,128)}, bf16[16,288,256]{2,1,0:T(8,128)(2,1)}, bf16[256,768]{1,0:T(8,128)(2,1)}) custom-call(s32[1]{0:T(128)} %dynamic_slice.33.length_ref, bf16[256,768]{1,0:T(8,128)(2,1)} %get-tuple-element.110.u_ref.lower_out_ref, f32[8,768]{1,0:T(8,128)} %get-tuple-element.111.gains_ref, ...), custom_call_target="tpu_custom_call" | custom-call | tf_op jit(solution)/shard_map/attn_backward/pallas_call | solution.py:1187
  278.2 44.0 %ffn_backward.3 = (f32[256,768]{1,0:T(8,128)}, f32[256,128]{1,0:T(8,128)}, bf16[16,1152,256]{2,1,0:T(8,128)(2,1)}, bf16[16,720,256]{2,1,0:T(8,128)(2,1)}) custom-call(bf16[4,256,768]{2,1,0:T(8,128)(2,1)} %get-tuple-element.108.b_ref, f32[4,256,1]{2,1,0:T(8,128)} %get-tuple-element.109.gate_ref, bf16[256,768]{1,0:T(8,128)(2,1)} %get-tuple-element.127.delta_own_ref.delta_ref, ...), custom_call_target="tpu_custom_call" | custom-call | tf_op jit(solution)/shard_map/ffn_backward/pallas_call | solution.py:1530
  322.2 53.7 %attn_backward.3 = (f32[256,768]{1,0:T(8,128)}, bf16[16,288,256]{2,1,0:T(8,128)(2,1)}, bf16[256,768]{1,0:T(8,128)(2,1)}, bf16[720,256]{1,0:T(8,128)(2,1)}) custom-call(s32[1]{0:T(128)} %dynamic_slice.33.length_ref, bf16[256,768]{1,0:T(8,128)(2,1)} %dynamic-slice_bitcast_fusion.u_ref, f32[8,768]{1,0:T(8,128)} %get-tuple-element.132.gains_ref, ...), custom_call_target="tpu_custom_call" | custom-call | tf_op jit(solution)/shard_map/attn_backward/pallas_call | solution.py:1187
  375.8 67.6 %sum_shards.1 = (bf16[4,1440,256]{2,1,0:T(8,128)(2,1)}, f32[8,128]{1,0:T(8,128)}, bf16[2,256,768]{2,1,0:T(8,128)(2,1)}, f32[2,256,768]{2,1,0:T(8,128)}) custom-call(bf16[4,4,1152,256]{3,2,1,0:T(8,128)(2,1)} %bitcast.93, bf16[4,4,288,256]{3,2,1,0:T(8,128)(2,1)} %bitcast.104, bf16[720,256]{1,0:T(8,128)(2,1)} %get-tuple-element.144.upper_half_ref, ...), custom_call_target="tpu_custom_call" | custom-call | tf_op jit(solution)/shard_map/sum_shards/pallas_call | solution.py:722
  443.5 0.0 copy-start.3
  443.5 18.0 %update.1 = (f32[6144,128]{1,0:T(8,128)}, f32[6144,128]{1,0:T(8,128)}, f32[6144,128]{1,0:T(8,128)}, f32[6144,128]{1,0:T(8,128)}, bf16[6144,128]{1,0:T(8,128)(2,1...) custom-call(f32[2]{0:T(128)} %pad_maximum_fusion.3.fixes_ref, ...), custom_call_target="tpu_custom_call" | custom-call | tf_op jit(solution)/shard_map/update/pallas_call | solution.py:1704
  461.5 0.0 copy-start.2
  461.5 1.4 copy.66
  462.9 1.2 slice.53
  464.1 0.0 copy-start.1
  464.1 0.0 copy-done.3
  464.1 0.9 copy.86
  464.9 0.0 copy-done.2
  464.9 1.1 copy.87
  466.1 0.0 copy-done.1
  (6 shorter events, 0.0 us)
Async XLA Ops:
  7.2 46.8 %copy-start = (bf16[2,256,768]{2,1,0:T(8,128)(2,1)S(1)}, bf16[2,256,768]{2,1,0:T(8,128)(2,1)}, u32[]{:S(2)}) copy-start(bf16[2,256,768]{2,1,0:T(8,128)(2,1)} %param.21) | copy-start | bytes 2359300
  7.2 87.9 %all-gather.5.cloned.1.call-start = ((), (), s32[]{:S(2)}) async-start(), calls=%async_computation | async-start | bytes 9732096 | tf_op jit(solution)/shard_map/all_gather | solution.py:1789
  10.0 4.5 copy-start.6
  10.0 4.6 copy-start.8
  10.1 7.4 %copy-start.9 = (s32[2]{0:T(128)S(1)}, s32[2]{0:T(128)}, u32[]{:S(2)}) copy-start(s32[2]{0:T(128)} %param.23) | copy-start | bytes 28
  10.1 8.0 %copy-start.7 = (s32[1,2,256,2]{2,3,1,0:T(2,128)S(1)}, s32[1,2,256,2]{2,3,1,0:T(2,128)}, u32[]{:S(2)}) copy-start(s32[1,2,256,2]{2,3,1,0:T(2,128)} %param.24) | copy-start | bytes 12292
  10.2 1.7 collective-permute-start
  12.8 153.2 %all-gather.7.cloned.1.call-start = ((), (), s32[]{:S(2)}) async-start(), calls=%async_computation.1 | async-start | bytes 9732096 | tf_op jit(solution)/shard_map/all_gather | solution.py:1789
  54.8 38.9 %copy-start.5 = (f32[2,4,8,256]{3,2,1,0:T(8,128)S(1)}, f32[2,4,8,256]{3,2,1,0:T(8,128)}, u32[]{:S(2)}) copy-start(f32[2,4,8,256]{3,2,1,0:T(8,128)} %get-tuple-element.106) | copy-start | bytes 196612
  54.8 39.5 %copy-start.4 = (bf16[2,256,768]{2,1,0:T(8,128)(2,1)S(1)}, bf16[2,256,768]{2,1,0:T(8,128)(2,1)}, u32[]{:S(2)}) copy-start(bf16[2,256,768]{2,1,0:T(8,128)(2,1)} %param.22) | copy-start | bytes 2359300
  443.5 20.6 %copy-start.3 = (bf16[2,256,768]{2,1,0:T(8,128)(2,1)S(1)}, bf16[2,256,768]{2,1,0:T(8,128)(2,1)}, u32[]{:S(2)}) copy-start(bf16[2,256,768]{2,1,0:T(8,128)(2,1)} %get-tuple-element.148) | copy-start | bytes 2359300
  461.5 3.5 copy-start.2
  464.1 2.0 copy-start.1
Sparse Core Ops, SparseCore 0:
  12.9 60.3 all-gather.4
  76.2 54.9 all-gather.6

commit v6 on v5

--- a/solution.py
+++ b/solution.py
@@ -1560,6 +1560,216 @@
     )(b_all, gate_col, delta_own, kept, weights, *upper)
 
 
+def ffn_both_kernel(
+    b_own_ref, residual_ref, codes_ref, router_ref, delta_own_ref, w_ref,
+    y_ref, gates_ref, db_ref, gate_grad_ref, dw_ref,
+    b_ref, gate_ref, delta, acc, slot_grad, hidden, acted, win, wout, staged, rows_out, rows_in, b_turned,
+    w_sem, dw_sem, send_b, recv_b, send_d, recv_d, send_g, recv_g, *sum_refs,
+):
+    ring = Ring("x")
+    peers = (ring.right, ring.left, ring.across)
+    greet_ids([ring.place(peer) for peer in peers])
+    loads = weight_copies(w_ref, win, wout, w_sem)
+    for group in loads:
+        for copy in group:
+            copy.start()
+    b_ref[ring.me] = b_own_ref[...]
+    delta[ring.me] = delta_own_ref[...]
+    met(3)
+    halves = (pl.ds(0, HALF), pl.ds(HALF, HALF))
+    rows = RingGather(ring, lambda b, h: b_ref.at[b, halves[h]], send_b, recv_b)
+    seeds = RingGather(ring, lambda b, h: delta.at[b, halves[h]], send_d, recv_d)
+    rows.start()
+    section = lax.axis_index("section")
+    lanes = lax.broadcasted_iota(jnp.int32, (ROWS, LANES), 1)
+    code_picker = jnp.where(lax.broadcasted_iota(jnp.int32, (8, LANES), 0) == section, 1.0, 0.0)
+    row_picker = jnp.where(lax.broadcasted_iota(jnp.int32, (8, LANES), 0) == ring.me, 1.0, 0.0)
+    handed = [
+        ring.copy(rows_out.at[peer], rows_in.at[index], send_g.at[index], recv_g.at[index], peer)
+        for index, peer in enumerate(peers)
+    ]
+    part_y, part_b = sum_refs[0], sum_refs[7]
+
+    def forward(index, block):
+        at = rows_of(block)
+        b_rows = b_ref[block]
+        for group in range(GROUPS):
+            if index == 0:
+                for copy in loads[group]:
+                    copy.wait()
+            acts = []
+            for inner in range(GROUP):
+                shard = group * GROUP + inner
+                values = dot(b_rows, win[shard])
+                hidden[shard, at, :] = values.astype(BF16)
+                gate_part = values[:, :LANES]
+                acts.append(
+                    (gate_part / (1.0 + jnp.exp(-gate_part)) * values[:, LANES:]).astype(BF16)
+                )
+            terms = dot(jnp.concatenate(acts, axis=1), wout_group(wout, group))
+            acc[...] = terms if group == 0 else acc[...] + terms
+        logits = dot(b_rows, router_ref[...])
+        codes = lax.dot_general(
+            codes_ref[block], code_picker, TN, precision=EXACT, preferred_element_type=F32
+        )
+        named = (lanes < EXPERTS) & (lanes != jnp.round(codes).astype(jnp.int32))
+        chosen = jnp.where(named, logits, MASK_VALUE)
+        raw = jnp.where(named, jnp.exp(chosen - jnp.max(chosen, axis=1, keepdims=True)), 0.0)
+        gates = raw / jnp.sum(raw, axis=1, keepdims=True)
+        if index == 0:
+            gates_ref[...] = gates
+        gates = jnp.where(lanes == EXPERTS, 1.0, gates)
+        gate = jnp.sum(jnp.where(lanes == ring.me, gates, 0.0), axis=1, keepdims=True)
+        gate_ref[block] = gate
+        part_y[block] = (acc[...] * gate).astype(BF16)
+
+    def backward(index, block):
+        at = rows_of(block)
+        gate = gate_ref[block]
+        delta_rows = delta[block]
+        slot_grad[at, :] = (delta_rows.astype(F32) * gate).astype(BF16)
+        gate_sum = jnp.zeros((ROWS, LANES), F32)
+        for group in range(GROUPS):
+            act_grad_all = dot_nt(delta_rows, wout_group(wout, group))
+            second_grad = None
+            for inner in range(GROUP):
+                shard = group * GROUP + inner
+                values = hidden[shard, at, :].astype(F32)
+                gate_part = values[:, :LANES]
+                up_part = values[:, LANES:]
+                act_grad = act_grad_all[:, inner * LANES : (inner + 1) * LANES]
+                sigmoid = 1.0 / (1.0 + jnp.exp(-gate_part))
+                silu = gate_part * sigmoid
+                act = (silu * up_part).astype(BF16)
+                acted[at, shard * LANES : (shard + 1) * LANES] = act
+                gate_sum += act.astype(F32) * act_grad
+                act_grad = act_grad * gate
+                gate_grad = act_grad * up_part * (sigmoid * (1.0 + gate_part * (1.0 - sigmoid)))
+                pair = jnp.concatenate([gate_grad, act_grad * silu], axis=1).astype(BF16)
+                hidden[shard, at, :] = pair
+                term = dot_nt(pair, win[shard])
+                second_grad = term if second_grad is None else second_grad + term
+            acc[...] = second_grad if group == 0 else acc[...] + second_grad
+        part_b[block] = acc[...].astype(BF16)
+        rows_out[block] = lax.dot_general(
+            row_picker, gate_sum, NT, precision=EXACT, preferred_element_type=F32
+        )
+        if index > 0:
+            handed[index - 1].start()
+
+    def summing(refs, make):
+        part, top_in, bottom_in, from_left, from_right, send, recv = refs
+        return RingSum(
+            ring, part, (top_in, bottom_in), from_left, from_right, send, recv, HALF,
+            lambda position, block: make((3, 1, 2, 0)[position], block),
+        )
+
+    ahead = summing(sum_refs[:7], forward)
+    behind = summing(sum_refs[7:], backward)
+    ahead.stage(4)
+    rows.forward()
+    rows.near()
+    seeds.start()
+    ahead.stage(1)
+    ahead.stage(2)
+    rows.far()
+    ahead.stage(0)
+    seeds.forward()
+    b_turned[...] = b_ref[...].reshape(SEQ, D).T
+    behind.stage(4)
+    ahead.stage(3)
+    seeds.near()
+    behind.stage(1)
+    behind.stage(2)
+    seeds.far()
+    behind.stage(0)
+    ahead.stage(5)
+    y_ref[...] = (residual_ref[...] + ahead.total()).astype(BF16)
+    stores = []
+    for group in range(GROUPS):
+        slot = group % 2
+        if group == 1:
+            behind.stage(3)
+        if group >= 2:
+            stores[group - 2].wait()
+        for inner in range(GROUP):
+            staged[slot, inner, :D, :] = dot(b_turned[...], hidden[group * GROUP + inner]).astype(BF16)
+        whole_out = dot_tn(
+            acted[:, group * GROUP_UNITS : (group + 1) * GROUP_UNITS], slot_grad[...]
+        ).astype(BF16)
+        for inner in range(GROUP):
+            for piece in range(D // UNIT):
+                at = D + piece * LANES
+                staged[slot, inner, at : at + LANES, :] = whole_out[
+                    inner * LANES : (inner + 1) * LANES, piece * UNIT : (piece + 1) * UNIT
+                ]
+        stores.append(
+            pltpu.make_async_copy(
+                staged.at[slot], dw_ref.at[pl.ds(group * GROUP, GROUP)], dw_sem.at[slot]
+            )
+        )
+        stores[-1].start()
+    behind.stage(5)
+    db_ref[...] = behind.total()
+    for copy in handed:
+        copy.wait()
+    rows_all = rows_out[ring.me] + rows_in[0] + rows_in[1] + rows_in[2]
+    diagonal = jnp.where(
+        lax.broadcasted_iota(jnp.int32, (8, LANES), 0)
+        == lax.broadcasted_iota(jnp.int32, (8, LANES), 1),
+        1.0,
+        0.0,
+    )
+    gate_grad_ref[...] = lax.dot_general(
+        rows_all, diagonal, TN, precision=EXACT, preferred_element_type=F32
+    )
+    rows.sent()
+    seeds.sent()
+    stores[2].wait()
+    stores[3].wait()
+
+
+def ffn_both(b_own, residual, codes, router, delta_own, weights):
+    return pl.pallas_call(
+        ffn_both_kernel,
+        out_shape=(
+            jax.ShapeDtypeStruct((ROWS, D), BF16),
+            jax.ShapeDtypeStruct((ROWS, LANES), F32),
+            jax.ShapeDtypeStruct((ROWS, D), F32),
+            jax.ShapeDtypeStruct((ROWS, LANES), F32),
+            jax.ShapeDtypeStruct((16, EXPERT_ROWS, UNIT), BF16),
+        ),
+        in_specs=[VMEM] * 5 + [ANY],
+        out_specs=[VMEM] * 4 + [ANY],
+        scratch_shapes=[
+            pltpu.VMEM((CTX, ROWS, D), BF16),
+            pltpu.VMEM((CTX, ROWS, 1), F32),
+            pltpu.VMEM((CTX, ROWS, D), BF16),
+            pltpu.VMEM((ROWS, D), F32),
+            pltpu.VMEM((SEQ, D), BF16),
+            pltpu.VMEM((16, SEQ, UNIT), BF16),
+            pltpu.VMEM((SEQ, FFN), BF16),
+            pltpu.VMEM((16, D, UNIT), BF16),
+            pltpu.VMEM((16, LANES, D), BF16),
+            pltpu.VMEM((2, GROUP, EXPERT_ROWS, UNIT), BF16),
+            pltpu.VMEM((CTX, 8, ROWS), F32),
+            pltpu.VMEM((3, 8, ROWS), F32),
+            pltpu.VMEM((D, SEQ), BF16),
+            SEMS((5 * GROUPS,)),
+            SEMS((2,)),
+            SEMS((6,)),
+            SEMS((6,)),
+            SEMS((6,)),
+            SEMS((6,)),
+            SEMS((3,)),
+            SEMS((3,)),
+        ]
+        + SUM_SCRATCH * 2,
+        compiler_params=params(6),
+        name="ffn_both",
+    )(b_own, residual, codes, router, delta_own, weights)
+
+
 def rotary_table():
     half_dim = HEAD_DIM // 2
     steps = 2.0 * np.arange(half_dim, dtype=np.float32) / np.float32(HEAD_DIM)
@@ -1569,30 +1779,34 @@
     return jnp.asarray(np.concatenate([cosine, cosine, sine, sine], axis=1), F32)
 
 
-def layer_forward(layer, packs, experts, tokens_in, length, codes, table):
+def lower_forward(packs, experts, tokens_in, length, codes, table):
     a_all, qkv, mass, attended, residual, second, *unpacked = attn_forward(
-        layer, length, tokens_in, packs, table
+        0, length, tokens_in, packs, table
     )
     output, b_all, gates, gate_col, kept = ffn_forward(
         second, residual, codes, unpacked[1], experts
     )
-    return output, (
-        tokens_in, a_all, qkv, mass, attended, residual, second, b_all, gates, gate_col, kept, unpacked,
-    )
-
-
-def layer_backward(experts, saved, delta_own, length, table, upper=()):
-    (
-        tokens_in, a_all, qkv, mass, attended, residual, second, b_all, gates, gate_col, kept, unpacked,
-    ) = saved
-    db, gate_grads, dexperts, *lent = ffn_backward(b_all, gate_col, delta_own, kept, experts, upper)
+    late = (a_all, qkv, mass, attended, residual, second, gates)
+    return output, (tokens_in, b_all, gate_col, kept, unpacked, late)
+
+
+def upper_layer(packs, experts, tokens_in, length, codes, table, seed):
+    a_all, qkv, mass, attended, residual, second, *unpacked = attn_forward(
+        1, length, tokens_in, packs, table
+    )
+    output, gates, db, gate_grads, dexperts = ffn_both(
+        second, residual, codes, unpacked[1], seed, experts
+    )
+    late = (a_all, qkv, mass, attended, residual, second, gates)
+    results = attn_backward(length, (tokens_in, *unpacked, table, *late, seed, db, gate_grads))
+    return output, dexperts, results
+
+
+def lower_backward(experts, saved, delta_own, length, table, upper):
+    tokens_in, b_all, gate_col, kept, unpacked, late = saved
+    db, gate_grads, dexperts, lent = ffn_backward(b_all, gate_col, delta_own, kept, experts, upper)
     results = attn_backward(
-        length,
-        (
-            tokens_in, *unpacked, table, a_all, qkv, mass,
-            attended, residual, second, gates, delta_own, db, gate_grads,
-        ),
-        tuple(upper) + tuple(lent),
+        length, (tokens_in, *unpacked, table, *late, delta_own, db, gate_grads), (*upper, lent)
     )
     return dexperts, results
 
@@ -1609,7 +1823,7 @@
     mean_new = BETA_ONE * mean_ref[at] + (1.0 - BETA_ONE) * clipped
     square_new = BETA_TWO * square_ref[at] + (1.0 - BETA_TWO) * clipped * clipped
     master_new = master - learn_rate * (
-        mean_new / fixes_ref[0] / (jnp.sqrt(square_new / fixes_ref[1]) + ADAM_EPS) + DECAY_RATE * master
+        mean_new * fixes_ref[0] / (jnp.sqrt(square_new * fixes_ref[1]) + ADAM_EPS) + DECAY_RATE * master
     )
     gradient_ref[at] = gradient
     mean_new_ref[at] = mean_new
@@ -1795,19 +2009,18 @@
     seed = jnp.where((positions < length[0])[:, None], seed, jnp.zeros_like(seed))
     table = rotary_table()
 
-    lower_out, lower_saved = layer_forward(0, packs, experts[0], tokens, length, codes[0], table)
-    upper_out, upper_saved = layer_forward(1, packs, experts[1], lower_out, length, codes[1], table)
-    upper_experts, (upper_grad, upper_attn, lower_seed) = layer_backward(
-        experts[1], upper_saved, seed, length, table
-    )
-    lower_experts, (lower_grad, lower_attn, _, upper_half) = layer_backward(
+    lower_out, lower_saved = lower_forward(packs, experts[0], tokens, length, codes[0], table)
+    upper_out, upper_experts, (upper_grad, upper_attn, lower_seed) = upper_layer(
+        packs, experts[1], lower_out, length, codes[1], table, seed
+    )
+    lower_experts, (lower_grad, lower_attn, _, upper_half) = lower_backward(
         experts[0], lower_saved, lower_seed, length, table, (upper_experts, upper_attn)
     )
     sums_all, squares, layer_outputs, input_grads = sum_shards(
         lower_experts, lower_attn, upper_half, lower_out, upper_out, lower_grad, upper_grad
     )
     step_value = step_count[0].astype(F32)
-    fixes = jnp.stack([1.0 - BETA_ONE**step_value, 1.0 - BETA_TWO**step_value])
+    fixes = 1.0 / jnp.stack([1.0 - BETA_ONE**step_value, 1.0 - BETA_TWO**step_value])
     changed = update(
         fixes,
         squares,

time: 476 us -> 467 us (0.981)
  Pallas kernels: 439 us -> 430 us
    pallas_call x0 -> x1, Pallas kernels: none -> 67.8 us  [ffn_both(): pl.pallas_call(ffn_both_kernel, out_shape=(jax.ShapeDtypeStruct((ROWS, D)...]
    pallas_call x2 -> x1, Pallas kernels: 85.2 us -> 43.8 us  [ffn_backward(): pl.pallas_call(functools.partial(ffn_backward_kernel, bool(upper)), out_s...]
    pallas_call x2 -> x1, Pallas kernels: 72 us -> 37.1 us  [ffn_forward(): pl.pallas_call(ffn_forward_kernel, out_shape=(jax.ShapeDtypeStruct((ROWS,...]
  transfers between devices with their start and end apart: 3 -> 3, of which waited for: 1 -> 1; matrix products, arithmetic and copies ran while one was open for 2% -> 2% of each run, Pallas kernels for 30% -> 31%
where the time goes in v6:
time: 467 us; the launch traced here: 464 us
  Pallas kernels  430 us (92%)
  between operations  15.3 us (3%)
  local copies, waits for them, and re-layouts  13.2 us (3%)
    pallas_call x2, Pallas kernels, attn_backward(): pl.pallas_call(functools.partial(attn_backward_kernel, bool(upper)), out_...  89.1 us
    pallas_call x2, Pallas kernels, attn_forward(): pl.pallas_call(functools.partial(attn_forward_kernel, layer), out_shape=(...  71.3 us
    pallas_call x1, Pallas kernels, ffn_both(): pl.pallas_call(ffn_both_kernel, out_shape=(jax.ShapeDtypeStruct((ROWS, D)...  67.8 us
    pallas_call x1, Pallas kernels, sum_shards(): pl.pallas_call(sum_shards_kernel, out_shape=(jax.ShapeDtypeStruct((CTX, S...  67.5 us
    pallas_call x1, Pallas kernels, ffn_backward(): pl.pallas_call(functools.partial(ffn_backward_kernel, bool(upper)), out_s...  43.8 us
    pallas_call x1, Pallas kernels, ffn_forward(): pl.pallas_call(ffn_forward_kernel, out_shape=(jax.ShapeDtypeStruct((ROWS,...  37.1 us
    pallas_call x1, Pallas kernels, gather_shards(): pl.pallas_call(gather_shards_kernel, out_shape=(jax.ShapeDtypeStruct((2,...  35.1 us
    pallas_call x1, Pallas kernels, update(): pl.pallas_call(update_kernel, grid=(CTX,), out_shape=five(in_shape) + fiv...  18 us
  transfers between devices with their start and end apart: 3, of which 1 were waited for; matrix products, arithmetic and copies ran while one was open for 2% of the time, Pallas kernels for 31%

profile of v6, /device:TPU:0, one launch (start us, length us, event | category | flops | bytes accessed | tf_op | source)
XLA Modules:
  0.0 463.7 jit_solution(8496837917383900667)
XLA Ops:
  7.2 0.0 copy-start
  7.2 0.0 all-gather.5.cloned.1.call-start
  7.3 1.5 dynamic-slice_convert_fusion
  8.8 0.2 slice.55
  9.0 1.0 fusion
  10.0 0.0 copy-start.6
  10.0 0.0 copy-start.8
  10.0 0.1 copy.82
  10.1 0.0 copy-start.9
  10.1 0.0 copy-start.7
  10.1 0.1 bitcast_select_fusion.2
  10.2 0.1 collective-permute-start
  10.3 1.6 collective-permute-done
  11.9 0.9 broadcast_select_fusion
  12.8 0.0 all-gather.5.cloned.1.call-update
  12.8 0.0 all-gather.7.cloned.1.call-start
  12.9 0.7 all-gather.7.cloned.1.call-update
  13.6 0.9 slice.62
  14.5 0.0 copy-done.6
  14.5 0.1 copy.61
  14.6 0.0 copy-done.8
  14.6 0.1 copy.62
  14.7 1.0 fusion.3
  15.8 0.1 concatenate.7
  15.9 0.2 convert_element_type.30
  16.1 0.7 copy.63
  17.5 0.0 copy-done.9
  17.5 0.6 dynamic_slice.33.length_ref
  18.1 0.0 copy-done.7
  18.1 0.6 pad.4.code_ref
  18.8 35.1 %gather_shards.1 = (bf16[2,4,4,288,256]{4,3,2,1,0:T(8,128)(2,1)}, f32[2,4,8,256]{3,2,1,0:T(8,128)}) custom-call(bf16[288,256]{1,0:T(8,128)(2,1)} %bitcast.114, f32[8,256]{1,0:T(8,128)} %pad.4.code_ref), custom_call_target="tpu_custom_call" | custom-call | tf_op jit(solution)/shard_map/gather_shards/pallas_call | solution.py:419
  53.9 0.0 copy-done
  53.9 0.8 dynamic-slice_bitcast_fusion.u_ref
  54.7 0.0 copy-start.5
  54.7 0.0 copy-start.4
  54.7 37.6 %attn_forward.2 = (bf16[1024,768]{1,0:T(8,128)(2,1)}, bf16[1024,1152]{1,0:T(8,128)(2,1)}, f32[3,1024,1]{2,1,0:T(8,128)}, bf16[4,256,192]{2,1,0:T(8,128)(2,1)}, f...) custom-call(s32[1]{0:T(128)} %dynamic_slice.33.length_ref, ...), custom_call_target="tpu_custom_call" | custom-call | tf_op jit(solution)/shard_map/attn_forward/pallas_call | solution.py:890
  92.3 0.7 add_compare_fusion
  92.9 0.6 maximum_divide_fusion.fixes_ref
  93.5 0.0 copy-done.5
  93.5 0.6 slice_bitcast_fusion
  94.1 0.0 copy-done.4
  94.1 0.9 bitcast_select_fusion.delta_own_ref.delta_ref
  95.0 0.0 all-gather.5.cloned.1.call-done
  95.0 37.1 %ffn_forward.1 = (bf16[256,768]{1,0:T(8,128)(2,1)}, bf16[4,256,768]{2,1,0:T(8,128)(2,1)}, f32[256,128]{1,0:T(8,128)}, f32[4,256,1]{2,1,0:T(8,128)}, bf16[4,16,256,256]{3,2,1,0:T(8,128)(2,1)}) custom-call(bf16[256,768]{1,0:T(8,128)(2,1)} %get-tuple-element.101.b_own_ref.second_in, f32[256,768]{1,0:T(8,128)} %get-tuple-element.102.residual_ref, ...), custom_call_target="tpu_custom_call" | custom-call | tf_op jit(solution)/shard_map/ffn_forward/pallas_call | solution.py:1324
  132.1 33.7 %attn_forward.3 = (bf16[1024,768]{1,0:T(8,128)(2,1)}, bf16[1024,1152]{1,0:T(8,128)(2,1)}, f32[3,1024,1]{2,1,0:T(8,128)}, bf16[4,256,192]{2,1,0:T(8,128)(2,1)}, f...) custom-call(s32[1]{0:T(128)} %dynamic_slice.33.length_ref, ...), custom_call_target="tpu_custom_call" | custom-call | tf_op jit(solution)/shard_map/attn_forward/pallas_call | solution.py:890
  165.8 0.0 all-gather.7.cloned.1.call-done
  165.8 67.8 %ffn_both.1 = (bf16[256,768]{1,0:T(8,128)(2,1)}, f32[256,128]{1,0:T(8,128)}, f32[256,768]{1,0:T(8,128)}, f32[256,128]{1,0:T(8,128)}, bf16[16,1152,256]{2,1,0:T(8,128)(2,1)}) custom-call(bf16[256,768]{1,0:T(8,128)(2,1)} %get-tuple-element.117.b_own_ref.second_in, f32[256,768]{1,0:T(8,128)} %get-tuple-element.116.residual_ref, ...), custom_call_target="tpu_custom_call" | custom-call | tf_op jit(solution)/shard_map/ffn_both/pallas_call | solution.py:1733
  233.7 36.1 %attn_backward.2 = (f32[256,768]{1,0:T(8,128)}, bf16[16,288,256]{2,1,0:T(8,128)(2,1)}, bf16[256,768]{1,0:T(8,128)(2,1)}) custom-call(s32[1]{0:T(128)} %dynamic_slice.33.length_ref, bf16[256,768]{1,0:T(8,128)(2,1)} %get-tuple-element.107.u_ref.lower_out_ref, f32[8,768]{1,0:T(8,128)} %get-tuple-element.108.gains_ref, ...), custom_call_target="tpu_custom_call" | custom-call | tf_op jit(solution)/shard_map/attn_backward/pallas_call | solution.py:1187
  269.9 43.8 %ffn_backward.1 = (f32[256,768]{1,0:T(8,128)}, f32[256,128]{1,0:T(8,128)}, bf16[16,1152,256]{2,1,0:T(8,128)(2,1)}, bf16[16,720,256]{2,1,0:T(8,128)(2,1)}) custom-call(bf16[4,256,768]{2,1,0:T(8,128)(2,1)} %get-tuple-element.105.b_ref, f32[4,256,1]{2,1,0:T(8,128)} %get-tuple-element.106.gate_ref, bf16[256,768]{1,0:T(8,128)(2,1)} %get-tuple-element.121.delta_own_ref.delta_ref, ...), custom_call_target="tpu_custom_call" | custom-call | tf_op jit(solution)/shard_map/ffn_backward/pallas_call | solution.py:1530
  313.7 52.9 %attn_backward.3 = (f32[256,768]{1,0:T(8,128)}, bf16[16,288,256]{2,1,0:T(8,128)(2,1)}, bf16[256,768]{1,0:T(8,128)(2,1)}, bf16[720,256]{1,0:T(8,128)(2,1)}) custom-call(s32[1]{0:T(128)} %dynamic_slice.33.length_ref, bf16[256,768]{1,0:T(8,128)(2,1)} %dynamic-slice_bitcast_fusion.u_ref, f32[8,768]{1,0:T(8,128)} %get-tuple-element.126.gains_ref, ...), custom_call_target="tpu_custom_call" | custom-call | tf_op jit(solution)/shard_map/attn_backward/pallas_call | solution.py:1187
  366.6 67.5 %sum_shards.1 = (bf16[4,1440,256]{2,1,0:T(8,128)(2,1)}, f32[8,128]{1,0:T(8,128)}, bf16[2,256,768]{2,1,0:T(8,128)(2,1)}, f32[2,256,768]{2,1,0:T(8,128)}) custom-call(bf16[4,4,1152,256]{3,2,1,0:T(8,128)(2,1)} %bitcast.92, bf16[4,4,288,256]{3,2,1,0:T(8,128)(2,1)} %bitcast.103, bf16[720,256]{1,0:T(8,128)(2,1)} %get-tuple-element.138.upper_half_ref, ...), custom_call_target="tpu_custom_call" | custom-call | tf_op jit(solution)/shard_map/sum_shards/pallas_call | solution.py:722
  434.1 0.0 copy-start.3
  434.1 18.0 %update.1 = (f32[6144,128]{1,0:T(8,128)}, f32[6144,128]{1,0:T(8,128)}, f32[6144,128]{1,0:T(8,128)}, f32[6144,128]{1,0:T(8,128)}, bf16[6144,128]{1,0:T(8,128)(2,1...) custom-call(f32[2]{0:T(128)} %maximum_divide_fusion.fixes_ref, ...), custom_call_target="tpu_custom_call" | custom-call | tf_op jit(solution)/shard_map/update/pallas_call | solution.py:1918
  452.0 0.0 copy-start.2
  452.1 1.4 copy.66
  453.4 1.2 slice.53
  454.6 0.0 copy-start.1
  454.6 0.0 copy-done.3
  454.6 0.9 copy.86
  455.5 0.0 copy-done.2
  455.5 1.1 copy.87
  456.6 0.0 copy-done.1
  (6 shorter events, 0.0 us)
Async XLA Ops:
  7.2 46.7 %copy-start = (bf16[2,256,768]{2,1,0:T(8,128)(2,1)S(1)}, bf16[2,256,768]{2,1,0:T(8,128)(2,1)}, u32[]{:S(2)}) copy-start(bf16[2,256,768]{2,1,0:T(8,128)(2,1)} %param.21) | copy-start | bytes 2359300
  7.2 87.8 %all-gather.5.cloned.1.call-start = ((), (), s32[]{:S(2)}) async-start(), calls=%async_computation | async-start | bytes 9732096 | tf_op jit(solution)/shard_map/all_gather | solution.py:2003
  10.0 4.5 copy-start.6
  10.0 4.6 copy-start.8
  10.1 7.4 %copy-start.9 = (s32[2]{0:T(128)S(1)}, s32[2]{0:T(128)}, u32[]{:S(2)}) copy-start(s32[2]{0:T(128)} %param.23) | copy-start | bytes 28
  10.1 8.0 %copy-start.7 = (s32[1,2,256,2]{2,3,1,0:T(2,128)S(1)}, s32[1,2,256,2]{2,3,1,0:T(2,128)}, u32[]{:S(2)}) copy-start(s32[1,2,256,2]{2,3,1,0:T(2,128)} %param.24) | copy-start | bytes 12292
  10.2 1.7 collective-permute-start
  12.8 153.0 %all-gather.7.cloned.1.call-start = ((), (), s32[]{:S(2)}) async-start(), calls=%async_computation.1 | async-start | bytes 9732096 | tf_op jit(solution)/shard_map/all_gather | solution.py:2003
  54.7 38.8 %copy-start.5 = (f32[2,4,8,256]{3,2,1,0:T(8,128)S(1)}, f32[2,4,8,256]{3,2,1,0:T(8,128)}, u32[]{:S(2)}) copy-start(f32[2,4,8,256]{3,2,1,0:T(8,128)} %get-tuple-element.103) | copy-start | bytes 196612
  54.7 39.5 %copy-start.4 = (bf16[2,256,768]{2,1,0:T(8,128)(2,1)S(1)}, bf16[2,256,768]{2,1,0:T(8,128)(2,1)}, u32[]{:S(2)}) copy-start(bf16[2,256,768]{2,1,0:T(8,128)(2,1)} %param.22) | copy-start | bytes 2359300
  434.1 20.6 %copy-start.3 = (bf16[2,256,768]{2,1,0:T(8,128)(2,1)S(1)}, bf16[2,256,768]{2,1,0:T(8,128)(2,1)}, u32[]{:S(2)}) copy-start(bf16[2,256,768]{2,1,0:T(8,128)(2,1)} %get-tuple-element.142) | copy-start | bytes 2359300
  452.0 3.5 copy-start.2
  454.6 2.0 copy-start.1
Sparse Core Ops, SparseCore 0:
  12.9 60.3 all-gather.4
  76.2 54.9 all-gather.6

commit v7 on v6

--- a/solution.py
+++ b/solution.py
@@ -299,13 +299,11 @@
         incoming = self.across_in[half]
         if len(self.part.shape) == 3:
             spot = (block, self.halves[half])
-            self.part[spot] = (self.part[spot].astype(F32) + incoming[...].astype(F32)).astype(BF16)
+            self.part[spot] = self.part[spot] + incoming[...]
             return
         start = (0, self.part.shape[1] - incoming.shape[0])[half]
         for index in range(incoming.shape[0]):
-            self.part[block, start + index] = (
-                self.part[block, start + index].astype(F32) + incoming[index].astype(F32)
-            ).astype(BF16)
+            self.part[block, start + index] = self.part[block, start + index] + incoming[index]
 
     def stage(self, number):
         ring = self.ring
@@ -352,7 +350,7 @@
 SEMS = pltpu.SemaphoreType.DMA
 
 
-def gather_shards_kernel(shard_ref, code_ref, out_ref, codes_ref, *sems):
+def gather_shards_kernel(shard_ref, code_ref, seed_ref, out_ref, codes_ref, seeds_ref, *sems):
     section = lax.axis_index("section")
     sibling = {"section": 1 - section}
     ring_y, ring_z = Ring("y"), Ring("z")
@@ -364,6 +362,9 @@
     )
     out_ref[section, z, y] = shard_ref[...]
     codes_ref[section, ring_x.me] = code_ref[...]
+    seeds_ref[ring_x.me] = seed_ref[...]
+    halves = (pl.ds(0, HALF), pl.ds(HALF, HALF))
+    seeds = RingGather(ring_x, lambda b, h: seeds_ref.at[b, halves[h]], sems[14], sems[15])
     met(8)
     spot = codes_ref.at[section, ring_x.me]
     code_copies = [
@@ -384,11 +385,15 @@
     far_y = RingGather(
         ring_y, lambda b, h: out_ref.at[section, pair[h], b, pl.ds(half, half)], sems[6], sems[7]
     )
-    for rings in ((near_y, near_z), (far_z, far_y)):
+    for first, rings in ((True, (near_y, near_z)), (False, (far_z, far_y))):
         for one in rings:
             one.start()
+        if first:
+            seeds.start()
         for one in rings:
             one.forward()
+        if not first:
+            seeds.forward()
         for one in rings:
             one.finish()
     across = pltpu.make_async_remote_copy(
@@ -412,22 +417,25 @@
     )
     codes_across.start()
     codes_across.wait()
+    seeds.finish()
     across.wait()
 
 
-def gather_shards(shard, codes):
+def gather_shards(shard, codes, seed):
     return pl.pallas_call(
         gather_shards_kernel,
         out_shape=(
             jax.ShapeDtypeStruct((2, CTX, CTX, ATTN_ROWS, UNIT), BF16),
             jax.ShapeDtypeStruct((2, CTX, 8, ROWS), F32),
+            jax.ShapeDtypeStruct((CTX, ROWS, D), BF16),
         ),
-        in_specs=[VMEM, VMEM],
-        out_specs=[VMEM, VMEM],
-        scratch_shapes=[SEMS((6,))] * 8 + [SEMS, SEMS, SEMS((3,)), SEMS((3,)), SEMS, SEMS],
+        in_specs=[VMEM] * 3,
+        out_specs=[VMEM] * 3,
+        scratch_shapes=[SEMS((6,))] * 8
+        + [SEMS, SEMS, SEMS((3,)), SEMS((3,)), SEMS, SEMS, SEMS((6,)), SEMS((6,))],
         compiler_params=params(7),
         name="gather_shards",
-    )(shard, codes)
+    )(shard, codes, seed)
 
 
 HALF_SHARD = SHARD_ROWS // 2
@@ -505,9 +513,7 @@
 
 def add_block(part, incoming, block):
     for other in range(CTX):
-        part[block, other] = (part[block, other].astype(F32) + incoming[block, other].astype(F32)).astype(
-            BF16
-        )
+        part[block, other] = part[block, other] + incoming[block, other]
 
 
 def shared_squares(all_ref, ring_y, ring_z, spread):
@@ -1561,10 +1567,10 @@
 
 
 def ffn_both_kernel(
-    b_own_ref, residual_ref, codes_ref, router_ref, delta_own_ref, w_ref,
+    b_own_ref, residual_ref, codes_ref, router_ref, delta_in, w_ref,
     y_ref, gates_ref, db_ref, gate_grad_ref, dw_ref,
     b_ref, gate_ref, delta, acc, slot_grad, hidden, acted, win, wout, staged, rows_out, rows_in, b_turned,
-    w_sem, dw_sem, send_b, recv_b, send_d, recv_d, send_g, recv_g, *sum_refs,
+    w_sem, dw_sem, send_b, recv_b, delta_sem, send_g, recv_g, *sum_refs,
 ):
     ring = Ring("x")
     peers = (ring.right, ring.left, ring.across)
@@ -1574,11 +1580,11 @@
         for copy in group:
             copy.start()
     b_ref[ring.me] = b_own_ref[...]
-    delta[ring.me] = delta_own_ref[...]
+    seeds = pltpu.make_async_copy(delta_in, delta, delta_sem)
+    seeds.start()
     met(3)
     halves = (pl.ds(0, HALF), pl.ds(HALF, HALF))
     rows = RingGather(ring, lambda b, h: b_ref.at[b, halves[h]], send_b, recv_b)
-    seeds = RingGather(ring, lambda b, h: delta.at[b, halves[h]], send_d, recv_d)
     rows.start()
     section = lax.axis_index("section")
     lanes = lax.broadcasted_iota(jnp.int32, (ROWS, LANES), 1)
@@ -1669,19 +1675,16 @@
     ahead.stage(4)
     rows.forward()
     rows.near()
-    seeds.start()
     ahead.stage(1)
     ahead.stage(2)
     rows.far()
     ahead.stage(0)
-    seeds.forward()
     b_turned[...] = b_ref[...].reshape(SEQ, D).T
+    seeds.wait()
     behind.stage(4)
     ahead.stage(3)
-    seeds.near()
     behind.stage(1)
     behind.stage(2)
-    seeds.far()
     behind.stage(0)
     ahead.stage(5)
     y_ref[...] = (residual_ref[...] + ahead.total()).astype(BF16)
@@ -1724,12 +1727,11 @@
         rows_all, diagonal, TN, precision=EXACT, preferred_element_type=F32
     )
     rows.sent()
-    seeds.sent()
     stores[2].wait()
     stores[3].wait()
 
 
-def ffn_both(b_own, residual, codes, router, delta_own, weights):
+def ffn_both(b_own, residual, codes, router, delta_all, weights):
     return pl.pallas_call(
         ffn_both_kernel,
         out_shape=(
@@ -1739,7 +1741,7 @@
             jax.ShapeDtypeStruct((ROWS, LANES), F32),
             jax.ShapeDtypeStruct((16, EXPERT_ROWS, UNIT), BF16),
         ),
-        in_specs=[VMEM] * 5 + [ANY],
+        in_specs=[VMEM] * 4 + [ANY] * 2,
         out_specs=[VMEM] * 4 + [ANY],
         scratch_shapes=[
             pltpu.VMEM((CTX, ROWS, D), BF16),
@@ -1759,15 +1761,14 @@
             SEMS((2,)),
             SEMS((6,)),
             SEMS((6,)),
-            SEMS((6,)),
-            SEMS((6,)),
+            SEMS,
             SEMS((3,)),
             SEMS((3,)),
         ]
         + SUM_SCRATCH * 2,
         compiler_params=params(6),
         name="ffn_both",
-    )(b_own, residual, codes, router, delta_own, weights)
+    )(b_own, residual, codes, router, delta_all, weights)
 
 
 def rotary_table():
@@ -1790,12 +1791,12 @@
     return output, (tokens_in, b_all, gate_col, kept, unpacked, late)
 
 
-def upper_layer(packs, experts, tokens_in, length, codes, table, seed):
+def upper_layer(packs, experts, tokens_in, length, codes, table, seed, seed_all):
     a_all, qkv, mass, attended, residual, second, *unpacked = attn_forward(
         1, length, tokens_in, packs, table
     )
     output, gates, db, gate_grads, dexperts = ffn_both(
-        second, residual, codes, unpacked[1], seed, experts
+        second, residual, codes, unpacked[1], seed_all, experts
     )
     late = (a_all, qkv, mass, attended, residual, second, gates)
     results = attn_backward(length, (tokens_in, *unpacked, table, *late, seed, db, gate_grads))
@@ -1985,8 +1986,15 @@
         axis=1,
     ).astype(BF16)
     attn_shard = attn_shard.reshape(shard_rows, 6, UNIT).transpose(1, 0, 2).reshape(-1, UNIT)
+    length = lax.dynamic_slice_in_dim(lengths, section, 1, 0)
+    tokens = lax.dynamic_index_in_dim(inputs, section, 0, keepdims=False)
+    positions = ctx_index * ROWS + jnp.arange(ROWS, dtype=jnp.int32)
+    seed = lax.dynamic_index_in_dim(cotangent, section, 0, keepdims=False)
+    seed = jnp.where((positions < length[0])[:, None], seed, jnp.zeros_like(seed))
     left_out = (3 - routes[0, :, :, 0] - routes[0, :, :, 1]).astype(F32)
-    packs, codes = gather_shards(attn_shard, jnp.pad(left_out, ((0, 8 - left_out.shape[0]), (0, 0))))
+    packs, codes, seed_all = gather_shards(
+        attn_shard, jnp.pad(left_out, ((0, 8 - left_out.shape[0]), (0, 0))), seed
+    )
     packs = packs.reshape(2, fsdp, ATTN_ROWS, UNIT)
     in_shard = (
         lax.dynamic_index_in_dim(expert_in[0], ctx_index, 0, keepdims=False)
@@ -2002,16 +2010,11 @@
     experts = [
         lax.all_gather(piece, everyone).reshape(2, fsdp, SPLIT, 2 * units) for piece in pieces
     ]
-    length = lax.dynamic_slice_in_dim(lengths, section, 1, 0)
-    tokens = lax.dynamic_index_in_dim(inputs, section, 0, keepdims=False)
-    positions = ctx_index * ROWS + jnp.arange(ROWS, dtype=jnp.int32)
-    seed = lax.dynamic_index_in_dim(cotangent, section, 0, keepdims=False)
-    seed = jnp.where((positions < length[0])[:, None], seed, jnp.zeros_like(seed))
     table = rotary_table()
 
     lower_out, lower_saved = lower_forward(packs, experts[0], tokens, length, codes[0], table)
     upper_out, upper_experts, (upper_grad, upper_attn, lower_seed) = upper_layer(
-        packs, experts[1], lower_out, length, codes[1], table, seed
+        packs, experts[1], lower_out, length, codes[1], table, seed, seed_all
     )
     lower_experts, (lower_grad, lower_attn, _, upper_half) = lower_backward(
         experts[0], lower_saved, lower_seed, length, table, (upper_experts, upper_attn)

time: 467 us -> 463 us (level)
  Pallas kernels: 430 us -> 425 us
    pallas_call x1, Pallas kernels: 67.8 us -> 62.6 us  [ffn_both(): pl.pallas_call(ffn_both_kernel, out_shape=(jax.ShapeDtypeStruct((ROWS, D)...]
  transfers between devices with their start and end apart: 3 -> 3, of which waited for: 1 -> 1; matrix products, arithmetic and copies ran while one was open for 2% -> 2% of each run, Pallas kernels for 31% -> 32%
where the time goes in v7:
time: 463 us; the launch traced here: 459 us
  Pallas kernels  425 us (92%)
  between operations  15.6 us (3%)
  local copies, waits for them, and re-layouts  13.2 us (3%)
    pallas_call x2, Pallas kernels, attn_backward(): pl.pallas_call(functools.partial(attn_backward_kernel, bool(upper)), out_...  88.6 us
    pallas_call x2, Pallas kernels, attn_forward(): pl.pallas_call(functools.partial(attn_forward_kernel, layer), out_shape=(...  70.4 us
    pallas_call x1, Pallas kernels, sum_shards(): pl.pallas_call(sum_shards_kernel, out_shape=(jax.ShapeDtypeStruct((CTX, S...  67 us
    pallas_call x1, Pallas kernels, ffn_both(): pl.pallas_call(ffn_both_kernel, out_shape=(jax.ShapeDtypeStruct((ROWS, D)...  62.6 us
    pallas_call x1, Pallas kernels, ffn_backward(): pl.pallas_call(functools.partial(ffn_backward_kernel, bool(upper)), out_s...  43.8 us
    pallas_call x1, Pallas kernels, ffn_forward(): pl.pallas_call(ffn_forward_kernel, out_shape=(jax.ShapeDtypeStruct((ROWS,...  38.1 us
    pallas_call x1, Pallas kernels, gather_shards(): pl.pallas_call(gather_shards_kernel, out_shape=(jax.ShapeDtypeStruct((2,...  36.8 us
    pallas_call x1, Pallas kernels, update(): pl.pallas_call(update_kernel, grid=(CTX,), out_shape=five(in_shape) + fiv...  17.9 us
  transfers between devices with their start and end apart: 3, of which 1 were waited for; matrix products, arithmetic and copies ran while one was open for 2% of the time, Pallas kernels for 32%

profile of v7, /device:TPU:0, one launch (start us, length us, event | category | flops | bytes accessed | tf_op | source)
XLA Modules:
  0.0 459.4 jit_solution(7450005391512476303)
XLA Ops:
  7.2 0.0 copy-start
  7.2 0.0 all-gather.5.cloned.1.call-start
  7.3 1.5 dynamic-slice_convert_fusion
  8.7 0.2 slice.55
  9.0 1.0 fusion
  10.0 0.1 copy.82
  10.1 0.0 copy-start.6
  10.1 0.0 copy-start.8
  10.1 0.1 bitcast_select_fusion.2
  10.2 0.0 copy-start.9
  10.2 0.0 copy-start.7
  10.2 0.0 copy-start.4
  10.2 0.1 collective-permute-start
  10.3 1.6 collective-permute-done
  11.9 0.9 broadcast_select_fusion
  12.8 0.0 all-gather.5.cloned.1.call-update
  12.8 0.0 all-gather.7.cloned.1.call-start
  12.9 0.7 all-gather.7.cloned.1.call-update
  13.6 0.9 slice.62
  14.5 0.0 copy-done.6
  14.5 0.1 copy.61
  14.6 0.0 copy-done.8
  14.6 0.1 copy.62
  14.7 1.0 fusion.3
  15.8 0.1 concatenate.7
  15.9 0.2 convert_element_type.30
  16.1 0.7 copy.63
  17.5 0.0 copy-done.9
  17.6 0.6 dynamic_slice.33.length_ref
  18.1 0.0 copy-done.7
  18.2 0.6 pad.4.code_ref
  18.8 0.7 add_compare_fusion
  19.4 0.0 copy-done.4
  19.4 0.9 bitcast_select_fusion.seed_ref.delta_ref
  20.3 36.8 %gather_shards.1 = (bf16[2,4,4,288,256]{4,3,2,1,0:T(8,128)(2,1)}, f32[2,4,8,256]{3,2,1,0:T(8,128)}, bf16[4,256,768]{2,1,0:T(8,128)(2,1)}) custom-call(bf16[288,256]{1,0:T(8,128)(2,1)} %bitcast.114, f32[8,256]{1,0:T(8,128)} %pad.4.code_ref, bf16[256,768]{1,0:T(8,128)(2,1)} %bitcast_select_fusion.seed_ref.delta_ref), custom_call_target="tpu_custom_call" | custom-call | tf_op jit(solution)/shard_map/gather_shards/pallas_call | solution.py:425
  57.1 0.0 copy-done
  57.1 0.8 dynamic-slice_bitcast_fusion.u_ref
  57.9 0.0 copy-start.5
  57.9 37.7 %attn_forward.2 = (bf16[1024,768]{1,0:T(8,128)(2,1)}, bf16[1024,1152]{1,0:T(8,128)(2,1)}, f32[3,1024,1]{2,1,0:T(8,128)}, bf16[4,256,192]{2,1,0:T(8,128)(2,1)}, f...) custom-call(s32[1]{0:T(128)} %dynamic_slice.33.length_ref, ...), custom_call_target="tpu_custom_call" | custom-call | tf_op jit(solution)/shard_map/attn_forward/pallas_call | solution.py:896
  95.6 0.6 maximum_divide_fusion.fixes_ref
  96.2 0.0 copy-done.5
  96.2 0.6 slice_bitcast_fusion
  96.8 0.0 all-gather.5.cloned.1.call-done
  96.8 38.1 %ffn_forward.1 = (bf16[256,768]{1,0:T(8,128)(2,1)}, bf16[4,256,768]{2,1,0:T(8,128)(2,1)}, f32[256,128]{1,0:T(8,128)}, f32[4,256,1]{2,1,0:T(8,128)}, bf16[4,16,256,256]{3,2,1,0:T(8,128)(2,1)}) custom-call(bf16[256,768]{1,0:T(8,128)(2,1)} %get-tuple-element.102.b_own_ref.second_in, f32[256,768]{1,0:T(8,128)} %get-tuple-element.103.residual_ref, ...), custom_call_target="tpu_custom_call" | custom-call | tf_op jit(solution)/shard_map/ffn_forward/pallas_call | solution.py:1330
  134.9 32.7 %attn_forward.3 = (bf16[1024,768]{1,0:T(8,128)(2,1)}, bf16[1024,1152]{1,0:T(8,128)(2,1)}, f32[3,1024,1]{2,1,0:T(8,128)}, bf16[4,256,192]{2,1,0:T(8,128)(2,1)}, f...) custom-call(s32[1]{0:T(128)} %dynamic_slice.33.length_ref, ...), custom_call_target="tpu_custom_call" | custom-call | tf_op jit(solution)/shard_map/attn_forward/pallas_call | solution.py:896
  167.6 0.0 all-gather.7.cloned.1.call-done
  167.6 62.6 %ffn_both.1 = (bf16[256,768]{1,0:T(8,128)(2,1)}, f32[256,128]{1,0:T(8,128)}, f32[256,768]{1,0:T(8,128)}, f32[256,128]{1,0:T(8,128)}, bf16[16,1152,256]{2,1,0:T(8,128)(2,1)}) custom-call(bf16[256,768]{1,0:T(8,128)(2,1)} %get-tuple-element.118.b_own_ref.second_in, f32[256,768]{1,0:T(8,128)} %get-tuple-element.117.residual_ref, ...), custom_call_target="tpu_custom_call" | custom-call | tf_op jit(solution)/shard_map/ffn_both/pallas_call | solution.py:1735
  230.2 35.5 %attn_backward.2 = (f32[256,768]{1,0:T(8,128)}, bf16[16,288,256]{2,1,0:T(8,128)(2,1)}, bf16[256,768]{1,0:T(8,128)(2,1)}) custom-call(s32[1]{0:T(128)} %dynamic_slice.33.length_ref, bf16[256,768]{1,0:T(8,128)(2,1)} %get-tuple-element.108.u_ref.lower_out_ref, f32[8,768]{1,0:T(8,128)} %get-tuple-element.109.gains_ref, ...), custom_call_target="tpu_custom_call" | custom-call | tf_op jit(solution)/shard_map/attn_backward/pallas_call | solution.py:1193
  265.7 43.8 %ffn_backward.1 = (f32[256,768]{1,0:T(8,128)}, f32[256,128]{1,0:T(8,128)}, bf16[16,1152,256]{2,1,0:T(8,128)(2,1)}, bf16[16,720,256]{2,1,0:T(8,128)(2,1)}) custom-call(bf16[4,256,768]{2,1,0:T(8,128)(2,1)} %get-tuple-element.106.b_ref, f32[4,256,1]{2,1,0:T(8,128)} %get-tuple-element.107.gate_ref, bf16[256,768]{1,0:T(8,128)(2,1)} %get-tuple-element.123.delta_own_ref.delta_ref, ...), custom_call_target="tpu_custom_call" | custom-call | tf_op jit(solution)/shard_map/ffn_backward/pallas_call | solution.py:1536
  309.5 53.2 %attn_backward.3 = (f32[256,768]{1,0:T(8,128)}, bf16[16,288,256]{2,1,0:T(8,128)(2,1)}, bf16[256,768]{1,0:T(8,128)(2,1)}, bf16[720,256]{1,0:T(8,128)(2,1)}) custom-call(s32[1]{0:T(128)} %dynamic_slice.33.length_ref, bf16[256,768]{1,0:T(8,128)(2,1)} %dynamic-slice_bitcast_fusion.u_ref, f32[8,768]{1,0:T(8,128)} %get-tuple-element.128.gains_ref, ...), custom_call_target="tpu_custom_call" | custom-call | tf_op jit(solution)/shard_map/attn_backward/pallas_call | solution.py:1193
  362.6 67.0 %sum_shards.1 = (bf16[4,1440,256]{2,1,0:T(8,128)(2,1)}, f32[8,128]{1,0:T(8,128)}, bf16[2,256,768]{2,1,0:T(8,128)(2,1)}, f32[2,256,768]{2,1,0:T(8,128)}) custom-call(bf16[4,4,1152,256]{3,2,1,0:T(8,128)(2,1)} %bitcast.92, bf16[4,4,288,256]{3,2,1,0:T(8,128)(2,1)} %bitcast.103, bf16[720,256]{1,0:T(8,128)(2,1)} %get-tuple-element.140.upper_half_ref, ...), custom_call_target="tpu_custom_call" | custom-call | tf_op jit(solution)/shard_map/sum_shards/pallas_call | solution.py:728
  429.7 0.0 copy-start.3
  429.7 17.9 %update.1 = (f32[6144,128]{1,0:T(8,128)}, f32[6144,128]{1,0:T(8,128)}, f32[6144,128]{1,0:T(8,128)}, f32[6144,128]{1,0:T(8,128)}, bf16[6144,128]{1,0:T(8,128)(2,1...) custom-call(f32[2]{0:T(128)} %maximum_divide_fusion.fixes_ref, ...), custom_call_target="tpu_custom_call" | custom-call | tf_op jit(solution)/shard_map/update/pallas_call | solution.py:1919
  447.6 0.0 copy-start.2
  447.6 1.4 copy.66
  448.9 1.2 slice.53
  450.1 0.0 copy-done.3
  450.1 0.0 copy-start.1
  450.1 0.9 copy.86
  451.0 0.0 copy-done.2
  451.0 1.1 copy.87
  452.2 0.0 copy-done.1
  (6 shorter events, 0.0 us)
Async XLA Ops:
  7.2 49.9 %copy-start = (bf16[2,256,768]{2,1,0:T(8,128)(2,1)S(1)}, bf16[2,256,768]{2,1,0:T(8,128)(2,1)}, u32[]{:S(2)}) copy-start(bf16[2,256,768]{2,1,0:T(8,128)(2,1)} %param.21) | copy-start | bytes 2359300
  7.2 89.6 %all-gather.5.cloned.1.call-start = ((), (), s32[]{:S(2)}) async-start(), calls=%async_computation | async-start | bytes 9732096 | tf_op jit(solution)/shard_map/all_gather | solution.py:2011
  10.1 4.4 copy-start.6
  10.1 4.5 copy-start.8
  10.2 7.4 %copy-start.9 = (s32[2]{0:T(128)S(1)}, s32[2]{0:T(128)}, u32[]{:S(2)}) copy-start(s32[2]{0:T(128)} %param.23) | copy-start | bytes 28
  10.2 7.9 %copy-start.7 = (s32[1,2,256,2]{2,3,1,0:T(2,128)S(1)}, s32[1,2,256,2]{2,3,1,0:T(2,128)}, u32[]{:S(2)}) copy-start(s32[1,2,256,2]{2,3,1,0:T(2,128)} %param.24) | copy-start | bytes 12292
  10.2 9.2 %copy-start.4 = (bf16[2,256,768]{2,1,0:T(8,128)(2,1)S(1)}, bf16[2,256,768]{2,1,0:T(8,128)(2,1)}, u32[]{:S(2)}) copy-start(bf16[2,256,768]{2,1,0:T(8,128)(2,1)} %param.22) | copy-start | bytes 2359300
  10.2 1.7 collective-permute-start
  12.8 154.8 %all-gather.7.cloned.1.call-start = ((), (), s32[]{:S(2)}) async-start(), calls=%async_computation.1 | async-start | bytes 9732096 | tf_op jit(solution)/shard_map/all_gather | solution.py:2011
  57.9 38.3 %copy-start.5 = (f32[2,4,8,256]{3,2,1,0:T(8,128)S(1)}, f32[2,4,8,256]{3,2,1,0:T(8,128)}, u32[]{:S(2)}) copy-start(f32[2,4,8,256]{3,2,1,0:T(8,128)} %get-tuple-element.104) | copy-start | bytes 196612
  429.7 20.4 %copy-start.3 = (bf16[2,256,768]{2,1,0:T(8,128)(2,1)S(1)}, bf16[2,256,768]{2,1,0:T(8,128)(2,1)}, u32[]{:S(2)}) copy-start(bf16[2,256,768]{2,1,0:T(8,128)(2,1)} %get-tuple-element.144) | copy-start | bytes 2359300
  447.6 3.5 copy-start.2
  450.1 2.0 copy-start.1
Sparse Core Ops, SparseCore 0:
  13.0 59.8 all-gather.4
  75.6 54.9 all-gather.6

commit v8 on v7

--- a/solution.py
+++ b/solution.py
@@ -54,9 +54,9 @@
     return lax.dot_general(left, right, TN, preferred_element_type=F32)
 
 
-def params(collective_id):
+def params(collective_id, limit=VMEM_LIMIT):
     return pltpu.CompilerParams(
-        vmem_limit_bytes=VMEM_LIMIT, collective_id=collective_id, has_side_effects=True
+        vmem_limit_bytes=limit, collective_id=collective_id, has_side_effects=True
     )
 
 
@@ -749,7 +749,7 @@
         + [pltpu.VMEM((CTX, 8, LANES), F32)] * 2
         + [SEMS((3,))] * 4
         + [SEMS((6,))] * 8,
-        compiler_params=params(8),
+        compiler_params=params(8, 37 * 1024 * 1024),
         name="sum_shards",
     )(by_place(lower_e), by_place(lower_a), upper_half, lower_out, upper_out, lower_grad, upper_grad)
 
@@ -1839,13 +1839,15 @@
     in_old, out_old, attn_old, gain_old, router_old = (refs[at : at + 3] for at in range(0, 15, 3))
     in_new, out_new, attn_new, gain_new, router_new = (refs[at : at + 5] for at in range(15, 40, 5))
     norms_ref, turned, wide = refs[40:]
-    turned[pl.ds(0, D, 2), :] = in_sum_ref[0, :, :LANES].astype(F32)
-    turned[pl.ds(1, D, 2), :] = in_sum_ref[0, :, LANES:].astype(F32)
+    turned[pl.ds(0, D // 2, 2), :] = in_sum_ref[0, :, :LANES].astype(F32)
+    turned[pl.ds(1, D // 2, 2), :] = in_sum_ref[0, :, LANES:].astype(F32)
+    part_rows = LANES // 2
+    start = lax.rem(pl.program_id(0), 2) * part_rows
     updated(
         fixes_ref, turned[...], factor_of(squares_ref, 3), in_old, in_new, RATE_FACTOR / D**0.5
     )
     pieces = [
-        out_sum_ref[0, piece * LANES : (piece + 1) * LANES, :].astype(F32)
+        out_sum_ref[0, pl.ds(pl.multiple_of(piece * LANES + start, part_rows), part_rows), :].astype(F32)
         for piece in range(D // UNIT)
     ]
     updated(
@@ -1908,8 +1910,8 @@
 def update(fixes, squares, sums_all, in_old, out_old, attn_old, gain_old, router_old):
     in_rows, units = 2 * D, LANES
     in_shape, out_shape, attn_shape = (CTX * in_rows, units), (CTX, units, D), (48, 4 * D)
-    in_spec = pl.BlockSpec((in_rows, units), lambda i: (i, 0))
-    out_spec = pl.BlockSpec((1, units, D), lambda i: (i, 0, 0))
+    in_spec = pl.BlockSpec((D, units), lambda i: (i, 0))
+    out_spec = pl.BlockSpec((1, units // 2, D), lambda i: (i // 2, i % 2, 0))
     attn_spec = whole(attn_shape)
     gain_shape, router_shape = (2, 48), (EXPERTS, 1, 48)
 
@@ -1918,7 +1920,7 @@
 
     return pl.pallas_call(
         update_kernel,
-        grid=(CTX,),
+        grid=(2 * CTX,),
         out_shape=five(in_shape)
         + five(out_shape)
         + five(attn_shape)
@@ -1928,8 +1930,8 @@
         in_specs=[
             SMEM,
             whole((8, LANES)),
-            pl.BlockSpec((1, D, UNIT), lambda i: (i, 0, 0)),
-            pl.BlockSpec((1, D // 2, UNIT), lambda i: (i, 2, 0)),
+            pl.BlockSpec((1, D // 2, UNIT), lambda i: (i // 2, i % 2, 0)),
+            pl.BlockSpec((1, D // 2, UNIT), lambda i: (i // 2, 2, 0)),
             pl.BlockSpec((CTX, ATTN_ROWS, UNIT), lambda i: (0, EXPERT_ROWS // ATTN_ROWS, 0)),
         ]
         + [in_spec] * 3
@@ -1943,8 +1945,8 @@
         + [whole(gain_shape)] * 5
         + [whole(router_shape)] * 5
         + [whole((8, LANES))],
-        scratch_shapes=[pltpu.VMEM((in_rows, units), F32), pltpu.VMEM(attn_shape, F32)],
-        compiler_params=pltpu.CompilerParams(vmem_limit_bytes=VMEM_LIMIT),
+        scratch_shapes=[pltpu.VMEM((D, units), F32), pltpu.VMEM(attn_shape, F32)],
+        compiler_params=pltpu.CompilerParams(vmem_limit_bytes=30 * 1024 * 1024),
         name="update",
     )(
         fixes, squares, sums_all, sums_all, sums_all,

time: 463 us -> 456 us (0.985)
  Pallas kernels: 425 us -> 415 us
    unnamed x25 -> x59, local copies, waits for them, and re-layouts: 3.6 us -> 9.76 us
    pallas_call x1, Pallas kernels: 17.9 us -> 12.3 us  [update(): pl.pallas_call(update_kernel, grid=(2 * CTX,), out_shape=five(in_shape) +...]
  transfers between devices with their start and end apart: 3 -> 3, of which waited for: 1 -> 1; matrix products, arithmetic and copies ran while one was open for 2% -> 1% of each run, Pallas kernels for 32% -> 32%
where the time goes in v8:
time: 456 us; the launch traced here: 453 us
  Pallas kernels  415 us (91%)
  local copies, waits for them, and re-layouts  16.8 us (4%)
  between operations  15.7 us (3%)
    pallas_call x2, Pallas kernels, attn_backward(): pl.pallas_call(functools.partial(attn_backward_kernel, bool(upper)), out_...  88.6 us
    pallas_call x2, Pallas kernels, attn_forward(): pl.pallas_call(functools.partial(attn_forward_kernel, layer), out_shape=(...  71.5 us
    pallas_call x1, Pallas kernels, sum_shards(): pl.pallas_call(sum_shards_kernel, out_shape=(jax.ShapeDtypeStruct((CTX, S...  63.4 us
    pallas_call x1, Pallas kernels, ffn_both(): pl.pallas_call(ffn_both_kernel, out_shape=(jax.ShapeDtypeStruct((ROWS, D)...  62.6 us
    pallas_call x1, Pallas kernels, ffn_backward(): pl.pallas_call(functools.partial(ffn_backward_kernel, bool(upper)), out_s...  43.7 us
    pallas_call x1, Pallas kernels, ffn_forward(): pl.pallas_call(ffn_forward_kernel, out_shape=(jax.ShapeDtypeStruct((ROWS,...  36.8 us
    pallas_call x1, Pallas kernels, gather_shards(): pl.pallas_call(gather_shards_kernel, out_shape=(jax.ShapeDtypeStruct((2,...  36.3 us
    pallas_call x1, Pallas kernels, update(): pl.pallas_call(update_kernel, grid=(2 * CTX,), out_shape=five(in_shape) +...  12.3 us
  transfers between devices with their start and end apart: 3, of which 1 were waited for; matrix products, arithmetic and copies ran while one was open for 1% of the time, Pallas kernels for 32%

profile of v8, /device:TPU:0, one launch (start us, length us, event | category | flops | bytes accessed | tf_op | source)
XLA Modules:
  0.0 452.8 jit_solution(7067533870495156116)
XLA Ops:
  7.2 0.0 copy-start
  7.2 0.0 all-gather.5.cloned.1.call-start
  7.3 1.5 dynamic-slice_convert_fusion
  8.7 0.2 slice.55
  9.0 1.0 fusion
  10.0 0.1 copy.82
  10.1 0.0 copy-start.10
  10.1 0.0 copy-start.17
  10.1 0.0 copy-start.20
  10.1 0.1 bitcast_select_fusion.2
  10.2 0.0 copy-start.26
  10.2 0.0 copy-start.25
  10.2 0.0 copy-start.23
  10.2 0.1 collective-permute-start
  10.3 1.6 collective-permute-done
  11.9 0.9 broadcast_select_fusion
  12.8 0.0 all-gather.5.cloned.1.call-update
  12.8 0.0 all-gather.7.cloned.1.call-start
  12.9 0.7 all-gather.7.cloned.1.call-update
  13.6 0.0 copy-done.10
  13.6 0.1 copy.61
  13.7 0.0 copy-done.20
  13.8 0.1 copy.62
  13.9 0.1 fusion.3
  14.0 0.1 concatenate.7
  14.1 0.2 convert_element_type.30
  14.3 0.7 copy.63
  15.7 0.0 copy-done.26
  15.7 0.6 dynamic_slice.33.length_ref
  16.3 0.6 pad.4.code_ref
  16.9 0.7 add_compare_fusion
  17.6 0.9 bitcast_select_fusion.seed_ref.delta_ref
  18.4 36.3 %gather_shards.1 = (bf16[2,4,4,288,256]{4,3,2,1,0:T(8,128)(2,1)}, f32[2,4,8,256]{3,2,1,0:T(8,128)}, bf16[4,256,768]{2,1,0:T(8,128)(2,1)}) custom-call(bf16[288,256]{1,0:T(8,128)(2,1)} %bitcast.121, f32[8,256]{1,0:T(8,128)} %pad.4.code_ref, bf16[256,768]{1,0:T(8,128)(2,1)} %bitcast_select_fusion.seed_ref.delta_ref), custom_call_target="tpu_custom_call" | custom-call | tf_op jit(solution)/shard_map/gather_shards/pallas_call | solution.py:425
  54.8 0.8 dynamic-slice_bitcast_fusion.u_ref
  55.5 37.4 %attn_forward.2 = (bf16[1024,768]{1,0:T(8,128)(2,1)}, bf16[1024,1152]{1,0:T(8,128)(2,1)}, f32[3,1024,1]{2,1,0:T(8,128)}, bf16[4,256,192]{2,1,0:T(8,128)(2,1)}, f...) custom-call(s32[1]{0:T(128)} %dynamic_slice.33.length_ref, ...), custom_call_target="tpu_custom_call" | custom-call | tf_op jit(solution)/shard_map/attn_forward/pallas_call | solution.py:896
  93.0 0.1 maximum_divide_fusion.fixes_ref
  93.1 0.6 slice_bitcast_fusion
  93.7 36.8 %ffn_forward.1 = (bf16[256,768]{1,0:T(8,128)(2,1)}, bf16[4,256,768]{2,1,0:T(8,128)(2,1)}, f32[256,128]{1,0:T(8,128)}, f32[4,256,1]{2,1,0:T(8,128)}, bf16[4,16,256,256]{3,2,1,0:T(8,128)(2,1)}) custom-call(bf16[256,768]{1,0:T(8,128)(2,1)} %get-tuple-element.102.b_own_ref.second_in, f32[256,768]{1,0:T(8,128)} %get-tuple-element.103.residual_ref, ...), custom_call_target="tpu_custom_call" | custom-call | tf_op jit(solution)/shard_map/ffn_forward/pallas_call | solution.py:1330
  130.5 34.0 %attn_forward.3 = (bf16[1024,768]{1,0:T(8,128)(2,1)}, bf16[1024,1152]{1,0:T(8,128)(2,1)}, f32[3,1024,1]{2,1,0:T(8,128)}, bf16[4,256,192]{2,1,0:T(8,128)(2,1)}, f...) custom-call(s32[1]{0:T(128)} %dynamic_slice.33.length_ref, ...), custom_call_target="tpu_custom_call" | custom-call | tf_op jit(solution)/shard_map/attn_forward/pallas_call | solution.py:896
  164.6 0.0 all-gather.7.cloned.1.call-done
  164.6 62.6 %ffn_both.1 = (bf16[256,768]{1,0:T(8,128)(2,1)}, f32[256,128]{1,0:T(8,128)}, f32[256,768]{1,0:T(8,128)}, f32[256,128]{1,0:T(8,128)}, bf16[16,1152,256]{2,1,0:T(8,128)(2,1)}) custom-call(bf16[256,768]{1,0:T(8,128)(2,1)} %get-tuple-element.118.b_own_ref.second_in, f32[256,768]{1,0:T(8,128)} %get-tuple-element.117.residual_ref, ...), custom_call_target="tpu_custom_call" | custom-call | tf_op jit(solution)/shard_map/ffn_both/pallas_call | solution.py:1735
  227.2 35.4 %attn_backward.2 = (f32[256,768]{1,0:T(8,128)}, bf16[16,288,256]{2,1,0:T(8,128)(2,1)}, bf16[256,768]{1,0:T(8,128)(2,1)}) custom-call(s32[1]{0:T(128)} %dynamic_slice.33.length_ref, bf16[256,768]{1,0:T(8,128)(2,1)} %get-tuple-element.108.u_ref.lower_out_ref, f32[8,768]{1,0:T(8,128)} %get-tuple-element.109.gains_ref, ...), custom_call_target="tpu_custom_call" | custom-call | tf_op jit(solution)/shard_map/attn_backward/pallas_call | solution.py:1193
  262.6 43.7 %ffn_backward.1 = (f32[256,768]{1,0:T(8,128)}, f32[256,128]{1,0:T(8,128)}, bf16[16,1152,256]{2,1,0:T(8,128)(2,1)}, bf16[16,720,256]{2,1,0:T(8,128)(2,1)}) custom-call(bf16[4,256,768]{2,1,0:T(8,128)(2,1)} %get-tuple-element.106.b_ref, f32[4,256,1]{2,1,0:T(8,128)} %get-tuple-element.107.gate_ref, bf16[256,768]{1,0:T(8,128)(2,1)} %get-tuple-element.123.delta_own_ref.delta_ref, ...), custom_call_target="tpu_custom_call" | custom-call | tf_op jit(solution)/shard_map/ffn_backward/pallas_call | solution.py:1536
  306.4 53.2 %attn_backward.3 = (f32[256,768]{1,0:T(8,128)}, bf16[16,288,256]{2,1,0:T(8,128)(2,1)}, bf16[256,768]{1,0:T(8,128)(2,1)}, bf16[720,256]{1,0:T(8,128)(2,1)}) custom-call(s32[1]{0:T(128)} %dynamic_slice.33.length_ref, bf16[256,768]{1,0:T(8,128)(2,1)} %dynamic-slice_bitcast_fusion.u_ref, f32[8,768]{1,0:T(8,128)} %get-tuple-element.128.gains_ref, ...), custom_call_target="tpu_custom_call" | custom-call | tf_op jit(solution)/shard_map/attn_backward/pallas_call | solution.py:1193
  359.7 1.7 copy-done.6
  361.3 1.1 copy-done.12
  362.5 1.0 copy-done.15
  363.5 1.0 copy-done.16
  364.5 0.0 copy-start.8
  364.5 0.0 copy-start.9
  364.5 0.0 copy-start.18
  364.5 0.0 copy-start.19
  364.5 0.0 copy-start.21
  364.5 0.0 copy-start.22
  364.5 63.4 %sum_shards.1 = (bf16[4,1440,256]{2,1,0:T(8,128)(2,1)S(1)}, f32[8,128]{1,0:T(8,128)S(1)}, bf16[2,256,768]{2,1,0:T(8,128)(2,1)S(1)}, f32[2,256,768]{2,1,0:T(8,128)S(1)}) custom-call(bf16[4,4,1152,256]{3,2,1,0:T(8,128)(2,1)} %bitcast.112, bf16[4,4,288,256]{3,2,1,0:T(8,128)(2,1)S(1)} %bitcast.89, bf16[720,256]{1,0:T(8,128)(2,1)S(1)} %copy-done.16, ...), custom_call_target="tpu_custom_call" | custom-call | tf_op jit(solution)/shard_map/sum_shards/pallas_call | solution.py:728
  428.0 0.0 copy-start.13
  428.0 1.1 copy-done.13
  429.1 1.1 copy-done.14
  430.1 12.3 %update.1 = (f32[6144,128]{1,0:T(8,128)}, f32[6144,128]{1,0:T(8,128)}, f32[6144,128]{1,0:T(8,128)}, f32[6144,128]{1,0:T(8,128)}, bf16[6144,128]{1,0:T(8,128)(2,1...) custom-call(f32[2]{0:T(128)S(1)} %maximum_divide_fusion.fixes_ref, ...), custom_call_target="tpu_custom_call" | custom-call | tf_op jit(solution)/shard_map/update/pallas_call | solution.py:1921
  442.5 0.6 copy.66
  443.0 0.5 slice.53
  443.5 0.9 copy.86
  444.4 1.1 copy.87
  445.6 0.0 copy-done.1
  (38 shorter events, 0.1 us)
Async XLA Ops:
  7.2 47.5 %copy-start = (bf16[2,256,768]{2,1,0:T(8,128)(2,1)S(1)}, bf16[2,256,768]{2,1,0:T(8,128)(2,1)}, u32[]{:S(2)}) copy-start(bf16[2,256,768]{2,1,0:T(8,128)(2,1)} %param.21) | copy-start | bytes 2359300
  7.2 86.5 %all-gather.5.cloned.1.call-start = ((), (), s32[]{:S(2)}) async-start(), calls=%async_computation | async-start | bytes 9732096 | tf_op jit(solution)/shard_map/all_gather | solution.py:2013
  10.1 3.5 copy-start.10
  10.1 3.5 copy-start.17
  10.1 3.6 copy-start.20
  10.2 5.5 %copy-start.26 = (s32[2]{0:T(128)S(1)}, s32[2]{0:T(128)}, u32[]{:S(2)}) copy-start(s32[2]{0:T(128)} %param.23) | copy-start | bytes 28
  10.2 6.1 %copy-start.25 = (s32[1,2,256,2]{2,3,1,0:T(2,128)S(1)}, s32[1,2,256,2]{2,3,1,0:T(2,128)}, u32[]{:S(2)}) copy-start(s32[1,2,256,2]{2,3,1,0:T(2,128)} %param.24) | copy-start | bytes 12292
  10.2 7.4 %copy-start.23 = (bf16[2,256,768]{2,1,0:T(8,128)(2,1)S(1)}, bf16[2,256,768]{2,1,0:T(8,128)(2,1)}, u32[]{:S(2)}) copy-start(bf16[2,256,768]{2,1,0:T(8,128)(2,1)} %param.22) | copy-start | bytes 2359300
  10.2 1.7 collective-permute-start
  12.8 151.7 %all-gather.7.cloned.1.call-start = ((), (), s32[]{:S(2)}) async-start(), calls=%async_computation.1 | async-start | bytes 9732096 | tf_op jit(solution)/shard_map/all_gather | solution.py:2013
  55.5 37.5 %copy-start.24 = (f32[2,4,8,256]{3,2,1,0:T(8,128)S(1)}, f32[2,4,8,256]{3,2,1,0:T(8,128)}, u32[]{:S(2)}) copy-start(f32[2,4,8,256]{3,2,1,0:T(8,128)} %get-tuple-element.104) | copy-start | bytes 196612
  306.4 53.3 %copy-start.3 = (bf16[256,768]{1,0:T(8,128)(2,1)S(1)}, bf16[256,768]{1,0:T(8,128)(2,1)}, u32[]{:S(2)}) copy-start(bf16[256,768]{1,0:T(8,128)(2,1)} %get-tuple-element.108.u_ref.lower_out_ref) | copy-start | bytes 1179652
  306.4 53.3 %copy-start.11 = (f32[256,768]{1,0:T(8,128)S(1)}, f32[256,768]{1,0:T(8,128)}, u32[]{:S(2)}) copy-start(f32[256,768]{1,0:T(8,128)} %get-tuple-element.143.upper_grad_ref) | copy-start | bytes 2359300
  359.7 1.7 copy-start.6
  361.3 1.1 copy-start.12
  362.5 1.0 copy-start.15
  363.5 1.0 copy-start.16
  364.4 63.4 %copy-start.2 = (f32[1,4,768,2,128]{4,3,2,1,0:T(2,128)S(1)}, f32[1,4,768,2,128]{4,3,2,1,0:T(2,128)}, u32[]{:S(2)}) copy-start(f32[1,4,768,2,128]{4,3,2,1,0:T(2,128)} %param.35) | copy-start | bytes 9437188
  364.4 63.5 %copy-start.4 = (f32[1,4,768,2,128]{4,3,2,1,0:T(2,128)S(1)}, f32[1,4,768,2,128]{4,3,2,1,0:T(2,128)}, u32[]{:S(2)}) copy-start(f32[1,4,768,2,128]{4,3,2,1,0:T(2,128)} %param.36) | copy-start | bytes 9437188
  364.5 63.5 %copy-start.5 = (f32[1,4,768,2,128]{4,3,2,1,0:T(2,128)S(1)}, f32[1,4,768,2,128]{4,3,2,1,0:T(2,128)}, u32[]{:S(2)}) copy-start(f32[1,4,768,2,128]{4,3,2,1,0:T(2,128)} %param.37) | copy-start | bytes 9437188
  364.5 63.5 %copy-start.7 = (f32[1,4,128,768]{3,2,1,0:T(8,128)S(1)}, f32[1,4,128,768]{3,2,1,0:T(8,128)}, u32[]{:S(2)}) copy-start(f32[1,4,128,768]{3,2,1,0:T(8,128)} %param.38) | copy-start | bytes 4718596
  364.5 63.5 %copy-start.8 = (f32[1,4,128,768]{3,2,1,0:T(8,128)S(1)}, f32[1,4,128,768]{3,2,1,0:T(8,128)}, u32[]{:S(2)}) copy-start(f32[1,4,128,768]{3,2,1,0:T(8,128)} %param.39) | copy-start | bytes 4718596
  364.5 63.5 %copy-start.9 = (f32[1,4,128,768]{3,2,1,0:T(8,128)S(1)}, f32[1,4,128,768]{3,2,1,0:T(8,128)}, u32[]{:S(2)}) copy-start(f32[1,4,128,768]{3,2,1,0:T(8,128)} %param.40) | copy-start | bytes 4718596
  364.5 63.5 %copy-start.18 = (f32[1,48,3]{1,0,2:T(1,128)S(1)}, f32[1,48,3]{1,0,2:T(1,128)}, u32[]{:S(2)}) copy-start(f32[1,48,3]{1,0,2:T(1,128)} %param.33) | copy-start | bytes 1732
  364.5 63.5 %copy-start.19 = (f32[1,48,3]{1,0,2:T(1,128)S(1)}, f32[1,48,3]{1,0,2:T(1,128)}, u32[]{:S(2)}) copy-start(f32[1,48,3]{1,0,2:T(1,128)} %param.34) | copy-start | bytes 1732
  364.5 63.5 %copy-start.21 = (f32[1,2,48]{2,1,0:T(2,128)S(1)}, f32[1,2,48]{2,1,0:T(2,128)}, u32[]{:S(2)}) copy-start(f32[1,2,48]{2,1,0:T(2,128)} %param.27) | copy-start | bytes 1156
  364.5 63.5 %copy-start.22 = (f32[1,2,48]{2,1,0:T(2,128)S(1)}, f32[1,2,48]{2,1,0:T(2,128)}, u32[]{:S(2)}) copy-start(f32[1,2,48]{2,1,0:T(2,128)} %param.28) | copy-start | bytes 1156
  428.0 1.1 copy-start.13
  429.1 1.1 copy-start.14
  443.5 2.0 copy-start.1
Sparse Core Ops, SparseCore 0:
  13.0 60.4 all-gather.4
  76.3 55.0 all-gather.6
